TPU v7x, 32 devices: a whole 2x2x4 slice. The times are simulated.
32 devices in a mesh: groups: 2 (over x), blk: 8 (over z, y), mand: 2 (over core).
Axes of the slice: x: 2, y: 2, z: 4, core: 2. Of those that a mesh axis runs over, the one named last changes fastest.
Arguments:
- holdings: float32 [256, 8192], P(('groups', 'mand'), 'blk'), parts along dimension 0, may hold values from -6 to 6
- eligible: int32 [256, 8192], P(('groups', 'mand'), 'blk'), parts along dimension 0, may hold values 0 or 1
- returns_mu: float32 [16384], P(('groups', 'blk')), parts along dimension 0, may hold values from -6 to 6
- cov_diag: bfloat16 [64, 256, 256], P(('groups', 'blk')), parts along dimension 0, as said below
- cov_pairs: bfloat16 [1024, 256, 256], P(('groups', 'blk')), parts along dimension 0, may hold values from -0.0625 to 0.0625
- pair_slots: int32 [16, 64, 2], P(('groups', 'blk')), parts along dimension 0, may hold values from 0 to 15, as said below
- need_table: int32 [16, 8, 2], P('groups'), parts along dimension 0, may hold values from -1 to 3, as said below
- break_index: int32 [64], P(('groups', 'blk')), parts along dimension 0, may hold values from 0 to 7
- break_levels: float32 [8], replicated, may hold values from 0.1 to 1
- cost_slopes: float32 [2, 128], P(None, 'mand'), may hold values from 0.05 to 0.5
Outputs:
- traded: float32 [256, 8192], P(('groups', 'mand'), 'blk'), parts along dimension 0
- dual: float32 [256, 8192], P(('groups', 'mand'), 'blk'), parts along dimension 0
There are 2 independent parts, one for each index of `groups`. A program takes and returns all parts, laid end to end along the dimension named above; an argument that names none is the same for every part. Nothing has to cross between parts.
Inputs may be any that keep to these rules, and one draw needn't show every extreme that they name: need_table[o, r, :] holds distinct local block indices of device r that device o needs, then -1 for the rest; every device needs all 2 slots from itself; some device needs 2 blocks from every device. `pair_slots`: each pair's two slot numbers differ and name non-empty entries of its device's need_table row; every non-empty entry is named by some pair of that device. `cov_diag`: each block is symmetric.
All inputs are finite; a program needn't handle non-finite values. No bound on the sum of `eligible` on one device may be relied on, other than what follows from the above.
Results may differ from a plain program's by a relative error of at most 0.0029.
Values may be sent and summed in bfloat16 or wider, within the bound.
No kernel may reach another device: no remote copies, remote signals or barrier semaphores. Data moves between devices by JAX's collectives and lax.ppermute only.
A program may use at most 128 MiB of HBM per device.

v0:
```python
import jax
import jax.numpy as jnp
from jax import lax
from jax.sharding import PartitionSpec as P

ITERS = 2


STEP_SIZE = 0.5
RISK_AVERSION = 1.0
PENALTY = 1.0


def trade_prox(values, slope_low, slope_high, cost_knee):
    magnitude = jnp.abs(values)
    lower_part = jnp.minimum(jnp.maximum(magnitude - slope_low, 0.0), cost_knee)
    upper_part = jnp.maximum(magnitude - slope_high - cost_knee, 0.0)
    return jnp.sign(values) * (lower_part + upper_part)


def body(
    holdings,
    eligible,
    returns_mu,
    cov_diag,
    cov_pairs,
    pair_slots,
    need_table,
    break_index,
    break_levels,
    cost_slopes,
):
    mand_rows = holdings.shape[0]
    blocks_dev = cov_diag.shape[0]
    block_size = cov_diag.shape[1]
    owners = lax.axis_size("blk")
    my_index = lax.axis_index("blk")
    capacity = need_table.shape[2]
    slot_total = owners * capacity

    def to_blocks(values):
        return values.reshape(mand_rows, blocks_dev, block_size).transpose(1, 0, 2)

    initial = to_blocks(holdings)
    allowed = to_blocks(eligible).astype(jnp.float32)
    expected = returns_mu.reshape(blocks_dev, 1, block_size)
    matches = break_index[:, None] == jnp.arange(break_levels.shape[0], dtype=jnp.int32)[None, :]
    cost_knee = jnp.sum(jnp.where(matches, break_levels[None, :], jnp.float32(0.0)), axis=1)[
        :, None, None
    ]
    slope_low = (cost_slopes[0] / PENALTY)[None, :, None]
    slope_high = ((cost_slopes[0] + cost_slopes[1]) / PENALTY)[None, :, None]
    served = lax.dynamic_index_in_dim(need_table, my_index, 1, keepdims=False).reshape(-1)
    picked_ids = jnp.maximum(served, 0)
    served_live = served >= 0
    first_slot = pair_slots[0, :, 0]
    second_slot = pair_slots[0, :, 1]
    primal = initial
    traded = initial
    dual = jnp.zeros_like(initial)
    for iteration in range(ITERS):
        x_wire = primal.astype(jnp.bfloat16)
        risk_grad = jnp.einsum("bmj,bjk->bmk", x_wire, cov_diag, preferred_element_type=jnp.float32)
        outgoing = jnp.take(x_wire, picked_ids, axis=0).reshape(
            owners, capacity, mand_rows, block_size
        )
        slot_rows = lax.all_to_all(
            outgoing, "blk", split_axis=0, concat_axis=0, tiled=True
        ).reshape(slot_total, mand_rows, block_size)
        to_first = jnp.einsum(
            "pmk,pjk->pmj", slot_rows[second_slot], cov_pairs, preferred_element_type=jnp.float32
        )
        to_second = jnp.einsum(
            "pmj,pjk->pmk", slot_rows[first_slot], cov_pairs, preferred_element_type=jnp.float32
        )
        partial_value = (
            jnp.zeros((slot_total, mand_rows, block_size), jnp.float32)
            .at[first_slot]
            .add(to_first)
            .at[second_slot]
            .add(to_second)
        )
        returned = lax.all_to_all(
            partial_value.reshape(owners, capacity, mand_rows, block_size),
            "blk",
            split_axis=0,
            concat_axis=0,
            tiled=True,
        )
        returned = returned.reshape(slot_total, mand_rows, block_size)
        kept = jnp.where(served_live[:, None, None], returned, jnp.float32(0.0))
        pair_terms = (
            jnp.zeros((blocks_dev, mand_rows, block_size), jnp.float32).at[picked_ids].add(kept)
        )
        grad = risk_grad + pair_terms
        primal = allowed * (
            primal
            - STEP_SIZE * (RISK_AVERSION * grad - expected + PENALTY * (primal - traded + dual))
        )
        shifted = primal + dual - initial
        traded = initial + trade_prox(shifted, slope_low, slope_high, cost_knee)
        dual = dual + primal - traded
    traded_out = traded.transpose(1, 0, 2).reshape(mand_rows, blocks_dev * block_size)
    dual_out = dual.transpose(1, 0, 2).reshape(mand_rows, blocks_dev * block_size)
    return (traded_out, dual_out)


def solution(mesh):
    placed = (
        P(("groups", "mand"), "blk"),
        P(("groups", "mand"), "blk"),
        P(("groups", "blk")),
        P(("groups", "blk"), None, None),
        P(("groups", "blk"), None, None),
        P(("groups", "blk"), None, None),
        P("groups", None, None),
        P(("groups", "blk")),
        P(),
        P(None, "mand"),
    )
    return jax.shard_map(
        body,
        mesh=mesh,
        in_specs=placed,
        out_specs=(P(("groups", "mand"), "blk"), P(("groups", "mand"), "blk")),
        check_vma=False,
    )
```

profile of v0, /device:TPU:0, one launch (start us, length us, event | category | flops | bytes accessed | tf_op | source)
XLA Modules:
  0.0 205.3 jit_solution(15724439658487341184)
XLA Ops:
  0.6 0.0 copy-start
  0.6 1.0 maximum_reduce_fusion
  1.7 0.1 reshape.216
  1.8 1.0 copy.44
  2.8 0.6 gather_fusion.4
  3.4 0.9 broadcast_select_fusion.1
  4.3 7.3 %all-to-all-start = ((bf16[8,2,64,256]{3,2,1,0:T(8,128)(2,1)}), bf16[8,2,64,256]{3,2,1,0:T(8,128)(2,1)S(1)}, u32[]{:S(2)}, u32[]{:S(2)}) async-start(bf16[8,2,64,256]{3,2,1,0:T(8,128)(2,1)} %bitcast.4), calls=%async_computation | async-start | bytes 1048576 | tf_op jit(solution)/shard_map/all_to_all | solution.py:67
  11.6 0.8 fusion.15
  12.3 0.0 copy-start.7
  12.4 13.7 %all-to-all-done = bf16[8,2,64,256]{3,2,1,0:T(8,128)(2,1)S(1)} async-done(((bf16[8,2,64,256]{3,2,1,0:T(8,128)(2,1)}), bf16[8,2,64,256]{3,2,1,0:T(8,128)(2,1)S(1)}, u32[]{:S(2)}, u32[]{:S(2)}) %all-to-all-start) | async-done | bytes 524320 | tf_op jit(solution)/shard_map/all_to_all | solution.py:67
  26.1 2.0 gather_fusion
  28.1 0.7 gather_fusion.1
  28.8 8.6 %fusion.19 = f32[64,64,256]{2,1,0:T(8,128)} fusion(bf16[64,64,256]{2,1,0:T(8,128)(2,1)} %gather_fusion, bf16[64,256,256]{2,1,0:T(8,128)(2,1)} %param.16), kind=kOutput, calls=%fused_computation.50 | convolution fusion | flops 536870912 | bytes 14680064 | tf_op jit(solution)/shard_map/pmk,pjk->pmj/dot_general | solution.py:70
  37.4 6.9 %fusion.20 = f32[64,64,256]{2,1,0:T(8,128)} fusion(bf16[64,64,256]{2,1,0:T(8,128)(2,1)S(1)} %gather_fusion.1, bf16[64,256,256]{2,1,0:T(8,128)(2,1)} %param.16), kind=kOutput, calls=%fused_computation.51 | convolution fusion | flops 536870912 | bytes 14680064 | tf_op jit(solution)/shard_map/pmj,pjk->pmk/dot_general | solution.py:73
  44.3 1.2 broadcast.82.clone
  45.5 13.2 %scatter_fusion = f32[16,64,256]{2,1,0:T(8,128)} fusion(f32[16,64,256]{2,1,0:T(8,128)} %broadcast.82.clone, s32[64]{0:T(128)S(1)} %get-tuple-element.6, f32[64,64,256]{2,1,0:T(8,128)} %fusion.19), kind=kCustom, calls=%fused_computation.6 | custom fusion | flops 1048576 | bytes 12583168 | tf_op jit(solution)/shard_map/scatter-add | solution.py:79
  58.7 13.2 %scatter_fusion.1 = f32[16,64,256]{2,1,0:T(8,128)} fusion(f32[16,64,256]{2,1,0:T(8,128)} %scatter_fusion, s32[64]{0:T(128)S(1)} %get-tuple-element.5, f32[64,64,256]{2,1,0:T(8,128)} %fusion.20), kind=kCustom, calls=%fused_computation.7 | custom fusion | flops 1048576 | bytes 12583168 | tf_op jit(solution)/shard_map/scatter-add | solution.py:81
  71.9 4.1 %all-to-all-start.1 = ((f32[8,2,64,256]{3,2,1,0:T(8,128)}), f32[8,2,64,256]{3,2,1,0:T(8,128)S(1)}, u32[]{:S(2)}, u32[]{:S(2)}) async-start(f32[8,2,64,256]{3,2,1,0:T(8,128)} %bitcast.8), calls=%async_computation.1 | async-start | bytes 2097152 | tf_op jit(solution)/shard_map/all_to_all | solution.py:83
  76.0 0.3 compare_reduce_fusion
  76.3 0.7 ge.15
  77.0 0.0 copy-start.3
  77.0 0.2 fusion.18
  77.2 24.7 %all-to-all-done.1 = f32[8,2,64,256]{3,2,1,0:T(8,128)S(1)} async-done(((f32[8,2,64,256]{3,2,1,0:T(8,128)}), f32[8,2,64,256]{3,2,1,0:T(8,128)S(1)}, u32[]{:S(2)}, u32[]{:S(2)}) %all-to-all-start.1) | async-done | bytes 1048608 | tf_op jit(solution)/shard_map/all_to_all | solution.py:83
  101.9 0.8 bitcast_select_fusion.1
  102.7 1.7 scatter_fusion.2
  104.5 0.1 fusion.13
  104.5 0.6 gather_fusion.5
  105.1 0.8 broadcast_select_fusion
  105.9 18.1 %all_to_all.20 = bf16[8,2,64,256]{3,2,1,0:T(8,128)(2,1)S(1)} all-to-all(bf16[8,2,64,256]{3,2,1,0:T(8,128)(2,1)S(1)} %bitcast.168), channel_id=1, replica_groups=mesh['groups'=2,'blk'=8,'mand'=2] {'blk'}, dimensions={0} | all-to-all | bytes 1048576 | tf_op jit(solution)/shard_map/all_to_all | solution.py:67
  124.0 2.2 %gather_fusion.2 = bf16[64,64,256]{2,1,0:T(8,128)(2,1)} fusion(bf16[16,64,256]{2,1,0:T(8,128)(2,1)S(1)} %bitcast.158, s32[1024]{0:T(1024)} %copy-done.7), kind=kCustom, calls=%fused_computation.4 | custom fusion | bytes 4194560 | tf_op jit(solution)/shard_map/gather | solution.py:71
  126.2 0.8 gather_fusion.3
  127.0 8.6 %fusion.22 = f32[64,64,256]{2,1,0:T(8,128)} fusion(bf16[64,64,256]{2,1,0:T(8,128)(2,1)} %gather_fusion.2, bf16[64,256,256]{2,1,0:T(8,128)(2,1)} %param.16), kind=kOutput, calls=%fused_computation.53 | convolution fusion | flops 536870912 | bytes 14680064 | tf_op jit(solution)/shard_map/pmk,pjk->pmj/dot_general | solution.py:70
  135.6 6.9 %fusion.23 = f32[64,64,256]{2,1,0:T(8,128)} fusion(bf16[64,64,256]{2,1,0:T(8,128)(2,1)S(1)} %gather_fusion.3, bf16[64,256,256]{2,1,0:T(8,128)(2,1)} %param.16), kind=kOutput, calls=%fused_computation.54 | convolution fusion | flops 536870912 | bytes 14680064 | tf_op jit(solution)/shard_map/pmj,pjk->pmk/dot_general | solution.py:73
  142.5 1.2 broadcast.82
  143.7 13.2 %scatter_fusion.3 = f32[16,64,256]{2,1,0:T(8,128)} fusion(f32[16,64,256]{2,1,0:T(8,128)} %broadcast.82, s32[64]{0:T(128)S(1)} %get-tuple-element.6, f32[64,64,256]{2,1,0:T(8,128)} %fusion.22), kind=kCustom, calls=%fused_computation.9 | custom fusion | flops 1048576 | bytes 12583168 | tf_op jit(solution)/shard_map/scatter-add | solution.py:79
  156.9 13.2 %scatter_fusion.4 = f32[16,64,256]{2,1,0:T(8,128)} fusion(f32[16,64,256]{2,1,0:T(8,128)} %scatter_fusion.3, s32[64]{0:T(128)S(1)} %get-tuple-element.5, f32[64,64,256]{2,1,0:T(8,128)} %fusion.23), kind=kCustom, calls=%fused_computation.10 | custom fusion | flops 1048576 | bytes 12583168 | tf_op jit(solution)/shard_map/scatter-add | solution.py:81
  170.1 4.1 %all-to-all-start.3 = ((f32[8,2,64,256]{3,2,1,0:T(8,128)}), f32[8,2,64,256]{3,2,1,0:T(8,128)S(1)}, u32[]{:S(2)}, u32[]{:S(2)}) async-start(f32[8,2,64,256]{3,2,1,0:T(8,128)} %bitcast.12), calls=%async_computation.3 | async-start | bytes 2097152 | tf_op jit(solution)/shard_map/all_to_all | solution.py:83
  174.2 0.2 select_reduce_fusion
  174.4 0.5 slice_bitcast_fusion
  174.9 0.2 fusion.21
  175.1 0.0 copy-start.11
  175.1 24.7 %all-to-all-done.3 = f32[8,2,64,256]{3,2,1,0:T(8,128)S(1)} async-done(((f32[8,2,64,256]{3,2,1,0:T(8,128)}), f32[8,2,64,256]{3,2,1,0:T(8,128)S(1)}, u32[]{:S(2)}, u32[]{:S(2)}) %all-to-all-start.3) | async-done | bytes 1048608 | tf_op jit(solution)/shard_map/all_to_all | solution.py:83
  199.8 0.8 bitcast_select_fusion
  200.6 1.6 scatter_fusion.5
  202.2 1.4 subtract_bitcast_fusion
  203.6 0.2 fusion.16
  203.8 0.7 copy.22
  204.5 0.7 copy.23
  (35 shorter events, 0.1 us)
Async XLA Ops:
  0.6 76.4 %copy-start = (bf16[4,256,256]{2,1,0:T(8,128)(2,1)S(1)}, bf16[4,256,256]{2,1,0:T(8,128)(2,1)}, u32[]{:S(2)}) copy-start(bf16[4,256,256]{2,1,0:T(8,128)(2,1)} %param.15) | copy-start | bytes 1572868
  1.8 1.0 copy-start.8
  1.8 10.5 %copy-start.12 = (pred[16]{0:T(512)(128)(4,1)}, pred[16]{0:T(512)(128)(4,1)S(1)}, u32[]{:S(2)}) copy-start(pred[16]{0:T(512)(128)(4,1)S(1)} %compare_and_fusion) | copy-start | bytes 52
  4.3 21.8 %all-to-all-start = ((bf16[8,2,64,256]{3,2,1,0:T(8,128)(2,1)}), bf16[8,2,64,256]{3,2,1,0:T(8,128)(2,1)S(1)}, u32[]{:S(2)}, u32[]{:S(2)}) async-start(bf16[8,2,64,256]{3,2,1,0:T(8,128)(2,1)} %bitcast.4), calls=%async_computation | async-start | bytes 1048576 | tf_op jit(solution)/shard_map/all_to_all | solution.py:67
  12.3 15.8 %copy-start.7 = (s32[1024]{0:T(1024)}, s32[1024]{0:T(1024)S(1)}, u32[]{:S(2)}) copy-start(s32[1024]{0:T(1024)S(1)} %get-tuple-element.8) | copy-start | bytes 12292
  12.4 16.4 %copy-start.6 = (s32[1024]{0:T(1024)}, s32[1024]{0:T(1024)S(1)}, u32[]{:S(2)}) copy-start(s32[1024]{0:T(1024)S(1)} %get-tuple-element.7) | copy-start | bytes 12292
  58.7 17.2 %copy-start.5 = (s32[8,8,2]{1,2,0:T(2,128)S(1)}, s32[8,8,2]{1,2,0:T(2,128)}, u32[]{:S(2)}) copy-start(s32[8,8,2]{1,2,0:T(2,128)} %param.18) | copy-start | bytes 1540
  58.7 18.2 %copy-start.4 = (s32[64,1024]{1,0:T(8,128)S(1)}, s32[64,1024]{1,0:T(8,128)}, u32[]{:S(2)}) copy-start(s32[64,1024]{1,0:T(8,128)} %param.13) | copy-start | bytes 786436
  58.7 18.2 %copy-start.10 = (f32[1024]{0:T(1024)S(1)}, f32[1024]{0:T(1024)}, u32[]{:S(2)}) copy-start(f32[1024]{0:T(1024)} %param.14) | copy-start | bytes 12292
  71.9 32.6 %copy-start.1 = (f32[64,1024]{1,0:T(8,128)S(1)}, f32[64,1024]{1,0:T(8,128)}, u32[]{:S(2)}) copy-start(f32[64,1024]{1,0:T(8,128)} %param.12) | copy-start | bytes 786436
  71.9 30.0 %all-to-all-start.1 = ((f32[8,2,64,256]{3,2,1,0:T(8,128)}), f32[8,2,64,256]{3,2,1,0:T(8,128)S(1)}, u32[]{:S(2)}, u32[]{:S(2)}) async-start(f32[8,2,64,256]{3,2,1,0:T(8,128)} %bitcast.8), calls=%async_computation.1 | async-start | bytes 2097152 | tf_op jit(solution)/shard_map/all_to_all | solution.py:83
  77.0 28.9 %copy-start.3 = (f32[64,1024]{1,0:T(8,128)}, f32[64,1024]{1,0:T(8,128)S(1)}, u32[]{:S(2)}) copy-start(f32[64,1024]{1,0:T(8,128)S(1)} %convert_element_type.15) | copy-start | bytes 786436
  156.9 17.2 %copy-start.14 = (f32[8]{0:T(128)S(1)}, f32[8]{0:T(128)}, u32[]{:S(2)}) copy-start(f32[8]{0:T(128)} %param.20) | copy-start | bytes 100
  156.9 17.3 %copy-start.15 = (s32[4]{0:T(128)S(1)}, s32[4]{0:T(128)}, u32[]{:S(2)}) copy-start(s32[4]{0:T(128)} %param.19) | copy-start | bytes 52
  156.9 17.4 %copy-start.13 = (f32[2,64]{1,0:T(2,128)S(1)}, f32[2,64]{1,0:T(2,128)}, u32[]{:S(2)}) copy-start(f32[2,64]{1,0:T(2,128)} %param.21) | copy-start | bytes 1540
  170.1 30.5 %copy-start.9 = (s32[16]{0:T(128)S(1)}, s32[16]{0:T(128)}, u32[]{:S(2)}) copy-start(s32[16]{0:T(128)} %copy-done.8) | copy-start | bytes 196
  170.1 32.1 %copy-start.2 = (f32[64,1024]{1,0:T(8,128)S(1)}, f32[64,1024]{1,0:T(8,128)}, u32[]{:S(2)}) copy-start(f32[64,1024]{1,0:T(8,128)} %param.12) | copy-start | bytes 786436
  170.1 29.7 %all-to-all-start.3 = ((f32[8,2,64,256]{3,2,1,0:T(8,128)}), f32[8,2,64,256]{3,2,1,0:T(8,128)S(1)}, u32[]{:S(2)}, u32[]{:S(2)}) async-start(f32[8,2,64,256]{3,2,1,0:T(8,128)} %bitcast.12), calls=%async_computation.3 | async-start | bytes 2097152 | tf_op jit(solution)/shard_map/all_to_all | solution.py:83
  175.1 27.1 %copy-start.11 = (f32[64]{0:T(128)S(1)}, f32[64]{0:T(128)}, u32[]{:S(2)}) copy-start(f32[64]{0:T(128)} %slice_bitcast_fusion) | copy-start | bytes 772
where the time goes:
time: 207 us; the launch traced here: 205 us
  other arithmetic  63.4 us (31%)
  waiting for transfers between devices  63 us (30%)
  matrix products  31.4 us (15%)
  blocking collectives  18.1 us (9%)
  starting transfers between devices  15.4 us (7%)
  local copies, waits for them, and re-layouts  13 us (6%)
    scatter-add x4, other arithmetic, body(): partial_value = jnp.zeros((slot_total, mand_rows, block_size), jnp.float3...  52.8 us
    all_to_all x2, waiting for transfers between devices, body(): lax.all_to_all(partial_value.reshape(owners, capacity, mand_rows, block_s...  49.3 us
    all_to_all x1, blocking collectives, body(): lax.all_to_all(outgoing, 'blk', split_axis=0, concat_axis=0, tiled=True)  18.1 us
    dot_general x2, matrix products, body(): jnp.einsum('pmk,pjk->pmj', slot_rows[second_slot], cov_pairs, preferred_e...  17.2 us
    dot_general x2, matrix products, body(): jnp.einsum('pmj,pjk->pmk', slot_rows[first_slot], cov_pairs, preferred_el...  13.7 us
    all_to_all x1, waiting for transfers between devices, body(): lax.all_to_all(outgoing, 'blk', split_axis=0, concat_axis=0, tiled=True)  13.7 us
    all_to_all x2, starting transfers between devices, body(): lax.all_to_all(partial_value.reshape(owners, capacity, mand_rows, block_s...  8.14 us
    all_to_all x1, starting transfers between devices, body(): lax.all_to_all(outgoing, 'blk', split_axis=0, concat_axis=0, tiled=True)  7.28 us
  transfers between devices with their start and end apart: 3, of which 3 were waited for; matrix products, arithmetic and copies ran while one was open for 1% of the time, Pallas kernels for 0%

commit v1 on v0

v1 whole, which is shorter than its diff:
```python
import functools

import jax
import jax.numpy as jnp
from jax import lax
from jax.experimental import pallas as pl
from jax.experimental.pallas import tpu as pltpu
from jax.sharding import PartitionSpec as P

ITERS = 2
STEP_SIZE = 0.5
RISK_AVERSION = 1.0
PENALTY = 1.0
CHUNKS = 8

VMEM = pl.BlockSpec(memory_space=pltpu.VMEM)
SMEM = pl.BlockSpec(memory_space=pltpu.SMEM)
ANY = pl.BlockSpec(memory_space=pl.ANY)
PARAMS = pltpu.CompilerParams(vmem_limit_bytes=48 * 1024 * 1024)


def fill_outgoing(served_ref, wire_ref, outgoing_ref):
    def one(slot, carry):
        outgoing_ref[slot] = wire_ref[jnp.maximum(served_ref[slot], 0)]
        return carry

    lax.fori_loop(0, outgoing_ref.shape[0], one, 0, unroll=4)


def pack_kernel(served_ref, holdings_ref, outgoing_ref, wire_ref):
    size = wire_ref.shape[2]
    for block in range(wire_ref.shape[0]):
        wire_ref[block] = holdings_ref[:, block * size : (block + 1) * size].astype(jnp.bfloat16)
    fill_outgoing(served_ref, wire_ref, outgoing_ref)


def pairs_kernel(pairs_ref, rows_ref, cov_ref, partial_ref, cov_vmem, total, sems):
    pairs = cov_ref.shape[0]
    step = pairs // CHUNKS
    copies = [
        pltpu.make_async_copy(
            cov_ref.at[pl.ds(chunk * step, step)],
            cov_vmem.at[pl.ds(chunk * step, step)],
            sems.at[chunk],
        )
        for chunk in range(CHUNKS)
    ]
    for copy in copies:
        copy.start()
    total[...] = jnp.zeros_like(total)
    for chunk, copy in enumerate(copies):
        copy.wait()

        def one(pair, carry):
            first = pairs_ref[0, pair, 0]
            second = pairs_ref[0, pair, 1]
            block = cov_vmem[pair]
            to_first = lax.dot_general(
                rows_ref[second], block, (((1,), (1,)), ((), ())), preferred_element_type=jnp.float32
            )
            to_second = jnp.dot(rows_ref[first], block, preferred_element_type=jnp.float32)
            total[first] += to_first
            total[second] += to_second
            return carry

        lax.fori_loop(chunk * step, (chunk + 1) * step, one, 0, unroll=4)
    partial_ref[...] = total[...].astype(jnp.bfloat16)


def column(row, rows):
    square = (rows, rows)
    on_diagonal = lax.broadcasted_iota(jnp.int32, square, 0) == lax.broadcasted_iota(jnp.int32, square, 1)
    return jnp.sum(jnp.where(on_diagonal, row, 0.0), axis=1, keepdims=True)


def update_kernel(
    last,
    served_ref,
    knee_index_ref,
    knee_levels_ref,
    returned_ref,
    slopes_ref,
    holdings_ref,
    eligible_ref,
    expected_ref,
    diag_ref,
    *refs,
):
    if last:
        primal_ref, traded_ref, dual_ref, traded_out, dual_out, terms = refs
    else:
        primal_out, traded_out, dual_out, outgoing_ref, terms, wire_ref = refs
    blocks, rows, size = terms.shape
    terms[...] = jnp.zeros_like(terms)

    def one(slot, carry):
        local = served_ref[slot]

        @pl.when(local >= 0)
        def _():
            terms[local] += returned_ref[slot].astype(jnp.float32)

        return carry

    lax.fori_loop(0, returned_ref.shape[0], one, 0, unroll=4)
    low = column(slopes_ref[0:1, :] / PENALTY, rows)
    high = column((slopes_ref[0:1, :] + slopes_ref[1:2, :]) / PENALTY, rows)
    for block in range(blocks):
        span = pl.ds(block * size, size)
        initial = holdings_ref[:, span]
        primal = primal_ref[:, span] if last else initial
        x_wire = primal.astype(jnp.bfloat16)
        grad = jnp.dot(x_wire, diag_ref[block], preferred_element_type=jnp.float32) + terms[block]
        expected = expected_ref[:, span]
        allowed = eligible_ref[:, span].astype(jnp.float32)
        if last:
            dual = dual_ref[:, span]
            gap = primal - traded_ref[:, span] + dual
        else:
            dual = jnp.zeros_like(initial)
            gap = dual
        primal = allowed * (primal - STEP_SIZE * (RISK_AVERSION * grad - expected + PENALTY * gap))
        shifted = primal + dual - initial
        knee = knee_levels_ref[knee_index_ref[block]]
        magnitude = jnp.abs(shifted)
        moved = jnp.minimum(jnp.maximum(magnitude - low, 0.0), knee) + jnp.maximum(
            magnitude - high - knee, 0.0
        )
        traded = initial + jnp.where(shifted < 0.0, -moved, moved)
        traded_out[:, span] = traded
        dual_out[:, span] = dual + primal - traded
        if not last:
            primal_out[:, span] = primal
            wire_ref[block] = primal.astype(jnp.bfloat16)
    if not last:
        fill_outgoing(served_ref, wire_ref, outgoing_ref)


def body(
    holdings,
    eligible,
    returns_mu,
    cov_diag,
    cov_pairs,
    pair_slots,
    need_table,
    break_index,
    break_levels,
    cost_slopes,
):
    rows, assets = holdings.shape
    blocks, size, _ = cov_diag.shape
    owners = lax.axis_size("blk")
    my_index = lax.axis_index("blk")
    capacity = need_table.shape[2]
    slots = owners * capacity
    served = lax.dynamic_index_in_dim(need_table, my_index, 1, keepdims=False).reshape(-1)
    slot_shape = (slots, rows, size)
    wire_shape = pltpu.VMEM((blocks, rows, size), jnp.bfloat16)
    whole = jax.ShapeDtypeStruct((rows, assets), jnp.float32)
    outgoing_shape = jax.ShapeDtypeStruct(slot_shape, jnp.bfloat16)

    def exchange(values):
        sent = values.reshape(owners, capacity, rows, size)
        return lax.all_to_all(sent, "blk", split_axis=0, concat_axis=0, tiled=True).reshape(slot_shape)

    outgoing = pl.pallas_call(
        pack_kernel,
        out_shape=outgoing_shape,
        in_specs=[SMEM, VMEM],
        out_specs=VMEM,
        scratch_shapes=[wire_shape],
        compiler_params=PARAMS,
        name="pack_holdings",
    )(served, holdings)
    expected = returns_mu.reshape(1, assets)
    state = ()
    for iteration in range(ITERS):
        last = iteration == ITERS - 1
        slot_rows = exchange(outgoing)
        partial_sums = pl.pallas_call(
            pairs_kernel,
            out_shape=outgoing_shape,
            in_specs=[SMEM, VMEM, ANY],
            out_specs=VMEM,
            scratch_shapes=[
                pltpu.VMEM(cov_pairs.shape, jnp.bfloat16),
                pltpu.VMEM(slot_shape, jnp.float32),
                pltpu.SemaphoreType.DMA((CHUNKS,)),
            ],
            compiler_params=PARAMS,
            name="pair_products",
        )(pair_slots, slot_rows, cov_pairs)
        returned = exchange(partial_sums)
        outs = pl.pallas_call(
            functools.partial(update_kernel, last),
            out_shape=(whole, whole) if last else (whole, whole, whole, outgoing_shape),
            in_specs=[SMEM] * 3 + [VMEM] * (6 + len(state)),
            out_specs=(VMEM,) * (2 if last else 4),
            scratch_shapes=[pltpu.VMEM((blocks, rows, size), jnp.float32)] + ([] if last else [wire_shape]),
            compiler_params=PARAMS,
            name="update",
        )(
            served,
            break_index,
            break_levels,
            returned,
            cost_slopes,
            holdings,
            eligible,
            expected,
            cov_diag,
            *state,
        )
        if not last:
            *state, outgoing = outs
    return outs


def solution(mesh):
    placed = (
        P(("groups", "mand"), "blk"),
        P(("groups", "mand"), "blk"),
        P(("groups", "blk")),
        P(("groups", "blk"), None, None),
        P(("groups", "blk"), None, None),
        P(("groups", "blk"), None, None),
        P("groups", None, None),
        P(("groups", "blk")),
        P(),
        P(None, "mand"),
    )
    return jax.shard_map(
        body,
        mesh=mesh,
        in_specs=placed,
        out_specs=(P(("groups", "mand"), "blk"), P(("groups", "mand"), "blk")),
        check_vma=False,
    )
```

time: 207 us -> 99.6 us (0.48)
  other arithmetic: 63.4 us -> 0 us
  waiting for transfers between devices: 63 us -> 13.7 us
  blocking collectives: 18.1 us -> 53.1 us
  matrix products: 31.4 us -> 0 us
  Pallas kernels: 0 us -> 21.6 us
  local copies, waits for them, and re-layouts: 13 us -> 2.77 us
  starting transfers between devices: 15.4 us -> 7.28 us
    scatter-add x6 -> x0, other arithmetic: 56.1 us -> none  [the longest x4 52.8 us: body(): partial_value = jnp.zeros((slot_total, mand_rows, block_size), jnp.float3...]
    all_to_all x3 -> x1, waiting for transfers between devices: 63 us -> 13.7 us  [exchange(): lax.all_to_all(sent, 'blk', split_axis=0, concat_axis=0, tiled=True)]
    all_to_all x1 -> x3, blocking collectives: 18.1 us -> 53.1 us  [exchange(): lax.all_to_all(sent, 'blk', split_axis=0, concat_axis=0, tiled=True)]
    dot_general x6 -> x0, matrix products: 31.4 us -> none  [the longest x2 17.2 us: body(): jnp.einsum('pmk,pjk->pmj', slot_rows[second_slot], cov_pairs, preferred_e...]
    pallas_call x0 -> x5, Pallas kernels: none -> 21.6 us  [the longest x2 17 us: body(): pl.pallas_call(pairs_kernel, out_shape=outgoing_shape, in_specs=[SMEM, VM...]
    all_to_all x3 -> x1, starting transfers between devices: 15.4 us -> 7.28 us  [exchange(): lax.all_to_all(sent, 'blk', split_axis=0, concat_axis=0, tiled=True)]
    gather x6 -> x0, local copies, waits for them, and re-layouts: 6.83 us -> none  [the longest x2 4.18 us: body(): slot_rows[second_slot]]
    select_n x6 -> x0, other arithmetic: 4.06 us -> none  [the longest x3 1.69 us: body(): jnp.take(x_wire, picked_ids, axis=0)]
  transfers between devices with their start and end apart: 3 -> 1, of which waited for: 3 -> 1; matrix products, arithmetic and copies ran while one was open for 1% -> 1% of each run, Pallas kernels for 0% -> 0%
where the time goes in v1:
time: 99.6 us; the launch traced here: 99.2 us
  blocking collectives  53.1 us (53%)
  Pallas kernels  21.6 us (22%)
  waiting for transfers between devices  13.7 us (14%)
  starting transfers between devices  7.28 us (7%)
  local copies, waits for them, and re-layouts  2.77 us (3%)
    all_to_all x3, blocking collectives, exchange(): lax.all_to_all(sent, 'blk', split_axis=0, concat_axis=0, tiled=True)  53.1 us
    pallas_call x2, Pallas kernels, body(): pl.pallas_call(pairs_kernel, out_shape=outgoing_shape, in_specs=[SMEM, VM...  17 us
    all_to_all x1, waiting for transfers between devices, exchange(): lax.all_to_all(sent, 'blk', split_axis=0, concat_axis=0, tiled=True)  13.7 us
    all_to_all x1, starting transfers between devices, exchange(): lax.all_to_all(sent, 'blk', split_axis=0, concat_axis=0, tiled=True)  7.28 us
    pallas_call x2, Pallas kernels, body(): pl.pallas_call(functools.partial(update_kernel, last), out_shape=(whole,...  3.14 us
    unnamed x19, local copies, waits for them, and re-layouts  2.41 us
  transfers between devices with their start and end apart: 1, of which 1 were waited for; matrix products, arithmetic and copies ran while one was open for 1% of the time, Pallas kernels for 0%

profile of v1, /device:TPU:0, one launch (start us, length us, event | category | flops | bytes accessed | tf_op | source)
XLA Modules:
  0.0 99.2 jit_solution(15640753042965154083)
XLA Ops:
  0.6 0.0 copy-start
  0.6 0.0 copy-start.6
  0.7 0.0 copy-start.8
  0.7 0.0 copy-start.7
  0.7 0.0 copy-start.5
  0.7 0.6 copy-done
  1.3 0.3 dynamic-slice_reduce_fusion
  1.6 0.1 reshape.35.served_ref
  1.7 0.0 copy-start.1
  1.7 1.0 copy-done.1
  2.7 0.0 copy-start.2
  2.7 0.0 copy-start.3
  2.7 0.0 copy-start.4
  2.7 1.4 %pack_holdings.1 = bf16[16,64,256]{2,1,0:T(8,128)(2,1)} custom-call(s32[16]{0:T(128)S(1)} %reshape.35.served_ref, f32[64,1024]{1,0:T(8,128)S(1)} %copy-done.1), custom_call_target="tpu_custom_call" | custom-call | tf_op jit(solution)/shard_map/pack_holdings/pallas_call | solution.py:167
  4.1 7.3 %all-to-all-start = ((bf16[8,2,64,256]{3,2,1,0:T(8,128)(2,1)}), bf16[8,2,64,256]{3,2,1,0:T(8,128)(2,1)S(1)}, u32[]{:S(2)}, u32[]{:S(2)}) async-start(bf16[8,2,64,256]{3,2,1,0:T(8,128)(2,1)} %bitcast), calls=%async_computation | async-start | bytes 1048576 | tf_op jit(solution)/shard_map/all_to_all | solution.py:165
  11.4 0.8 copy.15.pairs_ref
  12.1 13.7 %all-to-all-done = bf16[8,2,64,256]{3,2,1,0:T(8,128)(2,1)S(1)} async-done(((bf16[8,2,64,256]{3,2,1,0:T(8,128)(2,1)}), bf16[8,2,64,256]{3,2,1,0:T(8,128)(2,1)S(1)}, u32[]{:S(2)}, u32[]{:S(2)}) %all-to-all-start) | async-done | bytes 524320 | tf_op jit(solution)/shard_map/all_to_all | solution.py:165
  25.8 8.6 %pair_products.2 = bf16[16,64,256]{2,1,0:T(8,128)(2,1)S(1)} custom-call(s32[1,64,2]{2,1,0:T(8,128)S(1)} %copy.15.pairs_ref, bf16[16,64,256]{2,1,0:T(8,128)(2,1)S(1)} %bitcast.9, bf16[64,256,256]{2,1,0:T(8,128)(2,1)} %cov_ref.3), custom_call_target="tpu_custom_call" | custom-call | tf_op jit(solution)/shard_map/pair_products/pallas_call | solution.py:181
  34.5 18.1 %all_to_all.20 = bf16[8,2,64,256]{3,2,1,0:T(8,128)(2,1)S(1)} all-to-all(bf16[8,2,64,256]{3,2,1,0:T(8,128)(2,1)S(1)} %bitcast.13), channel_id=1, replica_groups=mesh['groups'=2,'blk'=8,'mand'=2] {'blk'}, dimensions={0} | all-to-all | bytes 1048576 | tf_op jit(solution)/shard_map/all_to_all | solution.py:165
  52.6 0.0 copy-done.6
  52.6 0.0 copy-done.8
  52.6 0.0 copy-done.7
  52.6 0.0 copy-done.5
  52.6 0.0 copy-done.2
  52.6 0.0 copy-done.3
  52.6 0.0 copy-done.4
  52.6 1.2 %update.2 = (f32[64,1024]{1,0:T(8,128)S(1)}, f32[64,1024]{1,0:T(8,128)S(1)}, f32[64,1024]{1,0:T(8,128)S(1)}, bf16[16,64,256]{2,1,0:T(8,128)(2,1)S(1)}) custom-call(s32[16]{0:T(128)S(1)} %reshape.35.served_ref, s32[4]{0:T(128)S(1)} %copy-done.7, f32[8]{0:T(128)S(1)} %copy-done.8, bf16[16,64,256]{2,1,0:T(8,128)(2,1)S(1)} %bitcast.10, f32[2,64]{1,0:T(2,128)S(1)} %copy-done.6, ...), custom_call_target="tpu_custom_call" | custom-call | tf_op jit(solution)/shard_map/update/pallas_call | solution.py:195
  53.8 17.6 %all_to_all.21 = bf16[8,2,64,256]{3,2,1,0:T(8,128)(2,1)S(1)} all-to-all(bf16[8,2,64,256]{3,2,1,0:T(8,128)(2,1)S(1)} %bitcast.15), channel_id=1, replica_groups=mesh['groups'=2,'blk'=8,'mand'=2] {'blk'}, dimensions={0} | all-to-all | bytes 1048576 | tf_op jit(solution)/shard_map/all_to_all | solution.py:165
  71.4 8.4 %pair_products.3 = bf16[16,64,256]{2,1,0:T(8,128)(2,1)S(1)} custom-call(s32[1,64,2]{2,1,0:T(8,128)S(1)} %copy.15.pairs_ref, bf16[16,64,256]{2,1,0:T(8,128)(2,1)S(1)} %bitcast.11, bf16[64,256,256]{2,1,0:T(8,128)(2,1)} %cov_ref.3), custom_call_target="tpu_custom_call" | custom-call | tf_op jit(solution)/shard_map/pair_products/pallas_call | solution.py:181
  79.8 17.4 %all_to_all.22 = bf16[8,2,64,256]{3,2,1,0:T(8,128)(2,1)S(1)} all-to-all(bf16[8,2,64,256]{3,2,1,0:T(8,128)(2,1)S(1)} %bitcast.12), channel_id=1, replica_groups=mesh['groups'=2,'blk'=8,'mand'=2] {'blk'}, dimensions={0} | all-to-all | bytes 1048576 | tf_op jit(solution)/shard_map/all_to_all | solution.py:165
  97.2 2.0 %update.3 = (f32[64,1024]{1,0:T(8,128)}, f32[64,1024]{1,0:T(8,128)}) custom-call(s32[16]{0:T(128)S(1)} %reshape.35.served_ref, s32[4]{0:T(128)S(1)} %copy-done.7, f32[8]{0:T(128)S(1)} %copy-done.8, bf16[16,64,256]{2,1,0:T(8,128)(2,1)S(1)} %bitcast.14, f32[2,64]{1,0:T(2,128)S(1)} %copy-done.6, f32[64,1024]{1,0:T(8,128)S(1)} %copy-done.2, ...), custom_call_target="tpu_custom_call" | custom-call | tf_op jit(solution)/shard_map/update/pallas_call | solution.py:195
Async XLA Ops:
  0.6 0.7 copy-start
  0.6 51.9 %copy-start.6 = (f32[2,64]{1,0:T(2,128)S(1)}, f32[2,64]{1,0:T(2,128)}, u32[]{:S(2)}) copy-start(f32[2,64]{1,0:T(2,128)} %slopes_ref.3) | copy-start | bytes 1540
  0.7 51.9 %copy-start.8 = (f32[8]{0:T(128)S(1)}, f32[8]{0:T(128)}, u32[]{:S(2)}) copy-start(f32[8]{0:T(128)} %knee_levels_ref.3) | copy-start | bytes 100
  0.7 51.9 %copy-start.7 = (s32[4]{0:T(128)S(1)}, s32[4]{0:T(128)}, u32[]{:S(2)}) copy-start(s32[4]{0:T(128)} %knee_index_ref.3) | copy-start | bytes 52
  0.7 51.9 %copy-start.5 = (f32[1024]{0:T(1024)S(1)}, f32[1024]{0:T(1024)}, u32[]{:S(2)}) copy-start(f32[1024]{0:T(1024)} %param.12) | copy-start | bytes 12292
  1.7 1.0 copy-start.1
  2.7 49.9 %copy-start.2 = (f32[64,1024]{1,0:T(8,128)S(1)}, f32[64,1024]{1,0:T(8,128)}, u32[]{:S(2)}) copy-start(f32[64,1024]{1,0:T(8,128)} %holdings_ref.5) | copy-start | bytes 786436
  2.7 49.9 %copy-start.3 = (bf16[4,256,256]{2,1,0:T(8,128)(2,1)S(1)}, bf16[4,256,256]{2,1,0:T(8,128)(2,1)}, u32[]{:S(2)}) copy-start(bf16[4,256,256]{2,1,0:T(8,128)(2,1)} %diag_ref.3) | copy-start | bytes 1572868
  2.7 49.9 %copy-start.4 = (s32[64,1024]{1,0:T(8,128)S(1)}, s32[64,1024]{1,0:T(8,128)}, u32[]{:S(2)}) copy-start(s32[64,1024]{1,0:T(8,128)} %eligible_ref.3) | copy-start | bytes 786436
  4.1 21.8 %all-to-all-start = ((bf16[8,2,64,256]{3,2,1,0:T(8,128)(2,1)}), bf16[8,2,64,256]{3,2,1,0:T(8,128)(2,1)S(1)}, u32[]{:S(2)}, u32[]{:S(2)}) async-start(bf16[8,2,64,256]{3,2,1,0:T(8,128)(2,1)} %bitcast), calls=%async_computation | async-start | bytes 1048576 | tf_op jit(solution)/shard_map/all_to_all | solution.py:165

commit v2 on v1

--- a/solution.py
+++ b/solution.py
@@ -11,12 +11,10 @@
 STEP_SIZE = 0.5
 RISK_AVERSION = 1.0
 PENALTY = 1.0
-CHUNKS = 8
 
 VMEM = pl.BlockSpec(memory_space=pltpu.VMEM)
 SMEM = pl.BlockSpec(memory_space=pltpu.SMEM)
-ANY = pl.BlockSpec(memory_space=pl.ANY)
-PARAMS = pltpu.CompilerParams(vmem_limit_bytes=48 * 1024 * 1024)
+PARAMS = pltpu.CompilerParams(vmem_limit_bytes=24 * 1024 * 1024)
 
 
 def fill_outgoing(served_ref, wire_ref, outgoing_ref):
@@ -34,36 +32,22 @@
     fill_outgoing(served_ref, wire_ref, outgoing_ref)
 
 
-def pairs_kernel(pairs_ref, rows_ref, cov_ref, partial_ref, cov_vmem, total, sems):
-    pairs = cov_ref.shape[0]
-    step = pairs // CHUNKS
-    copies = [
-        pltpu.make_async_copy(
-            cov_ref.at[pl.ds(chunk * step, step)],
-            cov_vmem.at[pl.ds(chunk * step, step)],
-            sems.at[chunk],
+def pairs_kernel(pairs_ref, rows_ref, cov_ref, partial_ref, total):
+    total[...] = jnp.zeros_like(total)
+
+    def one(pair, carry):
+        first = pairs_ref[0, pair, 0]
+        second = pairs_ref[0, pair, 1]
+        block = cov_ref[pair]
+        to_first = lax.dot_general(
+            rows_ref[second], block, (((1,), (1,)), ((), ())), preferred_element_type=jnp.float32
         )
-        for chunk in range(CHUNKS)
-    ]
-    for copy in copies:
-        copy.start()
-    total[...] = jnp.zeros_like(total)
-    for chunk, copy in enumerate(copies):
-        copy.wait()
-
-        def one(pair, carry):
-            first = pairs_ref[0, pair, 0]
-            second = pairs_ref[0, pair, 1]
-            block = cov_vmem[pair]
-            to_first = lax.dot_general(
-                rows_ref[second], block, (((1,), (1,)), ((), ())), preferred_element_type=jnp.float32
-            )
-            to_second = jnp.dot(rows_ref[first], block, preferred_element_type=jnp.float32)
-            total[first] += to_first
-            total[second] += to_second
-            return carry
-
-        lax.fori_loop(chunk * step, (chunk + 1) * step, one, 0, unroll=4)
+        to_second = jnp.dot(rows_ref[first], block, preferred_element_type=jnp.float32)
+        total[first] += to_first
+        total[second] += to_second
+        return carry
+
+    lax.fori_loop(0, cov_ref.shape[0], one, 0, unroll=16)
     partial_ref[...] = total[...].astype(jnp.bfloat16)
 
 
@@ -181,13 +165,9 @@
         partial_sums = pl.pallas_call(
             pairs_kernel,
             out_shape=outgoing_shape,
-            in_specs=[SMEM, VMEM, ANY],
+            in_specs=[SMEM, VMEM, VMEM],
             out_specs=VMEM,
-            scratch_shapes=[
-                pltpu.VMEM(cov_pairs.shape, jnp.bfloat16),
-                pltpu.VMEM(slot_shape, jnp.float32),
-                pltpu.SemaphoreType.DMA((CHUNKS,)),
-            ],
+            scratch_shapes=[pltpu.VMEM(slot_shape, jnp.float32)],
             compiler_params=PARAMS,
             name="pair_products",
         )(pair_slots, slot_rows, cov_pairs)

time: 99.6 us -> 97.3 us (0.977)
  Pallas kernels: 21.6 us -> 15.9 us
  local copies, waits for them, and re-layouts: 2.77 us -> 6.15 us
    pallas_call x2, Pallas kernels: 17 us -> 11.4 us  [body(): pl.pallas_call(pairs_kernel, out_shape=outgoing_shape, in_specs=[SMEM, VM...]
    unnamed x19 -> x23, local copies, waits for them, and re-layouts: 2.41 us -> 5.79 us
where the time goes in v2:
time: 97.3 us; the launch traced here: 96.9 us
  blocking collectives  53.1 us (55%)
  Pallas kernels  15.9 us (16%)
  waiting for transfers between devices  13.7 us (14%)
  starting transfers between devices  7.28 us (7%)
  local copies, waits for them, and re-layouts  6.15 us (6%)
    all_to_all x3, blocking collectives, exchange(): lax.all_to_all(sent, 'blk', split_axis=0, concat_axis=0, tiled=True)  53.1 us
    all_to_all x1, waiting for transfers between devices, exchange(): lax.all_to_all(sent, 'blk', split_axis=0, concat_axis=0, tiled=True)  13.7 us
    pallas_call x2, Pallas kernels, body(): pl.pallas_call(pairs_kernel, out_shape=outgoing_shape, in_specs=[SMEM, VM...  11.4 us
    all_to_all x1, starting transfers between devices, exchange(): lax.all_to_all(sent, 'blk', split_axis=0, concat_axis=0, tiled=True)  7.28 us
    unnamed x23, local copies, waits for them, and re-layouts  5.79 us
    pallas_call x2, Pallas kernels, body(): pl.pallas_call(functools.partial(update_kernel, last), out_shape=(whole,...  3.13 us
  transfers between devices with their start and end apart: 1, of which 1 were waited for; matrix products, arithmetic and copies ran while one was open for 1% of the time, Pallas kernels for 0%

profile of v2, /device:TPU:0, one launch (start us, length us, event | category | flops | bytes accessed | tf_op | source)
XLA Modules:
  0.0 96.9 jit_solution(3287028359138838505)
XLA Ops:
  0.6 0.0 copy-start
  0.6 0.0 copy-start.8
  0.7 0.0 copy-start.10
  0.7 0.0 copy-start.9
  0.7 0.0 copy-start.7
  0.7 0.6 copy-done
  1.3 0.3 dynamic-slice_reduce_fusion
  1.6 0.1 reshape.35.served_ref
  1.7 0.0 copy-start.3
  1.7 1.0 copy-done.3
  2.7 0.0 copy-start.4
  2.7 0.0 copy-start.5
  2.7 0.0 copy-start.6
  2.7 1.4 %pack_holdings.1 = bf16[16,64,256]{2,1,0:T(8,128)(2,1)} custom-call(s32[16]{0:T(128)S(1)} %reshape.35.served_ref, f32[64,1024]{1,0:T(8,128)S(1)} %copy-done.3), custom_call_target="tpu_custom_call" | custom-call | tf_op jit(solution)/shard_map/pack_holdings/pallas_call | solution.py:151
  4.1 7.3 %all-to-all-start = ((bf16[8,2,64,256]{3,2,1,0:T(8,128)(2,1)}), bf16[8,2,64,256]{3,2,1,0:T(8,128)(2,1)S(1)}, u32[]{:S(2)}, u32[]{:S(2)}) async-start(bf16[8,2,64,256]{3,2,1,0:T(8,128)(2,1)} %bitcast), calls=%async_computation | async-start | bytes 1048576 | tf_op jit(solution)/shard_map/all_to_all | solution.py:149
  11.4 0.8 copy.15.pairs_ref
  12.1 13.7 %all-to-all-done = bf16[8,2,64,256]{3,2,1,0:T(8,128)(2,1)S(1)} async-done(((bf16[8,2,64,256]{3,2,1,0:T(8,128)(2,1)}), bf16[8,2,64,256]{3,2,1,0:T(8,128)(2,1)S(1)}, u32[]{:S(2)}, u32[]{:S(2)}) %all-to-all-start) | async-done | bytes 524320 | tf_op jit(solution)/shard_map/all_to_all | solution.py:149
  25.8 0.0 copy-start.1
  25.8 3.4 %copy-done.1 = bf16[64,256,256]{2,1,0:T(8,128)(2,1)S(1)} copy-done((bf16[64,256,256]{2,1,0:T(8,128)(2,1)S(1)}, bf16[64,256,256]{2,1,0:T(8,128)(2,1)}, u32[]{:S(2)}) %copy-start.1) | copy-done | bytes 8388632
  29.2 0.0 copy-start.2
  29.2 5.8 %pair_products.2 = bf16[16,64,256]{2,1,0:T(8,128)(2,1)S(1)} custom-call(s32[1,64,2]{2,1,0:T(8,128)S(1)} %copy.15.pairs_ref, bf16[16,64,256]{2,1,0:T(8,128)(2,1)S(1)} %bitcast.9, bf16[64,256,256]{2,1,0:T(8,128)(2,1)S(1)} %copy-done.1), custom_call_target="tpu_custom_call" | custom-call | tf_op jit(solution)/shard_map/pair_products/pallas_call | solution.py:165
  35.0 18.1 %all_to_all.20 = bf16[8,2,64,256]{3,2,1,0:T(8,128)(2,1)S(1)} all-to-all(bf16[8,2,64,256]{3,2,1,0:T(8,128)(2,1)S(1)} %bitcast.13), channel_id=1, replica_groups=mesh['groups'=2,'blk'=8,'mand'=2] {'blk'}, dimensions={0} | all-to-all | bytes 1048576 | tf_op jit(solution)/shard_map/all_to_all | solution.py:149
  53.1 0.0 copy-done.8
  53.1 0.0 copy-done.10
  53.1 0.0 copy-done.9
  53.1 0.0 copy-done.7
  53.1 0.0 copy-done.4
  53.1 0.0 copy-done.5
  53.1 0.0 copy-done.6
  53.1 1.2 %update.2 = (f32[64,1024]{1,0:T(8,128)S(1)}, f32[64,1024]{1,0:T(8,128)S(1)}, f32[64,1024]{1,0:T(8,128)S(1)}, bf16[16,64,256]{2,1,0:T(8,128)(2,1)S(1)}) custom-call(s32[16]{0:T(128)S(1)} %reshape.35.served_ref, s32[4]{0:T(128)S(1)} %copy-done.9, f32[8]{0:T(128)S(1)} %copy-done.10, bf16[16,64,256]{2,1,0:T(8,128)(2,1)S(1)} %bitcast.10, f32[2,64]{1,0:T(2,128)S(1)} %copy-done.8, ...), custom_call_target="tpu_custom_call" | custom-call | tf_op jit(solution)/shard_map/update/pallas_call | solution.py:175
  54.3 17.6 %all_to_all.21 = bf16[8,2,64,256]{3,2,1,0:T(8,128)(2,1)S(1)} all-to-all(bf16[8,2,64,256]{3,2,1,0:T(8,128)(2,1)S(1)} %bitcast.15), channel_id=1, replica_groups=mesh['groups'=2,'blk'=8,'mand'=2] {'blk'}, dimensions={0} | all-to-all | bytes 1048576 | tf_op jit(solution)/shard_map/all_to_all | solution.py:149
  71.9 0.0 copy-done.2
  71.9 5.6 %pair_products.3 = bf16[16,64,256]{2,1,0:T(8,128)(2,1)S(1)} custom-call(s32[1,64,2]{2,1,0:T(8,128)S(1)} %copy.15.pairs_ref, bf16[16,64,256]{2,1,0:T(8,128)(2,1)S(1)} %bitcast.11, bf16[64,256,256]{2,1,0:T(8,128)(2,1)S(1)} %copy-done.2), custom_call_target="tpu_custom_call" | custom-call | tf_op jit(solution)/shard_map/pair_products/pallas_call | solution.py:165
  77.5 17.4 %all_to_all.22 = bf16[8,2,64,256]{3,2,1,0:T(8,128)(2,1)S(1)} all-to-all(bf16[8,2,64,256]{3,2,1,0:T(8,128)(2,1)S(1)} %bitcast.12), channel_id=1, replica_groups=mesh['groups'=2,'blk'=8,'mand'=2] {'blk'}, dimensions={0} | all-to-all | bytes 1048576 | tf_op jit(solution)/shard_map/all_to_all | solution.py:149
  94.9 2.0 %update.3 = (f32[64,1024]{1,0:T(8,128)}, f32[64,1024]{1,0:T(8,128)}) custom-call(s32[16]{0:T(128)S(1)} %reshape.35.served_ref, s32[4]{0:T(128)S(1)} %copy-done.9, f32[8]{0:T(128)S(1)} %copy-done.10, bf16[16,64,256]{2,1,0:T(8,128)(2,1)S(1)} %bitcast.14, f32[2,64]{1,0:T(2,128)S(1)} %copy-done.8, f32[64,1024]{1,0:T(8,128)S(1)} %copy-done.4, ...), custom_call_target="tpu_custom_call" | custom-call | tf_op jit(solution)/shard_map/update/pallas_call | solution.py:175
Async XLA Ops:
  0.6 0.7 copy-start
  0.6 52.5 %copy-start.8 = (f32[2,64]{1,0:T(2,128)S(1)}, f32[2,64]{1,0:T(2,128)}, u32[]{:S(2)}) copy-start(f32[2,64]{1,0:T(2,128)} %slopes_ref.3) | copy-start | bytes 1540
  0.7 52.4 %copy-start.10 = (f32[8]{0:T(128)S(1)}, f32[8]{0:T(128)}, u32[]{:S(2)}) copy-start(f32[8]{0:T(128)} %knee_levels_ref.3) | copy-start | bytes 100
  0.7 52.4 %copy-start.9 = (s32[4]{0:T(128)S(1)}, s32[4]{0:T(128)}, u32[]{:S(2)}) copy-start(s32[4]{0:T(128)} %knee_index_ref.3) | copy-start | bytes 52
  0.7 52.4 %copy-start.7 = (f32[1024]{0:T(1024)S(1)}, f32[1024]{0:T(1024)}, u32[]{:S(2)}) copy-start(f32[1024]{0:T(1024)} %param.12) | copy-start | bytes 12292
  1.7 1.0 copy-start.3
  2.7 50.5 %copy-start.4 = (f32[64,1024]{1,0:T(8,128)S(1)}, f32[64,1024]{1,0:T(8,128)}, u32[]{:S(2)}) copy-start(f32[64,1024]{1,0:T(8,128)} %holdings_ref.5) | copy-start | bytes 786436
  2.7 50.5 %copy-start.5 = (bf16[4,256,256]{2,1,0:T(8,128)(2,1)S(1)}, bf16[4,256,256]{2,1,0:T(8,128)(2,1)}, u32[]{:S(2)}) copy-start(bf16[4,256,256]{2,1,0:T(8,128)(2,1)} %diag_ref.3) | copy-start | bytes 1572868
  2.7 50.5 %copy-start.6 = (s32[64,1024]{1,0:T(8,128)S(1)}, s32[64,1024]{1,0:T(8,128)}, u32[]{:S(2)}) copy-start(s32[64,1024]{1,0:T(8,128)} %eligible_ref.3) | copy-start | bytes 786436
  4.1 21.8 %all-to-all-start = ((bf16[8,2,64,256]{3,2,1,0:T(8,128)(2,1)}), bf16[8,2,64,256]{3,2,1,0:T(8,128)(2,1)S(1)}, u32[]{:S(2)}, u32[]{:S(2)}) async-start(bf16[8,2,64,256]{3,2,1,0:T(8,128)(2,1)} %bitcast), calls=%async_computation | async-start | bytes 1048576 | tf_op jit(solution)/shard_map/all_to_all | solution.py:149
  25.8 3.4 %copy-start.1 = (bf16[64,256,256]{2,1,0:T(8,128)(2,1)S(1)}, bf16[64,256,256]{2,1,0:T(8,128)(2,1)}, u32[]{:S(2)}) copy-start(bf16[64,256,256]{2,1,0:T(8,128)(2,1)} %cov_ref.3) | copy-start | bytes 25165828
  29.2 42.7 %copy-start.2 = (bf16[64,256,256]{2,1,0:T(8,128)(2,1)S(1)}, bf16[64,256,256]{2,1,0:T(8,128)(2,1)}, u32[]{:S(2)}) copy-start(bf16[64,256,256]{2,1,0:T(8,128)(2,1)} %cov_ref.3) | copy-start | bytes 25165828

commit v3 on v2

v3 whole, which is shorter than its diff:
```python
import functools

import jax
import jax.numpy as jnp
from jax import lax
from jax.experimental import pallas as pl
from jax.experimental.pallas import tpu as pltpu
from jax.sharding import PartitionSpec as P

ITERS = 2
STEP_SIZE = 0.5
RISK_AVERSION = 1.0
PENALTY = 1.0

VMEM = pl.BlockSpec(memory_space=pltpu.VMEM)
SMEM = pl.BlockSpec(memory_space=pltpu.SMEM)
PARAMS = pltpu.CompilerParams(vmem_limit_bytes=24 * 1024 * 1024)


def order(owners):
    return (0, *reversed(range(1, owners)))


def fill_outgoing(served_ref, me_ref, wire_ref, outgoing):
    capacity = outgoing[0].shape[0]
    for offset, out_ref in zip(order(len(outgoing)), outgoing):
        for column_index in range(capacity):
            local = served_ref[(offset ^ me_ref[0]) * capacity + column_index]
            out_ref[column_index] = wire_ref[jnp.maximum(local, 0)]


def pack_kernel(served_ref, me_ref, holdings_ref, *refs):
    *outgoing, wire_ref = refs
    size = wire_ref.shape[2]
    for block in range(wire_ref.shape[0]):
        wire_ref[block] = holdings_ref[:, block * size : (block + 1) * size].astype(jnp.bfloat16)
    fill_outgoing(served_ref, me_ref, wire_ref, outgoing)


def pairs_kernel(owners, pairs_ref, me_ref, cov_ref, *refs):
    incoming, partial, (slot_rows, total) = refs[:owners], refs[owners : 2 * owners], refs[2 * owners :]
    capacity = incoming[0].shape[0]
    for offset, rows_ref in zip(order(owners), incoming):
        slot_rows[pl.ds(offset * capacity, capacity)] = rows_ref[...]
    total[...] = jnp.zeros_like(total)

    def place(slot):
        return ((slot // capacity) ^ me_ref[0]) * capacity + slot % capacity

    def one(pair, carry):
        first = place(pairs_ref[0, pair, 0])
        second = place(pairs_ref[0, pair, 1])
        block = cov_ref[pair]
        to_first = lax.dot_general(
            slot_rows[second], block, (((1,), (1,)), ((), ())), preferred_element_type=jnp.float32
        )
        to_second = jnp.dot(slot_rows[first], block, preferred_element_type=jnp.float32)
        total[first] += to_first
        total[second] += to_second
        return carry

    lax.fori_loop(0, cov_ref.shape[0], one, 0, unroll=16)
    for offset, out_ref in zip(order(owners), partial):
        out_ref[...] = total[pl.ds(offset * capacity, capacity)].astype(out_ref.dtype)


def column(row, rows):
    square = (rows, rows)
    on_diagonal = lax.broadcasted_iota(jnp.int32, square, 0) == lax.broadcasted_iota(jnp.int32, square, 1)
    return jnp.sum(jnp.where(on_diagonal, row, 0.0), axis=1, keepdims=True)


def update_kernel(
    last,
    owners,
    served_ref,
    me_ref,
    knee_index_ref,
    knee_levels_ref,
    slopes_ref,
    holdings_ref,
    eligible_ref,
    expected_ref,
    diag_ref,
    *refs,
):
    returned, refs = refs[:owners], refs[owners:]
    if last:
        primal_ref, traded_ref, dual_ref, traded_out, dual_out, terms = refs
    else:
        primal_out, traded_out, dual_out, *outgoing, terms, wire_ref = refs
    blocks, rows, size = terms.shape
    capacity = returned[0].shape[0]
    terms[...] = jnp.zeros_like(terms)
    for offset, back_ref in zip(order(owners), returned):
        for column_index in range(capacity):
            local = served_ref[(offset ^ me_ref[0]) * capacity + column_index]

            @pl.when(local >= 0)
            def _(local=local, back_ref=back_ref, column_index=column_index):
                terms[local] += back_ref[column_index].astype(jnp.float32)

    low = column(slopes_ref[0:1, :] / PENALTY, rows)
    high = column((slopes_ref[0:1, :] + slopes_ref[1:2, :]) / PENALTY, rows)
    for block in range(blocks):
        span = pl.ds(block * size, size)
        initial = holdings_ref[:, span]
        primal = primal_ref[:, span] if last else initial
        x_wire = primal.astype(jnp.bfloat16)
        grad = jnp.dot(x_wire, diag_ref[block], preferred_element_type=jnp.float32) + terms[block]
        expected = expected_ref[:, span]
        allowed = eligible_ref[:, span].astype(jnp.float32)
        if last:
            dual = dual_ref[:, span]
            gap = primal - traded_ref[:, span] + dual
        else:
            dual = jnp.zeros_like(initial)
            gap = dual
        primal = allowed * (primal - STEP_SIZE * (RISK_AVERSION * grad - expected + PENALTY * gap))
        shifted = primal + dual - initial
        knee = knee_levels_ref[knee_index_ref[block]]
        magnitude = jnp.abs(shifted)
        moved = jnp.minimum(jnp.maximum(magnitude - low, 0.0), knee) + jnp.maximum(
            magnitude - high - knee, 0.0
        )
        traded = initial + jnp.where(shifted < 0.0, -moved, moved)
        traded_out[:, span] = traded
        dual_out[:, span] = dual + primal - traded
        if not last:
            primal_out[:, span] = primal
            wire_ref[block] = primal.astype(jnp.bfloat16)
    if not last:
        fill_outgoing(served_ref, me_ref, wire_ref, outgoing)


def body(
    holdings,
    eligible,
    returns_mu,
    cov_diag,
    cov_pairs,
    pair_slots,
    need_table,
    break_index,
    break_levels,
    cost_slopes,
):
    rows, assets = holdings.shape
    blocks, size, _ = cov_diag.shape
    owners = lax.axis_size("blk")
    my_index = lax.axis_index("blk")
    capacity = need_table.shape[2]
    me = my_index.reshape(1)
    served = lax.dynamic_index_in_dim(need_table, my_index, 1, keepdims=False).reshape(-1)
    wire_scratch = pltpu.VMEM((blocks, rows, size), jnp.bfloat16)
    whole = jax.ShapeDtypeStruct((rows, assets), jnp.float32)
    sent = jax.ShapeDtypeStruct((capacity, rows, size), jnp.bfloat16)
    kept = jax.ShapeDtypeStruct((capacity, rows, size), jnp.float32)

    def exchange(values):
        return [values[0]] + [
            lax.ppermute(value, "blk", [(index, index ^ offset) for index in range(owners)])
            for offset, value in zip(order(owners)[1:], values[1:])
        ]

    outgoing = pl.pallas_call(
        pack_kernel,
        out_shape=[sent] * owners,
        in_specs=[SMEM, SMEM, VMEM],
        out_specs=[VMEM] * owners,
        scratch_shapes=[wire_scratch],
        compiler_params=PARAMS,
        name="pack_holdings",
    )(served, me, holdings)
    expected = returns_mu.reshape(1, assets)
    state = ()
    for iteration in range(ITERS):
        last = iteration == ITERS - 1
        incoming = exchange(outgoing)
        partial_sums = pl.pallas_call(
            functools.partial(pairs_kernel, owners),
            out_shape=[kept] + [sent] * (owners - 1),
            in_specs=[SMEM, SMEM] + [VMEM] * (1 + owners),
            out_specs=[VMEM] * owners,
            scratch_shapes=[
                pltpu.VMEM((owners * capacity, rows, size), jnp.bfloat16),
                pltpu.VMEM((owners * capacity, rows, size), jnp.float32),
            ],
            compiler_params=PARAMS,
            name="pair_products",
        )(pair_slots, me, cov_pairs, *incoming)
        returned = exchange(partial_sums)
        outs = pl.pallas_call(
            functools.partial(update_kernel, last, owners),
            out_shape=[whole] * 2 if last else [whole] * 3 + [sent] * owners,
            in_specs=[SMEM] * 4 + [VMEM] * (5 + owners + len(state)),
            out_specs=[VMEM] * (2 if last else 3 + owners),
            scratch_shapes=[pltpu.VMEM((blocks, rows, size), jnp.float32)] + ([] if last else [wire_scratch]),
            compiler_params=PARAMS,
            name="update",
        )(
            served,
            me,
            break_index,
            break_levels,
            cost_slopes,
            holdings,
            eligible,
            expected,
            cov_diag,
            *returned,
            *state,
        )
        if not last:
            state, outgoing = outs[:3], outs[3:]
    return tuple(outs)


def solution(mesh):
    placed = (
        P(("groups", "mand"), "blk"),
        P(("groups", "mand"), "blk"),
        P(("groups", "blk")),
        P(("groups", "blk"), None, None),
        P(("groups", "blk"), None, None),
        P(("groups", "blk"), None, None),
        P("groups", None, None),
        P(("groups", "blk")),
        P(),
        P(None, "mand"),
    )
    return jax.shard_map(
        body,
        mesh=mesh,
        in_specs=placed,
        out_specs=(P(("groups", "mand"), "blk"), P(("groups", "mand"), "blk")),
        check_vma=False,
    )
```

time: 97.3 us -> 84.7 us (0.87)
  blocking collectives: 53.1 us -> 0 us
  starting transfers between devices: 7.28 us -> 45.5 us
  waiting for transfers between devices: 13.7 us -> 15.9 us
    all_to_all x3 -> x0, blocking collectives: 53.1 us -> none  [exchange(): lax.all_to_all(sent, 'blk', split_axis=0, concat_axis=0, tiled=True)]
    ppermute x0 -> x28, starting transfers between devices: none -> 45.5 us  [exchange(): lax.ppermute(value, 'blk', [(index, index ^ offset) for index in range(ow...]
    ppermute x0 -> x28, waiting for transfers between devices: none -> 15.9 us  [exchange(): lax.ppermute(value, 'blk', [(index, index ^ offset) for index in range(ow...]
    all_to_all x1 -> x0, waiting for transfers between devices: 13.7 us -> none  [exchange(): lax.all_to_all(sent, 'blk', split_axis=0, concat_axis=0, tiled=True)]
    all_to_all x1 -> x0, starting transfers between devices: 7.28 us -> none  [exchange(): lax.all_to_all(sent, 'blk', split_axis=0, concat_axis=0, tiled=True)]
    unnamed x23 -> x25, local copies, waits for them, and re-layouts: 5.79 us -> 6.74 us
  transfers between devices with their start and end apart: 1 -> 28, of which waited for: 1 -> 16; matrix products, arithmetic and copies ran while one was open for 1% -> 1% of each run, Pallas kernels for 0% -> 0%
where the time goes in v3:
time: 84.7 us; the launch traced here: 84.4 us
  starting transfers between devices  45.5 us (54%)
  waiting for transfers between devices  15.9 us (19%)
  Pallas kernels  15.2 us (18%)
  local copies, waits for them, and re-layouts  7.1 us (8%)
    ppermute x28, starting transfers between devices, exchange(): lax.ppermute(value, 'blk', [(index, index ^ offset) for index in range(ow...  45.5 us
    ppermute x28, waiting for transfers between devices, exchange(): lax.ppermute(value, 'blk', [(index, index ^ offset) for index in range(ow...  15.9 us
    pallas_call x2, Pallas kernels, body(): pl.pallas_call(functools.partial(pairs_kernel, owners), out_shape=[kept]...  11.4 us
    unnamed x25, local copies, waits for them, and re-layouts  6.74 us
    pallas_call x2, Pallas kernels, body(): pl.pallas_call(functools.partial(update_kernel, last, owners), out_shape=...  3.16 us
  transfers between devices with their start and end apart: 28, of which 16 were waited for; matrix products, arithmetic and copies ran while one was open for 1% of the time, Pallas kernels for 0%

profile of v3, /device:TPU:0, one launch (start us, length us, event | category | flops | bytes accessed | tf_op | source)
XLA Modules:
  0.0 84.4 jit_solution(5051851735520441078)
XLA Ops:
  0.7 0.6 copy-done
  1.7 1.0 %copy-done.3 = f32[64,1024]{1,0:T(8,128)S(1)} copy-done((f32[64,1024]{1,0:T(8,128)S(1)}, f32[64,1024]{1,0:T(8,128)}, u32[]{:S(2)}) %copy-start.3) | copy-done | bytes 262168
  2.7 0.6 pack_holdings.1
  3.3 6.1 %collective-permute-start = (bf16[2,64,256]{2,1,0:T(8,128)(2,1)S(1)}, bf16[2,64,256]{2,1,0:T(8,128)(2,1)S(1)}, u32[]{:S(2)}, u32[]{:S(2)}) collective-permute-start(bf16[2,64,256]{2,1,0:T(8,128)(2,1)S(1)} %get-tuple-element.38), channel_id=1, source_target_pairs={{0,14},{2,12},{4,10},{6,8},{8,6},{10,4},{12,2},{14,0},{1,15},{3,13... | collective-permute-start | bytes 196616 | tf_op jit(solution)/shard_map/ppermute | solution.py:162
  9.6 0.7 collective-permute-start.2
  10.3 2.0 %collective-permute-start.3 = (bf16[2,64,256]{2,1,0:T(8,128)(2,1)S(1)}, bf16[2,64,256]{2,1,0:T(8,128)(2,1)S(1)}, u32[]{:S(2)}, u32[]{:S(2)}) collective-permute-start(bf16[2,64,256]{2,1,0:T(8,128)(2,1)S(1)} %get-tuple-element.41), channel_id=1, source_target_pairs={{0,8},{2,10},{4,12},{6,14},{8,0},{10,2},{12,4},{14,6},{1,9},{3,11}... | collective-permute-start | bytes 196616 | tf_op jit(solution)/shard_map/ppermute | solution.py:162
  12.3 2.3 %collective-permute-start.4 = (bf16[2,64,256]{2,1,0:T(8,128)(2,1)S(1)}, bf16[2,64,256]{2,1,0:T(8,128)(2,1)S(1)}, u32[]{:S(2)}, u32[]{:S(2)}) collective-permute-start(bf16[2,64,256]{2,1,0:T(8,128)(2,1)S(1)} %get-tuple-element.42), channel_id=1, source_target_pairs={{0,6},{2,4},{4,2},{6,0},{8,14},{10,12},{12,10},{14,8},{1,7},{3,5},... | collective-permute-start | bytes 196616 | tf_op jit(solution)/shard_map/ppermute | solution.py:162
  14.6 0.8 collective-permute-start.5
  15.6 0.5 collective-permute-start.6
  16.1 0.8 copy.15.pairs_ref
  16.8 2.7 %collective-permute-done.2.refs_3_ = bf16[2,64,256]{2,1,0:T(8,128)(2,1)S(1)} collective-permute-done((bf16[2,64,256]{2,1,0:T(8,128)(2,1)S(1)}, bf16[2,64,256]{2,1,0:T(8,128)(2,1)S(1)}, u32[]{:S(2)}, u32[]{:S(2)}) %collective-permute-start.2) | collective-permute-done | bytes 65568 | tf_op jit(solution)/shard_map/ppermute | solution.py:162
  19.5 1.1 %collective-permute-done.3.refs_4_ = bf16[2,64,256]{2,1,0:T(8,128)(2,1)S(1)} collective-permute-done((bf16[2,64,256]{2,1,0:T(8,128)(2,1)S(1)}, bf16[2,64,256]{2,1,0:T(8,128)(2,1)S(1)}, u32[]{:S(2)}, u32[]{:S(2)}) %collective-permute-start.3) | collective-permute-done | bytes 65568 | tf_op jit(solution)/shard_map/ppermute | solution.py:162
  20.6 0.4 collective-permute-done.5.refs_6_
  21.0 3.4 %copy-done.1 = bf16[64,256,256]{2,1,0:T(8,128)(2,1)S(1)} copy-done((bf16[64,256,256]{2,1,0:T(8,128)(2,1)S(1)}, bf16[64,256,256]{2,1,0:T(8,128)(2,1)}, u32[]{:S(2)}) %copy-start.1) | copy-done | bytes 8388632
  24.4 5.7 %pair_products.2 = (f32[2,64,256]{2,1,0:T(8,128)S(1)}, bf16[2,64,256]{2,1,0:T(8,128)(2,1)S(1)}, bf16[2,64,256]{2,1,0:T(8,128)(2,1)S(1)}, bf16[2,64,256]{2,1,0:T(...) custom-call(s32[1,64,2]{2,1,0:T(8,128)S(1)} %copy.15.pairs_ref, ...), custom_call_target="tpu_custom_call" | custom-call | tf_op jit(solution)/shard_map/pair_products/pallas_call | solution.py:180
  30.1 3.9 %collective-permute-start.7 = (bf16[2,64,256]{2,1,0:T(8,128)(2,1)S(1)}, bf16[2,64,256]{2,1,0:T(8,128)(2,1)S(1)}, u32[]{:S(2)}, u32[]{:S(2)}) collective-permute-start(bf16[2,64,256]{2,1,0:T(8,128)(2,1)S(1)} %get-tuple-element.46), channel_id=1, source_target_pairs={{0,14},{2,12},{4,10},{6,8},{8,6},{10,4},{12,2},{14,0},{1,15},{3,13... | collective-permute-start | bytes 196616 | tf_op jit(solution)/shard_map/ppermute | solution.py:162
  34.0 2.2 %collective-permute-start.9 = (bf16[2,64,256]{2,1,0:T(8,128)(2,1)S(1)}, bf16[2,64,256]{2,1,0:T(8,128)(2,1)S(1)}, u32[]{:S(2)}, u32[]{:S(2)}) collective-permute-start(bf16[2,64,256]{2,1,0:T(8,128)(2,1)S(1)} %get-tuple-element.48), channel_id=1, source_target_pairs={{0,10},{2,8},{4,14},{6,12},{8,2},{10,0},{12,6},{14,4},{1,11},{3,9}... | collective-permute-start | bytes 196616 | tf_op jit(solution)/shard_map/ppermute | solution.py:162
  36.3 1.5 %collective-permute-start.10 = (bf16[2,64,256]{2,1,0:T(8,128)(2,1)S(1)}, bf16[2,64,256]{2,1,0:T(8,128)(2,1)S(1)}, u32[]{:S(2)}, u32[]{:S(2)}) collective-permute-start(bf16[2,64,256]{2,1,0:T(8,128)(2,1)S(1)} %get-tuple-element.49), channel_id=1, source_target_pairs={{0,8},{2,10},{4,12},{6,14},{8,0},{10,2},{12,4},{14,6},{1,9},{3,11}... | collective-permute-start | bytes 196616 | tf_op jit(solution)/shard_map/ppermute | solution.py:162
  37.8 1.5 %collective-permute-start.11 = (bf16[2,64,256]{2,1,0:T(8,128)(2,1)S(1)}, bf16[2,64,256]{2,1,0:T(8,128)(2,1)S(1)}, u32[]{:S(2)}, u32[]{:S(2)}) collective-permute-start(bf16[2,64,256]{2,1,0:T(8,128)(2,1)S(1)} %get-tuple-element.50), channel_id=1, source_target_pairs={{0,6},{2,4},{4,2},{6,0},{8,14},{10,12},{12,10},{14,8},{1,7},{3,5},... | collective-permute-start | bytes 196616 | tf_op jit(solution)/shard_map/ppermute | solution.py:162
  39.3 1.2 %collective-permute-start.12 = (bf16[2,64,256]{2,1,0:T(8,128)(2,1)S(1)}, bf16[2,64,256]{2,1,0:T(8,128)(2,1)S(1)}, u32[]{:S(2)}, u32[]{:S(2)}) collective-permute-start(bf16[2,64,256]{2,1,0:T(8,128)(2,1)S(1)} %get-tuple-element.51), channel_id=1, source_target_pairs={{0,4},{2,6},{4,0},{6,2},{8,12},{10,14},{12,8},{14,10},{1,5},{3,7},... | collective-permute-start | bytes 196616 | tf_op jit(solution)/shard_map/ppermute | solution.py:162
  40.8 0.7 collective-permute-start.13
  41.5 3.2 %collective-permute-done.9.refs_3_ = bf16[2,64,256]{2,1,0:T(8,128)(2,1)S(1)} collective-permute-done((bf16[2,64,256]{2,1,0:T(8,128)(2,1)S(1)}, bf16[2,64,256]{2,1,0:T(8,128)(2,1)S(1)}, u32[]{:S(2)}, u32[]{:S(2)}) %collective-permute-start.9) | collective-permute-done | bytes 65568 | tf_op jit(solution)/shard_map/ppermute | solution.py:162
  44.7 0.5 collective-permute-done.13.refs_7_
  45.3 0.9 %copy-done.6 = s32[64,1024]{1,0:T(8,128)S(1)} copy-done((s32[64,1024]{1,0:T(8,128)S(1)}, s32[64,1024]{1,0:T(8,128)}, u32[]{:S(2)}) %copy-start.6) | copy-done | bytes 262168
  46.2 1.2 %update.2 = (f32[64,1024]{1,0:T(8,128)S(1)}, f32[64,1024]{1,0:T(8,128)S(1)}, f32[64,1024]{1,0:T(8,128)S(1)}, bf16[2,64,256]{2,1,0:T(8,128)(2,1)S(1)}, bf16[2,64,...) custom-call(s32[16]{0:T(128)S(1)} %reshape.14.served_ref, ...), custom_call_target="tpu_custom_call" | custom-call | tf_op jit(solution)/shard_map/update/pallas_call | solution.py:193
  47.4 4.0 %collective-permute-start.14 = (bf16[2,64,256]{2,1,0:T(8,128)(2,1)S(1)}, bf16[2,64,256]{2,1,0:T(8,128)(2,1)S(1)}, u32[]{:S(2)}, u32[]{:S(2)}) collective-permute-start(bf16[2,64,256]{2,1,0:T(8,128)(2,1)S(1)} %get-tuple-element.54), channel_id=1, source_target_pairs={{0,14},{2,12},{4,10},{6,8},{8,6},{10,4},{12,2},{14,0},{1,15},{3,13... | collective-permute-start | bytes 196616 | tf_op jit(solution)/shard_map/ppermute | solution.py:162
  51.8 2.0 %collective-permute-start.16 = (bf16[2,64,256]{2,1,0:T(8,128)(2,1)S(1)}, bf16[2,64,256]{2,1,0:T(8,128)(2,1)S(1)}, u32[]{:S(2)}, u32[]{:S(2)}) collective-permute-start(bf16[2,64,256]{2,1,0:T(8,128)(2,1)S(1)} %get-tuple-element.56), channel_id=1, source_target_pairs={{0,10},{2,8},{4,14},{6,12},{8,2},{10,0},{12,6},{14,4},{1,11},{3,9}... | collective-permute-start | bytes 196616 | tf_op jit(solution)/shard_map/ppermute | solution.py:162
  53.8 1.3 %collective-permute-start.17 = (bf16[2,64,256]{2,1,0:T(8,128)(2,1)S(1)}, bf16[2,64,256]{2,1,0:T(8,128)(2,1)S(1)}, u32[]{:S(2)}, u32[]{:S(2)}) collective-permute-start(bf16[2,64,256]{2,1,0:T(8,128)(2,1)S(1)} %get-tuple-element.57), channel_id=1, source_target_pairs={{0,8},{2,10},{4,12},{6,14},{8,0},{10,2},{12,4},{14,6},{1,9},{3,11}... | collective-permute-start | bytes 196616 | tf_op jit(solution)/shard_map/ppermute | solution.py:162
  55.1 1.6 %collective-permute-start.18 = (bf16[2,64,256]{2,1,0:T(8,128)(2,1)S(1)}, bf16[2,64,256]{2,1,0:T(8,128)(2,1)S(1)}, u32[]{:S(2)}, u32[]{:S(2)}) collective-permute-start(bf16[2,64,256]{2,1,0:T(8,128)(2,1)S(1)} %get-tuple-element.58), channel_id=1, source_target_pairs={{0,6},{2,4},{4,2},{6,0},{8,14},{10,12},{12,10},{14,8},{1,7},{3,5},... | collective-permute-start | bytes 196616 | tf_op jit(solution)/shard_map/ppermute | solution.py:162
  56.7 0.9 %collective-permute-start.19 = (bf16[2,64,256]{2,1,0:T(8,128)(2,1)S(1)}, bf16[2,64,256]{2,1,0:T(8,128)(2,1)S(1)}, u32[]{:S(2)}, u32[]{:S(2)}) collective-permute-start(bf16[2,64,256]{2,1,0:T(8,128)(2,1)S(1)} %get-tuple-element.59), channel_id=1, source_target_pairs={{0,4},{2,6},{4,0},{6,2},{8,12},{10,14},{12,8},{14,10},{1,5},{3,7},... | collective-permute-start | bytes 196616 | tf_op jit(solution)/shard_map/ppermute | solution.py:162
  57.7 0.6 collective-permute-done.15.refs_2_
  58.3 0.5 collective-permute-start.20
  58.7 1.9 %collective-permute-done.16.refs_3_ = bf16[2,64,256]{2,1,0:T(8,128)(2,1)S(1)} collective-permute-done((bf16[2,64,256]{2,1,0:T(8,128)(2,1)S(1)}, bf16[2,64,256]{2,1,0:T(8,128)(2,1)S(1)}, u32[]{:S(2)}, u32[]{:S(2)}) %collective-permute-start.16) | collective-permute-done | bytes 65568 | tf_op jit(solution)/shard_map/ppermute | solution.py:162
  60.6 0.6 collective-permute-done.17.refs_4_
  61.3 0.6 collective-permute-done.19.refs_6_
  61.9 0.7 collective-permute-done.20.refs_7_
  62.6 5.7 %pair_products.3 = (f32[2,64,256]{2,1,0:T(8,128)S(1)}, bf16[2,64,256]{2,1,0:T(8,128)(2,1)S(1)}, bf16[2,64,256]{2,1,0:T(8,128)(2,1)S(1)}, bf16[2,64,256]{2,1,0:T(...) custom-call(s32[1,64,2]{2,1,0:T(8,128)S(1)} %copy.15.pairs_ref, ...), custom_call_target="tpu_custom_call" | custom-call | tf_op jit(solution)/shard_map/pair_products/pallas_call | solution.py:180
  68.3 3.5 %collective-permute-start.21 = (bf16[2,64,256]{2,1,0:T(8,128)(2,1)S(1)}, bf16[2,64,256]{2,1,0:T(8,128)(2,1)S(1)}, u32[]{:S(2)}, u32[]{:S(2)}) collective-permute-start(bf16[2,64,256]{2,1,0:T(8,128)(2,1)S(1)} %get-tuple-element.62), channel_id=1, source_target_pairs={{0,14},{2,12},{4,10},{6,8},{8,6},{10,4},{12,2},{14,0},{1,15},{3,13... | collective-permute-start | bytes 196616 | tf_op jit(solution)/shard_map/ppermute | solution.py:162
  71.7 0.5 collective-permute-start.22
  72.2 2.1 %collective-permute-start.23 = (bf16[2,64,256]{2,1,0:T(8,128)(2,1)S(1)}, bf16[2,64,256]{2,1,0:T(8,128)(2,1)S(1)}, u32[]{:S(2)}, u32[]{:S(2)}) collective-permute-start(bf16[2,64,256]{2,1,0:T(8,128)(2,1)S(1)} %get-tuple-element.64), channel_id=1, source_target_pairs={{0,10},{2,8},{4,14},{6,12},{8,2},{10,0},{12,6},{14,4},{1,11},{3,9}... | collective-permute-start | bytes 196616 | tf_op jit(solution)/shard_map/ppermute | solution.py:162
  74.3 1.6 %collective-permute-start.24 = (bf16[2,64,256]{2,1,0:T(8,128)(2,1)S(1)}, bf16[2,64,256]{2,1,0:T(8,128)(2,1)S(1)}, u32[]{:S(2)}, u32[]{:S(2)}) collective-permute-start(bf16[2,64,256]{2,1,0:T(8,128)(2,1)S(1)} %get-tuple-element.65), channel_id=1, source_target_pairs={{0,8},{2,10},{4,12},{6,14},{8,0},{10,2},{12,4},{14,6},{1,9},{3,11}... | collective-permute-start | bytes 196616 | tf_op jit(solution)/shard_map/ppermute | solution.py:162
  76.0 1.1 %collective-permute-start.25 = (bf16[2,64,256]{2,1,0:T(8,128)(2,1)S(1)}, bf16[2,64,256]{2,1,0:T(8,128)(2,1)S(1)}, u32[]{:S(2)}, u32[]{:S(2)}) collective-permute-start(bf16[2,64,256]{2,1,0:T(8,128)(2,1)S(1)} %get-tuple-element.66), channel_id=1, source_target_pairs={{0,6},{2,4},{4,2},{6,0},{8,14},{10,12},{12,10},{14,8},{1,7},{3,5},... | collective-permute-start | bytes 196616 | tf_op jit(solution)/shard_map/ppermute | solution.py:162
  77.0 1.0 %collective-permute-start.26 = (bf16[2,64,256]{2,1,0:T(8,128)(2,1)S(1)}, bf16[2,64,256]{2,1,0:T(8,128)(2,1)S(1)}, u32[]{:S(2)}, u32[]{:S(2)}) collective-permute-start(bf16[2,64,256]{2,1,0:T(8,128)(2,1)S(1)} %get-tuple-element.67), channel_id=1, source_target_pairs={{0,4},{2,6},{4,0},{6,2},{8,12},{10,14},{12,8},{14,10},{1,5},{3,7},... | collective-permute-start | bytes 196616 | tf_op jit(solution)/shard_map/ppermute | solution.py:162
  78.2 1.3 %collective-permute-start.27 = (bf16[2,64,256]{2,1,0:T(8,128)(2,1)S(1)}, bf16[2,64,256]{2,1,0:T(8,128)(2,1)S(1)}, u32[]{:S(2)}, u32[]{:S(2)}) collective-permute-start(bf16[2,64,256]{2,1,0:T(8,128)(2,1)S(1)} %get-tuple-element.68), channel_id=1, source_target_pairs={{0,2},{2,0},{4,6},{6,4},{8,10},{10,8},{12,14},{14,12},{1,3},{3,1},... | collective-permute-start | bytes 196616 | tf_op jit(solution)/shard_map/ppermute | solution.py:162
  79.5 1.2 %collective-permute-done.23.refs_3_ = bf16[2,64,256]{2,1,0:T(8,128)(2,1)S(1)} collective-permute-done((bf16[2,64,256]{2,1,0:T(8,128)(2,1)S(1)}, bf16[2,64,256]{2,1,0:T(8,128)(2,1)S(1)}, u32[]{:S(2)}, u32[]{:S(2)}) %collective-permute-start.23) | collective-permute-done | bytes 65568 | tf_op jit(solution)/shard_map/ppermute | solution.py:162
  80.6 1.1 %collective-permute-done.25.refs_5_ = bf16[2,64,256]{2,1,0:T(8,128)(2,1)S(1)} collective-permute-done((bf16[2,64,256]{2,1,0:T(8,128)(2,1)S(1)}, bf16[2,64,256]{2,1,0:T(8,128)(2,1)S(1)}, u32[]{:S(2)}, u32[]{:S(2)}) %collective-permute-start.25) | collective-permute-done | bytes 65568 | tf_op jit(solution)/shard_map/ppermute | solution.py:162
  81.7 0.7 collective-permute-done.27.refs_7_
  82.4 2.0 %update.3 = (f32[64,1024]{1,0:T(8,128)}, f32[64,1024]{1,0:T(8,128)}) custom-call(s32[16]{0:T(128)S(1)} %reshape.14.served_ref, s32[1]{0:T(128)} %bitcast.me_ref, s32[4]{0:T(128)S(1)} %copy-done.10, f32[8]{0:T(128)S(1)} %copy-done.11, f32[2,64]{1,0:T(2,128)S(1)} %copy-done.9, f32[64,1024]{1,0:T(8,128)S(1)} %copy-done.4, s32[64,1024]{1,0:T(8,128)S(1)} %copy-done.7, ...), custom_call_target="tpu_custom_call" | custom-call | tf_op jit(solution)/shard_map/update/pallas_call | solution.py:193
  (40 shorter events, 1.7 us)
Async XLA Ops:
  0.6 0.7 copy-start
  0.6 44.6 %copy-start.9 = (f32[2,64]{1,0:T(2,128)S(1)}, f32[2,64]{1,0:T(2,128)}, u32[]{:S(2)}) copy-start(f32[2,64]{1,0:T(2,128)} %slopes_ref.3) | copy-start | bytes 1540
  0.7 44.6 %copy-start.11 = (f32[8]{0:T(128)S(1)}, f32[8]{0:T(128)}, u32[]{:S(2)}) copy-start(f32[8]{0:T(128)} %knee_levels_ref.3) | copy-start | bytes 100
  0.7 44.6 %copy-start.10 = (s32[4]{0:T(128)S(1)}, s32[4]{0:T(128)}, u32[]{:S(2)}) copy-start(s32[4]{0:T(128)} %knee_index_ref.3) | copy-start | bytes 52
  0.7 44.6 %copy-start.8 = (f32[1024]{0:T(1024)S(1)}, f32[1024]{0:T(1024)}, u32[]{:S(2)}) copy-start(f32[1024]{0:T(1024)} %param.12) | copy-start | bytes 12292
  1.7 1.0 %copy-start.3 = (f32[64,1024]{1,0:T(8,128)S(1)}, f32[64,1024]{1,0:T(8,128)}, u32[]{:S(2)}) copy-start(f32[64,1024]{1,0:T(8,128)} %holdings_ref.5) | copy-start | bytes 786436
  2.7 42.6 %copy-start.4 = (f32[64,1024]{1,0:T(8,128)S(1)}, f32[64,1024]{1,0:T(8,128)}, u32[]{:S(2)}) copy-start(f32[64,1024]{1,0:T(8,128)} %holdings_ref.5) | copy-start | bytes 786436
  3.3 11.4 %collective-permute-start = (bf16[2,64,256]{2,1,0:T(8,128)(2,1)S(1)}, bf16[2,64,256]{2,1,0:T(8,128)(2,1)S(1)}, u32[]{:S(2)}, u32[]{:S(2)}) collective-permute-start(bf16[2,64,256]{2,1,0:T(8,128)(2,1)S(1)} %get-tuple-element.38), channel_id=1, source_target_pairs={{0,14},{2,12},{4,10},{6,8},{8,6},{10,4},{12,2},{14,0},{1,15},{3,13... | collective-permute-start | bytes 196616 | tf_op jit(solution)/shard_map/ppermute | solution.py:162
  9.3 6.3 %collective-permute-start.1 = (bf16[2,64,256]{2,1,0:T(8,128)(2,1)S(1)}, bf16[2,64,256]{2,1,0:T(8,128)(2,1)S(1)}, u32[]{:S(2)}, u32[]{:S(2)}) collective-permute-start(bf16[2,64,256]{2,1,0:T(8,128)(2,1)S(1)} %get-tuple-element.39), channel_id=1, source_target_pairs={{0,12},{2,14},{4,8},{6,10},{8,4},{10,6},{12,0},{14,2},{1,13},{3,15... | collective-permute-start | bytes 196616 | tf_op jit(solution)/shard_map/ppermute | solution.py:162
  9.6 9.9 %collective-permute-start.2 = (bf16[2,64,256]{2,1,0:T(8,128)(2,1)S(1)}, bf16[2,64,256]{2,1,0:T(8,128)(2,1)S(1)}, u32[]{:S(2)}, u32[]{:S(2)}) collective-permute-start(bf16[2,64,256]{2,1,0:T(8,128)(2,1)S(1)} %get-tuple-element.40), channel_id=1, source_target_pairs={{0,10},{2,8},{4,14},{6,12},{8,2},{10,0},{12,6},{14,4},{1,11},{3,9}... | collective-permute-start | bytes 196616 | tf_op jit(solution)/shard_map/ppermute | solution.py:162
  10.3 10.3 %collective-permute-start.3 = (bf16[2,64,256]{2,1,0:T(8,128)(2,1)S(1)}, bf16[2,64,256]{2,1,0:T(8,128)(2,1)S(1)}, u32[]{:S(2)}, u32[]{:S(2)}) collective-permute-start(bf16[2,64,256]{2,1,0:T(8,128)(2,1)S(1)} %get-tuple-element.41), channel_id=1, source_target_pairs={{0,8},{2,10},{4,12},{6,14},{8,0},{10,2},{12,4},{14,6},{1,9},{3,11}... | collective-permute-start | bytes 196616 | tf_op jit(solution)/shard_map/ppermute | solution.py:162
  12.3 8.3 %collective-permute-start.4 = (bf16[2,64,256]{2,1,0:T(8,128)(2,1)S(1)}, bf16[2,64,256]{2,1,0:T(8,128)(2,1)S(1)}, u32[]{:S(2)}, u32[]{:S(2)}) collective-permute-start(bf16[2,64,256]{2,1,0:T(8,128)(2,1)S(1)} %get-tuple-element.42), channel_id=1, source_target_pairs={{0,6},{2,4},{4,2},{6,0},{8,14},{10,12},{12,10},{14,8},{1,7},{3,5},... | collective-permute-start | bytes 196616 | tf_op jit(solution)/shard_map/ppermute | solution.py:162
  14.6 6.4 %collective-permute-start.5 = (bf16[2,64,256]{2,1,0:T(8,128)(2,1)S(1)}, bf16[2,64,256]{2,1,0:T(8,128)(2,1)S(1)}, u32[]{:S(2)}, u32[]{:S(2)}) collective-permute-start(bf16[2,64,256]{2,1,0:T(8,128)(2,1)S(1)} %get-tuple-element.43), channel_id=1, source_target_pairs={{0,4},{2,6},{4,0},{6,2},{8,12},{10,14},{12,8},{14,10},{1,5},{3,7},... | collective-permute-start | bytes 196616 | tf_op jit(solution)/shard_map/ppermute | solution.py:162
  15.6 5.4 %collective-permute-start.6 = (bf16[2,64,256]{2,1,0:T(8,128)(2,1)S(1)}, bf16[2,64,256]{2,1,0:T(8,128)(2,1)S(1)}, u32[]{:S(2)}, u32[]{:S(2)}) collective-permute-start(bf16[2,64,256]{2,1,0:T(8,128)(2,1)S(1)} %get-tuple-element.44), channel_id=1, source_target_pairs={{0,2},{2,0},{4,6},{6,4},{8,10},{10,8},{12,14},{14,12},{1,3},{3,1},... | collective-permute-start | bytes 196616 | tf_op jit(solution)/shard_map/ppermute | solution.py:162
  21.0 3.4 %copy-start.1 = (bf16[64,256,256]{2,1,0:T(8,128)(2,1)S(1)}, bf16[64,256,256]{2,1,0:T(8,128)(2,1)}, u32[]{:S(2)}) copy-start(bf16[64,256,256]{2,1,0:T(8,128)(2,1)} %cov_ref.3) | copy-start | bytes 25165828
  24.4 20.9 %copy-start.5 = (bf16[4,256,256]{2,1,0:T(8,128)(2,1)S(1)}, bf16[4,256,256]{2,1,0:T(8,128)(2,1)}, u32[]{:S(2)}) copy-start(bf16[4,256,256]{2,1,0:T(8,128)(2,1)} %diag_ref.3) | copy-start | bytes 1572868
  24.4 38.2 %copy-start.2 = (bf16[64,256,256]{2,1,0:T(8,128)(2,1)S(1)}, bf16[64,256,256]{2,1,0:T(8,128)(2,1)}, u32[]{:S(2)}) copy-start(bf16[64,256,256]{2,1,0:T(8,128)(2,1)} %cov_ref.3) | copy-start | bytes 25165828
  30.1 9.2 %collective-permute-start.7 = (bf16[2,64,256]{2,1,0:T(8,128)(2,1)S(1)}, bf16[2,64,256]{2,1,0:T(8,128)(2,1)S(1)}, u32[]{:S(2)}, u32[]{:S(2)}) collective-permute-start(bf16[2,64,256]{2,1,0:T(8,128)(2,1)S(1)} %get-tuple-element.46), channel_id=1, source_target_pairs={{0,14},{2,12},{4,10},{6,8},{8,6},{10,4},{12,2},{14,0},{1,15},{3,13... | collective-permute-start | bytes 196616 | tf_op jit(solution)/shard_map/ppermute | solution.py:162
  34.0 6.8 %collective-permute-start.8 = (bf16[2,64,256]{2,1,0:T(8,128)(2,1)S(1)}, bf16[2,64,256]{2,1,0:T(8,128)(2,1)S(1)}, u32[]{:S(2)}, u32[]{:S(2)}) collective-permute-start(bf16[2,64,256]{2,1,0:T(8,128)(2,1)S(1)} %get-tuple-element.47), channel_id=1, source_target_pairs={{0,12},{2,14},{4,8},{6,10},{8,4},{10,6},{12,0},{14,2},{1,13},{3,15... | collective-permute-start | bytes 196616 | tf_op jit(solution)/shard_map/ppermute | solution.py:162
  34.0 10.6 %collective-permute-start.9 = (bf16[2,64,256]{2,1,0:T(8,128)(2,1)S(1)}, bf16[2,64,256]{2,1,0:T(8,128)(2,1)S(1)}, u32[]{:S(2)}, u32[]{:S(2)}) collective-permute-start(bf16[2,64,256]{2,1,0:T(8,128)(2,1)S(1)} %get-tuple-element.48), channel_id=1, source_target_pairs={{0,10},{2,8},{4,14},{6,12},{8,2},{10,0},{12,6},{14,4},{1,11},{3,9}... | collective-permute-start | bytes 196616 | tf_op jit(solution)/shard_map/ppermute | solution.py:162
  36.3 8.4 %collective-permute-start.10 = (bf16[2,64,256]{2,1,0:T(8,128)(2,1)S(1)}, bf16[2,64,256]{2,1,0:T(8,128)(2,1)S(1)}, u32[]{:S(2)}, u32[]{:S(2)}) collective-permute-start(bf16[2,64,256]{2,1,0:T(8,128)(2,1)S(1)} %get-tuple-element.49), channel_id=1, source_target_pairs={{0,8},{2,10},{4,12},{6,14},{8,0},{10,2},{12,4},{14,6},{1,9},{3,11}... | collective-permute-start | bytes 196616 | tf_op jit(solution)/shard_map/ppermute | solution.py:162
  37.8 6.9 %collective-permute-start.11 = (bf16[2,64,256]{2,1,0:T(8,128)(2,1)S(1)}, bf16[2,64,256]{2,1,0:T(8,128)(2,1)S(1)}, u32[]{:S(2)}, u32[]{:S(2)}) collective-permute-start(bf16[2,64,256]{2,1,0:T(8,128)(2,1)S(1)} %get-tuple-element.50), channel_id=1, source_target_pairs={{0,6},{2,4},{4,2},{6,0},{8,14},{10,12},{12,10},{14,8},{1,7},{3,5},... | collective-permute-start | bytes 196616 | tf_op jit(solution)/shard_map/ppermute | solution.py:162
  39.3 5.4 %collective-permute-start.12 = (bf16[2,64,256]{2,1,0:T(8,128)(2,1)S(1)}, bf16[2,64,256]{2,1,0:T(8,128)(2,1)S(1)}, u32[]{:S(2)}, u32[]{:S(2)}) collective-permute-start(bf16[2,64,256]{2,1,0:T(8,128)(2,1)S(1)} %get-tuple-element.51), channel_id=1, source_target_pairs={{0,4},{2,6},{4,0},{6,2},{8,12},{10,14},{12,8},{14,10},{1,5},{3,7},... | collective-permute-start | bytes 196616 | tf_op jit(solution)/shard_map/ppermute | solution.py:162
  40.8 4.5 %collective-permute-start.13 = (bf16[2,64,256]{2,1,0:T(8,128)(2,1)S(1)}, bf16[2,64,256]{2,1,0:T(8,128)(2,1)S(1)}, u32[]{:S(2)}, u32[]{:S(2)}) collective-permute-start(bf16[2,64,256]{2,1,0:T(8,128)(2,1)S(1)} %get-tuple-element.52), channel_id=1, source_target_pairs={{0,2},{2,0},{4,6},{6,4},{8,10},{10,8},{12,14},{14,12},{1,3},{3,1},... | collective-permute-start | bytes 196616 | tf_op jit(solution)/shard_map/ppermute | solution.py:162
  45.3 1.0 %copy-start.6 = (s32[64,1024]{1,0:T(8,128)S(1)}, s32[64,1024]{1,0:T(8,128)}, u32[]{:S(2)}) copy-start(s32[64,1024]{1,0:T(8,128)} %eligible_ref.3) | copy-start | bytes 786436
  46.2 36.2 %copy-start.7 = (s32[64,1024]{1,0:T(8,128)S(1)}, s32[64,1024]{1,0:T(8,128)}, u32[]{:S(2)}) copy-start(s32[64,1024]{1,0:T(8,128)} %eligible_ref.3) | copy-start | bytes 786436
  47.4 9.3 %collective-permute-start.14 = (bf16[2,64,256]{2,1,0:T(8,128)(2,1)S(1)}, bf16[2,64,256]{2,1,0:T(8,128)(2,1)S(1)}, u32[]{:S(2)}, u32[]{:S(2)}) collective-permute-start(bf16[2,64,256]{2,1,0:T(8,128)(2,1)S(1)} %get-tuple-element.54), channel_id=1, source_target_pairs={{0,14},{2,12},{4,10},{6,8},{8,6},{10,4},{12,2},{14,0},{1,15},{3,13... | collective-permute-start | bytes 196616 | tf_op jit(solution)/shard_map/ppermute | solution.py:162
  51.4 6.8 %collective-permute-start.15 = (bf16[2,64,256]{2,1,0:T(8,128)(2,1)S(1)}, bf16[2,64,256]{2,1,0:T(8,128)(2,1)S(1)}, u32[]{:S(2)}, u32[]{:S(2)}) collective-permute-start(bf16[2,64,256]{2,1,0:T(8,128)(2,1)S(1)} %get-tuple-element.55), channel_id=1, source_target_pairs={{0,12},{2,14},{4,8},{6,10},{8,4},{10,6},{12,0},{14,2},{1,13},{3,15... | collective-permute-start | bytes 196616 | tf_op jit(solution)/shard_map/ppermute | solution.py:162
  51.8 8.8 %collective-permute-start.16 = (bf16[2,64,256]{2,1,0:T(8,128)(2,1)S(1)}, bf16[2,64,256]{2,1,0:T(8,128)(2,1)S(1)}, u32[]{:S(2)}, u32[]{:S(2)}) collective-permute-start(bf16[2,64,256]{2,1,0:T(8,128)(2,1)S(1)} %get-tuple-element.56), channel_id=1, source_target_pairs={{0,10},{2,8},{4,14},{6,12},{8,2},{10,0},{12,6},{14,4},{1,11},{3,9}... | collective-permute-start | bytes 196616 | tf_op jit(solution)/shard_map/ppermute | solution.py:162
  53.8 7.4 %collective-permute-start.17 = (bf16[2,64,256]{2,1,0:T(8,128)(2,1)S(1)}, bf16[2,64,256]{2,1,0:T(8,128)(2,1)S(1)}, u32[]{:S(2)}, u32[]{:S(2)}) collective-permute-start(bf16[2,64,256]{2,1,0:T(8,128)(2,1)S(1)} %get-tuple-element.57), channel_id=1, source_target_pairs={{0,8},{2,10},{4,12},{6,14},{8,0},{10,2},{12,4},{14,6},{1,9},{3,11}... | collective-permute-start | bytes 196616 | tf_op jit(solution)/shard_map/ppermute | solution.py:162
  55.1 6.2 %collective-permute-start.18 = (bf16[2,64,256]{2,1,0:T(8,128)(2,1)S(1)}, bf16[2,64,256]{2,1,0:T(8,128)(2,1)S(1)}, u32[]{:S(2)}, u32[]{:S(2)}) collective-permute-start(bf16[2,64,256]{2,1,0:T(8,128)(2,1)S(1)} %get-tuple-element.58), channel_id=1, source_target_pairs={{0,6},{2,4},{4,2},{6,0},{8,14},{10,12},{12,10},{14,8},{1,7},{3,5},... | collective-permute-start | bytes 196616 | tf_op jit(solution)/shard_map/ppermute | solution.py:162
  56.7 5.1 %collective-permute-start.19 = (bf16[2,64,256]{2,1,0:T(8,128)(2,1)S(1)}, bf16[2,64,256]{2,1,0:T(8,128)(2,1)S(1)}, u32[]{:S(2)}, u32[]{:S(2)}) collective-permute-start(bf16[2,64,256]{2,1,0:T(8,128)(2,1)S(1)} %get-tuple-element.59), channel_id=1, source_target_pairs={{0,4},{2,6},{4,0},{6,2},{8,12},{10,14},{12,8},{14,10},{1,5},{3,7},... | collective-permute-start | bytes 196616 | tf_op jit(solution)/shard_map/ppermute | solution.py:162
  58.3 4.3 %collective-permute-start.20 = (bf16[2,64,256]{2,1,0:T(8,128)(2,1)S(1)}, bf16[2,64,256]{2,1,0:T(8,128)(2,1)S(1)}, u32[]{:S(2)}, u32[]{:S(2)}) collective-permute-start(bf16[2,64,256]{2,1,0:T(8,128)(2,1)S(1)} %get-tuple-element.60), channel_id=1, source_target_pairs={{0,2},{2,0},{4,6},{6,4},{8,10},{10,8},{12,14},{14,12},{1,3},{3,1},... | collective-permute-start | bytes 196616 | tf_op jit(solution)/shard_map/ppermute | solution.py:162
  68.3 8.8 %collective-permute-start.21 = (bf16[2,64,256]{2,1,0:T(8,128)(2,1)S(1)}, bf16[2,64,256]{2,1,0:T(8,128)(2,1)S(1)}, u32[]{:S(2)}, u32[]{:S(2)}) collective-permute-start(bf16[2,64,256]{2,1,0:T(8,128)(2,1)S(1)} %get-tuple-element.62), channel_id=1, source_target_pairs={{0,14},{2,12},{4,10},{6,8},{8,6},{10,4},{12,2},{14,0},{1,15},{3,13... | collective-permute-start | bytes 196616 | tf_op jit(solution)/shard_map/ppermute | solution.py:162
  71.7 6.4 %collective-permute-start.22 = (bf16[2,64,256]{2,1,0:T(8,128)(2,1)S(1)}, bf16[2,64,256]{2,1,0:T(8,128)(2,1)S(1)}, u32[]{:S(2)}, u32[]{:S(2)}) collective-permute-start(bf16[2,64,256]{2,1,0:T(8,128)(2,1)S(1)} %get-tuple-element.63), channel_id=1, source_target_pairs={{0,12},{2,14},{4,8},{6,10},{8,4},{10,6},{12,0},{14,2},{1,13},{3,15... | collective-permute-start | bytes 196616 | tf_op jit(solution)/shard_map/ppermute | solution.py:162
  72.2 8.4 %collective-permute-start.23 = (bf16[2,64,256]{2,1,0:T(8,128)(2,1)S(1)}, bf16[2,64,256]{2,1,0:T(8,128)(2,1)S(1)}, u32[]{:S(2)}, u32[]{:S(2)}) collective-permute-start(bf16[2,64,256]{2,1,0:T(8,128)(2,1)S(1)} %get-tuple-element.64), channel_id=1, source_target_pairs={{0,10},{2,8},{4,14},{6,12},{8,2},{10,0},{12,6},{14,4},{1,11},{3,9}... | collective-permute-start | bytes 196616 | tf_op jit(solution)/shard_map/ppermute | solution.py:162
  74.3 6.3 %collective-permute-start.24 = (bf16[2,64,256]{2,1,0:T(8,128)(2,1)S(1)}, bf16[2,64,256]{2,1,0:T(8,128)(2,1)S(1)}, u32[]{:S(2)}, u32[]{:S(2)}) collective-permute-start(bf16[2,64,256]{2,1,0:T(8,128)(2,1)S(1)} %get-tuple-element.65), channel_id=1, source_target_pairs={{0,8},{2,10},{4,12},{6,14},{8,0},{10,2},{12,4},{14,6},{1,9},{3,11}... | collective-permute-start | bytes 196616 | tf_op jit(solution)/shard_map/ppermute | solution.py:162
  76.0 5.8 %collective-permute-start.25 = (bf16[2,64,256]{2,1,0:T(8,128)(2,1)S(1)}, bf16[2,64,256]{2,1,0:T(8,128)(2,1)S(1)}, u32[]{:S(2)}, u32[]{:S(2)}) collective-permute-start(bf16[2,64,256]{2,1,0:T(8,128)(2,1)S(1)} %get-tuple-element.66), channel_id=1, source_target_pairs={{0,6},{2,4},{4,2},{6,0},{8,14},{10,12},{12,10},{14,8},{1,7},{3,5},... | collective-permute-start | bytes 196616 | tf_op jit(solution)/shard_map/ppermute | solution.py:162
  77.0 4.7 %collective-permute-start.26 = (bf16[2,64,256]{2,1,0:T(8,128)(2,1)S(1)}, bf16[2,64,256]{2,1,0:T(8,128)(2,1)S(1)}, u32[]{:S(2)}, u32[]{:S(2)}) collective-permute-start(bf16[2,64,256]{2,1,0:T(8,128)(2,1)S(1)} %get-tuple-element.67), channel_id=1, source_target_pairs={{0,4},{2,6},{4,0},{6,2},{8,12},{10,14},{12,8},{14,10},{1,5},{3,7},... | collective-permute-start | bytes 196616 | tf_op jit(solution)/shard_map/ppermute | solution.py:162
  78.2 4.3 %collective-permute-start.27 = (bf16[2,64,256]{2,1,0:T(8,128)(2,1)S(1)}, bf16[2,64,256]{2,1,0:T(8,128)(2,1)S(1)}, u32[]{:S(2)}, u32[]{:S(2)}) collective-permute-start(bf16[2,64,256]{2,1,0:T(8,128)(2,1)S(1)} %get-tuple-element.68), channel_id=1, source_target_pairs={{0,2},{2,0},{4,6},{6,4},{8,10},{10,8},{12,14},{14,12},{1,3},{3,1},... | collective-permute-start | bytes 196616 | tf_op jit(solution)/shard_map/ppermute | solution.py:162

commit v4 on v3

--- a/solution.py
+++ b/solution.py
@@ -14,6 +14,7 @@
 
 VMEM = pl.BlockSpec(memory_space=pltpu.VMEM)
 SMEM = pl.BlockSpec(memory_space=pltpu.SMEM)
+HBM = pl.BlockSpec(memory_space=pltpu.HBM)
 PARAMS = pltpu.CompilerParams(vmem_limit_bytes=24 * 1024 * 1024)
 
 
@@ -35,6 +36,21 @@
     for block in range(wire_ref.shape[0]):
         wire_ref[block] = holdings_ref[:, block * size : (block + 1) * size].astype(jnp.bfloat16)
     fill_outgoing(served_ref, me_ref, wire_ref, outgoing)
+
+
+def stage_kernel(cov_ref, staged_ref, sems):
+    parts = sems.shape[0]
+    step = cov_ref.shape[0] // parts
+    copies = [
+        pltpu.make_async_copy(
+            cov_ref.at[pl.ds(part * step, step)], staged_ref.at[pl.ds(part * step, step)], sems.at[part]
+        )
+        for part in range(parts)
+    ]
+    for copy in copies:
+        copy.start()
+    for copy in copies:
+        copy.wait()
 
 
 def pairs_kernel(owners, pairs_ref, me_ref, cov_ref, *refs):
@@ -172,6 +188,16 @@
         compiler_params=PARAMS,
         name="pack_holdings",
     )(served, me, holdings)
+    staged = pl.pallas_call(
+        stage_kernel,
+        out_shape=jax.ShapeDtypeStruct(cov_pairs.shape, cov_pairs.dtype),
+        in_specs=[HBM],
+        out_specs=VMEM,
+        scratch_shapes=[pltpu.SemaphoreType.DMA((4,))],
+        compiler_params=pltpu.CompilerParams(vmem_limit_bytes=12 * 1024 * 1024),
+        cost_estimate=pl.CostEstimate(flops=0, bytes_accessed=2 * cov_pairs.size, transcendentals=0),
+        name="stage_pairs",
+    )(cov_pairs)
     expected = returns_mu.reshape(1, assets)
     state = ()
     for iteration in range(ITERS):
@@ -188,7 +214,7 @@
             ],
             compiler_params=PARAMS,
             name="pair_products",
-        )(pair_slots, me, cov_pairs, *incoming)
+        )(pair_slots, me, staged, *incoming)
         returned = exchange(partial_sums)
         outs = pl.pallas_call(
             functools.partial(update_kernel, last, owners),

time: 84.7 us -> 81.8 us (0.966)
  waiting for transfers between devices: 15.9 us -> 9.9 us
  starting transfers between devices: 45.5 us -> 48.9 us
  local copies, waits for them, and re-layouts: 7.1 us -> 6.2 us
    ppermute x28, waiting for transfers between devices: 15.9 us -> 9.9 us  [exchange(): lax.ppermute(value, 'blk', [(index, index ^ offset) for index in range(ow...]
    ppermute x28, starting transfers between devices: 45.5 us -> 48.9 us  [exchange(): lax.ppermute(value, 'blk', [(index, index ^ offset) for index in range(ow...]
    unnamed x25 -> x21, local copies, waits for them, and re-layouts: 6.74 us -> 5.84 us
  transfers between devices with their start and end apart: 28 -> 28, of which waited for: 16 -> 12; matrix products, arithmetic and copies ran while one was open for 1% -> 1% of each run, Pallas kernels for 0% -> 1%
where the time goes in v4:
time: 81.8 us; the launch traced here: 81.6 us
  starting transfers between devices  48.9 us (60%)
  Pallas kernels  15.8 us (19%)
  waiting for transfers between devices  9.9 us (12%)
  local copies, waits for them, and re-layouts  6.2 us (8%)
  between operations  0.83 us (1%)
    ppermute x28, starting transfers between devices, exchange(): lax.ppermute(value, 'blk', [(index, index ^ offset) for index in range(ow...  48.9 us
    pallas_call x2, Pallas kernels, body(): pl.pallas_call(functools.partial(pairs_kernel, owners), out_shape=[kept]...  11.4 us
    ppermute x28, waiting for transfers between devices, exchange(): lax.ppermute(value, 'blk', [(index, index ^ offset) for index in range(ow...  9.9 us
    unnamed x21, local copies, waits for them, and re-layouts  5.84 us
    pallas_call x2, Pallas kernels, body(): pl.pallas_call(functools.partial(update_kernel, last, owners), out_shape=...  3.19 us
  transfers between devices with their start and end apart: 28, of which 12 were waited for; matrix products, arithmetic and copies ran while one was open for 1% of the time, Pallas kernels for 1%

profile of v4, /device:TPU:0, one launch (start us, length us, event | category | flops | bytes accessed | tf_op | source)
XLA Modules:
  0.0 81.6 jit_solution(1890887537563552035)
XLA Ops:
  0.6 0.7 copy-done
  1.3 0.3 dynamic-slice_reduce_fusion
  1.6 0.1 reshape.14.served_ref
  1.7 1.0 %copy-done.2 = f32[64,1024]{1,0:T(8,128)S(1)} copy-done((f32[64,1024]{1,0:T(8,128)S(1)}, f32[64,1024]{1,0:T(8,128)}, u32[]{:S(2)}) %copy-start.2) | copy-done | bytes 262168
  2.7 0.6 pack_holdings.1
  3.3 6.1 %collective-permute-start = (bf16[2,64,256]{2,1,0:T(8,128)(2,1)S(1)}, bf16[2,64,256]{2,1,0:T(8,128)(2,1)S(1)}, u32[]{:S(2)}, u32[]{:S(2)}) collective-permute-start(bf16[2,64,256]{2,1,0:T(8,128)(2,1)S(1)} %get-tuple-element.38), channel_id=1, source_target_pairs={{0,14},{2,12},{4,10},{6,8},{8,6},{10,4},{12,2},{14,0},{1,15},{3,13... | collective-permute-start | bytes 196616 | tf_op jit(solution)/shard_map/ppermute | solution.py:178
  9.3 0.2 collective-permute-start.1
  9.5 0.7 collective-permute-start.2
  10.3 2.0 %collective-permute-start.3 = (bf16[2,64,256]{2,1,0:T(8,128)(2,1)S(1)}, bf16[2,64,256]{2,1,0:T(8,128)(2,1)S(1)}, u32[]{:S(2)}, u32[]{:S(2)}) collective-permute-start(bf16[2,64,256]{2,1,0:T(8,128)(2,1)S(1)} %get-tuple-element.41), channel_id=1, source_target_pairs={{0,8},{2,10},{4,12},{6,14},{8,0},{10,2},{12,4},{14,6},{1,9},{3,11}... | collective-permute-start | bytes 196616 | tf_op jit(solution)/shard_map/ppermute | solution.py:178
  12.3 2.3 %collective-permute-start.4 = (bf16[2,64,256]{2,1,0:T(8,128)(2,1)S(1)}, bf16[2,64,256]{2,1,0:T(8,128)(2,1)S(1)}, u32[]{:S(2)}, u32[]{:S(2)}) collective-permute-start(bf16[2,64,256]{2,1,0:T(8,128)(2,1)S(1)} %get-tuple-element.42), channel_id=1, source_target_pairs={{0,6},{2,4},{4,2},{6,0},{8,14},{10,12},{12,10},{14,8},{1,7},{3,5},... | collective-permute-start | bytes 196616 | tf_op jit(solution)/shard_map/ppermute | solution.py:178
  14.6 0.8 collective-permute-start.5
  15.4 0.2 collective-permute-done.1.refs_2_
  15.6 0.5 collective-permute-start.6
  16.1 0.8 copy.15.pairs_ref
  16.8 3.4 %copy-done.1 = bf16[64,256,256]{2,1,0:T(8,128)(2,1)S(1)} copy-done((bf16[64,256,256]{2,1,0:T(8,128)(2,1)S(1)}, bf16[64,256,256]{2,1,0:T(8,128)(2,1)}, u32[]{:S(2)}) %copy-start.1) | copy-done | bytes 8388632
  20.2 0.6 stage_pairs.1.cov_ref
  21.0 5.7 %pair_products.2 = (f32[2,64,256]{2,1,0:T(8,128)S(1)}, bf16[2,64,256]{2,1,0:T(8,128)(2,1)S(1)}, bf16[2,64,256]{2,1,0:T(8,128)(2,1)S(1)}, bf16[2,64,256]{2,1,0:T(...) custom-call(s32[1,64,2]{2,1,0:T(8,128)S(1)} %copy.15.pairs_ref, ...), custom_call_target="tpu_custom_call" | custom-call | tf_op jit(solution)/shard_map/pair_products/pallas_call | solution.py:206
  26.7 4.7 %collective-permute-start.7 = (bf16[2,64,256]{2,1,0:T(8,128)(2,1)S(1)}, bf16[2,64,256]{2,1,0:T(8,128)(2,1)S(1)}, u32[]{:S(2)}, u32[]{:S(2)}) collective-permute-start(bf16[2,64,256]{2,1,0:T(8,128)(2,1)S(1)} %get-tuple-element.46), channel_id=1, source_target_pairs={{0,14},{2,12},{4,10},{6,8},{8,6},{10,4},{12,2},{14,0},{1,15},{3,13... | collective-permute-start | bytes 196616 | tf_op jit(solution)/shard_map/ppermute | solution.py:178
  31.4 0.2 collective-permute-start.8
  31.6 2.5 %collective-permute-start.9 = (bf16[2,64,256]{2,1,0:T(8,128)(2,1)S(1)}, bf16[2,64,256]{2,1,0:T(8,128)(2,1)S(1)}, u32[]{:S(2)}, u32[]{:S(2)}) collective-permute-start(bf16[2,64,256]{2,1,0:T(8,128)(2,1)S(1)} %get-tuple-element.48), channel_id=1, source_target_pairs={{0,10},{2,8},{4,14},{6,12},{8,2},{10,0},{12,6},{14,4},{1,11},{3,9}... | collective-permute-start | bytes 196616 | tf_op jit(solution)/shard_map/ppermute | solution.py:178
  34.0 1.1 %collective-permute-start.10 = (bf16[2,64,256]{2,1,0:T(8,128)(2,1)S(1)}, bf16[2,64,256]{2,1,0:T(8,128)(2,1)S(1)}, u32[]{:S(2)}, u32[]{:S(2)}) collective-permute-start(bf16[2,64,256]{2,1,0:T(8,128)(2,1)S(1)} %get-tuple-element.49), channel_id=1, source_target_pairs={{0,8},{2,10},{4,12},{6,14},{8,0},{10,2},{12,4},{14,6},{1,9},{3,11}... | collective-permute-start | bytes 196616 | tf_op jit(solution)/shard_map/ppermute | solution.py:178
  35.2 1.6 %collective-permute-start.11 = (bf16[2,64,256]{2,1,0:T(8,128)(2,1)S(1)}, bf16[2,64,256]{2,1,0:T(8,128)(2,1)S(1)}, u32[]{:S(2)}, u32[]{:S(2)}) collective-permute-start(bf16[2,64,256]{2,1,0:T(8,128)(2,1)S(1)} %get-tuple-element.50), channel_id=1, source_target_pairs={{0,6},{2,4},{4,2},{6,0},{8,14},{10,12},{12,10},{14,8},{1,7},{3,5},... | collective-permute-start | bytes 196616 | tf_op jit(solution)/shard_map/ppermute | solution.py:178
  36.7 0.8 %collective-permute-start.12 = (bf16[2,64,256]{2,1,0:T(8,128)(2,1)S(1)}, bf16[2,64,256]{2,1,0:T(8,128)(2,1)S(1)}, u32[]{:S(2)}, u32[]{:S(2)}) collective-permute-start(bf16[2,64,256]{2,1,0:T(8,128)(2,1)S(1)} %get-tuple-element.51), channel_id=1, source_target_pairs={{0,4},{2,6},{4,0},{6,2},{8,12},{10,14},{12,8},{14,10},{1,5},{3,7},... | collective-permute-start | bytes 196616 | tf_op jit(solution)/shard_map/ppermute | solution.py:178
  37.5 0.2 collective-permute-done.8.refs_2_
  37.8 3.0 %collective-permute-start.13 = (bf16[2,64,256]{2,1,0:T(8,128)(2,1)S(1)}, bf16[2,64,256]{2,1,0:T(8,128)(2,1)S(1)}, u32[]{:S(2)}, u32[]{:S(2)}) collective-permute-start(bf16[2,64,256]{2,1,0:T(8,128)(2,1)S(1)} %get-tuple-element.52), channel_id=1, source_target_pairs={{0,2},{2,0},{4,6},{6,4},{8,10},{10,8},{12,14},{14,12},{1,3},{3,1},... | collective-permute-start | bytes 196616 | tf_op jit(solution)/shard_map/ppermute | solution.py:178
  40.8 0.7 collective-permute-done.9.refs_3_
  41.5 0.9 %collective-permute-done.10.refs_4_ = bf16[2,64,256]{2,1,0:T(8,128)(2,1)S(1)} collective-permute-done((bf16[2,64,256]{2,1,0:T(8,128)(2,1)S(1)}, bf16[2,64,256]{2,1,0:T(8,128)(2,1)S(1)}, u32[]{:S(2)}, u32[]{:S(2)}) %collective-permute-start.10) | collective-permute-done | bytes 65568 | tf_op jit(solution)/shard_map/ppermute | solution.py:178
  42.3 0.7 collective-permute-done.13.refs_7_
  43.1 1.2 %update.2 = (f32[64,1024]{1,0:T(8,128)S(1)}, f32[64,1024]{1,0:T(8,128)S(1)}, f32[64,1024]{1,0:T(8,128)S(1)}, bf16[2,64,256]{2,1,0:T(8,128)(2,1)S(1)}, bf16[2,64,...) custom-call(s32[16]{0:T(128)S(1)} %reshape.14.served_ref, ...), custom_call_target="tpu_custom_call" | custom-call | tf_op jit(solution)/shard_map/update/pallas_call | solution.py:219
  44.3 3.3 %collective-permute-start.14 = (bf16[2,64,256]{2,1,0:T(8,128)(2,1)S(1)}, bf16[2,64,256]{2,1,0:T(8,128)(2,1)S(1)}, u32[]{:S(2)}, u32[]{:S(2)}) collective-permute-start(bf16[2,64,256]{2,1,0:T(8,128)(2,1)S(1)} %get-tuple-element.54), channel_id=1, source_target_pairs={{0,14},{2,12},{4,10},{6,8},{8,6},{10,4},{12,2},{14,0},{1,15},{3,13... | collective-permute-start | bytes 196616 | tf_op jit(solution)/shard_map/ppermute | solution.py:178
  47.6 2.1 %collective-permute-start.15 = (bf16[2,64,256]{2,1,0:T(8,128)(2,1)S(1)}, bf16[2,64,256]{2,1,0:T(8,128)(2,1)S(1)}, u32[]{:S(2)}, u32[]{:S(2)}) collective-permute-start(bf16[2,64,256]{2,1,0:T(8,128)(2,1)S(1)} %get-tuple-element.55), channel_id=1, source_target_pairs={{0,12},{2,14},{4,8},{6,10},{8,4},{10,6},{12,0},{14,2},{1,13},{3,15... | collective-permute-start | bytes 196616 | tf_op jit(solution)/shard_map/ppermute | solution.py:178
  49.6 0.6 collective-permute-start.16
  50.2 1.8 %collective-permute-start.17 = (bf16[2,64,256]{2,1,0:T(8,128)(2,1)S(1)}, bf16[2,64,256]{2,1,0:T(8,128)(2,1)S(1)}, u32[]{:S(2)}, u32[]{:S(2)}) collective-permute-start(bf16[2,64,256]{2,1,0:T(8,128)(2,1)S(1)} %get-tuple-element.57), channel_id=1, source_target_pairs={{0,8},{2,10},{4,12},{6,14},{8,0},{10,2},{12,4},{14,6},{1,9},{3,11}... | collective-permute-start | bytes 196616 | tf_op jit(solution)/shard_map/ppermute | solution.py:178
  52.0 0.8 %collective-permute-start.18 = (bf16[2,64,256]{2,1,0:T(8,128)(2,1)S(1)}, bf16[2,64,256]{2,1,0:T(8,128)(2,1)S(1)}, u32[]{:S(2)}, u32[]{:S(2)}) collective-permute-start(bf16[2,64,256]{2,1,0:T(8,128)(2,1)S(1)} %get-tuple-element.58), channel_id=1, source_target_pairs={{0,6},{2,4},{4,2},{6,0},{8,14},{10,12},{12,10},{14,8},{1,7},{3,5},... | collective-permute-start | bytes 196616 | tf_op jit(solution)/shard_map/ppermute | solution.py:178
  52.9 2.6 %collective-permute-start.19 = (bf16[2,64,256]{2,1,0:T(8,128)(2,1)S(1)}, bf16[2,64,256]{2,1,0:T(8,128)(2,1)S(1)}, u32[]{:S(2)}, u32[]{:S(2)}) collective-permute-start(bf16[2,64,256]{2,1,0:T(8,128)(2,1)S(1)} %get-tuple-element.59), channel_id=1, source_target_pairs={{0,4},{2,6},{4,0},{6,2},{8,12},{10,14},{12,8},{14,10},{1,5},{3,7},... | collective-permute-start | bytes 196616 | tf_op jit(solution)/shard_map/ppermute | solution.py:178
  55.5 0.6 collective-permute-done.16.refs_3_
  56.1 1.7 %collective-permute-done.17.refs_4_ = bf16[2,64,256]{2,1,0:T(8,128)(2,1)S(1)} collective-permute-done((bf16[2,64,256]{2,1,0:T(8,128)(2,1)S(1)}, bf16[2,64,256]{2,1,0:T(8,128)(2,1)S(1)}, u32[]{:S(2)}, u32[]{:S(2)}) %collective-permute-start.17) | collective-permute-done | bytes 65568 | tf_op jit(solution)/shard_map/ppermute | solution.py:178
  57.8 1.3 %collective-permute-done.19.refs_6_ = bf16[2,64,256]{2,1,0:T(8,128)(2,1)S(1)} collective-permute-done((bf16[2,64,256]{2,1,0:T(8,128)(2,1)S(1)}, bf16[2,64,256]{2,1,0:T(8,128)(2,1)S(1)}, u32[]{:S(2)}, u32[]{:S(2)}) %collective-permute-start.19) | collective-permute-done | bytes 65568 | tf_op jit(solution)/shard_map/ppermute | solution.py:178
  59.1 0.6 collective-permute-done.20.refs_7_
  59.8 5.7 %pair_products.3 = (f32[2,64,256]{2,1,0:T(8,128)S(1)}, bf16[2,64,256]{2,1,0:T(8,128)(2,1)S(1)}, bf16[2,64,256]{2,1,0:T(8,128)(2,1)S(1)}, bf16[2,64,256]{2,1,0:T(...) custom-call(s32[1,64,2]{2,1,0:T(8,128)S(1)} %copy.15.pairs_ref, ...), custom_call_target="tpu_custom_call" | custom-call | tf_op jit(solution)/shard_map/pair_products/pallas_call | solution.py:206
  65.5 2.1 %collective-permute-start.21 = (bf16[2,64,256]{2,1,0:T(8,128)(2,1)S(1)}, bf16[2,64,256]{2,1,0:T(8,128)(2,1)S(1)}, u32[]{:S(2)}, u32[]{:S(2)}) collective-permute-start(bf16[2,64,256]{2,1,0:T(8,128)(2,1)S(1)} %get-tuple-element.62), channel_id=1, source_target_pairs={{0,14},{2,12},{4,10},{6,8},{8,6},{10,4},{12,2},{14,0},{1,15},{3,13... | collective-permute-start | bytes 196616 | tf_op jit(solution)/shard_map/ppermute | solution.py:178
  67.6 1.9 %collective-permute-start.22 = (bf16[2,64,256]{2,1,0:T(8,128)(2,1)S(1)}, bf16[2,64,256]{2,1,0:T(8,128)(2,1)S(1)}, u32[]{:S(2)}, u32[]{:S(2)}) collective-permute-start(bf16[2,64,256]{2,1,0:T(8,128)(2,1)S(1)} %get-tuple-element.63), channel_id=1, source_target_pairs={{0,12},{2,14},{4,8},{6,10},{8,4},{10,6},{12,0},{14,2},{1,13},{3,15... | collective-permute-start | bytes 196616 | tf_op jit(solution)/shard_map/ppermute | solution.py:178
  69.5 3.7 %collective-permute-start.24 = (bf16[2,64,256]{2,1,0:T(8,128)(2,1)S(1)}, bf16[2,64,256]{2,1,0:T(8,128)(2,1)S(1)}, u32[]{:S(2)}, u32[]{:S(2)}) collective-permute-start(bf16[2,64,256]{2,1,0:T(8,128)(2,1)S(1)} %get-tuple-element.65), channel_id=1, source_target_pairs={{0,8},{2,10},{4,12},{6,14},{8,0},{10,2},{12,4},{14,6},{1,9},{3,11}... | collective-permute-start | bytes 196616 | tf_op jit(solution)/shard_map/ppermute | solution.py:178
  73.2 2.1 %collective-permute-start.26 = (bf16[2,64,256]{2,1,0:T(8,128)(2,1)S(1)}, bf16[2,64,256]{2,1,0:T(8,128)(2,1)S(1)}, u32[]{:S(2)}, u32[]{:S(2)}) collective-permute-start(bf16[2,64,256]{2,1,0:T(8,128)(2,1)S(1)} %get-tuple-element.67), channel_id=1, source_target_pairs={{0,4},{2,6},{4,0},{6,2},{8,12},{10,14},{12,8},{14,10},{1,5},{3,7},... | collective-permute-start | bytes 196616 | tf_op jit(solution)/shard_map/ppermute | solution.py:178
  75.3 1.4 %collective-permute-start.27 = (bf16[2,64,256]{2,1,0:T(8,128)(2,1)S(1)}, bf16[2,64,256]{2,1,0:T(8,128)(2,1)S(1)}, u32[]{:S(2)}, u32[]{:S(2)}) collective-permute-start(bf16[2,64,256]{2,1,0:T(8,128)(2,1)S(1)} %get-tuple-element.68), channel_id=1, source_target_pairs={{0,2},{2,0},{4,6},{6,4},{8,10},{10,8},{12,14},{14,12},{1,3},{3,1},... | collective-permute-start | bytes 196616 | tf_op jit(solution)/shard_map/ppermute | solution.py:178
  76.7 1.7 %collective-permute-done.25.refs_5_ = bf16[2,64,256]{2,1,0:T(8,128)(2,1)S(1)} collective-permute-done((bf16[2,64,256]{2,1,0:T(8,128)(2,1)S(1)}, bf16[2,64,256]{2,1,0:T(8,128)(2,1)S(1)}, u32[]{:S(2)}, u32[]{:S(2)}) %collective-permute-start.25) | collective-permute-done | bytes 65568 | tf_op jit(solution)/shard_map/ppermute | solution.py:178
  78.4 1.2 %collective-permute-done.27.refs_7_ = bf16[2,64,256]{2,1,0:T(8,128)(2,1)S(1)} collective-permute-done((bf16[2,64,256]{2,1,0:T(8,128)(2,1)S(1)}, bf16[2,64,256]{2,1,0:T(8,128)(2,1)S(1)}, u32[]{:S(2)}, u32[]{:S(2)}) %collective-permute-start.27) | collective-permute-done | bytes 65568 | tf_op jit(solution)/shard_map/ppermute | solution.py:178
  79.6 2.0 %update.3 = (f32[64,1024]{1,0:T(8,128)}, f32[64,1024]{1,0:T(8,128)}) custom-call(s32[16]{0:T(128)S(1)} %reshape.14.served_ref, s32[1]{0:T(128)} %bitcast.me_ref, s32[4]{0:T(128)S(1)} %copy-done.8, f32[8]{0:T(128)S(1)} %copy-done.9, f32[2,64]{1,0:T(2,128)S(1)} %copy-done.7, f32[64,1024]{1,0:T(8,128)S(1)} %copy-done.3, s32[64,1024]{1,0:T(8,128)S(1)} %copy-done.5, ...), custom_call_target="tpu_custom_call" | custom-call | tf_op jit(solution)/shard_map/update/pallas_call | solution.py:219
  (37 shorter events, 0.2 us)
Async XLA Ops:
  0.6 0.7 copy-start
  1.7 1.0 %copy-start.2 = (f32[64,1024]{1,0:T(8,128)S(1)}, f32[64,1024]{1,0:T(8,128)}, u32[]{:S(2)}) copy-start(f32[64,1024]{1,0:T(8,128)} %holdings_ref.5) | copy-start | bytes 786436
  3.3 11.4 %collective-permute-start = (bf16[2,64,256]{2,1,0:T(8,128)(2,1)S(1)}, bf16[2,64,256]{2,1,0:T(8,128)(2,1)S(1)}, u32[]{:S(2)}, u32[]{:S(2)}) collective-permute-start(bf16[2,64,256]{2,1,0:T(8,128)(2,1)S(1)} %get-tuple-element.38), channel_id=1, source_target_pairs={{0,14},{2,12},{4,10},{6,8},{8,6},{10,4},{12,2},{14,0},{1,15},{3,13... | collective-permute-start | bytes 196616 | tf_op jit(solution)/shard_map/ppermute | solution.py:178
  9.3 6.3 %collective-permute-start.1 = (bf16[2,64,256]{2,1,0:T(8,128)(2,1)S(1)}, bf16[2,64,256]{2,1,0:T(8,128)(2,1)S(1)}, u32[]{:S(2)}, u32[]{:S(2)}) collective-permute-start(bf16[2,64,256]{2,1,0:T(8,128)(2,1)S(1)} %get-tuple-element.39), channel_id=1, source_target_pairs={{0,12},{2,14},{4,8},{6,10},{8,4},{10,6},{12,0},{14,2},{1,13},{3,15... | collective-permute-start | bytes 196616 | tf_op jit(solution)/shard_map/ppermute | solution.py:178
  9.5 11.3 %collective-permute-start.2 = (bf16[2,64,256]{2,1,0:T(8,128)(2,1)S(1)}, bf16[2,64,256]{2,1,0:T(8,128)(2,1)S(1)}, u32[]{:S(2)}, u32[]{:S(2)}) collective-permute-start(bf16[2,64,256]{2,1,0:T(8,128)(2,1)S(1)} %get-tuple-element.40), channel_id=1, source_target_pairs={{0,10},{2,8},{4,14},{6,12},{8,2},{10,0},{12,6},{14,4},{1,11},{3,9}... | collective-permute-start | bytes 196616 | tf_op jit(solution)/shard_map/ppermute | solution.py:178
  10.3 10.6 %collective-permute-start.3 = (bf16[2,64,256]{2,1,0:T(8,128)(2,1)S(1)}, bf16[2,64,256]{2,1,0:T(8,128)(2,1)S(1)}, u32[]{:S(2)}, u32[]{:S(2)}) collective-permute-start(bf16[2,64,256]{2,1,0:T(8,128)(2,1)S(1)} %get-tuple-element.41), channel_id=1, source_target_pairs={{0,8},{2,10},{4,12},{6,14},{8,0},{10,2},{12,4},{14,6},{1,9},{3,11}... | collective-permute-start | bytes 196616 | tf_op jit(solution)/shard_map/ppermute | solution.py:178
  12.3 8.6 %collective-permute-start.4 = (bf16[2,64,256]{2,1,0:T(8,128)(2,1)S(1)}, bf16[2,64,256]{2,1,0:T(8,128)(2,1)S(1)}, u32[]{:S(2)}, u32[]{:S(2)}) collective-permute-start(bf16[2,64,256]{2,1,0:T(8,128)(2,1)S(1)} %get-tuple-element.42), channel_id=1, source_target_pairs={{0,6},{2,4},{4,2},{6,0},{8,14},{10,12},{12,10},{14,8},{1,7},{3,5},... | collective-permute-start | bytes 196616 | tf_op jit(solution)/shard_map/ppermute | solution.py:178
  14.6 6.4 %collective-permute-start.5 = (bf16[2,64,256]{2,1,0:T(8,128)(2,1)S(1)}, bf16[2,64,256]{2,1,0:T(8,128)(2,1)S(1)}, u32[]{:S(2)}, u32[]{:S(2)}) collective-permute-start(bf16[2,64,256]{2,1,0:T(8,128)(2,1)S(1)} %get-tuple-element.43), channel_id=1, source_target_pairs={{0,4},{2,6},{4,0},{6,2},{8,12},{10,14},{12,8},{14,10},{1,5},{3,7},... | collective-permute-start | bytes 196616 | tf_op jit(solution)/shard_map/ppermute | solution.py:178
  15.6 5.4 %collective-permute-start.6 = (bf16[2,64,256]{2,1,0:T(8,128)(2,1)S(1)}, bf16[2,64,256]{2,1,0:T(8,128)(2,1)S(1)}, u32[]{:S(2)}, u32[]{:S(2)}) collective-permute-start(bf16[2,64,256]{2,1,0:T(8,128)(2,1)S(1)} %get-tuple-element.44), channel_id=1, source_target_pairs={{0,2},{2,0},{4,6},{6,4},{8,10},{10,8},{12,14},{14,12},{1,3},{3,1},... | collective-permute-start | bytes 196616 | tf_op jit(solution)/shard_map/ppermute | solution.py:178
  16.8 3.4 %copy-start.1 = (bf16[64,256,256]{2,1,0:T(8,128)(2,1)S(1)}, bf16[64,256,256]{2,1,0:T(8,128)(2,1)}, u32[]{:S(2)}) copy-start(bf16[64,256,256]{2,1,0:T(8,128)(2,1)} %cov_ref.1) | copy-start | bytes 25165828
  20.8 22.2 %copy-start.3 = (f32[64,1024]{1,0:T(8,128)S(1)}, f32[64,1024]{1,0:T(8,128)}, u32[]{:S(2)}) copy-start(f32[64,1024]{1,0:T(8,128)} %holdings_ref.5) | copy-start | bytes 786436
  20.8 22.2 %copy-start.4 = (bf16[4,256,256]{2,1,0:T(8,128)(2,1)S(1)}, bf16[4,256,256]{2,1,0:T(8,128)(2,1)}, u32[]{:S(2)}) copy-start(bf16[4,256,256]{2,1,0:T(8,128)(2,1)} %diag_ref.3) | copy-start | bytes 1572868
  20.8 22.2 %copy-start.5 = (s32[64,1024]{1,0:T(8,128)S(1)}, s32[64,1024]{1,0:T(8,128)}, u32[]{:S(2)}) copy-start(s32[64,1024]{1,0:T(8,128)} %eligible_ref.3) | copy-start | bytes 786436
  20.8 22.2 %copy-start.6 = (f32[1024]{0:T(1024)S(1)}, f32[1024]{0:T(1024)}, u32[]{:S(2)}) copy-start(f32[1024]{0:T(1024)} %param.12) | copy-start | bytes 12292
  20.9 22.2 %copy-start.7 = (f32[2,64]{1,0:T(2,128)S(1)}, f32[2,64]{1,0:T(2,128)}, u32[]{:S(2)}) copy-start(f32[2,64]{1,0:T(2,128)} %slopes_ref.3) | copy-start | bytes 1540
  20.9 22.2 %copy-start.8 = (s32[4]{0:T(128)S(1)}, s32[4]{0:T(128)}, u32[]{:S(2)}) copy-start(s32[4]{0:T(128)} %knee_index_ref.3) | copy-start | bytes 52
  20.9 22.2 %copy-start.9 = (f32[8]{0:T(128)S(1)}, f32[8]{0:T(128)}, u32[]{:S(2)}) copy-start(f32[8]{0:T(128)} %knee_levels_ref.3) | copy-start | bytes 100
  26.7 10.0 %collective-permute-start.7 = (bf16[2,64,256]{2,1,0:T(8,128)(2,1)S(1)}, bf16[2,64,256]{2,1,0:T(8,128)(2,1)S(1)}, u32[]{:S(2)}, u32[]{:S(2)}) collective-permute-start(bf16[2,64,256]{2,1,0:T(8,128)(2,1)S(1)} %get-tuple-element.46), channel_id=1, source_target_pairs={{0,14},{2,12},{4,10},{6,8},{8,6},{10,4},{12,2},{14,0},{1,15},{3,13... | collective-permute-start | bytes 196616 | tf_op jit(solution)/shard_map/ppermute | solution.py:178
  31.4 6.4 %collective-permute-start.8 = (bf16[2,64,256]{2,1,0:T(8,128)(2,1)S(1)}, bf16[2,64,256]{2,1,0:T(8,128)(2,1)S(1)}, u32[]{:S(2)}, u32[]{:S(2)}) collective-permute-start(bf16[2,64,256]{2,1,0:T(8,128)(2,1)S(1)} %get-tuple-element.47), channel_id=1, source_target_pairs={{0,12},{2,14},{4,8},{6,10},{8,4},{10,6},{12,0},{14,2},{1,13},{3,15... | collective-permute-start | bytes 196616 | tf_op jit(solution)/shard_map/ppermute | solution.py:178
  31.6 9.9 %collective-permute-start.9 = (bf16[2,64,256]{2,1,0:T(8,128)(2,1)S(1)}, bf16[2,64,256]{2,1,0:T(8,128)(2,1)S(1)}, u32[]{:S(2)}, u32[]{:S(2)}) collective-permute-start(bf16[2,64,256]{2,1,0:T(8,128)(2,1)S(1)} %get-tuple-element.48), channel_id=1, source_target_pairs={{0,10},{2,8},{4,14},{6,12},{8,2},{10,0},{12,6},{14,4},{1,11},{3,9}... | collective-permute-start | bytes 196616 | tf_op jit(solution)/shard_map/ppermute | solution.py:178
  34.0 8.3 %collective-permute-start.10 = (bf16[2,64,256]{2,1,0:T(8,128)(2,1)S(1)}, bf16[2,64,256]{2,1,0:T(8,128)(2,1)S(1)}, u32[]{:S(2)}, u32[]{:S(2)}) collective-permute-start(bf16[2,64,256]{2,1,0:T(8,128)(2,1)S(1)} %get-tuple-element.49), channel_id=1, source_target_pairs={{0,8},{2,10},{4,12},{6,14},{8,0},{10,2},{12,4},{14,6},{1,9},{3,11}... | collective-permute-start | bytes 196616 | tf_op jit(solution)/shard_map/ppermute | solution.py:178
  35.2 7.2 %collective-permute-start.11 = (bf16[2,64,256]{2,1,0:T(8,128)(2,1)S(1)}, bf16[2,64,256]{2,1,0:T(8,128)(2,1)S(1)}, u32[]{:S(2)}, u32[]{:S(2)}) collective-permute-start(bf16[2,64,256]{2,1,0:T(8,128)(2,1)S(1)} %get-tuple-element.50), channel_id=1, source_target_pairs={{0,6},{2,4},{4,2},{6,0},{8,14},{10,12},{12,10},{14,8},{1,7},{3,5},... | collective-permute-start | bytes 196616 | tf_op jit(solution)/shard_map/ppermute | solution.py:178
  36.7 5.6 %collective-permute-start.12 = (bf16[2,64,256]{2,1,0:T(8,128)(2,1)S(1)}, bf16[2,64,256]{2,1,0:T(8,128)(2,1)S(1)}, u32[]{:S(2)}, u32[]{:S(2)}) collective-permute-start(bf16[2,64,256]{2,1,0:T(8,128)(2,1)S(1)} %get-tuple-element.51), channel_id=1, source_target_pairs={{0,4},{2,6},{4,0},{6,2},{8,12},{10,14},{12,8},{14,10},{1,5},{3,7},... | collective-permute-start | bytes 196616 | tf_op jit(solution)/shard_map/ppermute | solution.py:178
  37.8 5.3 %collective-permute-start.13 = (bf16[2,64,256]{2,1,0:T(8,128)(2,1)S(1)}, bf16[2,64,256]{2,1,0:T(8,128)(2,1)S(1)}, u32[]{:S(2)}, u32[]{:S(2)}) collective-permute-start(bf16[2,64,256]{2,1,0:T(8,128)(2,1)S(1)} %get-tuple-element.52), channel_id=1, source_target_pairs={{0,2},{2,0},{4,6},{6,4},{8,10},{10,8},{12,14},{14,12},{1,3},{3,1},... | collective-permute-start | bytes 196616 | tf_op jit(solution)/shard_map/ppermute | solution.py:178
  44.3 8.6 %collective-permute-start.14 = (bf16[2,64,256]{2,1,0:T(8,128)(2,1)S(1)}, bf16[2,64,256]{2,1,0:T(8,128)(2,1)S(1)}, u32[]{:S(2)}, u32[]{:S(2)}) collective-permute-start(bf16[2,64,256]{2,1,0:T(8,128)(2,1)S(1)} %get-tuple-element.54), channel_id=1, source_target_pairs={{0,14},{2,12},{4,10},{6,8},{8,6},{10,4},{12,2},{14,0},{1,15},{3,13... | collective-permute-start | bytes 196616 | tf_op jit(solution)/shard_map/ppermute | solution.py:178
  47.6 7.9 %collective-permute-start.15 = (bf16[2,64,256]{2,1,0:T(8,128)(2,1)S(1)}, bf16[2,64,256]{2,1,0:T(8,128)(2,1)S(1)}, u32[]{:S(2)}, u32[]{:S(2)}) collective-permute-start(bf16[2,64,256]{2,1,0:T(8,128)(2,1)S(1)} %get-tuple-element.55), channel_id=1, source_target_pairs={{0,12},{2,14},{4,8},{6,10},{8,4},{10,6},{12,0},{14,2},{1,13},{3,15... | collective-permute-start | bytes 196616 | tf_op jit(solution)/shard_map/ppermute | solution.py:178
  49.6 6.5 %collective-permute-start.16 = (bf16[2,64,256]{2,1,0:T(8,128)(2,1)S(1)}, bf16[2,64,256]{2,1,0:T(8,128)(2,1)S(1)}, u32[]{:S(2)}, u32[]{:S(2)}) collective-permute-start(bf16[2,64,256]{2,1,0:T(8,128)(2,1)S(1)} %get-tuple-element.56), channel_id=1, source_target_pairs={{0,10},{2,8},{4,14},{6,12},{8,2},{10,0},{12,6},{14,4},{1,11},{3,9}... | collective-permute-start | bytes 196616 | tf_op jit(solution)/shard_map/ppermute | solution.py:178
  50.2 7.6 %collective-permute-start.17 = (bf16[2,64,256]{2,1,0:T(8,128)(2,1)S(1)}, bf16[2,64,256]{2,1,0:T(8,128)(2,1)S(1)}, u32[]{:S(2)}, u32[]{:S(2)}) collective-permute-start(bf16[2,64,256]{2,1,0:T(8,128)(2,1)S(1)} %get-tuple-element.57), channel_id=1, source_target_pairs={{0,8},{2,10},{4,12},{6,14},{8,0},{10,2},{12,4},{14,6},{1,9},{3,11}... | collective-permute-start | bytes 196616 | tf_op jit(solution)/shard_map/ppermute | solution.py:178
  52.0 5.8 %collective-permute-start.18 = (bf16[2,64,256]{2,1,0:T(8,128)(2,1)S(1)}, bf16[2,64,256]{2,1,0:T(8,128)(2,1)S(1)}, u32[]{:S(2)}, u32[]{:S(2)}) collective-permute-start(bf16[2,64,256]{2,1,0:T(8,128)(2,1)S(1)} %get-tuple-element.58), channel_id=1, source_target_pairs={{0,6},{2,4},{4,2},{6,0},{8,14},{10,12},{12,10},{14,8},{1,7},{3,5},... | collective-permute-start | bytes 196616 | tf_op jit(solution)/shard_map/ppermute | solution.py:178
  52.9 6.3 %collective-permute-start.19 = (bf16[2,64,256]{2,1,0:T(8,128)(2,1)S(1)}, bf16[2,64,256]{2,1,0:T(8,128)(2,1)S(1)}, u32[]{:S(2)}, u32[]{:S(2)}) collective-permute-start(bf16[2,64,256]{2,1,0:T(8,128)(2,1)S(1)} %get-tuple-element.59), channel_id=1, source_target_pairs={{0,4},{2,6},{4,0},{6,2},{8,12},{10,14},{12,8},{14,10},{1,5},{3,7},... | collective-permute-start | bytes 196616 | tf_op jit(solution)/shard_map/ppermute | solution.py:178
  55.5 4.3 %collective-permute-start.20 = (bf16[2,64,256]{2,1,0:T(8,128)(2,1)S(1)}, bf16[2,64,256]{2,1,0:T(8,128)(2,1)S(1)}, u32[]{:S(2)}, u32[]{:S(2)}) collective-permute-start(bf16[2,64,256]{2,1,0:T(8,128)(2,1)S(1)} %get-tuple-element.60), channel_id=1, source_target_pairs={{0,2},{2,0},{4,6},{6,4},{8,10},{10,8},{12,14},{14,12},{1,3},{3,1},... | collective-permute-start | bytes 196616 | tf_op jit(solution)/shard_map/ppermute | solution.py:178
  65.5 7.8 %collective-permute-start.21 = (bf16[2,64,256]{2,1,0:T(8,128)(2,1)S(1)}, bf16[2,64,256]{2,1,0:T(8,128)(2,1)S(1)}, u32[]{:S(2)}, u32[]{:S(2)}) collective-permute-start(bf16[2,64,256]{2,1,0:T(8,128)(2,1)S(1)} %get-tuple-element.62), channel_id=1, source_target_pairs={{0,14},{2,12},{4,10},{6,8},{8,6},{10,4},{12,2},{14,0},{1,15},{3,13... | collective-permute-start | bytes 196616 | tf_op jit(solution)/shard_map/ppermute | solution.py:178
  67.6 7.8 %collective-permute-start.22 = (bf16[2,64,256]{2,1,0:T(8,128)(2,1)S(1)}, bf16[2,64,256]{2,1,0:T(8,128)(2,1)S(1)}, u32[]{:S(2)}, u32[]{:S(2)}) collective-permute-start(bf16[2,64,256]{2,1,0:T(8,128)(2,1)S(1)} %get-tuple-element.63), channel_id=1, source_target_pairs={{0,12},{2,14},{4,8},{6,10},{8,4},{10,6},{12,0},{14,2},{1,13},{3,15... | collective-permute-start | bytes 196616 | tf_op jit(solution)/shard_map/ppermute | solution.py:178
  69.5 7.2 %collective-permute-start.23 = (bf16[2,64,256]{2,1,0:T(8,128)(2,1)S(1)}, bf16[2,64,256]{2,1,0:T(8,128)(2,1)S(1)}, u32[]{:S(2)}, u32[]{:S(2)}) collective-permute-start(bf16[2,64,256]{2,1,0:T(8,128)(2,1)S(1)} %get-tuple-element.64), channel_id=1, source_target_pairs={{0,10},{2,8},{4,14},{6,12},{8,2},{10,0},{12,6},{14,4},{1,11},{3,9}... | collective-permute-start | bytes 196616 | tf_op jit(solution)/shard_map/ppermute | solution.py:178
  69.5 7.2 %collective-permute-start.24 = (bf16[2,64,256]{2,1,0:T(8,128)(2,1)S(1)}, bf16[2,64,256]{2,1,0:T(8,128)(2,1)S(1)}, u32[]{:S(2)}, u32[]{:S(2)}) collective-permute-start(bf16[2,64,256]{2,1,0:T(8,128)(2,1)S(1)} %get-tuple-element.65), channel_id=1, source_target_pairs={{0,8},{2,10},{4,12},{6,14},{8,0},{10,2},{12,4},{14,6},{1,9},{3,11}... | collective-permute-start | bytes 196616 | tf_op jit(solution)/shard_map/ppermute | solution.py:178
  73.2 5.2 %collective-permute-start.25 = (bf16[2,64,256]{2,1,0:T(8,128)(2,1)S(1)}, bf16[2,64,256]{2,1,0:T(8,128)(2,1)S(1)}, u32[]{:S(2)}, u32[]{:S(2)}) collective-permute-start(bf16[2,64,256]{2,1,0:T(8,128)(2,1)S(1)} %get-tuple-element.66), channel_id=1, source_target_pairs={{0,6},{2,4},{4,2},{6,0},{8,14},{10,12},{12,10},{14,8},{1,7},{3,5},... | collective-permute-start | bytes 196616 | tf_op jit(solution)/shard_map/ppermute | solution.py:178
  73.2 5.1 %collective-permute-start.26 = (bf16[2,64,256]{2,1,0:T(8,128)(2,1)S(1)}, bf16[2,64,256]{2,1,0:T(8,128)(2,1)S(1)}, u32[]{:S(2)}, u32[]{:S(2)}) collective-permute-start(bf16[2,64,256]{2,1,0:T(8,128)(2,1)S(1)} %get-tuple-element.67), channel_id=1, source_target_pairs={{0,4},{2,6},{4,0},{6,2},{8,12},{10,14},{12,8},{14,10},{1,5},{3,7},... | collective-permute-start | bytes 196616 | tf_op jit(solution)/shard_map/ppermute | solution.py:178
  75.3 4.3 %collective-permute-start.27 = (bf16[2,64,256]{2,1,0:T(8,128)(2,1)S(1)}, bf16[2,64,256]{2,1,0:T(8,128)(2,1)S(1)}, u32[]{:S(2)}, u32[]{:S(2)}) collective-permute-start(bf16[2,64,256]{2,1,0:T(8,128)(2,1)S(1)} %get-tuple-element.68), channel_id=1, source_target_pairs={{0,2},{2,0},{4,6},{6,4},{8,10},{10,8},{12,14},{14,12},{1,3},{3,1},... | collective-permute-start | bytes 196616 | tf_op jit(solution)/shard_map/ppermute | solution.py:178

commit v5 on v4

--- a/solution.py
+++ b/solution.py
@@ -19,7 +19,11 @@
 
 
 def order(owners):
-    return (0, *reversed(range(1, owners)))
+    offsets = list(reversed(range(1, owners)))
+    offsets[:2] = reversed(offsets[:2])
+    offsets.remove(owners // 2 - 1)
+    offsets.insert(1, owners // 2 - 1)
+    return (0, *offsets)
 
 
 def fill_outgoing(served_ref, me_ref, wire_ref, outgoing):
@@ -38,7 +42,7 @@
     fill_outgoing(served_ref, me_ref, wire_ref, outgoing)
 
 
-def stage_kernel(cov_ref, staged_ref, sems):
+def stage_kernel(owners, capacity, cov_ref, pairs_ref, me_ref, staged_ref, places_ref, sems):
     parts = sems.shape[0]
     step = cov_ref.shape[0] // parts
     copies = [
@@ -49,23 +53,36 @@
     ]
     for copy in copies:
         copy.start()
+    pairs, width = pairs_ref.shape[1], places_ref.shape[1]
+    shape = (pairs, width)
+    lane_is_pair = lax.broadcasted_iota(jnp.int32, shape, 0) == lax.broadcasted_iota(jnp.int32, shape, 1)
+    offset_rank = [0] * owners
+    for rank, offset in enumerate(order(owners)):
+        offset_rank[offset] = rank
+    places_ref[...] = jnp.zeros_like(places_ref)
+    for side in range(2):
+        slot = pairs_ref[0, :, side : side + 1]
+        owner = lax.div(slot, jnp.full_like(slot, capacity))
+        offset = owner ^ me_ref[0]
+        rank = jnp.zeros_like(slot)
+        for candidate in range(1, owners):
+            rank = jnp.where(offset == candidate, offset_rank[candidate], rank)
+        place = rank * capacity + slot - owner * capacity
+        places_ref[pl.ds(side, 1), :] = jnp.sum(jnp.where(lane_is_pair, place, 0), axis=0, keepdims=True)
     for copy in copies:
         copy.wait()
 
 
-def pairs_kernel(owners, pairs_ref, me_ref, cov_ref, *refs):
+def pairs_kernel(owners, places_ref, cov_ref, *refs):
     incoming, partial, (slot_rows, total) = refs[:owners], refs[owners : 2 * owners], refs[2 * owners :]
     capacity = incoming[0].shape[0]
-    for offset, rows_ref in zip(order(owners), incoming):
-        slot_rows[pl.ds(offset * capacity, capacity)] = rows_ref[...]
+    for rank, rows_ref in enumerate(incoming):
+        slot_rows[pl.ds(rank * capacity, capacity)] = rows_ref[...]
     total[...] = jnp.zeros_like(total)
 
-    def place(slot):
-        return ((slot // capacity) ^ me_ref[0]) * capacity + slot % capacity
-
     def one(pair, carry):
-        first = place(pairs_ref[0, pair, 0])
-        second = place(pairs_ref[0, pair, 1])
+        first = places_ref[0, pair]
+        second = places_ref[1, pair]
         block = cov_ref[pair]
         to_first = lax.dot_general(
             slot_rows[second], block, (((1,), (1,)), ((), ())), preferred_element_type=jnp.float32
@@ -75,9 +92,9 @@
         total[second] += to_second
         return carry
 
-    lax.fori_loop(0, cov_ref.shape[0], one, 0, unroll=16)
-    for offset, out_ref in zip(order(owners), partial):
-        out_ref[...] = total[pl.ds(offset * capacity, capacity)].astype(out_ref.dtype)
+    lax.fori_loop(0, cov_ref.shape[0], one, 0, unroll=32)
+    for rank, out_ref in enumerate(partial):
+        out_ref[...] = total[pl.ds(rank * capacity, capacity)].astype(out_ref.dtype)
 
 
 def column(row, rows):
@@ -188,16 +205,20 @@
         compiler_params=PARAMS,
         name="pack_holdings",
     )(served, me, holdings)
-    staged = pl.pallas_call(
-        stage_kernel,
-        out_shape=jax.ShapeDtypeStruct(cov_pairs.shape, cov_pairs.dtype),
-        in_specs=[HBM],
-        out_specs=VMEM,
+    pairs = cov_pairs.shape[0]
+    staged, places = pl.pallas_call(
+        functools.partial(stage_kernel, owners, capacity),
+        out_shape=[
+            jax.ShapeDtypeStruct(cov_pairs.shape, cov_pairs.dtype),
+            jax.ShapeDtypeStruct((8, -(-pairs // 128) * 128), jnp.int32),
+        ],
+        in_specs=[HBM, VMEM, SMEM],
+        out_specs=[VMEM, VMEM],
         scratch_shapes=[pltpu.SemaphoreType.DMA((4,))],
         compiler_params=pltpu.CompilerParams(vmem_limit_bytes=12 * 1024 * 1024),
         cost_estimate=pl.CostEstimate(flops=0, bytes_accessed=2 * cov_pairs.size, transcendentals=0),
         name="stage_pairs",
-    )(cov_pairs)
+    )(cov_pairs, pair_slots, me)
     expected = returns_mu.reshape(1, assets)
     state = ()
     for iteration in range(ITERS):
@@ -206,7 +227,7 @@
         partial_sums = pl.pallas_call(
             functools.partial(pairs_kernel, owners),
             out_shape=[kept] + [sent] * (owners - 1),
-            in_specs=[SMEM, SMEM] + [VMEM] * (1 + owners),
+            in_specs=[SMEM] + [VMEM] * (1 + owners),
             out_specs=[VMEM] * owners,
             scratch_shapes=[
                 pltpu.VMEM((owners * capacity, rows, size), jnp.bfloat16),
@@ -214,7 +235,7 @@
             ],
             compiler_params=PARAMS,
             name="pair_products",
-        )(pair_slots, me, staged, *incoming)
+        )(places, staged, *incoming)
         returned = exchange(partial_sums)
         outs = pl.pallas_call(
             functools.partial(update_kernel, last, owners),

time: 81.8 us -> 78.4 us (0.958)
  starting transfers between devices: 48.9 us -> 43.5 us
  waiting for transfers between devices: 9.9 us -> 13.1 us
  Pallas kernels: 15.8 us -> 14.6 us
    ppermute x28, starting transfers between devices: 48.9 us -> 43.5 us  [exchange(): lax.ppermute(value, 'blk', [(index, index ^ offset) for index in range(ow...]
    ppermute x28, waiting for transfers between devices: 9.9 us -> 13.1 us  [exchange(): lax.ppermute(value, 'blk', [(index, index ^ offset) for index in range(ow...]
    pallas_call x2, Pallas kernels: 11.4 us -> 10.1 us  [body(): pl.pallas_call(functools.partial(pairs_kernel, owners), out_shape=[kept]...]
  transfers between devices with their start and end apart: 28 -> 28, of which waited for: 12 -> 7; matrix products, arithmetic and copies ran while one was open for 1% -> 1% of each run, Pallas kernels for 1% -> 1%
where the time goes in v5:
time: 78.4 us; the launch traced here: 78.2 us
  starting transfers between devices  43.5 us (55%)
  Pallas kernels  14.6 us (19%)
  waiting for transfers between devices  13.1 us (17%)
  local copies, waits for them, and re-layouts  6.19 us (8%)
  between operations  0.81 us (1%)
    ppermute x28, starting transfers between devices, exchange(): lax.ppermute(value, 'blk', [(index, index ^ offset) for index in range(ow...  43.5 us
    ppermute x28, waiting for transfers between devices, exchange(): lax.ppermute(value, 'blk', [(index, index ^ offset) for index in range(ow...  13.1 us
    pallas_call x2, Pallas kernels, body(): pl.pallas_call(functools.partial(pairs_kernel, owners), out_shape=[kept]...  10.1 us
    unnamed x21, local copies, waits for them, and re-layouts  5.83 us
    pallas_call x2, Pallas kernels, body(): pl.pallas_call(functools.partial(update_kernel, last, owners), out_shape=...  3.2 us
  transfers between devices with their start and end apart: 28, of which 7 were waited for; matrix products, arithmetic and copies ran while one was open for 1% of the time, Pallas kernels for 1%

profile of v5, /device:TPU:0, one launch (start us, length us, event | category | flops | bytes accessed | tf_op | source)
XLA Modules:
  0.0 78.2 jit_solution(13199015464312813002)
XLA Ops:
  0.6 0.0 copy-start
  0.6 0.7 copy-done
  1.3 0.3 dynamic-slice_reduce_fusion
  1.6 0.1 reshape.14.served_ref
  1.7 1.0 %copy-done.2 = f32[64,1024]{1,0:T(8,128)S(1)} copy-done((f32[64,1024]{1,0:T(8,128)S(1)}, f32[64,1024]{1,0:T(8,128)}, u32[]{:S(2)}) %copy-start.2) | copy-done | bytes 262168
  2.7 0.6 pack_holdings.1
  3.3 5.1 %collective-permute-start = (bf16[2,64,256]{2,1,0:T(8,128)(2,1)S(1)}, bf16[2,64,256]{2,1,0:T(8,128)(2,1)S(1)}, u32[]{:S(2)}, u32[]{:S(2)}) collective-permute-start(bf16[2,64,256]{2,1,0:T(8,128)(2,1)S(1)} %get-tuple-element.42), channel_id=1, source_target_pairs={{0,12},{2,14},{4,8},{6,10},{8,4},{10,6},{12,0},{14,2},{1,13},{3,15... | collective-permute-start | bytes 196616 | tf_op jit(solution)/shard_map/ppermute | solution.py:195
  8.4 0.5 collective-permute-start.1
  8.9 1.3 %collective-permute-start.2 = (bf16[2,64,256]{2,1,0:T(8,128)(2,1)S(1)}, bf16[2,64,256]{2,1,0:T(8,128)(2,1)S(1)}, u32[]{:S(2)}, u32[]{:S(2)}) collective-permute-start(bf16[2,64,256]{2,1,0:T(8,128)(2,1)S(1)} %get-tuple-element.44), channel_id=1, source_target_pairs={{0,14},{2,12},{4,10},{6,8},{8,6},{10,4},{12,2},{14,0},{1,15},{3,13... | collective-permute-start | bytes 196616 | tf_op jit(solution)/shard_map/ppermute | solution.py:195
  10.2 3.5 %collective-permute-start.3 = (bf16[2,64,256]{2,1,0:T(8,128)(2,1)S(1)}, bf16[2,64,256]{2,1,0:T(8,128)(2,1)S(1)}, u32[]{:S(2)}, u32[]{:S(2)}) collective-permute-start(bf16[2,64,256]{2,1,0:T(8,128)(2,1)S(1)} %get-tuple-element.45), channel_id=1, source_target_pairs={{0,10},{2,8},{4,14},{6,12},{8,2},{10,0},{12,6},{14,4},{1,11},{3,9}... | collective-permute-start | bytes 196616 | tf_op jit(solution)/shard_map/ppermute | solution.py:195
  13.7 0.3 collective-permute-start.4
  14.1 0.5 collective-permute-start.5
  14.5 1.3 %collective-permute-start.6 = (bf16[2,64,256]{2,1,0:T(8,128)(2,1)S(1)}, bf16[2,64,256]{2,1,0:T(8,128)(2,1)S(1)}, u32[]{:S(2)}, u32[]{:S(2)}) collective-permute-start(bf16[2,64,256]{2,1,0:T(8,128)(2,1)S(1)} %get-tuple-element.48), channel_id=1, source_target_pairs={{0,2},{2,0},{4,6},{6,4},{8,10},{10,8},{12,14},{14,12},{1,3},{3,1},... | collective-permute-start | bytes 196616 | tf_op jit(solution)/shard_map/ppermute | solution.py:195
  15.8 0.8 copy.13.pairs_ref
  16.6 3.4 %copy-done.1 = bf16[64,256,256]{2,1,0:T(8,128)(2,1)S(1)} copy-done((bf16[64,256,256]{2,1,0:T(8,128)(2,1)S(1)}, bf16[64,256,256]{2,1,0:T(8,128)(2,1)}, u32[]{:S(2)}) %copy-start.1) | copy-done | bytes 8388632
  20.0 0.0 copy-start.9
  20.0 0.7 stage_pairs.1
  20.8 0.0 collective-permute-done.3.refs_4_
  20.8 0.2 collective-permute-done.4.refs_5_
  21.0 5.0 %pair_products.2 = (f32[2,64,256]{2,1,0:T(8,128)S(1)}, bf16[2,64,256]{2,1,0:T(8,128)(2,1)S(1)}, bf16[2,64,256]{2,1,0:T(8,128)(2,1)S(1)}, bf16[2,64,256]{2,1,0:T(...) custom-call(s32[8,128]{1,0:T(8,128)S(1)} %get-tuple-element.39.place, ...), custom_call_target="tpu_custom_call" | custom-call | tf_op jit(solution)/shard_map/pair_products/pallas_call | solution.py:227
  26.1 2.7 %collective-permute-start.7 = (bf16[2,64,256]{2,1,0:T(8,128)(2,1)S(1)}, bf16[2,64,256]{2,1,0:T(8,128)(2,1)S(1)}, u32[]{:S(2)}, u32[]{:S(2)}) collective-permute-start(bf16[2,64,256]{2,1,0:T(8,128)(2,1)S(1)} %get-tuple-element.50), channel_id=1, source_target_pairs={{0,12},{2,14},{4,8},{6,10},{8,4},{10,6},{12,0},{14,2},{1,13},{3,15... | collective-permute-start | bytes 196616 | tf_op jit(solution)/shard_map/ppermute | solution.py:195
  28.7 0.5 collective-permute-start.8
  29.2 1.6 %collective-permute-start.9 = (bf16[2,64,256]{2,1,0:T(8,128)(2,1)S(1)}, bf16[2,64,256]{2,1,0:T(8,128)(2,1)S(1)}, u32[]{:S(2)}, u32[]{:S(2)}) collective-permute-start(bf16[2,64,256]{2,1,0:T(8,128)(2,1)S(1)} %get-tuple-element.52), channel_id=1, source_target_pairs={{0,14},{2,12},{4,10},{6,8},{8,6},{10,4},{12,2},{14,0},{1,15},{3,13... | collective-permute-start | bytes 196616 | tf_op jit(solution)/shard_map/ppermute | solution.py:195
  30.8 3.3 %collective-permute-start.10 = (bf16[2,64,256]{2,1,0:T(8,128)(2,1)S(1)}, bf16[2,64,256]{2,1,0:T(8,128)(2,1)S(1)}, u32[]{:S(2)}, u32[]{:S(2)}) collective-permute-start(bf16[2,64,256]{2,1,0:T(8,128)(2,1)S(1)} %get-tuple-element.53), channel_id=1, source_target_pairs={{0,10},{2,8},{4,14},{6,12},{8,2},{10,0},{12,6},{14,4},{1,11},{3,9}... | collective-permute-start | bytes 196616 | tf_op jit(solution)/shard_map/ppermute | solution.py:195
  34.1 0.3 collective-permute-start.11
  34.4 1.4 %collective-permute-start.12 = (bf16[2,64,256]{2,1,0:T(8,128)(2,1)S(1)}, bf16[2,64,256]{2,1,0:T(8,128)(2,1)S(1)}, u32[]{:S(2)}, u32[]{:S(2)}) collective-permute-start(bf16[2,64,256]{2,1,0:T(8,128)(2,1)S(1)} %get-tuple-element.55), channel_id=1, source_target_pairs={{0,4},{2,6},{4,0},{6,2},{8,12},{10,14},{12,8},{14,10},{1,5},{3,7},... | collective-permute-start | bytes 196616 | tf_op jit(solution)/shard_map/ppermute | solution.py:195
  35.8 0.7 collective-permute-start.13
  36.5 0.1 collective-permute-done.9.refs_3_
  36.6 4.4 %collective-permute-done.10.refs_4_ = bf16[2,64,256]{2,1,0:T(8,128)(2,1)S(1)} collective-permute-done((bf16[2,64,256]{2,1,0:T(8,128)(2,1)S(1)}, bf16[2,64,256]{2,1,0:T(8,128)(2,1)S(1)}, u32[]{:S(2)}, u32[]{:S(2)}) %collective-permute-start.10) | collective-permute-done | bytes 65568 | tf_op jit(solution)/shard_map/ppermute | solution.py:195
  41.1 1.2 %update.2 = (f32[64,1024]{1,0:T(8,128)S(1)}, f32[64,1024]{1,0:T(8,128)S(1)}, f32[64,1024]{1,0:T(8,128)S(1)}, bf16[2,64,256]{2,1,0:T(8,128)(2,1)S(1)}, bf16[2,64,...) custom-call(s32[16]{0:T(128)S(1)} %reshape.14.served_ref, ...), custom_call_target="tpu_custom_call" | custom-call | tf_op jit(solution)/shard_map/update/pallas_call | solution.py:240
  42.3 2.3 %collective-permute-start.14 = (bf16[2,64,256]{2,1,0:T(8,128)(2,1)S(1)}, bf16[2,64,256]{2,1,0:T(8,128)(2,1)S(1)}, u32[]{:S(2)}, u32[]{:S(2)}) collective-permute-start(bf16[2,64,256]{2,1,0:T(8,128)(2,1)S(1)} %get-tuple-element.58), channel_id=1, source_target_pairs={{0,12},{2,14},{4,8},{6,10},{8,4},{10,6},{12,0},{14,2},{1,13},{3,15... | collective-permute-start | bytes 196616 | tf_op jit(solution)/shard_map/ppermute | solution.py:195
  44.7 2.2 %collective-permute-start.16 = (bf16[2,64,256]{2,1,0:T(8,128)(2,1)S(1)}, bf16[2,64,256]{2,1,0:T(8,128)(2,1)S(1)}, u32[]{:S(2)}, u32[]{:S(2)}) collective-permute-start(bf16[2,64,256]{2,1,0:T(8,128)(2,1)S(1)} %get-tuple-element.60), channel_id=1, source_target_pairs={{0,14},{2,12},{4,10},{6,8},{8,6},{10,4},{12,2},{14,0},{1,15},{3,13... | collective-permute-start | bytes 196616 | tf_op jit(solution)/shard_map/ppermute | solution.py:195
  46.9 2.5 %collective-permute-start.17 = (bf16[2,64,256]{2,1,0:T(8,128)(2,1)S(1)}, bf16[2,64,256]{2,1,0:T(8,128)(2,1)S(1)}, u32[]{:S(2)}, u32[]{:S(2)}) collective-permute-start(bf16[2,64,256]{2,1,0:T(8,128)(2,1)S(1)} %get-tuple-element.61), channel_id=1, source_target_pairs={{0,10},{2,8},{4,14},{6,12},{8,2},{10,0},{12,6},{14,4},{1,11},{3,9}... | collective-permute-start | bytes 196616 | tf_op jit(solution)/shard_map/ppermute | solution.py:195
  49.4 0.6 collective-permute-start.18
  50.0 1.8 %collective-permute-start.19 = (bf16[2,64,256]{2,1,0:T(8,128)(2,1)S(1)}, bf16[2,64,256]{2,1,0:T(8,128)(2,1)S(1)}, u32[]{:S(2)}, u32[]{:S(2)}) collective-permute-start(bf16[2,64,256]{2,1,0:T(8,128)(2,1)S(1)} %get-tuple-element.63), channel_id=1, source_target_pairs={{0,4},{2,6},{4,0},{6,2},{8,12},{10,14},{12,8},{14,10},{1,5},{3,7},... | collective-permute-start | bytes 196616 | tf_op jit(solution)/shard_map/ppermute | solution.py:195
  51.8 0.8 collective-permute-start.20
  52.6 4.2 %collective-permute-done.17.refs_4_ = bf16[2,64,256]{2,1,0:T(8,128)(2,1)S(1)} collective-permute-done((bf16[2,64,256]{2,1,0:T(8,128)(2,1)S(1)}, bf16[2,64,256]{2,1,0:T(8,128)(2,1)S(1)}, u32[]{:S(2)}, u32[]{:S(2)}) %collective-permute-start.17) | collective-permute-done | bytes 65568 | tf_op jit(solution)/shard_map/ppermute | solution.py:195
  56.8 0.1 collective-permute-done.18.refs_5_
  56.9 5.0 %pair_products.3 = (f32[2,64,256]{2,1,0:T(8,128)S(1)}, bf16[2,64,256]{2,1,0:T(8,128)(2,1)S(1)}, bf16[2,64,256]{2,1,0:T(8,128)(2,1)S(1)}, bf16[2,64,256]{2,1,0:T(...) custom-call(s32[8,128]{1,0:T(8,128)S(1)} %get-tuple-element.39.place, ...), custom_call_target="tpu_custom_call" | custom-call | tf_op jit(solution)/shard_map/pair_products/pallas_call | solution.py:227
  61.9 1.9 %collective-permute-start.21 = (bf16[2,64,256]{2,1,0:T(8,128)(2,1)S(1)}, bf16[2,64,256]{2,1,0:T(8,128)(2,1)S(1)}, u32[]{:S(2)}, u32[]{:S(2)}) collective-permute-start(bf16[2,64,256]{2,1,0:T(8,128)(2,1)S(1)} %get-tuple-element.66), channel_id=1, source_target_pairs={{0,12},{2,14},{4,8},{6,10},{8,4},{10,6},{12,0},{14,2},{1,13},{3,15... | collective-permute-start | bytes 196616 | tf_op jit(solution)/shard_map/ppermute | solution.py:195
  63.8 2.5 %collective-permute-start.23 = (bf16[2,64,256]{2,1,0:T(8,128)(2,1)S(1)}, bf16[2,64,256]{2,1,0:T(8,128)(2,1)S(1)}, u32[]{:S(2)}, u32[]{:S(2)}) collective-permute-start(bf16[2,64,256]{2,1,0:T(8,128)(2,1)S(1)} %get-tuple-element.68), channel_id=1, source_target_pairs={{0,14},{2,12},{4,10},{6,8},{8,6},{10,4},{12,2},{14,0},{1,15},{3,13... | collective-permute-start | bytes 196616 | tf_op jit(solution)/shard_map/ppermute | solution.py:195
  66.3 2.5 %collective-permute-start.24 = (bf16[2,64,256]{2,1,0:T(8,128)(2,1)S(1)}, bf16[2,64,256]{2,1,0:T(8,128)(2,1)S(1)}, u32[]{:S(2)}, u32[]{:S(2)}) collective-permute-start(bf16[2,64,256]{2,1,0:T(8,128)(2,1)S(1)} %get-tuple-element.69), channel_id=1, source_target_pairs={{0,10},{2,8},{4,14},{6,12},{8,2},{10,0},{12,6},{14,4},{1,11},{3,9}... | collective-permute-start | bytes 196616 | tf_op jit(solution)/shard_map/ppermute | solution.py:195
  68.8 0.8 %collective-permute-start.25 = (bf16[2,64,256]{2,1,0:T(8,128)(2,1)S(1)}, bf16[2,64,256]{2,1,0:T(8,128)(2,1)S(1)}, u32[]{:S(2)}, u32[]{:S(2)}) collective-permute-start(bf16[2,64,256]{2,1,0:T(8,128)(2,1)S(1)} %get-tuple-element.70), channel_id=1, source_target_pairs={{0,8},{2,10},{4,12},{6,14},{8,0},{10,2},{12,4},{14,6},{1,9},{3,11}... | collective-permute-start | bytes 196616 | tf_op jit(solution)/shard_map/ppermute | solution.py:195
  69.6 1.7 %collective-permute-start.26 = (bf16[2,64,256]{2,1,0:T(8,128)(2,1)S(1)}, bf16[2,64,256]{2,1,0:T(8,128)(2,1)S(1)}, u32[]{:S(2)}, u32[]{:S(2)}) collective-permute-start(bf16[2,64,256]{2,1,0:T(8,128)(2,1)S(1)} %get-tuple-element.71), channel_id=1, source_target_pairs={{0,4},{2,6},{4,0},{6,2},{8,12},{10,14},{12,8},{14,10},{1,5},{3,7},... | collective-permute-start | bytes 196616 | tf_op jit(solution)/shard_map/ppermute | solution.py:195
  71.3 0.9 %collective-permute-start.27 = (bf16[2,64,256]{2,1,0:T(8,128)(2,1)S(1)}, bf16[2,64,256]{2,1,0:T(8,128)(2,1)S(1)}, u32[]{:S(2)}, u32[]{:S(2)}) collective-permute-start(bf16[2,64,256]{2,1,0:T(8,128)(2,1)S(1)} %get-tuple-element.72), channel_id=1, source_target_pairs={{0,2},{2,0},{4,6},{6,4},{8,10},{10,8},{12,14},{14,12},{1,3},{3,1},... | collective-permute-start | bytes 196616 | tf_op jit(solution)/shard_map/ppermute | solution.py:195
  72.2 3.7 %collective-permute-done.24.refs_4_ = bf16[2,64,256]{2,1,0:T(8,128)(2,1)S(1)} collective-permute-done((bf16[2,64,256]{2,1,0:T(8,128)(2,1)S(1)}, bf16[2,64,256]{2,1,0:T(8,128)(2,1)S(1)}, u32[]{:S(2)}, u32[]{:S(2)}) %collective-permute-start.24) | collective-permute-done | bytes 65568 | tf_op jit(solution)/shard_map/ppermute | solution.py:195
  75.9 0.3 collective-permute-done.27.refs_7_
  76.2 2.0 %update.3 = (f32[64,1024]{1,0:T(8,128)}, f32[64,1024]{1,0:T(8,128)}) custom-call(s32[16]{0:T(128)S(1)} %reshape.14.served_ref, s32[1]{0:T(128)} %bitcast.me_ref, s32[4]{0:T(128)S(1)} %copy-done.8, f32[8]{0:T(128)S(1)} %copy-done.9, f32[2,64]{1,0:T(2,128)S(1)} %copy-done.7, f32[64,1024]{1,0:T(8,128)S(1)} %copy-done.3, s32[64,1024]{1,0:T(8,128)S(1)} %copy-done.5, ...), custom_call_target="tpu_custom_call" | custom-call | tf_op jit(solution)/shard_map/update/pallas_call | solution.py:240
  (37 shorter events, 0.1 us)
Async XLA Ops:
  0.6 0.7 copy-start
  1.7 1.0 %copy-start.2 = (f32[64,1024]{1,0:T(8,128)S(1)}, f32[64,1024]{1,0:T(8,128)}, u32[]{:S(2)}) copy-start(f32[64,1024]{1,0:T(8,128)} %holdings_ref.5) | copy-start | bytes 786436
  3.3 10.8 %collective-permute-start = (bf16[2,64,256]{2,1,0:T(8,128)(2,1)S(1)}, bf16[2,64,256]{2,1,0:T(8,128)(2,1)S(1)}, u32[]{:S(2)}, u32[]{:S(2)}) collective-permute-start(bf16[2,64,256]{2,1,0:T(8,128)(2,1)S(1)} %get-tuple-element.42), channel_id=1, source_target_pairs={{0,12},{2,14},{4,8},{6,10},{8,4},{10,6},{12,0},{14,2},{1,13},{3,15... | collective-permute-start | bytes 196616 | tf_op jit(solution)/shard_map/ppermute | solution.py:195
  8.4 6.1 %collective-permute-start.1 = (bf16[2,64,256]{2,1,0:T(8,128)(2,1)S(1)}, bf16[2,64,256]{2,1,0:T(8,128)(2,1)S(1)}, u32[]{:S(2)}, u32[]{:S(2)}) collective-permute-start(bf16[2,64,256]{2,1,0:T(8,128)(2,1)S(1)} %get-tuple-element.43), channel_id=1, source_target_pairs={{0,6},{2,4},{4,2},{6,0},{8,14},{10,12},{12,10},{14,8},{1,7},{3,5},... | collective-permute-start | bytes 196616 | tf_op jit(solution)/shard_map/ppermute | solution.py:195
  8.9 11.9 %collective-permute-start.2 = (bf16[2,64,256]{2,1,0:T(8,128)(2,1)S(1)}, bf16[2,64,256]{2,1,0:T(8,128)(2,1)S(1)}, u32[]{:S(2)}, u32[]{:S(2)}) collective-permute-start(bf16[2,64,256]{2,1,0:T(8,128)(2,1)S(1)} %get-tuple-element.44), channel_id=1, source_target_pairs={{0,14},{2,12},{4,10},{6,8},{8,6},{10,4},{12,2},{14,0},{1,15},{3,13... | collective-permute-start | bytes 196616 | tf_op jit(solution)/shard_map/ppermute | solution.py:195
  10.2 10.6 %collective-permute-start.3 = (bf16[2,64,256]{2,1,0:T(8,128)(2,1)S(1)}, bf16[2,64,256]{2,1,0:T(8,128)(2,1)S(1)}, u32[]{:S(2)}, u32[]{:S(2)}) collective-permute-start(bf16[2,64,256]{2,1,0:T(8,128)(2,1)S(1)} %get-tuple-element.45), channel_id=1, source_target_pairs={{0,10},{2,8},{4,14},{6,12},{8,2},{10,0},{12,6},{14,4},{1,11},{3,9}... | collective-permute-start | bytes 196616 | tf_op jit(solution)/shard_map/ppermute | solution.py:195
  13.7 7.3 %collective-permute-start.4 = (bf16[2,64,256]{2,1,0:T(8,128)(2,1)S(1)}, bf16[2,64,256]{2,1,0:T(8,128)(2,1)S(1)}, u32[]{:S(2)}, u32[]{:S(2)}) collective-permute-start(bf16[2,64,256]{2,1,0:T(8,128)(2,1)S(1)} %get-tuple-element.46), channel_id=1, source_target_pairs={{0,8},{2,10},{4,12},{6,14},{8,0},{10,2},{12,4},{14,6},{1,9},{3,11}... | collective-permute-start | bytes 196616 | tf_op jit(solution)/shard_map/ppermute | solution.py:195
  14.1 7.0 %collective-permute-start.5 = (bf16[2,64,256]{2,1,0:T(8,128)(2,1)S(1)}, bf16[2,64,256]{2,1,0:T(8,128)(2,1)S(1)}, u32[]{:S(2)}, u32[]{:S(2)}) collective-permute-start(bf16[2,64,256]{2,1,0:T(8,128)(2,1)S(1)} %get-tuple-element.47), channel_id=1, source_target_pairs={{0,4},{2,6},{4,0},{6,2},{8,12},{10,14},{12,8},{14,10},{1,5},{3,7},... | collective-permute-start | bytes 196616 | tf_op jit(solution)/shard_map/ppermute | solution.py:195
  14.5 6.5 %collective-permute-start.6 = (bf16[2,64,256]{2,1,0:T(8,128)(2,1)S(1)}, bf16[2,64,256]{2,1,0:T(8,128)(2,1)S(1)}, u32[]{:S(2)}, u32[]{:S(2)}) collective-permute-start(bf16[2,64,256]{2,1,0:T(8,128)(2,1)S(1)} %get-tuple-element.48), channel_id=1, source_target_pairs={{0,2},{2,0},{4,6},{6,4},{8,10},{10,8},{12,14},{14,12},{1,3},{3,1},... | collective-permute-start | bytes 196616 | tf_op jit(solution)/shard_map/ppermute | solution.py:195
  16.6 3.4 %copy-start.1 = (bf16[64,256,256]{2,1,0:T(8,128)(2,1)S(1)}, bf16[64,256,256]{2,1,0:T(8,128)(2,1)}, u32[]{:S(2)}) copy-start(bf16[64,256,256]{2,1,0:T(8,128)(2,1)} %cov_ref.1) | copy-start | bytes 25165828
  20.0 21.0 %copy-start.3 = (f32[64,1024]{1,0:T(8,128)S(1)}, f32[64,1024]{1,0:T(8,128)}, u32[]{:S(2)}) copy-start(f32[64,1024]{1,0:T(8,128)} %holdings_ref.5) | copy-start | bytes 786436
  20.0 21.1 %copy-start.4 = (bf16[4,256,256]{2,1,0:T(8,128)(2,1)S(1)}, bf16[4,256,256]{2,1,0:T(8,128)(2,1)}, u32[]{:S(2)}) copy-start(bf16[4,256,256]{2,1,0:T(8,128)(2,1)} %diag_ref.3) | copy-start | bytes 1572868
  20.0 21.1 %copy-start.5 = (s32[64,1024]{1,0:T(8,128)S(1)}, s32[64,1024]{1,0:T(8,128)}, u32[]{:S(2)}) copy-start(s32[64,1024]{1,0:T(8,128)} %eligible_ref.3) | copy-start | bytes 786436
  20.0 21.1 %copy-start.6 = (f32[1024]{0:T(1024)S(1)}, f32[1024]{0:T(1024)}, u32[]{:S(2)}) copy-start(f32[1024]{0:T(1024)} %param.12) | copy-start | bytes 12292
  20.0 21.1 %copy-start.7 = (f32[2,64]{1,0:T(2,128)S(1)}, f32[2,64]{1,0:T(2,128)}, u32[]{:S(2)}) copy-start(f32[2,64]{1,0:T(2,128)} %slopes_ref.3) | copy-start | bytes 1540
  20.0 21.1 %copy-start.8 = (s32[4]{0:T(128)S(1)}, s32[4]{0:T(128)}, u32[]{:S(2)}) copy-start(s32[4]{0:T(128)} %knee_index_ref.3) | copy-start | bytes 52
  20.0 21.1 %copy-start.9 = (f32[8]{0:T(128)S(1)}, f32[8]{0:T(128)}, u32[]{:S(2)}) copy-start(f32[8]{0:T(128)} %knee_levels_ref.3) | copy-start | bytes 100
  26.1 8.3 %collective-permute-start.7 = (bf16[2,64,256]{2,1,0:T(8,128)(2,1)S(1)}, bf16[2,64,256]{2,1,0:T(8,128)(2,1)S(1)}, u32[]{:S(2)}, u32[]{:S(2)}) collective-permute-start(bf16[2,64,256]{2,1,0:T(8,128)(2,1)S(1)} %get-tuple-element.50), channel_id=1, source_target_pairs={{0,12},{2,14},{4,8},{6,10},{8,4},{10,6},{12,0},{14,2},{1,13},{3,15... | collective-permute-start | bytes 196616 | tf_op jit(solution)/shard_map/ppermute | solution.py:195
  28.7 7.0 %collective-permute-start.8 = (bf16[2,64,256]{2,1,0:T(8,128)(2,1)S(1)}, bf16[2,64,256]{2,1,0:T(8,128)(2,1)S(1)}, u32[]{:S(2)}, u32[]{:S(2)}) collective-permute-start(bf16[2,64,256]{2,1,0:T(8,128)(2,1)S(1)} %get-tuple-element.51), channel_id=1, source_target_pairs={{0,6},{2,4},{4,2},{6,0},{8,14},{10,12},{12,10},{14,8},{1,7},{3,5},... | collective-permute-start | bytes 196616 | tf_op jit(solution)/shard_map/ppermute | solution.py:195
  29.2 7.4 %collective-permute-start.9 = (bf16[2,64,256]{2,1,0:T(8,128)(2,1)S(1)}, bf16[2,64,256]{2,1,0:T(8,128)(2,1)S(1)}, u32[]{:S(2)}, u32[]{:S(2)}) collective-permute-start(bf16[2,64,256]{2,1,0:T(8,128)(2,1)S(1)} %get-tuple-element.52), channel_id=1, source_target_pairs={{0,14},{2,12},{4,10},{6,8},{8,6},{10,4},{12,2},{14,0},{1,15},{3,13... | collective-permute-start | bytes 196616 | tf_op jit(solution)/shard_map/ppermute | solution.py:195
  30.8 10.2 %collective-permute-start.10 = (bf16[2,64,256]{2,1,0:T(8,128)(2,1)S(1)}, bf16[2,64,256]{2,1,0:T(8,128)(2,1)S(1)}, u32[]{:S(2)}, u32[]{:S(2)}) collective-permute-start(bf16[2,64,256]{2,1,0:T(8,128)(2,1)S(1)} %get-tuple-element.53), channel_id=1, source_target_pairs={{0,10},{2,8},{4,14},{6,12},{8,2},{10,0},{12,6},{14,4},{1,11},{3,9}... | collective-permute-start | bytes 196616 | tf_op jit(solution)/shard_map/ppermute | solution.py:195
  34.1 6.9 %collective-permute-start.11 = (bf16[2,64,256]{2,1,0:T(8,128)(2,1)S(1)}, bf16[2,64,256]{2,1,0:T(8,128)(2,1)S(1)}, u32[]{:S(2)}, u32[]{:S(2)}) collective-permute-start(bf16[2,64,256]{2,1,0:T(8,128)(2,1)S(1)} %get-tuple-element.54), channel_id=1, source_target_pairs={{0,8},{2,10},{4,12},{6,14},{8,0},{10,2},{12,4},{14,6},{1,9},{3,11}... | collective-permute-start | bytes 196616 | tf_op jit(solution)/shard_map/ppermute | solution.py:195
  34.4 6.6 %collective-permute-start.12 = (bf16[2,64,256]{2,1,0:T(8,128)(2,1)S(1)}, bf16[2,64,256]{2,1,0:T(8,128)(2,1)S(1)}, u32[]{:S(2)}, u32[]{:S(2)}) collective-permute-start(bf16[2,64,256]{2,1,0:T(8,128)(2,1)S(1)} %get-tuple-element.55), channel_id=1, source_target_pairs={{0,4},{2,6},{4,0},{6,2},{8,12},{10,14},{12,8},{14,10},{1,5},{3,7},... | collective-permute-start | bytes 196616 | tf_op jit(solution)/shard_map/ppermute | solution.py:195
  35.8 5.2 %collective-permute-start.13 = (bf16[2,64,256]{2,1,0:T(8,128)(2,1)S(1)}, bf16[2,64,256]{2,1,0:T(8,128)(2,1)S(1)}, u32[]{:S(2)}, u32[]{:S(2)}) collective-permute-start(bf16[2,64,256]{2,1,0:T(8,128)(2,1)S(1)} %get-tuple-element.56), channel_id=1, source_target_pairs={{0,2},{2,0},{4,6},{6,4},{8,10},{10,8},{12,14},{14,12},{1,3},{3,1},... | collective-permute-start | bytes 196616 | tf_op jit(solution)/shard_map/ppermute | solution.py:195
  42.3 7.7 %collective-permute-start.14 = (bf16[2,64,256]{2,1,0:T(8,128)(2,1)S(1)}, bf16[2,64,256]{2,1,0:T(8,128)(2,1)S(1)}, u32[]{:S(2)}, u32[]{:S(2)}) collective-permute-start(bf16[2,64,256]{2,1,0:T(8,128)(2,1)S(1)} %get-tuple-element.58), channel_id=1, source_target_pairs={{0,12},{2,14},{4,8},{6,10},{8,4},{10,6},{12,0},{14,2},{1,13},{3,15... | collective-permute-start | bytes 196616 | tf_op jit(solution)/shard_map/ppermute | solution.py:195
  44.7 7.2 %collective-permute-start.15 = (bf16[2,64,256]{2,1,0:T(8,128)(2,1)S(1)}, bf16[2,64,256]{2,1,0:T(8,128)(2,1)S(1)}, u32[]{:S(2)}, u32[]{:S(2)}) collective-permute-start(bf16[2,64,256]{2,1,0:T(8,128)(2,1)S(1)} %get-tuple-element.59), channel_id=1, source_target_pairs={{0,6},{2,4},{4,2},{6,0},{8,14},{10,12},{12,10},{14,8},{1,7},{3,5},... | collective-permute-start | bytes 196616 | tf_op jit(solution)/shard_map/ppermute | solution.py:195
  44.7 8.0 %collective-permute-start.16 = (bf16[2,64,256]{2,1,0:T(8,128)(2,1)S(1)}, bf16[2,64,256]{2,1,0:T(8,128)(2,1)S(1)}, u32[]{:S(2)}, u32[]{:S(2)}) collective-permute-start(bf16[2,64,256]{2,1,0:T(8,128)(2,1)S(1)} %get-tuple-element.60), channel_id=1, source_target_pairs={{0,14},{2,12},{4,10},{6,8},{8,6},{10,4},{12,2},{14,0},{1,15},{3,13... | collective-permute-start | bytes 196616 | tf_op jit(solution)/shard_map/ppermute | solution.py:195
  46.9 9.9 %collective-permute-start.17 = (bf16[2,64,256]{2,1,0:T(8,128)(2,1)S(1)}, bf16[2,64,256]{2,1,0:T(8,128)(2,1)S(1)}, u32[]{:S(2)}, u32[]{:S(2)}) collective-permute-start(bf16[2,64,256]{2,1,0:T(8,128)(2,1)S(1)} %get-tuple-element.61), channel_id=1, source_target_pairs={{0,10},{2,8},{4,14},{6,12},{8,2},{10,0},{12,6},{14,4},{1,11},{3,9}... | collective-permute-start | bytes 196616 | tf_op jit(solution)/shard_map/ppermute | solution.py:195
  49.4 7.5 %collective-permute-start.18 = (bf16[2,64,256]{2,1,0:T(8,128)(2,1)S(1)}, bf16[2,64,256]{2,1,0:T(8,128)(2,1)S(1)}, u32[]{:S(2)}, u32[]{:S(2)}) collective-permute-start(bf16[2,64,256]{2,1,0:T(8,128)(2,1)S(1)} %get-tuple-element.62), channel_id=1, source_target_pairs={{0,8},{2,10},{4,12},{6,14},{8,0},{10,2},{12,4},{14,6},{1,9},{3,11}... | collective-permute-start | bytes 196616 | tf_op jit(solution)/shard_map/ppermute | solution.py:195
  50.0 6.8 %collective-permute-start.19 = (bf16[2,64,256]{2,1,0:T(8,128)(2,1)S(1)}, bf16[2,64,256]{2,1,0:T(8,128)(2,1)S(1)}, u32[]{:S(2)}, u32[]{:S(2)}) collective-permute-start(bf16[2,64,256]{2,1,0:T(8,128)(2,1)S(1)} %get-tuple-element.63), channel_id=1, source_target_pairs={{0,4},{2,6},{4,0},{6,2},{8,12},{10,14},{12,8},{14,10},{1,5},{3,7},... | collective-permute-start | bytes 196616 | tf_op jit(solution)/shard_map/ppermute | solution.py:195
  51.8 5.0 %collective-permute-start.20 = (bf16[2,64,256]{2,1,0:T(8,128)(2,1)S(1)}, bf16[2,64,256]{2,1,0:T(8,128)(2,1)S(1)}, u32[]{:S(2)}, u32[]{:S(2)}) collective-permute-start(bf16[2,64,256]{2,1,0:T(8,128)(2,1)S(1)} %get-tuple-element.64), channel_id=1, source_target_pairs={{0,2},{2,0},{4,6},{6,4},{8,10},{10,8},{12,14},{14,12},{1,3},{3,1},... | collective-permute-start | bytes 196616 | tf_op jit(solution)/shard_map/ppermute | solution.py:195
  61.9 7.7 %collective-permute-start.21 = (bf16[2,64,256]{2,1,0:T(8,128)(2,1)S(1)}, bf16[2,64,256]{2,1,0:T(8,128)(2,1)S(1)}, u32[]{:S(2)}, u32[]{:S(2)}) collective-permute-start(bf16[2,64,256]{2,1,0:T(8,128)(2,1)S(1)} %get-tuple-element.66), channel_id=1, source_target_pairs={{0,12},{2,14},{4,8},{6,10},{8,4},{10,6},{12,0},{14,2},{1,13},{3,15... | collective-permute-start | bytes 196616 | tf_op jit(solution)/shard_map/ppermute | solution.py:195
  63.8 7.4 %collective-permute-start.22 = (bf16[2,64,256]{2,1,0:T(8,128)(2,1)S(1)}, bf16[2,64,256]{2,1,0:T(8,128)(2,1)S(1)}, u32[]{:S(2)}, u32[]{:S(2)}) collective-permute-start(bf16[2,64,256]{2,1,0:T(8,128)(2,1)S(1)} %get-tuple-element.67), channel_id=1, source_target_pairs={{0,6},{2,4},{4,2},{6,0},{8,14},{10,12},{12,10},{14,8},{1,7},{3,5},... | collective-permute-start | bytes 196616 | tf_op jit(solution)/shard_map/ppermute | solution.py:195
  63.8 8.4 %collective-permute-start.23 = (bf16[2,64,256]{2,1,0:T(8,128)(2,1)S(1)}, bf16[2,64,256]{2,1,0:T(8,128)(2,1)S(1)}, u32[]{:S(2)}, u32[]{:S(2)}) collective-permute-start(bf16[2,64,256]{2,1,0:T(8,128)(2,1)S(1)} %get-tuple-element.68), channel_id=1, source_target_pairs={{0,14},{2,12},{4,10},{6,8},{8,6},{10,4},{12,2},{14,0},{1,15},{3,13... | collective-permute-start | bytes 196616 | tf_op jit(solution)/shard_map/ppermute | solution.py:195
  66.3 9.6 %collective-permute-start.24 = (bf16[2,64,256]{2,1,0:T(8,128)(2,1)S(1)}, bf16[2,64,256]{2,1,0:T(8,128)(2,1)S(1)}, u32[]{:S(2)}, u32[]{:S(2)}) collective-permute-start(bf16[2,64,256]{2,1,0:T(8,128)(2,1)S(1)} %get-tuple-element.69), channel_id=1, source_target_pairs={{0,10},{2,8},{4,14},{6,12},{8,2},{10,0},{12,6},{14,4},{1,11},{3,9}... | collective-permute-start | bytes 196616 | tf_op jit(solution)/shard_map/ppermute | solution.py:195
  68.8 7.1 %collective-permute-start.25 = (bf16[2,64,256]{2,1,0:T(8,128)(2,1)S(1)}, bf16[2,64,256]{2,1,0:T(8,128)(2,1)S(1)}, u32[]{:S(2)}, u32[]{:S(2)}) collective-permute-start(bf16[2,64,256]{2,1,0:T(8,128)(2,1)S(1)} %get-tuple-element.70), channel_id=1, source_target_pairs={{0,8},{2,10},{4,12},{6,14},{8,0},{10,2},{12,4},{14,6},{1,9},{3,11}... | collective-permute-start | bytes 196616 | tf_op jit(solution)/shard_map/ppermute | solution.py:195
  69.6 6.3 %collective-permute-start.26 = (bf16[2,64,256]{2,1,0:T(8,128)(2,1)S(1)}, bf16[2,64,256]{2,1,0:T(8,128)(2,1)S(1)}, u32[]{:S(2)}, u32[]{:S(2)}) collective-permute-start(bf16[2,64,256]{2,1,0:T(8,128)(2,1)S(1)} %get-tuple-element.71), channel_id=1, source_target_pairs={{0,4},{2,6},{4,0},{6,2},{8,12},{10,14},{12,8},{14,10},{1,5},{3,7},... | collective-permute-start | bytes 196616 | tf_op jit(solution)/shard_map/ppermute | solution.py:195
  71.3 4.9 %collective-permute-start.27 = (bf16[2,64,256]{2,1,0:T(8,128)(2,1)S(1)}, bf16[2,64,256]{2,1,0:T(8,128)(2,1)S(1)}, u32[]{:S(2)}, u32[]{:S(2)}) collective-permute-start(bf16[2,64,256]{2,1,0:T(8,128)(2,1)S(1)} %get-tuple-element.72), channel_id=1, source_target_pairs={{0,2},{2,0},{4,6},{6,4},{8,10},{10,8},{12,14},{14,12},{1,3},{3,1},... | collective-permute-start | bytes 196616 | tf_op jit(solution)/shard_map/ppermute | solution.py:195

commit v6 on v5

--- a/solution.py
+++ b/solution.py
@@ -8,12 +8,15 @@
 from jax.sharding import PartitionSpec as P
 
 ITERS = 2
+UNROLL = (16, 4, 8)
+OWN = True
 STEP_SIZE = 0.5
 RISK_AVERSION = 1.0
 PENALTY = 1.0
 
 VMEM = pl.BlockSpec(memory_space=pltpu.VMEM)
 SMEM = pl.BlockSpec(memory_space=pltpu.SMEM)
+ANY = pl.BlockSpec(memory_space=pl.ANY)
 HBM = pl.BlockSpec(memory_space=pltpu.HBM)
 PARAMS = pltpu.CompilerParams(vmem_limit_bytes=24 * 1024 * 1024)
 
@@ -40,6 +43,14 @@
     for block in range(wire_ref.shape[0]):
         wire_ref[block] = holdings_ref[:, block * size : (block + 1) * size].astype(jnp.bfloat16)
     fill_outgoing(served_ref, me_ref, wire_ref, outgoing)
+
+
+def ranked(slot, me, owners, capacity):
+    owner = lax.div(slot, jnp.full_like(slot, capacity))
+    rank = jnp.zeros_like(slot)
+    for candidate, offset in enumerate(order(owners)):
+        rank = jnp.where(owner ^ me == offset, candidate, rank)
+    return rank, rank * capacity + slot - owner * capacity
 
 
 def stage_kernel(owners, capacity, cov_ref, pairs_ref, me_ref, staged_ref, places_ref, sems):
@@ -56,18 +67,9 @@
     pairs, width = pairs_ref.shape[1], places_ref.shape[1]
     shape = (pairs, width)
     lane_is_pair = lax.broadcasted_iota(jnp.int32, shape, 0) == lax.broadcasted_iota(jnp.int32, shape, 1)
-    offset_rank = [0] * owners
-    for rank, offset in enumerate(order(owners)):
-        offset_rank[offset] = rank
     places_ref[...] = jnp.zeros_like(places_ref)
     for side in range(2):
-        slot = pairs_ref[0, :, side : side + 1]
-        owner = lax.div(slot, jnp.full_like(slot, capacity))
-        offset = owner ^ me_ref[0]
-        rank = jnp.zeros_like(slot)
-        for candidate in range(1, owners):
-            rank = jnp.where(offset == candidate, offset_rank[candidate], rank)
-        place = rank * capacity + slot - owner * capacity
+        place = ranked(pairs_ref[0, :, side : side + 1], me_ref[0], owners, capacity)[1]
         places_ref[pl.ds(side, 1), :] = jnp.sum(jnp.where(lane_is_pair, place, 0), axis=0, keepdims=True)
     for copy in copies:
         copy.wait()
@@ -95,6 +97,96 @@
     lax.fori_loop(0, cov_ref.shape[0], one, 0, unroll=32)
     for rank, out_ref in enumerate(partial):
         out_ref[...] = total[pl.ds(rank * capacity, capacity)].astype(out_ref.dtype)
+
+
+def plan_kernel(owners, capacity, late, pairs_ref, me_ref, after_ref, plan_ref):
+    pairs, width = pairs_ref.shape[1], plan_ref.shape[1]
+    slots = owners * capacity
+    bits = slots.bit_length()
+    shape = (pairs, width)
+    pair = lax.broadcasted_iota(jnp.int32, (pairs, 1), 0)
+    lane = lax.broadcasted_iota(jnp.int32, shape, 1)
+
+    (rank0, place0), (rank1, place1) = (
+        ranked(pairs_ref[0, :, side : side + 1], me_ref[0], owners, capacity) for side in range(2)
+    )
+    sides = []
+    for side, (rank, source, target) in enumerate(((rank0, place0, place1), (rank1, place1, place0))):
+        group = jnp.zeros_like(rank)
+        for late_rank in late:
+            group = jnp.where(rank == late_rank, 1, group)
+        if OWN:
+            group = jnp.where(target < capacity, 2, group)
+        entry = (((pair << bits) | source) << bits) | target
+        sides.append((group, entry, (lane == 2 * group + side).astype(jnp.float32)))
+    square = (pairs, pairs)
+    before = lax.broadcasted_iota(jnp.int32, square, 1) <= lax.broadcasted_iota(jnp.int32, square, 0)
+    counts = jnp.dot(
+        before.astype(jnp.bfloat16),
+        (sides[0][2] + sides[1][2]).astype(jnp.bfloat16),
+        preferred_element_type=jnp.float32,
+    )
+    for side, (group, entry, member) in enumerate(sides):
+        position = jnp.sum(member * counts, axis=1, keepdims=True).astype(jnp.int32) - 1
+        for index in range(3):
+            listed = (position == lane) & (group == index)
+            row = jnp.sum(jnp.where(listed, (entry - slots).astype(jnp.float32), 0.0), axis=0, keepdims=True)
+            plan_ref[pl.ds(2 * index + side, 1), :] = row.astype(jnp.int32) + slots
+    plan_ref[pl.ds(6, 1), :] = counts[pairs - 1 : pairs, :].astype(jnp.int32)
+    plan_ref[pl.ds(7, 1), :] = jnp.zeros((1, width), jnp.int32)
+
+
+def products(group, plan_ref, cov_ref, slot_rows, total):
+    bits = slot_rows.shape[0].bit_length()
+    mask = (1 << bits) - 1
+    longest = jnp.maximum(plan_ref[6, 2 * group], plan_ref[6, 2 * group + 1])
+
+    def one(step, carry):
+        for lane in range(UNROLL[group]):
+            for side in range(2):
+                entry = plan_ref[2 * group + side, step * UNROLL[group] + lane]
+                term = lax.dot_general(
+                    slot_rows[(entry >> bits) & mask],
+                    cov_ref[entry >> (2 * bits)],
+                    (((1,), (side,)), ((), ())),
+                    preferred_element_type=jnp.float32,
+                )
+                total[entry & mask] += term
+        return carry
+
+    lax.fori_loop(0, lax.div(longest + UNROLL[group] - 1, UNROLL[group]), one, 0)
+
+
+def gather_rows(ranks, incoming, slot_rows):
+    capacity = incoming[0].shape[0]
+    for rank, rows_ref in zip(ranks, incoming):
+        slot_rows[pl.ds(rank * capacity, capacity)] = rows_ref[...]
+
+
+def early_kernel(ranks, plan_ref, cov_ref, *refs):
+    *incoming, total, slot_rows = refs
+    gather_rows(ranks, incoming, slot_rows)
+    total[...] = jnp.zeros_like(total)
+    products(0, plan_ref, cov_ref, slot_rows, total)
+
+
+def late_kernel(ranks, plan_ref, cov_ref, early_ref, *refs):
+    incoming, outs, (slot_rows, total) = refs[: len(ranks)], refs[len(ranks) : -2], refs[-2:]
+    capacity = incoming[0].shape[0]
+    gather_rows(ranks, incoming, slot_rows)
+    total[...] = early_ref[...]
+    products(1, plan_ref, cov_ref, slot_rows, total)
+    for rank, out_ref in enumerate(outs, int(OWN)):
+        out_ref[...] = total[pl.ds(rank * capacity, capacity)].astype(out_ref.dtype)
+
+
+def own_kernel(owners, plan_ref, cov_ref, *refs):
+    incoming, (out_ref, slot_rows, total) = refs[:owners], refs[owners:]
+    capacity = incoming[0].shape[0]
+    gather_rows(range(owners), incoming, slot_rows)
+    total[pl.ds(0, capacity)] = jnp.zeros(out_ref.shape, jnp.float32)
+    products(2, plan_ref, cov_ref, slot_rows, total)
+    out_ref[...] = total[pl.ds(0, capacity)]
 
 
 def column(row, rows):
@@ -183,12 +275,23 @@
     owners = lax.axis_size("blk")
     my_index = lax.axis_index("blk")
     capacity = need_table.shape[2]
+    slots = owners * capacity
+    pairs = cov_pairs.shape[0]
+    late = tuple(rank for rank, offset in enumerate(order(owners)) if offset in (owners // 2 + 1, owners // 2))
+    early = tuple(rank for rank in range(owners) if rank not in late)
+    width = -(-(pairs + max(UNROLL)) // 128) * 128
     me = my_index.reshape(1)
     served = lax.dynamic_index_in_dim(need_table, my_index, 1, keepdims=False).reshape(-1)
     wire_scratch = pltpu.VMEM((blocks, rows, size), jnp.bfloat16)
     whole = jax.ShapeDtypeStruct((rows, assets), jnp.float32)
+    slot_scratch = pltpu.VMEM((slots, rows, size), jnp.bfloat16)
     sent = jax.ShapeDtypeStruct((capacity, rows, size), jnp.bfloat16)
     kept = jax.ShapeDtypeStruct((capacity, rows, size), jnp.float32)
+
+    def cost(count):
+        return pl.CostEstimate(
+            flops=2 * count * rows * size * size, bytes_accessed=2 * count * size * size, transcendentals=0
+        )
 
     def exchange(values):
         return [values[0]] + [
@@ -205,7 +308,6 @@
         compiler_params=PARAMS,
         name="pack_holdings",
     )(served, me, holdings)
-    pairs = cov_pairs.shape[0]
     staged, places = pl.pallas_call(
         functools.partial(stage_kernel, owners, capacity),
         out_shape=[
@@ -224,18 +326,62 @@
     for iteration in range(ITERS):
         last = iteration == ITERS - 1
         incoming = exchange(outgoing)
-        partial_sums = pl.pallas_call(
-            functools.partial(pairs_kernel, owners),
-            out_shape=[kept] + [sent] * (owners - 1),
-            in_specs=[SMEM] + [VMEM] * (1 + owners),
-            out_specs=[VMEM] * owners,
-            scratch_shapes=[
-                pltpu.VMEM((owners * capacity, rows, size), jnp.bfloat16),
-                pltpu.VMEM((owners * capacity, rows, size), jnp.float32),
-            ],
-            compiler_params=PARAMS,
-            name="pair_products",
-        )(places, staged, *incoming)
+        if iteration == 0:
+            partial_sums = pl.pallas_call(
+                functools.partial(pairs_kernel, owners),
+                out_shape=[kept] + [sent] * (owners - 1),
+                in_specs=[SMEM] + [VMEM] * (1 + owners),
+                out_specs=[VMEM] * owners,
+                scratch_shapes=[
+                    pltpu.VMEM((owners * capacity, rows, size), jnp.bfloat16),
+                    pltpu.VMEM((owners * capacity, rows, size), jnp.float32),
+                ],
+                compiler_params=PARAMS,
+                name="pair_products",
+            )(places, staged, *incoming)
+            plan = pl.pallas_call(
+                functools.partial(plan_kernel, owners, capacity, late),
+                out_shape=jax.ShapeDtypeStruct((8, width), jnp.int32),
+                in_specs=[VMEM, SMEM, ANY],
+                out_specs=VMEM,
+                compiler_params=PARAMS,
+                cost_estimate=pl.CostEstimate(flops=0, bytes_accessed=1 << 20, transcendentals=0),
+                name="plan_products",
+            )(pair_slots, me, partial_sums[0])
+        else:
+            total_shape = (slots + 1, rows, size)
+            total = pl.pallas_call(
+                functools.partial(early_kernel, early),
+                out_shape=jax.ShapeDtypeStruct(total_shape, jnp.float32),
+                in_specs=[SMEM] + [VMEM] * (1 + len(early)),
+                out_specs=VMEM,
+                scratch_shapes=[slot_scratch],
+                compiler_params=PARAMS,
+                cost_estimate=cost(pairs),
+                name="early_products",
+            )(plan, cov_pairs, *(incoming[rank] for rank in early))
+            partial_sums = pl.pallas_call(
+                functools.partial(late_kernel, late),
+                out_shape=([] if OWN else [kept]) + [sent] * (owners - 1),
+                in_specs=[SMEM] + [VMEM] * (2 + len(late)),
+                out_specs=[VMEM] * (owners - int(OWN)),
+                scratch_shapes=[slot_scratch, pltpu.VMEM(total_shape, jnp.float32)],
+                compiler_params=PARAMS,
+                cost_estimate=cost(pairs),
+                name="late_products",
+            )(plan, cov_pairs, total, *(incoming[rank] for rank in late))
+            if OWN:
+                own = pl.pallas_call(
+                    functools.partial(own_kernel, owners),
+                    out_shape=kept,
+                    in_specs=[SMEM] + [VMEM] * (1 + owners),
+                    out_specs=VMEM,
+                    scratch_shapes=[slot_scratch, pltpu.VMEM(total_shape, jnp.float32)],
+                    compiler_params=PARAMS,
+                    cost_estimate=cost(pairs // 2),
+                    name="own_products",
+                )(plan, cov_pairs, *incoming)
+                partial_sums = [own, *partial_sums]
         returned = exchange(partial_sums)
         outs = pl.pallas_call(
             functools.partial(update_kernel, last, owners),

time: 78.4 us -> 77.3 us (0.986)
  waiting for transfers between devices: 13.1 us -> 5.75 us
  Pallas kernels: 14.6 us -> 19.9 us
    pallas_call x0 -> x4, Pallas kernels: none -> 10.4 us  [the longest x1 4.22 us: body(): pl.pallas_call(functools.partial(early_kernel, early), out_shape=jax.Shap...]
    ppermute x28, waiting for transfers between devices: 13.1 us -> 5.75 us  [exchange(): lax.ppermute(value, 'blk', [(index, index ^ offset) for index in range(ow...]
    pallas_call x2 -> x1, Pallas kernels: 10.1 us -> 5.05 us  [body(): pl.pallas_call(functools.partial(pairs_kernel, owners), out_shape=[kept]...]
    unnamed x21 -> x25, local copies, waits for them, and re-layouts: 5.83 us -> 5.84 us
  transfers between devices with their start and end apart: 28 -> 28, of which waited for: 7 -> 6; matrix products, arithmetic and copies ran while one was open for 1% -> 1% of each run, Pallas kernels for 1% -> 10%
where the time goes in v6:
time: 77.3 us; the launch traced here: 76.5 us
  starting transfers between devices  43.7 us (57%)
  Pallas kernels  19.9 us (26%)
  local copies, waits for them, and re-layouts  6.2 us (8%)
  waiting for transfers between devices  5.75 us (7%)
  between operations  0.93 us (1%)
    ppermute x28, starting transfers between devices, exchange(): lax.ppermute(value, 'blk', [(index, index ^ offset) for index in range(ow...  43.7 us
    unnamed x25, local copies, waits for them, and re-layouts  5.84 us
    ppermute x28, waiting for transfers between devices, exchange(): lax.ppermute(value, 'blk', [(index, index ^ offset) for index in range(ow...  5.75 us
    pallas_call x1, Pallas kernels, body(): pl.pallas_call(functools.partial(pairs_kernel, owners), out_shape=[kept]...  5.05 us
    pallas_call x1, Pallas kernels, body(): pl.pallas_call(functools.partial(early_kernel, early), out_shape=jax.Shap...  4.22 us
    pallas_call x2, Pallas kernels, body(): pl.pallas_call(functools.partial(update_kernel, last, owners), out_shape=...  3.18 us
    pallas_call x1, Pallas kernels, body(): pl.pallas_call(functools.partial(late_kernel, late), out_shape=([] if OWN...  3.14 us
    pallas_call x1, Pallas kernels, body(): pl.pallas_call(functools.partial(own_kernel, owners), out_shape=kept, in_...  2.63 us
  transfers between devices with their start and end apart: 28, of which 6 were waited for; matrix products, arithmetic and copies ran while one was open for 1% of the time, Pallas kernels for 10%

profile of v6, /device:TPU:0, one launch (start us, length us, event | category | flops | bytes accessed | tf_op | source)
XLA Modules:
  0.0 76.5 jit_solution(8469870771455091461)
XLA Ops:
  0.6 0.7 copy-done
  1.3 0.3 dynamic-slice_reduce_fusion
  1.6 0.1 reshape.14.served_ref
  1.7 1.0 %copy-done.2 = f32[64,1024]{1,0:T(8,128)S(1)} copy-done((f32[64,1024]{1,0:T(8,128)S(1)}, f32[64,1024]{1,0:T(8,128)}, u32[]{:S(2)}) %copy-start.2) | copy-done | bytes 262168
  2.7 0.6 pack_holdings.1
  3.3 5.1 %collective-permute-start = (bf16[2,64,256]{2,1,0:T(8,128)(2,1)S(1)}, bf16[2,64,256]{2,1,0:T(8,128)(2,1)S(1)}, u32[]{:S(2)}, u32[]{:S(2)}) collective-permute-start(bf16[2,64,256]{2,1,0:T(8,128)(2,1)S(1)} %get-tuple-element.41), channel_id=1, source_target_pairs={{0,12},{2,14},{4,8},{6,10},{8,4},{10,6},{12,0},{14,2},{1,13},{3,15... | collective-permute-start | bytes 196616 | tf_op jit(solution)/shard_map/ppermute | solution.py:298
  8.4 0.5 collective-permute-start.1
  8.9 1.3 %collective-permute-start.2 = (bf16[2,64,256]{2,1,0:T(8,128)(2,1)S(1)}, bf16[2,64,256]{2,1,0:T(8,128)(2,1)S(1)}, u32[]{:S(2)}, u32[]{:S(2)}) collective-permute-start(bf16[2,64,256]{2,1,0:T(8,128)(2,1)S(1)} %get-tuple-element.43), channel_id=1, source_target_pairs={{0,14},{2,12},{4,10},{6,8},{8,6},{10,4},{12,2},{14,0},{1,15},{3,13... | collective-permute-start | bytes 196616 | tf_op jit(solution)/shard_map/ppermute | solution.py:298
  10.2 3.5 %collective-permute-start.3 = (bf16[2,64,256]{2,1,0:T(8,128)(2,1)S(1)}, bf16[2,64,256]{2,1,0:T(8,128)(2,1)S(1)}, u32[]{:S(2)}, u32[]{:S(2)}) collective-permute-start(bf16[2,64,256]{2,1,0:T(8,128)(2,1)S(1)} %get-tuple-element.44), channel_id=1, source_target_pairs={{0,10},{2,8},{4,14},{6,12},{8,2},{10,0},{12,6},{14,4},{1,11},{3,9}... | collective-permute-start | bytes 196616 | tf_op jit(solution)/shard_map/ppermute | solution.py:298
  13.7 0.3 collective-permute-start.4
  14.1 0.5 collective-permute-start.5
  14.5 1.3 %collective-permute-start.6 = (bf16[2,64,256]{2,1,0:T(8,128)(2,1)S(1)}, bf16[2,64,256]{2,1,0:T(8,128)(2,1)S(1)}, u32[]{:S(2)}, u32[]{:S(2)}) collective-permute-start(bf16[2,64,256]{2,1,0:T(8,128)(2,1)S(1)} %get-tuple-element.47), channel_id=1, source_target_pairs={{0,2},{2,0},{4,6},{6,4},{8,10},{10,8},{12,14},{14,12},{1,3},{3,1},... | collective-permute-start | bytes 196616 | tf_op jit(solution)/shard_map/ppermute | solution.py:298
  15.8 0.8 %copy.15.pairs_ref = s32[1,64,2]{2,1,0:T(8,128)S(1)} copy(s32[1,64,2]{1,2,0:T(2,128)} %param.15) | data formatting | bytes 1024 | tf_op args[5]
  16.6 3.4 %copy-done.1 = bf16[64,256,256]{2,1,0:T(8,128)(2,1)S(1)} copy-done((bf16[64,256,256]{2,1,0:T(8,128)(2,1)S(1)}, bf16[64,256,256]{2,1,0:T(8,128)(2,1)}, u32[]{:S(2)}) %copy-start.1) | copy-done | bytes 8388632
  20.0 0.7 stage_pairs.1
  20.8 0.2 collective-permute-done.4.refs_5_
  21.0 5.0 %pair_products.1 = (f32[2,64,256]{2,1,0:T(8,128)S(1)}, bf16[2,64,256]{2,1,0:T(8,128)(2,1)S(1)}, bf16[2,64,256]{2,1,0:T(8,128)(2,1)S(1)}, bf16[2,64,256]{2,1,0:T(...) custom-call(s32[8,128]{1,0:T(8,128)S(1)} %get-tuple-element.38.place, ...), custom_call_target="tpu_custom_call" | custom-call | tf_op jit(solution)/shard_map/pair_products/pallas_call | solution.py:330
  26.1 2.7 %collective-permute-start.7 = (bf16[2,64,256]{2,1,0:T(8,128)(2,1)S(1)}, bf16[2,64,256]{2,1,0:T(8,128)(2,1)S(1)}, u32[]{:S(2)}, u32[]{:S(2)}) collective-permute-start(bf16[2,64,256]{2,1,0:T(8,128)(2,1)S(1)} %get-tuple-element.49), channel_id=1, source_target_pairs={{0,12},{2,14},{4,8},{6,10},{8,4},{10,6},{12,0},{14,2},{1,13},{3,15... | collective-permute-start | bytes 196616 | tf_op jit(solution)/shard_map/ppermute | solution.py:298
  28.8 0.5 collective-permute-start.8
  29.3 1.6 %collective-permute-start.9 = (bf16[2,64,256]{2,1,0:T(8,128)(2,1)S(1)}, bf16[2,64,256]{2,1,0:T(8,128)(2,1)S(1)}, u32[]{:S(2)}, u32[]{:S(2)}) collective-permute-start(bf16[2,64,256]{2,1,0:T(8,128)(2,1)S(1)} %get-tuple-element.51), channel_id=1, source_target_pairs={{0,14},{2,12},{4,10},{6,8},{8,6},{10,4},{12,2},{14,0},{1,15},{3,13... | collective-permute-start | bytes 196616 | tf_op jit(solution)/shard_map/ppermute | solution.py:298
  30.8 3.3 %collective-permute-start.10 = (bf16[2,64,256]{2,1,0:T(8,128)(2,1)S(1)}, bf16[2,64,256]{2,1,0:T(8,128)(2,1)S(1)}, u32[]{:S(2)}, u32[]{:S(2)}) collective-permute-start(bf16[2,64,256]{2,1,0:T(8,128)(2,1)S(1)} %get-tuple-element.52), channel_id=1, source_target_pairs={{0,10},{2,8},{4,14},{6,12},{8,2},{10,0},{12,6},{14,4},{1,11},{3,9}... | collective-permute-start | bytes 196616 | tf_op jit(solution)/shard_map/ppermute | solution.py:298
  34.1 0.3 collective-permute-start.11
  34.4 1.3 %collective-permute-start.12 = (bf16[2,64,256]{2,1,0:T(8,128)(2,1)S(1)}, bf16[2,64,256]{2,1,0:T(8,128)(2,1)S(1)}, u32[]{:S(2)}, u32[]{:S(2)}) collective-permute-start(bf16[2,64,256]{2,1,0:T(8,128)(2,1)S(1)} %get-tuple-element.54), channel_id=1, source_target_pairs={{0,4},{2,6},{4,0},{6,2},{8,12},{10,14},{12,8},{14,10},{1,5},{3,7},... | collective-permute-start | bytes 196616 | tf_op jit(solution)/shard_map/ppermute | solution.py:298
  35.8 0.7 collective-permute-start.13
  36.5 0.2 collective-permute-done.9.refs_3_
  36.6 4.4 %collective-permute-done.10.refs_4_ = bf16[2,64,256]{2,1,0:T(8,128)(2,1)S(1)} collective-permute-done((bf16[2,64,256]{2,1,0:T(8,128)(2,1)S(1)}, bf16[2,64,256]{2,1,0:T(8,128)(2,1)S(1)}, u32[]{:S(2)}, u32[]{:S(2)}) %collective-permute-start.10) | collective-permute-done | bytes 65568 | tf_op jit(solution)/shard_map/ppermute | solution.py:298
  41.1 1.2 %update.2 = (f32[64,1024]{1,0:T(8,128)S(1)}, f32[64,1024]{1,0:T(8,128)S(1)}, f32[64,1024]{1,0:T(8,128)S(1)}, bf16[2,64,256]{2,1,0:T(8,128)(2,1)S(1)}, bf16[2,64,...) custom-call(s32[16]{0:T(128)S(1)} %reshape.14.served_ref, ...), custom_call_target="tpu_custom_call" | custom-call | tf_op jit(solution)/shard_map/update/pallas_call | solution.py:386
  42.3 2.3 %collective-permute-start.14 = (bf16[2,64,256]{2,1,0:T(8,128)(2,1)S(1)}, bf16[2,64,256]{2,1,0:T(8,128)(2,1)S(1)}, u32[]{:S(2)}, u32[]{:S(2)}) collective-permute-start(bf16[2,64,256]{2,1,0:T(8,128)(2,1)S(1)} %get-tuple-element.57), channel_id=1, source_target_pairs={{0,12},{2,14},{4,8},{6,10},{8,4},{10,6},{12,0},{14,2},{1,13},{3,15... | collective-permute-start | bytes 196616 | tf_op jit(solution)/shard_map/ppermute | solution.py:298
  44.7 2.2 %collective-permute-start.16 = (bf16[2,64,256]{2,1,0:T(8,128)(2,1)S(1)}, bf16[2,64,256]{2,1,0:T(8,128)(2,1)S(1)}, u32[]{:S(2)}, u32[]{:S(2)}) collective-permute-start(bf16[2,64,256]{2,1,0:T(8,128)(2,1)S(1)} %get-tuple-element.59), channel_id=1, source_target_pairs={{0,14},{2,12},{4,10},{6,8},{8,6},{10,4},{12,2},{14,0},{1,15},{3,13... | collective-permute-start | bytes 196616 | tf_op jit(solution)/shard_map/ppermute | solution.py:298
  46.9 1.3 %collective-permute-start.19 = (bf16[2,64,256]{2,1,0:T(8,128)(2,1)S(1)}, bf16[2,64,256]{2,1,0:T(8,128)(2,1)S(1)}, u32[]{:S(2)}, u32[]{:S(2)}) collective-permute-start(bf16[2,64,256]{2,1,0:T(8,128)(2,1)S(1)} %get-tuple-element.62), channel_id=1, source_target_pairs={{0,4},{2,6},{4,0},{6,2},{8,12},{10,14},{12,8},{14,10},{1,5},{3,7},... | collective-permute-start | bytes 196616 | tf_op jit(solution)/shard_map/ppermute | solution.py:298
  48.2 1.3 %collective-permute-start.20 = (bf16[2,64,256]{2,1,0:T(8,128)(2,1)S(1)}, bf16[2,64,256]{2,1,0:T(8,128)(2,1)S(1)}, u32[]{:S(2)}, u32[]{:S(2)}) collective-permute-start(bf16[2,64,256]{2,1,0:T(8,128)(2,1)S(1)} %get-tuple-element.63), channel_id=1, source_target_pairs={{0,2},{2,0},{4,6},{6,4},{8,10},{10,8},{12,14},{14,12},{1,3},{3,1},... | collective-permute-start | bytes 196616 | tf_op jit(solution)/shard_map/ppermute | solution.py:298
  49.5 1.4 %collective-permute-start.17 = (bf16[2,64,256]{2,1,0:T(8,128)(2,1)S(1)}, bf16[2,64,256]{2,1,0:T(8,128)(2,1)S(1)}, u32[]{:S(2)}, u32[]{:S(2)}) collective-permute-start(bf16[2,64,256]{2,1,0:T(8,128)(2,1)S(1)} %get-tuple-element.60), channel_id=1, source_target_pairs={{0,10},{2,8},{4,14},{6,12},{8,2},{10,0},{12,6},{14,4},{1,11},{3,9}... | collective-permute-start | bytes 196616 | tf_op jit(solution)/shard_map/ppermute | solution.py:298
  50.9 0.1 collective-permute-done.15.refs_2_
  51.0 1.9 %collective-permute-start.18 = (bf16[2,64,256]{2,1,0:T(8,128)(2,1)S(1)}, bf16[2,64,256]{2,1,0:T(8,128)(2,1)S(1)}, u32[]{:S(2)}, u32[]{:S(2)}) collective-permute-start(bf16[2,64,256]{2,1,0:T(8,128)(2,1)S(1)} %get-tuple-element.61), channel_id=1, source_target_pairs={{0,8},{2,10},{4,12},{6,14},{8,0},{10,2},{12,4},{14,6},{1,9},{3,11}... | collective-permute-start | bytes 196616 | tf_op jit(solution)/shard_map/ppermute | solution.py:298
  52.9 0.4 plan_products.1.plan_ref
  53.4 4.2 %early_products.1.early_ref = f32[17,64,256]{2,1,0:T(8,128)S(1)} custom-call(s32[8,128]{1,0:T(8,128)S(1)} %plan_products.1.plan_ref, bf16[64,256,256]{2,1,0:T(8,128)(2,1)S(1)} %bitcast.3, bf16[2,64,256]{2,1,0:T(8,128)(2,1)S(1)} %get-tuple-element.56.refs_0_, bf16[2,64,256]{2,1,0:T(8,128)(2,1)S(1)} %collective-permute-done.14.refs_1_, ...), custom_call_target="tpu_custom_call" | custom-call | flops 536870912 | bytes 8388608 | tf_op jit(solution)/shard_map/early_products/pallas_call | solution.py:353
  57.6 3.1 %late_products.1 = (bf16[2,64,256]{2,1,0:T(8,128)(2,1)S(1)}, bf16[2,64,256]{2,1,0:T(8,128)(2,1)S(1)}, bf16[2,64,256]{2,1,0:T(8,128)(2,1)S(1)}, bf16[2,64,256]{2,...) custom-call(s32[8,128]{1,0:T(8,128)S(1)} %plan_products.1.plan_ref, ...), custom_call_target="tpu_custom_call" | custom-call | flops 536870912 | bytes 8388608 | tf_op jit(solution)/shard_map/late_products/pallas_call | solution.py:363
  60.8 2.1 %collective-permute-start.21 = (bf16[2,64,256]{2,1,0:T(8,128)(2,1)S(1)}, bf16[2,64,256]{2,1,0:T(8,128)(2,1)S(1)}, u32[]{:S(2)}, u32[]{:S(2)}) collective-permute-start(bf16[2,64,256]{2,1,0:T(8,128)(2,1)S(1)} %get-tuple-element.64), channel_id=1, source_target_pairs={{0,12},{2,14},{4,8},{6,10},{8,4},{10,6},{12,0},{14,2},{1,13},{3,15... | collective-permute-start | bytes 196616 | tf_op jit(solution)/shard_map/ppermute | solution.py:298
  62.9 0.1 collective-permute-start.22
  63.0 2.6 %collective-permute-start.23 = (bf16[2,64,256]{2,1,0:T(8,128)(2,1)S(1)}, bf16[2,64,256]{2,1,0:T(8,128)(2,1)S(1)}, u32[]{:S(2)}, u32[]{:S(2)}) collective-permute-start(bf16[2,64,256]{2,1,0:T(8,128)(2,1)S(1)} %get-tuple-element.66), channel_id=1, source_target_pairs={{0,14},{2,12},{4,10},{6,8},{8,6},{10,4},{12,2},{14,0},{1,15},{3,13... | collective-permute-start | bytes 196616 | tf_op jit(solution)/shard_map/ppermute | solution.py:298
  65.6 1.2 %collective-permute-start.24 = (bf16[2,64,256]{2,1,0:T(8,128)(2,1)S(1)}, bf16[2,64,256]{2,1,0:T(8,128)(2,1)S(1)}, u32[]{:S(2)}, u32[]{:S(2)}) collective-permute-start(bf16[2,64,256]{2,1,0:T(8,128)(2,1)S(1)} %get-tuple-element.67), channel_id=1, source_target_pairs={{0,10},{2,8},{4,14},{6,12},{8,2},{10,0},{12,6},{14,4},{1,11},{3,9}... | collective-permute-start | bytes 196616 | tf_op jit(solution)/shard_map/ppermute | solution.py:298
  66.8 2.4 %collective-permute-start.25 = (bf16[2,64,256]{2,1,0:T(8,128)(2,1)S(1)}, bf16[2,64,256]{2,1,0:T(8,128)(2,1)S(1)}, u32[]{:S(2)}, u32[]{:S(2)}) collective-permute-start(bf16[2,64,256]{2,1,0:T(8,128)(2,1)S(1)} %get-tuple-element.68), channel_id=1, source_target_pairs={{0,8},{2,10},{4,12},{6,14},{8,0},{10,2},{12,4},{14,6},{1,9},{3,11}... | collective-permute-start | bytes 196616 | tf_op jit(solution)/shard_map/ppermute | solution.py:298
  69.2 0.9 %collective-permute-start.26 = (bf16[2,64,256]{2,1,0:T(8,128)(2,1)S(1)}, bf16[2,64,256]{2,1,0:T(8,128)(2,1)S(1)}, u32[]{:S(2)}, u32[]{:S(2)}) collective-permute-start(bf16[2,64,256]{2,1,0:T(8,128)(2,1)S(1)} %get-tuple-element.69), channel_id=1, source_target_pairs={{0,4},{2,6},{4,0},{6,2},{8,12},{10,14},{12,8},{14,10},{1,5},{3,7},... | collective-permute-start | bytes 196616 | tf_op jit(solution)/shard_map/ppermute | solution.py:298
  70.2 0.9 %collective-permute-start.27 = (bf16[2,64,256]{2,1,0:T(8,128)(2,1)S(1)}, bf16[2,64,256]{2,1,0:T(8,128)(2,1)S(1)}, u32[]{:S(2)}, u32[]{:S(2)}) collective-permute-start(bf16[2,64,256]{2,1,0:T(8,128)(2,1)S(1)} %get-tuple-element.70), channel_id=1, source_target_pairs={{0,2},{2,0},{4,6},{6,4},{8,10},{10,8},{12,14},{14,12},{1,3},{3,1},... | collective-permute-start | bytes 196616 | tf_op jit(solution)/shard_map/ppermute | solution.py:298
  71.1 2.6 %own_products.1.refs_0_ = f32[2,64,256]{2,1,0:T(8,128)S(1)} custom-call(s32[8,128]{1,0:T(8,128)S(1)} %plan_products.1.plan_ref, bf16[64,256,256]{2,1,0:T(8,128)(2,1)S(1)} %bitcast.3, bf16[2,64,256]{2,1,0:T(8,128)(2,1)S(1)} %get-tuple-element.56.refs_0_, bf16[2,64,256]{2,1,0:T(8,128)(2,1)S(1)} %collective-permute-done.14.refs_1_, ...), custom_call_target="tpu_custom_call" | custom-call | flops 268435456 | bytes 4194304 | tf_op jit(solution)/shard_map/own_products/pallas_call | solution.py:374
  73.7 0.4 collective-permute-done.25.refs_5_
  74.2 0.4 collective-permute-done.26.refs_6_
  74.6 2.0 %update.3 = (f32[64,1024]{1,0:T(8,128)}, f32[64,1024]{1,0:T(8,128)}) custom-call(s32[16]{0:T(128)S(1)} %reshape.14.served_ref, s32[1]{0:T(128)} %bitcast.me_ref, s32[4]{0:T(128)S(1)} %copy-done.8, f32[8]{0:T(128)S(1)} %copy-done.9, f32[2,64]{1,0:T(2,128)S(1)} %copy-done.7, f32[64,1024]{1,0:T(8,128)S(1)} %copy-done.3, s32[64,1024]{1,0:T(8,128)S(1)} %copy-done.5, ...), custom_call_target="tpu_custom_call" | custom-call | tf_op jit(solution)/shard_map/update/pallas_call | solution.py:386
  (45 shorter events, 0.1 us)
Async XLA Ops:
  0.6 0.7 copy-start
  1.7 1.0 %copy-start.2 = (f32[64,1024]{1,0:T(8,128)S(1)}, f32[64,1024]{1,0:T(8,128)}, u32[]{:S(2)}) copy-start(f32[64,1024]{1,0:T(8,128)} %holdings_ref.5) | copy-start | bytes 786436
  3.3 10.8 %collective-permute-start = (bf16[2,64,256]{2,1,0:T(8,128)(2,1)S(1)}, bf16[2,64,256]{2,1,0:T(8,128)(2,1)S(1)}, u32[]{:S(2)}, u32[]{:S(2)}) collective-permute-start(bf16[2,64,256]{2,1,0:T(8,128)(2,1)S(1)} %get-tuple-element.41), channel_id=1, source_target_pairs={{0,12},{2,14},{4,8},{6,10},{8,4},{10,6},{12,0},{14,2},{1,13},{3,15... | collective-permute-start | bytes 196616 | tf_op jit(solution)/shard_map/ppermute | solution.py:298
  8.4 6.1 %collective-permute-start.1 = (bf16[2,64,256]{2,1,0:T(8,128)(2,1)S(1)}, bf16[2,64,256]{2,1,0:T(8,128)(2,1)S(1)}, u32[]{:S(2)}, u32[]{:S(2)}) collective-permute-start(bf16[2,64,256]{2,1,0:T(8,128)(2,1)S(1)} %get-tuple-element.42), channel_id=1, source_target_pairs={{0,6},{2,4},{4,2},{6,0},{8,14},{10,12},{12,10},{14,8},{1,7},{3,5},... | collective-permute-start | bytes 196616 | tf_op jit(solution)/shard_map/ppermute | solution.py:298
  8.9 11.9 %collective-permute-start.2 = (bf16[2,64,256]{2,1,0:T(8,128)(2,1)S(1)}, bf16[2,64,256]{2,1,0:T(8,128)(2,1)S(1)}, u32[]{:S(2)}, u32[]{:S(2)}) collective-permute-start(bf16[2,64,256]{2,1,0:T(8,128)(2,1)S(1)} %get-tuple-element.43), channel_id=1, source_target_pairs={{0,14},{2,12},{4,10},{6,8},{8,6},{10,4},{12,2},{14,0},{1,15},{3,13... | collective-permute-start | bytes 196616 | tf_op jit(solution)/shard_map/ppermute | solution.py:298
  10.2 10.6 %collective-permute-start.3 = (bf16[2,64,256]{2,1,0:T(8,128)(2,1)S(1)}, bf16[2,64,256]{2,1,0:T(8,128)(2,1)S(1)}, u32[]{:S(2)}, u32[]{:S(2)}) collective-permute-start(bf16[2,64,256]{2,1,0:T(8,128)(2,1)S(1)} %get-tuple-element.44), channel_id=1, source_target_pairs={{0,10},{2,8},{4,14},{6,12},{8,2},{10,0},{12,6},{14,4},{1,11},{3,9}... | collective-permute-start | bytes 196616 | tf_op jit(solution)/shard_map/ppermute | solution.py:298
  13.7 7.3 %collective-permute-start.4 = (bf16[2,64,256]{2,1,0:T(8,128)(2,1)S(1)}, bf16[2,64,256]{2,1,0:T(8,128)(2,1)S(1)}, u32[]{:S(2)}, u32[]{:S(2)}) collective-permute-start(bf16[2,64,256]{2,1,0:T(8,128)(2,1)S(1)} %get-tuple-element.45), channel_id=1, source_target_pairs={{0,8},{2,10},{4,12},{6,14},{8,0},{10,2},{12,4},{14,6},{1,9},{3,11}... | collective-permute-start | bytes 196616 | tf_op jit(solution)/shard_map/ppermute | solution.py:298
  14.1 7.0 %collective-permute-start.5 = (bf16[2,64,256]{2,1,0:T(8,128)(2,1)S(1)}, bf16[2,64,256]{2,1,0:T(8,128)(2,1)S(1)}, u32[]{:S(2)}, u32[]{:S(2)}) collective-permute-start(bf16[2,64,256]{2,1,0:T(8,128)(2,1)S(1)} %get-tuple-element.46), channel_id=1, source_target_pairs={{0,4},{2,6},{4,0},{6,2},{8,12},{10,14},{12,8},{14,10},{1,5},{3,7},... | collective-permute-start | bytes 196616 | tf_op jit(solution)/shard_map/ppermute | solution.py:298
  14.5 6.5 %collective-permute-start.6 = (bf16[2,64,256]{2,1,0:T(8,128)(2,1)S(1)}, bf16[2,64,256]{2,1,0:T(8,128)(2,1)S(1)}, u32[]{:S(2)}, u32[]{:S(2)}) collective-permute-start(bf16[2,64,256]{2,1,0:T(8,128)(2,1)S(1)} %get-tuple-element.47), channel_id=1, source_target_pairs={{0,2},{2,0},{4,6},{6,4},{8,10},{10,8},{12,14},{14,12},{1,3},{3,1},... | collective-permute-start | bytes 196616 | tf_op jit(solution)/shard_map/ppermute | solution.py:298
  16.6 3.4 %copy-start.1 = (bf16[64,256,256]{2,1,0:T(8,128)(2,1)S(1)}, bf16[64,256,256]{2,1,0:T(8,128)(2,1)}, u32[]{:S(2)}) copy-start(bf16[64,256,256]{2,1,0:T(8,128)(2,1)} %cov_ref.7) | copy-start | bytes 25165828
  20.0 21.1 %copy-start.3 = (f32[64,1024]{1,0:T(8,128)S(1)}, f32[64,1024]{1,0:T(8,128)}, u32[]{:S(2)}) copy-start(f32[64,1024]{1,0:T(8,128)} %holdings_ref.5) | copy-start | bytes 786436
  20.0 21.1 %copy-start.4 = (bf16[4,256,256]{2,1,0:T(8,128)(2,1)S(1)}, bf16[4,256,256]{2,1,0:T(8,128)(2,1)}, u32[]{:S(2)}) copy-start(bf16[4,256,256]{2,1,0:T(8,128)(2,1)} %diag_ref.3) | copy-start | bytes 1572868
  20.0 21.1 %copy-start.5 = (s32[64,1024]{1,0:T(8,128)S(1)}, s32[64,1024]{1,0:T(8,128)}, u32[]{:S(2)}) copy-start(s32[64,1024]{1,0:T(8,128)} %eligible_ref.3) | copy-start | bytes 786436
  20.0 21.1 %copy-start.6 = (f32[1024]{0:T(1024)S(1)}, f32[1024]{0:T(1024)}, u32[]{:S(2)}) copy-start(f32[1024]{0:T(1024)} %param.12) | copy-start | bytes 12292
  20.0 21.1 %copy-start.7 = (f32[2,64]{1,0:T(2,128)S(1)}, f32[2,64]{1,0:T(2,128)}, u32[]{:S(2)}) copy-start(f32[2,64]{1,0:T(2,128)} %slopes_ref.3) | copy-start | bytes 1540
  20.0 21.1 %copy-start.8 = (s32[4]{0:T(128)S(1)}, s32[4]{0:T(128)}, u32[]{:S(2)}) copy-start(s32[4]{0:T(128)} %knee_index_ref.3) | copy-start | bytes 52
  20.0 21.1 %copy-start.9 = (f32[8]{0:T(128)S(1)}, f32[8]{0:T(128)}, u32[]{:S(2)}) copy-start(f32[8]{0:T(128)} %knee_levels_ref.3) | copy-start | bytes 100
  20.0 33.3 %slice-start = ((s8[8388608]{0:T(1024)(128)(4,1)}), s8[4194304]{0:T(1024)(128)(4,1)S(1)}, s32[]{:S(2)}) async-start(s8[8388608]{0:T(1024)(128)(4,1)} %bitcast.2), calls=%async_computation | async-start | bytes 8388608
  21.0 32.3 %slice-start.1 = ((s8[8388608]{0:T(1024)(128)(4,1)}), s8[4194304]{0:T(1024)(128)(4,1)S(1)}, s32[]{:S(2)}) async-start(s8[8388608]{0:T(1024)(128)(4,1)} %bitcast.2), calls=%async_computation.1 | async-start | bytes 8388608
  26.1 8.3 %collective-permute-start.7 = (bf16[2,64,256]{2,1,0:T(8,128)(2,1)S(1)}, bf16[2,64,256]{2,1,0:T(8,128)(2,1)S(1)}, u32[]{:S(2)}, u32[]{:S(2)}) collective-permute-start(bf16[2,64,256]{2,1,0:T(8,128)(2,1)S(1)} %get-tuple-element.49), channel_id=1, source_target_pairs={{0,12},{2,14},{4,8},{6,10},{8,4},{10,6},{12,0},{14,2},{1,13},{3,15... | collective-permute-start | bytes 196616 | tf_op jit(solution)/shard_map/ppermute | solution.py:298
  28.8 7.0 %collective-permute-start.8 = (bf16[2,64,256]{2,1,0:T(8,128)(2,1)S(1)}, bf16[2,64,256]{2,1,0:T(8,128)(2,1)S(1)}, u32[]{:S(2)}, u32[]{:S(2)}) collective-permute-start(bf16[2,64,256]{2,1,0:T(8,128)(2,1)S(1)} %get-tuple-element.50), channel_id=1, source_target_pairs={{0,6},{2,4},{4,2},{6,0},{8,14},{10,12},{12,10},{14,8},{1,7},{3,5},... | collective-permute-start | bytes 196616 | tf_op jit(solution)/shard_map/ppermute | solution.py:298
  29.3 7.4 %collective-permute-start.9 = (bf16[2,64,256]{2,1,0:T(8,128)(2,1)S(1)}, bf16[2,64,256]{2,1,0:T(8,128)(2,1)S(1)}, u32[]{:S(2)}, u32[]{:S(2)}) collective-permute-start(bf16[2,64,256]{2,1,0:T(8,128)(2,1)S(1)} %get-tuple-element.51), channel_id=1, source_target_pairs={{0,14},{2,12},{4,10},{6,8},{8,6},{10,4},{12,2},{14,0},{1,15},{3,13... | collective-permute-start | bytes 196616 | tf_op jit(solution)/shard_map/ppermute | solution.py:298
  30.8 10.2 %collective-permute-start.10 = (bf16[2,64,256]{2,1,0:T(8,128)(2,1)S(1)}, bf16[2,64,256]{2,1,0:T(8,128)(2,1)S(1)}, u32[]{:S(2)}, u32[]{:S(2)}) collective-permute-start(bf16[2,64,256]{2,1,0:T(8,128)(2,1)S(1)} %get-tuple-element.52), channel_id=1, source_target_pairs={{0,10},{2,8},{4,14},{6,12},{8,2},{10,0},{12,6},{14,4},{1,11},{3,9}... | collective-permute-start | bytes 196616 | tf_op jit(solution)/shard_map/ppermute | solution.py:298
  34.1 6.9 %collective-permute-start.11 = (bf16[2,64,256]{2,1,0:T(8,128)(2,1)S(1)}, bf16[2,64,256]{2,1,0:T(8,128)(2,1)S(1)}, u32[]{:S(2)}, u32[]{:S(2)}) collective-permute-start(bf16[2,64,256]{2,1,0:T(8,128)(2,1)S(1)} %get-tuple-element.53), channel_id=1, source_target_pairs={{0,8},{2,10},{4,12},{6,14},{8,0},{10,2},{12,4},{14,6},{1,9},{3,11}... | collective-permute-start | bytes 196616 | tf_op jit(solution)/shard_map/ppermute | solution.py:298
  34.4 6.6 %collective-permute-start.12 = (bf16[2,64,256]{2,1,0:T(8,128)(2,1)S(1)}, bf16[2,64,256]{2,1,0:T(8,128)(2,1)S(1)}, u32[]{:S(2)}, u32[]{:S(2)}) collective-permute-start(bf16[2,64,256]{2,1,0:T(8,128)(2,1)S(1)} %get-tuple-element.54), channel_id=1, source_target_pairs={{0,4},{2,6},{4,0},{6,2},{8,12},{10,14},{12,8},{14,10},{1,5},{3,7},... | collective-permute-start | bytes 196616 | tf_op jit(solution)/shard_map/ppermute | solution.py:298
  35.8 5.2 %collective-permute-start.13 = (bf16[2,64,256]{2,1,0:T(8,128)(2,1)S(1)}, bf16[2,64,256]{2,1,0:T(8,128)(2,1)S(1)}, u32[]{:S(2)}, u32[]{:S(2)}) collective-permute-start(bf16[2,64,256]{2,1,0:T(8,128)(2,1)S(1)} %get-tuple-element.55), channel_id=1, source_target_pairs={{0,2},{2,0},{4,6},{6,4},{8,10},{10,8},{12,14},{14,12},{1,3},{3,1},... | collective-permute-start | bytes 196616 | tf_op jit(solution)/shard_map/ppermute | solution.py:298
  42.3 7.2 %collective-permute-start.14 = (bf16[2,64,256]{2,1,0:T(8,128)(2,1)S(1)}, bf16[2,64,256]{2,1,0:T(8,128)(2,1)S(1)}, u32[]{:S(2)}, u32[]{:S(2)}) collective-permute-start(bf16[2,64,256]{2,1,0:T(8,128)(2,1)S(1)} %get-tuple-element.57), channel_id=1, source_target_pairs={{0,12},{2,14},{4,8},{6,10},{8,4},{10,6},{12,0},{14,2},{1,13},{3,15... | collective-permute-start | bytes 196616 | tf_op jit(solution)/shard_map/ppermute | solution.py:298
  44.7 6.3 %collective-permute-start.15 = (bf16[2,64,256]{2,1,0:T(8,128)(2,1)S(1)}, bf16[2,64,256]{2,1,0:T(8,128)(2,1)S(1)}, u32[]{:S(2)}, u32[]{:S(2)}) collective-permute-start(bf16[2,64,256]{2,1,0:T(8,128)(2,1)S(1)} %get-tuple-element.58), channel_id=1, source_target_pairs={{0,6},{2,4},{4,2},{6,0},{8,14},{10,12},{12,10},{14,8},{1,7},{3,5},... | collective-permute-start | bytes 196616 | tf_op jit(solution)/shard_map/ppermute | solution.py:298
  44.7 8.6 %collective-permute-start.16 = (bf16[2,64,256]{2,1,0:T(8,128)(2,1)S(1)}, bf16[2,64,256]{2,1,0:T(8,128)(2,1)S(1)}, u32[]{:S(2)}, u32[]{:S(2)}) collective-permute-start(bf16[2,64,256]{2,1,0:T(8,128)(2,1)S(1)} %get-tuple-element.59), channel_id=1, source_target_pairs={{0,14},{2,12},{4,10},{6,8},{8,6},{10,4},{12,2},{14,0},{1,15},{3,13... | collective-permute-start | bytes 196616 | tf_op jit(solution)/shard_map/ppermute | solution.py:298
  46.9 6.4 %collective-permute-start.19 = (bf16[2,64,256]{2,1,0:T(8,128)(2,1)S(1)}, bf16[2,64,256]{2,1,0:T(8,128)(2,1)S(1)}, u32[]{:S(2)}, u32[]{:S(2)}) collective-permute-start(bf16[2,64,256]{2,1,0:T(8,128)(2,1)S(1)} %get-tuple-element.62), channel_id=1, source_target_pairs={{0,4},{2,6},{4,0},{6,2},{8,12},{10,14},{12,8},{14,10},{1,5},{3,7},... | collective-permute-start | bytes 196616 | tf_op jit(solution)/shard_map/ppermute | solution.py:298
  48.2 5.1 %collective-permute-start.20 = (bf16[2,64,256]{2,1,0:T(8,128)(2,1)S(1)}, bf16[2,64,256]{2,1,0:T(8,128)(2,1)S(1)}, u32[]{:S(2)}, u32[]{:S(2)}) collective-permute-start(bf16[2,64,256]{2,1,0:T(8,128)(2,1)S(1)} %get-tuple-element.63), channel_id=1, source_target_pairs={{0,2},{2,0},{4,6},{6,4},{8,10},{10,8},{12,14},{14,12},{1,3},{3,1},... | collective-permute-start | bytes 196616 | tf_op jit(solution)/shard_map/ppermute | solution.py:298
  49.5 8.1 %collective-permute-start.17 = (bf16[2,64,256]{2,1,0:T(8,128)(2,1)S(1)}, bf16[2,64,256]{2,1,0:T(8,128)(2,1)S(1)}, u32[]{:S(2)}, u32[]{:S(2)}) collective-permute-start(bf16[2,64,256]{2,1,0:T(8,128)(2,1)S(1)} %get-tuple-element.60), channel_id=1, source_target_pairs={{0,10},{2,8},{4,14},{6,12},{8,2},{10,0},{12,6},{14,4},{1,11},{3,9}... | collective-permute-start | bytes 196616 | tf_op jit(solution)/shard_map/ppermute | solution.py:298
  51.0 6.6 %collective-permute-start.18 = (bf16[2,64,256]{2,1,0:T(8,128)(2,1)S(1)}, bf16[2,64,256]{2,1,0:T(8,128)(2,1)S(1)}, u32[]{:S(2)}, u32[]{:S(2)}) collective-permute-start(bf16[2,64,256]{2,1,0:T(8,128)(2,1)S(1)} %get-tuple-element.61), channel_id=1, source_target_pairs={{0,8},{2,10},{4,12},{6,14},{8,0},{10,2},{12,4},{14,6},{1,9},{3,11}... | collective-permute-start | bytes 196616 | tf_op jit(solution)/shard_map/ppermute | solution.py:298
  60.8 8.5 %collective-permute-start.21 = (bf16[2,64,256]{2,1,0:T(8,128)(2,1)S(1)}, bf16[2,64,256]{2,1,0:T(8,128)(2,1)S(1)}, u32[]{:S(2)}, u32[]{:S(2)}) collective-permute-start(bf16[2,64,256]{2,1,0:T(8,128)(2,1)S(1)} %get-tuple-element.64), channel_id=1, source_target_pairs={{0,12},{2,14},{4,8},{6,10},{8,4},{10,6},{12,0},{14,2},{1,13},{3,15... | collective-permute-start | bytes 196616 | tf_op jit(solution)/shard_map/ppermute | solution.py:298
  62.9 7.3 %collective-permute-start.22 = (bf16[2,64,256]{2,1,0:T(8,128)(2,1)S(1)}, bf16[2,64,256]{2,1,0:T(8,128)(2,1)S(1)}, u32[]{:S(2)}, u32[]{:S(2)}) collective-permute-start(bf16[2,64,256]{2,1,0:T(8,128)(2,1)S(1)} %get-tuple-element.65), channel_id=1, source_target_pairs={{0,6},{2,4},{4,2},{6,0},{8,14},{10,12},{12,10},{14,8},{1,7},{3,5},... | collective-permute-start | bytes 196616 | tf_op jit(solution)/shard_map/ppermute | solution.py:298
  63.0 10.7 %collective-permute-start.23 = (bf16[2,64,256]{2,1,0:T(8,128)(2,1)S(1)}, bf16[2,64,256]{2,1,0:T(8,128)(2,1)S(1)}, u32[]{:S(2)}, u32[]{:S(2)}) collective-permute-start(bf16[2,64,256]{2,1,0:T(8,128)(2,1)S(1)} %get-tuple-element.66), channel_id=1, source_target_pairs={{0,14},{2,12},{4,10},{6,8},{8,6},{10,4},{12,2},{14,0},{1,15},{3,13... | collective-permute-start | bytes 196616 | tf_op jit(solution)/shard_map/ppermute | solution.py:298
  65.6 8.1 %collective-permute-start.24 = (bf16[2,64,256]{2,1,0:T(8,128)(2,1)S(1)}, bf16[2,64,256]{2,1,0:T(8,128)(2,1)S(1)}, u32[]{:S(2)}, u32[]{:S(2)}) collective-permute-start(bf16[2,64,256]{2,1,0:T(8,128)(2,1)S(1)} %get-tuple-element.67), channel_id=1, source_target_pairs={{0,10},{2,8},{4,14},{6,12},{8,2},{10,0},{12,6},{14,4},{1,11},{3,9}... | collective-permute-start | bytes 196616 | tf_op jit(solution)/shard_map/ppermute | solution.py:298
  66.8 7.3 %collective-permute-start.25 = (bf16[2,64,256]{2,1,0:T(8,128)(2,1)S(1)}, bf16[2,64,256]{2,1,0:T(8,128)(2,1)S(1)}, u32[]{:S(2)}, u32[]{:S(2)}) collective-permute-start(bf16[2,64,256]{2,1,0:T(8,128)(2,1)S(1)} %get-tuple-element.68), channel_id=1, source_target_pairs={{0,8},{2,10},{4,12},{6,14},{8,0},{10,2},{12,4},{14,6},{1,9},{3,11}... | collective-permute-start | bytes 196616 | tf_op jit(solution)/shard_map/ppermute | solution.py:298
  69.2 5.3 %collective-permute-start.26 = (bf16[2,64,256]{2,1,0:T(8,128)(2,1)S(1)}, bf16[2,64,256]{2,1,0:T(8,128)(2,1)S(1)}, u32[]{:S(2)}, u32[]{:S(2)}) collective-permute-start(bf16[2,64,256]{2,1,0:T(8,128)(2,1)S(1)} %get-tuple-element.69), channel_id=1, source_target_pairs={{0,4},{2,6},{4,0},{6,2},{8,12},{10,14},{12,8},{14,10},{1,5},{3,7},... | collective-permute-start | bytes 196616 | tf_op jit(solution)/shard_map/ppermute | solution.py:298
  70.2 4.4 %collective-permute-start.27 = (bf16[2,64,256]{2,1,0:T(8,128)(2,1)S(1)}, bf16[2,64,256]{2,1,0:T(8,128)(2,1)S(1)}, u32[]{:S(2)}, u32[]{:S(2)}) collective-permute-start(bf16[2,64,256]{2,1,0:T(8,128)(2,1)S(1)} %get-tuple-element.70), channel_id=1, source_target_pairs={{0,2},{2,0},{4,6},{6,4},{8,10},{10,8},{12,14},{14,12},{1,3},{3,1},... | collective-permute-start | bytes 196616 | tf_op jit(solution)/shard_map/ppermute | solution.py:298

commit v7 on v6

--- a/solution.py
+++ b/solution.py
@@ -8,7 +8,8 @@
 from jax.sharding import PartitionSpec as P
 
 ITERS = 2
-UNROLL = (16, 4, 8)
+LANES = 8
+LANES_LEFT = 4
 OWN = True
 STEP_SIZE = 0.5
 RISK_AVERSION = 1.0
@@ -24,8 +25,9 @@
 def order(owners):
     offsets = list(reversed(range(1, owners)))
     offsets[:2] = reversed(offsets[:2])
-    offsets.remove(owners // 2 - 1)
-    offsets.insert(1, owners // 2 - 1)
+    for place, offset in ((1, owners // 2 - 1), (3, owners // 2 - 2)):
+        offsets.remove(offset)
+        offsets.insert(place, offset)
     return (0, *offsets)
 
 
@@ -141,20 +143,26 @@
     mask = (1 << bits) - 1
     longest = jnp.maximum(plan_ref[6, 2 * group], plan_ref[6, 2 * group + 1])
 
-    def one(step, carry):
-        for lane in range(UNROLL[group]):
-            for side in range(2):
-                entry = plan_ref[2 * group + side, step * UNROLL[group] + lane]
-                term = lax.dot_general(
-                    slot_rows[(entry >> bits) & mask],
-                    cov_ref[entry >> (2 * bits)],
-                    (((1,), (side,)), ((), ())),
-                    preferred_element_type=jnp.float32,
-                )
-                total[entry & mask] += term
-        return carry
-
-    lax.fori_loop(0, lax.div(longest + UNROLL[group] - 1, UNROLL[group]), one, 0)
+    def steps(start, lanes):
+        def one(step, carry):
+            for lane in range(lanes):
+                for side in range(2):
+                    entry = plan_ref[2 * group + side, start + step * lanes + lane]
+                    term = lax.dot_general(
+                        slot_rows[(entry >> bits) & mask],
+                        cov_ref[entry >> (2 * bits)],
+                        (((1,), (side,)), ((), ())),
+                        preferred_element_type=jnp.float32,
+                    )
+                    total[entry & mask] += term
+            return carry
+
+        return one
+
+    whole = lax.div(longest, LANES)
+    done = whole * LANES
+    lax.fori_loop(0, whole, steps(0, LANES), 0)
+    lax.fori_loop(0, lax.div(longest - done + LANES_LEFT - 1, LANES_LEFT), steps(done, LANES_LEFT), 0)
 
 
 def gather_rows(ranks, incoming, slot_rows):
@@ -279,7 +287,7 @@
     pairs = cov_pairs.shape[0]
     late = tuple(rank for rank, offset in enumerate(order(owners)) if offset in (owners // 2 + 1, owners // 2))
     early = tuple(rank for rank in range(owners) if rank not in late)
-    width = -(-(pairs + max(UNROLL)) // 128) * 128
+    width = -(-(pairs + LANES) // 128) * 128
     me = my_index.reshape(1)
     served = lax.dynamic_index_in_dim(need_table, my_index, 1, keepdims=False).reshape(-1)
     wire_scratch = pltpu.VMEM((blocks, rows, size), jnp.bfloat16)
@@ -306,6 +314,7 @@
         out_specs=[VMEM] * owners,
         scratch_shapes=[wire_scratch],
         compiler_params=PARAMS,
+        cost_estimate=pl.CostEstimate(flops=10**11, bytes_accessed=64 << 20, transcendentals=10**8),
         name="pack_holdings",
     )(served, me, holdings)
     staged, places = pl.pallas_call(

time: 77.3 us -> 76.2 us (0.986); the launches traced: 76.5 us -> 76.5 us
  waiting for transfers between devices: 5.75 us -> 7 us
    ppermute x28, waiting for transfers between devices: 5.75 us -> 7 us  [exchange(): lax.ppermute(value, 'blk', [(index, index ^ offset) for index in range(ow...]
    pallas_call x1, Pallas kernels: 4.22 us -> 5.33 us  [body(): pl.pallas_call(functools.partial(early_kernel, early), out_shape=jax.Shap...]
    pallas_call x1, Pallas kernels: 3.14 us -> 2.07 us  [body(): pl.pallas_call(functools.partial(late_kernel, late), out_shape=([] if OWN...]
    unnamed x25 -> x27, local copies, waits for them, and re-layouts: 5.84 us -> 5.18 us
  transfers between devices with their start and end apart: 28 -> 28, of which waited for: 6 -> 5; matrix products, arithmetic and copies ran while one was open for 1% -> 0% of each run, Pallas kernels for 10% -> 11%
where the time goes in v7:
time: 76.2 us; the launch traced here: 76.5 us
  starting transfers between devices  43.7 us (57%)
  Pallas kernels  19.3 us (25%)
  waiting for transfers between devices  7 us (9%)
  local copies, waits for them, and re-layouts  5.54 us (7%)
  between operations  0.92 us (1%)
    ppermute x28, starting transfers between devices, exchange(): lax.ppermute(value, 'blk', [(index, index ^ offset) for index in range(ow...  43.7 us
    ppermute x28, waiting for transfers between devices, exchange(): lax.ppermute(value, 'blk', [(index, index ^ offset) for index in range(ow...  7 us
    pallas_call x1, Pallas kernels, body(): pl.pallas_call(functools.partial(early_kernel, early), out_shape=jax.Shap...  5.33 us
    unnamed x27, local copies, waits for them, and re-layouts  5.18 us
    pallas_call x1, Pallas kernels, body(): pl.pallas_call(functools.partial(pairs_kernel, owners), out_shape=[kept]...  5.05 us
    pallas_call x2, Pallas kernels, body(): pl.pallas_call(functools.partial(update_kernel, last, owners), out_shape=...  3.17 us
    pallas_call x1, Pallas kernels, body(): pl.pallas_call(functools.partial(late_kernel, late), out_shape=([] if OWN...  2.07 us
    pallas_call x1, Pallas kernels, body(): pl.pallas_call(functools.partial(own_kernel, owners), out_shape=kept, in_...  1.98 us
  transfers between devices with their start and end apart: 28, of which 5 were waited for; matrix products, arithmetic and copies ran while one was open for 0% of the time, Pallas kernels for 11%

profile of v7, /device:TPU:0, one launch (start us, length us, event | category | flops | bytes accessed | tf_op | source)
XLA Modules:
  0.0 76.5 jit_solution(10235286513531685947)
XLA Ops:
  0.6 0.0 copy-start
  0.6 0.7 copy-done
  1.3 0.3 dynamic-slice_reduce_fusion
  1.6 0.1 reshape.14.served_ref
  1.7 1.0 %copy-done.3 = f32[64,1024]{1,0:T(8,128)S(1)} copy-done((f32[64,1024]{1,0:T(8,128)S(1)}, f32[64,1024]{1,0:T(8,128)}, u32[]{:S(2)}) %copy-start.3) | copy-done | bytes 262168
  2.7 0.6 pack_holdings.1
  3.3 5.1 %collective-permute-start = (bf16[2,64,256]{2,1,0:T(8,128)(2,1)S(1)}, bf16[2,64,256]{2,1,0:T(8,128)(2,1)S(1)}, u32[]{:S(2)}, u32[]{:S(2)}) collective-permute-start(bf16[2,64,256]{2,1,0:T(8,128)(2,1)S(1)} %get-tuple-element.41), channel_id=1, source_target_pairs={{0,12},{2,14},{4,8},{6,10},{8,4},{10,6},{12,0},{14,2},{1,13},{3,15... | collective-permute-start | bytes 196616 | tf_op jit(solution)/shard_map/ppermute | solution.py:306
  8.4 0.5 collective-permute-start.1
  8.9 1.3 %collective-permute-start.2 = (bf16[2,64,256]{2,1,0:T(8,128)(2,1)S(1)}, bf16[2,64,256]{2,1,0:T(8,128)(2,1)S(1)}, u32[]{:S(2)}, u32[]{:S(2)}) collective-permute-start(bf16[2,64,256]{2,1,0:T(8,128)(2,1)S(1)} %get-tuple-element.43), channel_id=1, source_target_pairs={{0,14},{2,12},{4,10},{6,8},{8,6},{10,4},{12,2},{14,0},{1,15},{3,13... | collective-permute-start | bytes 196616 | tf_op jit(solution)/shard_map/ppermute | solution.py:306
  10.2 1.2 %collective-permute-start.3 = (bf16[2,64,256]{2,1,0:T(8,128)(2,1)S(1)}, bf16[2,64,256]{2,1,0:T(8,128)(2,1)S(1)}, u32[]{:S(2)}, u32[]{:S(2)}) collective-permute-start(bf16[2,64,256]{2,1,0:T(8,128)(2,1)S(1)} %get-tuple-element.44), channel_id=1, source_target_pairs={{0,4},{2,6},{4,0},{6,2},{8,12},{10,14},{12,8},{14,10},{1,5},{3,7},... | collective-permute-start | bytes 196616 | tf_op jit(solution)/shard_map/ppermute | solution.py:306
  11.4 2.8 %collective-permute-start.4 = (bf16[2,64,256]{2,1,0:T(8,128)(2,1)S(1)}, bf16[2,64,256]{2,1,0:T(8,128)(2,1)S(1)}, u32[]{:S(2)}, u32[]{:S(2)}) collective-permute-start(bf16[2,64,256]{2,1,0:T(8,128)(2,1)S(1)} %get-tuple-element.45), channel_id=1, source_target_pairs={{0,10},{2,8},{4,14},{6,12},{8,2},{10,0},{12,6},{14,4},{1,11},{3,9}... | collective-permute-start | bytes 196616 | tf_op jit(solution)/shard_map/ppermute | solution.py:306
  14.2 0.3 collective-permute-start.5
  14.5 0.3 collective-permute-done.1.refs_2_
  14.8 1.6 %collective-permute-start.6 = (bf16[2,64,256]{2,1,0:T(8,128)(2,1)S(1)}, bf16[2,64,256]{2,1,0:T(8,128)(2,1)S(1)}, u32[]{:S(2)}, u32[]{:S(2)}) collective-permute-start(bf16[2,64,256]{2,1,0:T(8,128)(2,1)S(1)} %get-tuple-element.47), channel_id=1, source_target_pairs={{0,2},{2,0},{4,6},{6,4},{8,10},{10,8},{12,14},{14,12},{1,3},{3,1},... | collective-permute-start | bytes 196616 | tf_op jit(solution)/shard_map/ppermute | solution.py:306
  16.4 0.1 copy.15.pairs_ref
  16.5 3.4 %copy-done.1 = bf16[64,256,256]{2,1,0:T(8,128)(2,1)S(1)} copy-done((bf16[64,256,256]{2,1,0:T(8,128)(2,1)S(1)}, bf16[64,256,256]{2,1,0:T(8,128)(2,1)}, u32[]{:S(2)}) %copy-start.1) | copy-done | bytes 8388632
  19.9 0.7 stage_pairs.1
  20.7 0.5 collective-permute-done.4.refs_5_
  21.2 5.0 %pair_products.1 = (f32[2,64,256]{2,1,0:T(8,128)S(1)}, bf16[2,64,256]{2,1,0:T(8,128)(2,1)S(1)}, bf16[2,64,256]{2,1,0:T(8,128)(2,1)S(1)}, bf16[2,64,256]{2,1,0:T(...) custom-call(s32[8,128]{1,0:T(8,128)S(1)} %get-tuple-element.38.place, ...), custom_call_target="tpu_custom_call" | custom-call | tf_op jit(solution)/shard_map/pair_products/pallas_call | solution.py:339
  26.2 2.0 %collective-permute-start.7 = (bf16[2,64,256]{2,1,0:T(8,128)(2,1)S(1)}, bf16[2,64,256]{2,1,0:T(8,128)(2,1)S(1)}, u32[]{:S(2)}, u32[]{:S(2)}) collective-permute-start(bf16[2,64,256]{2,1,0:T(8,128)(2,1)S(1)} %get-tuple-element.49), channel_id=1, source_target_pairs={{0,12},{2,14},{4,8},{6,10},{8,4},{10,6},{12,0},{14,2},{1,13},{3,15... | collective-permute-start | bytes 196616 | tf_op jit(solution)/shard_map/ppermute | solution.py:306
  28.2 0.3 collective-permute-start.8
  28.6 2.2 %collective-permute-start.9 = (bf16[2,64,256]{2,1,0:T(8,128)(2,1)S(1)}, bf16[2,64,256]{2,1,0:T(8,128)(2,1)S(1)}, u32[]{:S(2)}, u32[]{:S(2)}) collective-permute-start(bf16[2,64,256]{2,1,0:T(8,128)(2,1)S(1)} %get-tuple-element.51), channel_id=1, source_target_pairs={{0,14},{2,12},{4,10},{6,8},{8,6},{10,4},{12,2},{14,0},{1,15},{3,13... | collective-permute-start | bytes 196616 | tf_op jit(solution)/shard_map/ppermute | solution.py:306
  30.8 1.3 %collective-permute-start.10 = (bf16[2,64,256]{2,1,0:T(8,128)(2,1)S(1)}, bf16[2,64,256]{2,1,0:T(8,128)(2,1)S(1)}, u32[]{:S(2)}, u32[]{:S(2)}) collective-permute-start(bf16[2,64,256]{2,1,0:T(8,128)(2,1)S(1)} %get-tuple-element.52), channel_id=1, source_target_pairs={{0,4},{2,6},{4,0},{6,2},{8,12},{10,14},{12,8},{14,10},{1,5},{3,7},... | collective-permute-start | bytes 196616 | tf_op jit(solution)/shard_map/ppermute | solution.py:306
  32.2 1.7 %collective-permute-start.11 = (bf16[2,64,256]{2,1,0:T(8,128)(2,1)S(1)}, bf16[2,64,256]{2,1,0:T(8,128)(2,1)S(1)}, u32[]{:S(2)}, u32[]{:S(2)}) collective-permute-start(bf16[2,64,256]{2,1,0:T(8,128)(2,1)S(1)} %get-tuple-element.53), channel_id=1, source_target_pairs={{0,10},{2,8},{4,14},{6,12},{8,2},{10,0},{12,6},{14,4},{1,11},{3,9}... | collective-permute-start | bytes 196616 | tf_op jit(solution)/shard_map/ppermute | solution.py:306
  33.9 1.9 %collective-permute-start.12 = (bf16[2,64,256]{2,1,0:T(8,128)(2,1)S(1)}, bf16[2,64,256]{2,1,0:T(8,128)(2,1)S(1)}, u32[]{:S(2)}, u32[]{:S(2)}) collective-permute-start(bf16[2,64,256]{2,1,0:T(8,128)(2,1)S(1)} %get-tuple-element.54), channel_id=1, source_target_pairs={{0,8},{2,10},{4,12},{6,14},{8,0},{10,2},{12,4},{14,6},{1,9},{3,11}... | collective-permute-start | bytes 196616 | tf_op jit(solution)/shard_map/ppermute | solution.py:306
  35.8 0.8 %collective-permute-start.13 = (bf16[2,64,256]{2,1,0:T(8,128)(2,1)S(1)}, bf16[2,64,256]{2,1,0:T(8,128)(2,1)S(1)}, u32[]{:S(2)}, u32[]{:S(2)}) collective-permute-start(bf16[2,64,256]{2,1,0:T(8,128)(2,1)S(1)} %get-tuple-element.55), channel_id=1, source_target_pairs={{0,2},{2,0},{4,6},{6,4},{8,10},{10,8},{12,14},{14,12},{1,3},{3,1},... | collective-permute-start | bytes 196616 | tf_op jit(solution)/shard_map/ppermute | solution.py:306
  36.6 4.2 %collective-permute-done.11.refs_5_ = bf16[2,64,256]{2,1,0:T(8,128)(2,1)S(1)} collective-permute-done((bf16[2,64,256]{2,1,0:T(8,128)(2,1)S(1)}, bf16[2,64,256]{2,1,0:T(8,128)(2,1)S(1)}, u32[]{:S(2)}, u32[]{:S(2)}) %collective-permute-start.11) | collective-permute-done | bytes 65568 | tf_op jit(solution)/shard_map/ppermute | solution.py:306
  40.8 0.3 collective-permute-done.12.refs_6_
  41.1 1.2 %update.2 = (f32[64,1024]{1,0:T(8,128)S(1)}, f32[64,1024]{1,0:T(8,128)S(1)}, f32[64,1024]{1,0:T(8,128)S(1)}, bf16[2,64,256]{2,1,0:T(8,128)(2,1)S(1)}, bf16[2,64,...) custom-call(s32[16]{0:T(128)S(1)} %reshape.14.served_ref, ...), custom_call_target="tpu_custom_call" | custom-call | tf_op jit(solution)/shard_map/update/pallas_call | solution.py:395
  42.3 2.1 %collective-permute-start.14 = (bf16[2,64,256]{2,1,0:T(8,128)(2,1)S(1)}, bf16[2,64,256]{2,1,0:T(8,128)(2,1)S(1)}, u32[]{:S(2)}, u32[]{:S(2)}) collective-permute-start(bf16[2,64,256]{2,1,0:T(8,128)(2,1)S(1)} %get-tuple-element.57), channel_id=1, source_target_pairs={{0,12},{2,14},{4,8},{6,10},{8,4},{10,6},{12,0},{14,2},{1,13},{3,15... | collective-permute-start | bytes 196616 | tf_op jit(solution)/shard_map/ppermute | solution.py:306
  44.4 2.2 %collective-permute-start.16 = (bf16[2,64,256]{2,1,0:T(8,128)(2,1)S(1)}, bf16[2,64,256]{2,1,0:T(8,128)(2,1)S(1)}, u32[]{:S(2)}, u32[]{:S(2)}) collective-permute-start(bf16[2,64,256]{2,1,0:T(8,128)(2,1)S(1)} %get-tuple-element.59), channel_id=1, source_target_pairs={{0,14},{2,12},{4,10},{6,8},{8,6},{10,4},{12,2},{14,0},{1,15},{3,13... | collective-permute-start | bytes 196616 | tf_op jit(solution)/shard_map/ppermute | solution.py:306
  46.6 1.6 %collective-permute-start.17 = (bf16[2,64,256]{2,1,0:T(8,128)(2,1)S(1)}, bf16[2,64,256]{2,1,0:T(8,128)(2,1)S(1)}, u32[]{:S(2)}, u32[]{:S(2)}) collective-permute-start(bf16[2,64,256]{2,1,0:T(8,128)(2,1)S(1)} %get-tuple-element.60), channel_id=1, source_target_pairs={{0,4},{2,6},{4,0},{6,2},{8,12},{10,14},{12,8},{14,10},{1,5},{3,7},... | collective-permute-start | bytes 196616 | tf_op jit(solution)/shard_map/ppermute | solution.py:306
  48.2 1.0 %collective-permute-start.20 = (bf16[2,64,256]{2,1,0:T(8,128)(2,1)S(1)}, bf16[2,64,256]{2,1,0:T(8,128)(2,1)S(1)}, u32[]{:S(2)}, u32[]{:S(2)}) collective-permute-start(bf16[2,64,256]{2,1,0:T(8,128)(2,1)S(1)} %get-tuple-element.63), channel_id=1, source_target_pairs={{0,2},{2,0},{4,6},{6,4},{8,10},{10,8},{12,14},{14,12},{1,3},{3,1},... | collective-permute-start | bytes 196616 | tf_op jit(solution)/shard_map/ppermute | solution.py:306
  49.2 1.6 %collective-permute-start.18 = (bf16[2,64,256]{2,1,0:T(8,128)(2,1)S(1)}, bf16[2,64,256]{2,1,0:T(8,128)(2,1)S(1)}, u32[]{:S(2)}, u32[]{:S(2)}) collective-permute-start(bf16[2,64,256]{2,1,0:T(8,128)(2,1)S(1)} %get-tuple-element.61), channel_id=1, source_target_pairs={{0,10},{2,8},{4,14},{6,12},{8,2},{10,0},{12,6},{14,4},{1,11},{3,9}... | collective-permute-start | bytes 196616 | tf_op jit(solution)/shard_map/ppermute | solution.py:306
  50.9 1.7 %collective-permute-start.19 = (bf16[2,64,256]{2,1,0:T(8,128)(2,1)S(1)}, bf16[2,64,256]{2,1,0:T(8,128)(2,1)S(1)}, u32[]{:S(2)}, u32[]{:S(2)}) collective-permute-start(bf16[2,64,256]{2,1,0:T(8,128)(2,1)S(1)} %get-tuple-element.62), channel_id=1, source_target_pairs={{0,8},{2,10},{4,12},{6,14},{8,0},{10,2},{12,4},{14,6},{1,9},{3,11}... | collective-permute-start | bytes 196616 | tf_op jit(solution)/shard_map/ppermute | solution.py:306
  52.6 0.4 plan_products.1.plan_ref
  53.1 5.3 %early_products.1.early_ref = f32[17,64,256]{2,1,0:T(8,128)S(1)} custom-call(s32[8,128]{1,0:T(8,128)S(1)} %plan_products.1.plan_ref, bf16[64,256,256]{2,1,0:T(8,128)(2,1)S(1)} %bitcast.3, bf16[2,64,256]{2,1,0:T(8,128)(2,1)S(1)} %get-tuple-element.56.refs_0_, bf16[2,64,256]{2,1,0:T(8,128)(2,1)S(1)} %collective-permute-done.14.refs_1_, ...), custom_call_target="tpu_custom_call" | custom-call | flops 536870912 | bytes 8388608 | tf_op jit(solution)/shard_map/early_products/pallas_call | solution.py:362
  58.4 2.1 %late_products.1 = (bf16[2,64,256]{2,1,0:T(8,128)(2,1)S(1)}, bf16[2,64,256]{2,1,0:T(8,128)(2,1)S(1)}, bf16[2,64,256]{2,1,0:T(8,128)(2,1)S(1)}, bf16[2,64,256]{2,...) custom-call(s32[8,128]{1,0:T(8,128)S(1)} %plan_products.1.plan_ref, ...), custom_call_target="tpu_custom_call" | custom-call | flops 536870912 | bytes 8388608 | tf_op jit(solution)/shard_map/late_products/pallas_call | solution.py:372
  60.5 1.6 %collective-permute-start.21 = (bf16[2,64,256]{2,1,0:T(8,128)(2,1)S(1)}, bf16[2,64,256]{2,1,0:T(8,128)(2,1)S(1)}, u32[]{:S(2)}, u32[]{:S(2)}) collective-permute-start(bf16[2,64,256]{2,1,0:T(8,128)(2,1)S(1)} %get-tuple-element.64), channel_id=1, source_target_pairs={{0,12},{2,14},{4,8},{6,10},{8,4},{10,6},{12,0},{14,2},{1,13},{3,15... | collective-permute-start | bytes 196616 | tf_op jit(solution)/shard_map/ppermute | solution.py:306
  62.1 0.5 collective-permute-start.22
  62.5 3.7 %collective-permute-start.23 = (bf16[2,64,256]{2,1,0:T(8,128)(2,1)S(1)}, bf16[2,64,256]{2,1,0:T(8,128)(2,1)S(1)}, u32[]{:S(2)}, u32[]{:S(2)}) collective-permute-start(bf16[2,64,256]{2,1,0:T(8,128)(2,1)S(1)} %get-tuple-element.66), channel_id=1, source_target_pairs={{0,14},{2,12},{4,10},{6,8},{8,6},{10,4},{12,2},{14,0},{1,15},{3,13... | collective-permute-start | bytes 196616 | tf_op jit(solution)/shard_map/ppermute | solution.py:306
  66.2 0.2 collective-permute-start.24
  66.4 1.4 %collective-permute-start.25 = (bf16[2,64,256]{2,1,0:T(8,128)(2,1)S(1)}, bf16[2,64,256]{2,1,0:T(8,128)(2,1)S(1)}, u32[]{:S(2)}, u32[]{:S(2)}) collective-permute-start(bf16[2,64,256]{2,1,0:T(8,128)(2,1)S(1)} %get-tuple-element.68), channel_id=1, source_target_pairs={{0,10},{2,8},{4,14},{6,12},{8,2},{10,0},{12,6},{14,4},{1,11},{3,9}... | collective-permute-start | bytes 196616 | tf_op jit(solution)/shard_map/ppermute | solution.py:306
  67.8 1.9 %collective-permute-start.26 = (bf16[2,64,256]{2,1,0:T(8,128)(2,1)S(1)}, bf16[2,64,256]{2,1,0:T(8,128)(2,1)S(1)}, u32[]{:S(2)}, u32[]{:S(2)}) collective-permute-start(bf16[2,64,256]{2,1,0:T(8,128)(2,1)S(1)} %get-tuple-element.69), channel_id=1, source_target_pairs={{0,8},{2,10},{4,12},{6,14},{8,0},{10,2},{12,4},{14,6},{1,9},{3,11}... | collective-permute-start | bytes 196616 | tf_op jit(solution)/shard_map/ppermute | solution.py:306
  69.7 1.1 %collective-permute-start.27 = (bf16[2,64,256]{2,1,0:T(8,128)(2,1)S(1)}, bf16[2,64,256]{2,1,0:T(8,128)(2,1)S(1)}, u32[]{:S(2)}, u32[]{:S(2)}) collective-permute-start(bf16[2,64,256]{2,1,0:T(8,128)(2,1)S(1)} %get-tuple-element.70), channel_id=1, source_target_pairs={{0,2},{2,0},{4,6},{6,4},{8,10},{10,8},{12,14},{14,12},{1,3},{3,1},... | collective-permute-start | bytes 196616 | tf_op jit(solution)/shard_map/ppermute | solution.py:306
  70.8 2.0 %own_products.1.refs_0_ = f32[2,64,256]{2,1,0:T(8,128)S(1)} custom-call(s32[8,128]{1,0:T(8,128)S(1)} %plan_products.1.plan_ref, bf16[64,256,256]{2,1,0:T(8,128)(2,1)S(1)} %bitcast.3, bf16[2,64,256]{2,1,0:T(8,128)(2,1)S(1)} %get-tuple-element.56.refs_0_, bf16[2,64,256]{2,1,0:T(8,128)(2,1)S(1)} %collective-permute-done.14.refs_1_, ...), custom_call_target="tpu_custom_call" | custom-call | flops 268435456 | bytes 4194304 | tf_op jit(solution)/shard_map/own_products/pallas_call | solution.py:383
  72.9 1.7 %collective-permute-done.26.refs_6_ = bf16[2,64,256]{2,1,0:T(8,128)(2,1)S(1)} collective-permute-done((bf16[2,64,256]{2,1,0:T(8,128)(2,1)S(1)}, bf16[2,64,256]{2,1,0:T(8,128)(2,1)S(1)}, u32[]{:S(2)}, u32[]{:S(2)}) %collective-permute-start.26) | collective-permute-done | bytes 65568 | tf_op jit(solution)/shard_map/ppermute | solution.py:306
  74.5 2.0 %update.3 = (f32[64,1024]{1,0:T(8,128)}, f32[64,1024]{1,0:T(8,128)}) custom-call(s32[16]{0:T(128)S(1)} %reshape.14.served_ref, s32[1]{0:T(128)} %bitcast.me_ref, s32[4]{0:T(128)S(1)} %copy-done.8, f32[8]{0:T(128)S(1)} %copy-done.9, f32[2,64]{1,0:T(2,128)S(1)} %copy-done.7, f32[64,1024]{1,0:T(8,128)S(1)} %copy-done.4, s32[64,1024]{1,0:T(8,128)S(1)} %copy-done.5, ...), custom_call_target="tpu_custom_call" | custom-call | tf_op jit(solution)/shard_map/update/pallas_call | solution.py:395
  (47 shorter events, 0.1 us)
Async XLA Ops:
  0.6 0.7 copy-start
  1.7 1.0 %copy-start.3 = (f32[64,1024]{1,0:T(8,128)S(1)}, f32[64,1024]{1,0:T(8,128)}, u32[]{:S(2)}) copy-start(f32[64,1024]{1,0:T(8,128)} %holdings_ref.5) | copy-start | bytes 786436
  2.7 13.7 %copy-start.10 = (s32[1,64,2]{1,2,0:T(2,128)S(1)}, s32[1,64,2]{1,2,0:T(2,128)}, u32[]{:S(2)}) copy-start(s32[1,64,2]{1,2,0:T(2,128)} %param.15) | copy-start | bytes 1540
  3.3 10.9 %collective-permute-start = (bf16[2,64,256]{2,1,0:T(8,128)(2,1)S(1)}, bf16[2,64,256]{2,1,0:T(8,128)(2,1)S(1)}, u32[]{:S(2)}, u32[]{:S(2)}) collective-permute-start(bf16[2,64,256]{2,1,0:T(8,128)(2,1)S(1)} %get-tuple-element.41), channel_id=1, source_target_pairs={{0,12},{2,14},{4,8},{6,10},{8,4},{10,6},{12,0},{14,2},{1,13},{3,15... | collective-permute-start | bytes 196616 | tf_op jit(solution)/shard_map/ppermute | solution.py:306
  8.4 6.4 %collective-permute-start.1 = (bf16[2,64,256]{2,1,0:T(8,128)(2,1)S(1)}, bf16[2,64,256]{2,1,0:T(8,128)(2,1)S(1)}, u32[]{:S(2)}, u32[]{:S(2)}) collective-permute-start(bf16[2,64,256]{2,1,0:T(8,128)(2,1)S(1)} %get-tuple-element.42), channel_id=1, source_target_pairs={{0,6},{2,4},{4,2},{6,0},{8,14},{10,12},{12,10},{14,8},{1,7},{3,5},... | collective-permute-start | bytes 196616 | tf_op jit(solution)/shard_map/ppermute | solution.py:306
  8.9 11.8 %collective-permute-start.2 = (bf16[2,64,256]{2,1,0:T(8,128)(2,1)S(1)}, bf16[2,64,256]{2,1,0:T(8,128)(2,1)S(1)}, u32[]{:S(2)}, u32[]{:S(2)}) collective-permute-start(bf16[2,64,256]{2,1,0:T(8,128)(2,1)S(1)} %get-tuple-element.43), channel_id=1, source_target_pairs={{0,14},{2,12},{4,10},{6,8},{8,6},{10,4},{12,2},{14,0},{1,15},{3,13... | collective-permute-start | bytes 196616 | tf_op jit(solution)/shard_map/ppermute | solution.py:306
  10.2 10.5 %collective-permute-start.3 = (bf16[2,64,256]{2,1,0:T(8,128)(2,1)S(1)}, bf16[2,64,256]{2,1,0:T(8,128)(2,1)S(1)}, u32[]{:S(2)}, u32[]{:S(2)}) collective-permute-start(bf16[2,64,256]{2,1,0:T(8,128)(2,1)S(1)} %get-tuple-element.44), channel_id=1, source_target_pairs={{0,4},{2,6},{4,0},{6,2},{8,12},{10,14},{12,8},{14,10},{1,5},{3,7},... | collective-permute-start | bytes 196616 | tf_op jit(solution)/shard_map/ppermute | solution.py:306
  11.4 9.8 %collective-permute-start.4 = (bf16[2,64,256]{2,1,0:T(8,128)(2,1)S(1)}, bf16[2,64,256]{2,1,0:T(8,128)(2,1)S(1)}, u32[]{:S(2)}, u32[]{:S(2)}) collective-permute-start(bf16[2,64,256]{2,1,0:T(8,128)(2,1)S(1)} %get-tuple-element.45), channel_id=1, source_target_pairs={{0,10},{2,8},{4,14},{6,12},{8,2},{10,0},{12,6},{14,4},{1,11},{3,9}... | collective-permute-start | bytes 196616 | tf_op jit(solution)/shard_map/ppermute | solution.py:306
  14.2 7.0 %collective-permute-start.5 = (bf16[2,64,256]{2,1,0:T(8,128)(2,1)S(1)}, bf16[2,64,256]{2,1,0:T(8,128)(2,1)S(1)}, u32[]{:S(2)}, u32[]{:S(2)}) collective-permute-start(bf16[2,64,256]{2,1,0:T(8,128)(2,1)S(1)} %get-tuple-element.46), channel_id=1, source_target_pairs={{0,8},{2,10},{4,12},{6,14},{8,0},{10,2},{12,4},{14,6},{1,9},{3,11}... | collective-permute-start | bytes 196616 | tf_op jit(solution)/shard_map/ppermute | solution.py:306
  14.8 6.4 %collective-permute-start.6 = (bf16[2,64,256]{2,1,0:T(8,128)(2,1)S(1)}, bf16[2,64,256]{2,1,0:T(8,128)(2,1)S(1)}, u32[]{:S(2)}, u32[]{:S(2)}) collective-permute-start(bf16[2,64,256]{2,1,0:T(8,128)(2,1)S(1)} %get-tuple-element.47), channel_id=1, source_target_pairs={{0,2},{2,0},{4,6},{6,4},{8,10},{10,8},{12,14},{14,12},{1,3},{3,1},... | collective-permute-start | bytes 196616 | tf_op jit(solution)/shard_map/ppermute | solution.py:306
  16.5 3.4 %copy-start.1 = (bf16[64,256,256]{2,1,0:T(8,128)(2,1)S(1)}, bf16[64,256,256]{2,1,0:T(8,128)(2,1)}, u32[]{:S(2)}) copy-start(bf16[64,256,256]{2,1,0:T(8,128)(2,1)} %cov_ref.7) | copy-start | bytes 25165828
  19.9 21.2 %copy-start.2 = (bf16[4,256,256]{2,1,0:T(8,128)(2,1)S(1)}, bf16[4,256,256]{2,1,0:T(8,128)(2,1)}, u32[]{:S(2)}) copy-start(bf16[4,256,256]{2,1,0:T(8,128)(2,1)} %diag_ref.3) | copy-start | bytes 1572868
  19.9 21.2 %copy-start.4 = (f32[64,1024]{1,0:T(8,128)S(1)}, f32[64,1024]{1,0:T(8,128)}, u32[]{:S(2)}) copy-start(f32[64,1024]{1,0:T(8,128)} %holdings_ref.5) | copy-start | bytes 786436
  19.9 21.2 %copy-start.5 = (s32[64,1024]{1,0:T(8,128)S(1)}, s32[64,1024]{1,0:T(8,128)}, u32[]{:S(2)}) copy-start(s32[64,1024]{1,0:T(8,128)} %eligible_ref.3) | copy-start | bytes 786436
  19.9 21.2 %copy-start.6 = (f32[1024]{0:T(1024)S(1)}, f32[1024]{0:T(1024)}, u32[]{:S(2)}) copy-start(f32[1024]{0:T(1024)} %param.12) | copy-start | bytes 12292
  19.9 21.2 %copy-start.7 = (f32[2,64]{1,0:T(2,128)S(1)}, f32[2,64]{1,0:T(2,128)}, u32[]{:S(2)}) copy-start(f32[2,64]{1,0:T(2,128)} %slopes_ref.3) | copy-start | bytes 1540
  19.9 21.2 %copy-start.8 = (s32[4]{0:T(128)S(1)}, s32[4]{0:T(128)}, u32[]{:S(2)}) copy-start(s32[4]{0:T(128)} %knee_index_ref.3) | copy-start | bytes 52
  19.9 21.2 %copy-start.9 = (f32[8]{0:T(128)S(1)}, f32[8]{0:T(128)}, u32[]{:S(2)}) copy-start(f32[8]{0:T(128)} %knee_levels_ref.3) | copy-start | bytes 100
  19.9 33.1 %slice-start = ((s8[8388608]{0:T(1024)(128)(4,1)}), s8[4194304]{0:T(1024)(128)(4,1)S(1)}, s32[]{:S(2)}) async-start(s8[8388608]{0:T(1024)(128)(4,1)} %bitcast.2), calls=%async_computation | async-start | bytes 8388608
  21.2 31.9 %slice-start.1 = ((s8[8388608]{0:T(1024)(128)(4,1)}), s8[4194304]{0:T(1024)(128)(4,1)S(1)}, s32[]{:S(2)}) async-start(s8[8388608]{0:T(1024)(128)(4,1)} %bitcast.2), calls=%async_computation.1 | async-start | bytes 8388608
  26.2 7.6 %collective-permute-start.7 = (bf16[2,64,256]{2,1,0:T(8,128)(2,1)S(1)}, bf16[2,64,256]{2,1,0:T(8,128)(2,1)S(1)}, u32[]{:S(2)}, u32[]{:S(2)}) collective-permute-start(bf16[2,64,256]{2,1,0:T(8,128)(2,1)S(1)} %get-tuple-element.49), channel_id=1, source_target_pairs={{0,12},{2,14},{4,8},{6,10},{8,4},{10,6},{12,0},{14,2},{1,13},{3,15... | collective-permute-start | bytes 196616 | tf_op jit(solution)/shard_map/ppermute | solution.py:306
  28.2 7.5 %collective-permute-start.8 = (bf16[2,64,256]{2,1,0:T(8,128)(2,1)S(1)}, bf16[2,64,256]{2,1,0:T(8,128)(2,1)S(1)}, u32[]{:S(2)}, u32[]{:S(2)}) collective-permute-start(bf16[2,64,256]{2,1,0:T(8,128)(2,1)S(1)} %get-tuple-element.50), channel_id=1, source_target_pairs={{0,6},{2,4},{4,2},{6,0},{8,14},{10,12},{12,10},{14,8},{1,7},{3,5},... | collective-permute-start | bytes 196616 | tf_op jit(solution)/shard_map/ppermute | solution.py:306
  28.6 8.0 %collective-permute-start.9 = (bf16[2,64,256]{2,1,0:T(8,128)(2,1)S(1)}, bf16[2,64,256]{2,1,0:T(8,128)(2,1)S(1)}, u32[]{:S(2)}, u32[]{:S(2)}) collective-permute-start(bf16[2,64,256]{2,1,0:T(8,128)(2,1)S(1)} %get-tuple-element.51), channel_id=1, source_target_pairs={{0,14},{2,12},{4,10},{6,8},{8,6},{10,4},{12,2},{14,0},{1,15},{3,13... | collective-permute-start | bytes 196616 | tf_op jit(solution)/shard_map/ppermute | solution.py:306
  30.8 5.7 %collective-permute-start.10 = (bf16[2,64,256]{2,1,0:T(8,128)(2,1)S(1)}, bf16[2,64,256]{2,1,0:T(8,128)(2,1)S(1)}, u32[]{:S(2)}, u32[]{:S(2)}) collective-permute-start(bf16[2,64,256]{2,1,0:T(8,128)(2,1)S(1)} %get-tuple-element.52), channel_id=1, source_target_pairs={{0,4},{2,6},{4,0},{6,2},{8,12},{10,14},{12,8},{14,10},{1,5},{3,7},... | collective-permute-start | bytes 196616 | tf_op jit(solution)/shard_map/ppermute | solution.py:306
  32.2 8.6 %collective-permute-start.11 = (bf16[2,64,256]{2,1,0:T(8,128)(2,1)S(1)}, bf16[2,64,256]{2,1,0:T(8,128)(2,1)S(1)}, u32[]{:S(2)}, u32[]{:S(2)}) collective-permute-start(bf16[2,64,256]{2,1,0:T(8,128)(2,1)S(1)} %get-tuple-element.53), channel_id=1, source_target_pairs={{0,10},{2,8},{4,14},{6,12},{8,2},{10,0},{12,6},{14,4},{1,11},{3,9}... | collective-permute-start | bytes 196616 | tf_op jit(solution)/shard_map/ppermute | solution.py:306
  33.9 7.1 %collective-permute-start.12 = (bf16[2,64,256]{2,1,0:T(8,128)(2,1)S(1)}, bf16[2,64,256]{2,1,0:T(8,128)(2,1)S(1)}, u32[]{:S(2)}, u32[]{:S(2)}) collective-permute-start(bf16[2,64,256]{2,1,0:T(8,128)(2,1)S(1)} %get-tuple-element.54), channel_id=1, source_target_pairs={{0,8},{2,10},{4,12},{6,14},{8,0},{10,2},{12,4},{14,6},{1,9},{3,11}... | collective-permute-start | bytes 196616 | tf_op jit(solution)/shard_map/ppermute | solution.py:306
  35.8 5.3 %collective-permute-start.13 = (bf16[2,64,256]{2,1,0:T(8,128)(2,1)S(1)}, bf16[2,64,256]{2,1,0:T(8,128)(2,1)S(1)}, u32[]{:S(2)}, u32[]{:S(2)}) collective-permute-start(bf16[2,64,256]{2,1,0:T(8,128)(2,1)S(1)} %get-tuple-element.55), channel_id=1, source_target_pairs={{0,2},{2,0},{4,6},{6,4},{8,10},{10,8},{12,14},{14,12},{1,3},{3,1},... | collective-permute-start | bytes 196616 | tf_op jit(solution)/shard_map/ppermute | solution.py:306
  42.3 6.9 %collective-permute-start.14 = (bf16[2,64,256]{2,1,0:T(8,128)(2,1)S(1)}, bf16[2,64,256]{2,1,0:T(8,128)(2,1)S(1)}, u32[]{:S(2)}, u32[]{:S(2)}) collective-permute-start(bf16[2,64,256]{2,1,0:T(8,128)(2,1)S(1)} %get-tuple-element.57), channel_id=1, source_target_pairs={{0,12},{2,14},{4,8},{6,10},{8,4},{10,6},{12,0},{14,2},{1,13},{3,15... | collective-permute-start | bytes 196616 | tf_op jit(solution)/shard_map/ppermute | solution.py:306
  44.4 6.5 %collective-permute-start.15 = (bf16[2,64,256]{2,1,0:T(8,128)(2,1)S(1)}, bf16[2,64,256]{2,1,0:T(8,128)(2,1)S(1)}, u32[]{:S(2)}, u32[]{:S(2)}) collective-permute-start(bf16[2,64,256]{2,1,0:T(8,128)(2,1)S(1)} %get-tuple-element.58), channel_id=1, source_target_pairs={{0,6},{2,4},{4,2},{6,0},{8,14},{10,12},{12,10},{14,8},{1,7},{3,5},... | collective-permute-start | bytes 196616 | tf_op jit(solution)/shard_map/ppermute | solution.py:306
  44.4 8.6 %collective-permute-start.16 = (bf16[2,64,256]{2,1,0:T(8,128)(2,1)S(1)}, bf16[2,64,256]{2,1,0:T(8,128)(2,1)S(1)}, u32[]{:S(2)}, u32[]{:S(2)}) collective-permute-start(bf16[2,64,256]{2,1,0:T(8,128)(2,1)S(1)} %get-tuple-element.59), channel_id=1, source_target_pairs={{0,14},{2,12},{4,10},{6,8},{8,6},{10,4},{12,2},{14,0},{1,15},{3,13... | collective-permute-start | bytes 196616 | tf_op jit(solution)/shard_map/ppermute | solution.py:306
  46.6 6.4 %collective-permute-start.17 = (bf16[2,64,256]{2,1,0:T(8,128)(2,1)S(1)}, bf16[2,64,256]{2,1,0:T(8,128)(2,1)S(1)}, u32[]{:S(2)}, u32[]{:S(2)}) collective-permute-start(bf16[2,64,256]{2,1,0:T(8,128)(2,1)S(1)} %get-tuple-element.60), channel_id=1, source_target_pairs={{0,4},{2,6},{4,0},{6,2},{8,12},{10,14},{12,8},{14,10},{1,5},{3,7},... | collective-permute-start | bytes 196616 | tf_op jit(solution)/shard_map/ppermute | solution.py:306
  48.2 4.8 %collective-permute-start.20 = (bf16[2,64,256]{2,1,0:T(8,128)(2,1)S(1)}, bf16[2,64,256]{2,1,0:T(8,128)(2,1)S(1)}, u32[]{:S(2)}, u32[]{:S(2)}) collective-permute-start(bf16[2,64,256]{2,1,0:T(8,128)(2,1)S(1)} %get-tuple-element.63), channel_id=1, source_target_pairs={{0,2},{2,0},{4,6},{6,4},{8,10},{10,8},{12,14},{14,12},{1,3},{3,1},... | collective-permute-start | bytes 196616 | tf_op jit(solution)/shard_map/ppermute | solution.py:306
  49.2 9.2 %collective-permute-start.18 = (bf16[2,64,256]{2,1,0:T(8,128)(2,1)S(1)}, bf16[2,64,256]{2,1,0:T(8,128)(2,1)S(1)}, u32[]{:S(2)}, u32[]{:S(2)}) collective-permute-start(bf16[2,64,256]{2,1,0:T(8,128)(2,1)S(1)} %get-tuple-element.61), channel_id=1, source_target_pairs={{0,10},{2,8},{4,14},{6,12},{8,2},{10,0},{12,6},{14,4},{1,11},{3,9}... | collective-permute-start | bytes 196616 | tf_op jit(solution)/shard_map/ppermute | solution.py:306
  50.9 7.6 %collective-permute-start.19 = (bf16[2,64,256]{2,1,0:T(8,128)(2,1)S(1)}, bf16[2,64,256]{2,1,0:T(8,128)(2,1)S(1)}, u32[]{:S(2)}, u32[]{:S(2)}) collective-permute-start(bf16[2,64,256]{2,1,0:T(8,128)(2,1)S(1)} %get-tuple-element.62), channel_id=1, source_target_pairs={{0,8},{2,10},{4,12},{6,14},{8,0},{10,2},{12,4},{14,6},{1,9},{3,11}... | collective-permute-start | bytes 196616 | tf_op jit(solution)/shard_map/ppermute | solution.py:306
  60.5 7.3 %collective-permute-start.21 = (bf16[2,64,256]{2,1,0:T(8,128)(2,1)S(1)}, bf16[2,64,256]{2,1,0:T(8,128)(2,1)S(1)}, u32[]{:S(2)}, u32[]{:S(2)}) collective-permute-start(bf16[2,64,256]{2,1,0:T(8,128)(2,1)S(1)} %get-tuple-element.64), channel_id=1, source_target_pairs={{0,12},{2,14},{4,8},{6,10},{8,4},{10,6},{12,0},{14,2},{1,13},{3,15... | collective-permute-start | bytes 196616 | tf_op jit(solution)/shard_map/ppermute | solution.py:306
  62.1 7.7 %collective-permute-start.22 = (bf16[2,64,256]{2,1,0:T(8,128)(2,1)S(1)}, bf16[2,64,256]{2,1,0:T(8,128)(2,1)S(1)}, u32[]{:S(2)}, u32[]{:S(2)}) collective-permute-start(bf16[2,64,256]{2,1,0:T(8,128)(2,1)S(1)} %get-tuple-element.65), channel_id=1, source_target_pairs={{0,6},{2,4},{4,2},{6,0},{8,14},{10,12},{12,10},{14,8},{1,7},{3,5},... | collective-permute-start | bytes 196616 | tf_op jit(solution)/shard_map/ppermute | solution.py:306
  62.5 10.3 %collective-permute-start.23 = (bf16[2,64,256]{2,1,0:T(8,128)(2,1)S(1)}, bf16[2,64,256]{2,1,0:T(8,128)(2,1)S(1)}, u32[]{:S(2)}, u32[]{:S(2)}) collective-permute-start(bf16[2,64,256]{2,1,0:T(8,128)(2,1)S(1)} %get-tuple-element.66), channel_id=1, source_target_pairs={{0,14},{2,12},{4,10},{6,8},{8,6},{10,4},{12,2},{14,0},{1,15},{3,13... | collective-permute-start | bytes 196616 | tf_op jit(solution)/shard_map/ppermute | solution.py:306
  66.2 6.6 %collective-permute-start.24 = (bf16[2,64,256]{2,1,0:T(8,128)(2,1)S(1)}, bf16[2,64,256]{2,1,0:T(8,128)(2,1)S(1)}, u32[]{:S(2)}, u32[]{:S(2)}) collective-permute-start(bf16[2,64,256]{2,1,0:T(8,128)(2,1)S(1)} %get-tuple-element.67), channel_id=1, source_target_pairs={{0,4},{2,6},{4,0},{6,2},{8,12},{10,14},{12,8},{14,10},{1,5},{3,7},... | collective-permute-start | bytes 196616 | tf_op jit(solution)/shard_map/ppermute | solution.py:306
  66.4 6.4 %collective-permute-start.25 = (bf16[2,64,256]{2,1,0:T(8,128)(2,1)S(1)}, bf16[2,64,256]{2,1,0:T(8,128)(2,1)S(1)}, u32[]{:S(2)}, u32[]{:S(2)}) collective-permute-start(bf16[2,64,256]{2,1,0:T(8,128)(2,1)S(1)} %get-tuple-element.68), channel_id=1, source_target_pairs={{0,10},{2,8},{4,14},{6,12},{8,2},{10,0},{12,6},{14,4},{1,11},{3,9}... | collective-permute-start | bytes 196616 | tf_op jit(solution)/shard_map/ppermute | solution.py:306
  67.8 6.7 %collective-permute-start.26 = (bf16[2,64,256]{2,1,0:T(8,128)(2,1)S(1)}, bf16[2,64,256]{2,1,0:T(8,128)(2,1)S(1)}, u32[]{:S(2)}, u32[]{:S(2)}) collective-permute-start(bf16[2,64,256]{2,1,0:T(8,128)(2,1)S(1)} %get-tuple-element.69), channel_id=1, source_target_pairs={{0,8},{2,10},{4,12},{6,14},{8,0},{10,2},{12,4},{14,6},{1,9},{3,11}... | collective-permute-start | bytes 196616 | tf_op jit(solution)/shard_map/ppermute | solution.py:306
  69.7 4.8 %collective-permute-start.27 = (bf16[2,64,256]{2,1,0:T(8,128)(2,1)S(1)}, bf16[2,64,256]{2,1,0:T(8,128)(2,1)S(1)}, u32[]{:S(2)}, u32[]{:S(2)}) collective-permute-start(bf16[2,64,256]{2,1,0:T(8,128)(2,1)S(1)} %get-tuple-element.70), channel_id=1, source_target_pairs={{0,2},{2,0},{4,6},{6,4},{8,10},{10,8},{12,14},{14,12},{1,3},{3,1},... | collective-permute-start | bytes 196616 | tf_op jit(solution)/shard_map/ppermute | solution.py:306

commit v8 on v7

--- a/solution.py
+++ b/solution.py
@@ -203,9 +203,29 @@
     return jnp.sum(jnp.where(on_diagonal, row, 0.0), axis=1, keepdims=True)
 
 
+def add_returned(served_ref, me_ref, offsets, returned, terms):
+    capacity = returned[0].shape[0]
+    for offset, back_ref in zip(offsets, returned):
+        for column_index in range(capacity):
+            local = served_ref[(offset ^ me_ref[0]) * capacity + column_index]
+
+            @pl.when(local >= 0)
+            def _(local=local, back_ref=back_ref, column_index=column_index):
+                terms[local] += back_ref[column_index].astype(jnp.float32)
+
+
+def terms_kernel(offsets, served_ref, me_ref, diag_ref, primal_ref, *refs):
+    *returned, terms = refs
+    blocks, _, size = terms.shape
+    for block in range(blocks):
+        x_wire = primal_ref[:, block * size : (block + 1) * size].astype(jnp.bfloat16)
+        terms[block] = jnp.dot(x_wire, diag_ref[block], preferred_element_type=jnp.float32)
+    add_returned(served_ref, me_ref, offsets, returned, terms)
+
+
 def update_kernel(
     last,
-    owners,
+    offsets,
     served_ref,
     me_ref,
     knee_index_ref,
@@ -214,33 +234,24 @@
     holdings_ref,
     eligible_ref,
     expected_ref,
-    diag_ref,
+    terms_ref,
     *refs,
 ):
-    returned, refs = refs[:owners], refs[owners:]
+    returned, refs = refs[: len(offsets)], refs[len(offsets) :]
     if last:
         primal_ref, traded_ref, dual_ref, traded_out, dual_out, terms = refs
     else:
         primal_out, traded_out, dual_out, *outgoing, terms, wire_ref = refs
     blocks, rows, size = terms.shape
-    capacity = returned[0].shape[0]
-    terms[...] = jnp.zeros_like(terms)
-    for offset, back_ref in zip(order(owners), returned):
-        for column_index in range(capacity):
-            local = served_ref[(offset ^ me_ref[0]) * capacity + column_index]
-
-            @pl.when(local >= 0)
-            def _(local=local, back_ref=back_ref, column_index=column_index):
-                terms[local] += back_ref[column_index].astype(jnp.float32)
-
+    terms[...] = terms_ref[...]
+    add_returned(served_ref, me_ref, offsets, returned, terms)
     low = column(slopes_ref[0:1, :] / PENALTY, rows)
     high = column((slopes_ref[0:1, :] + slopes_ref[1:2, :]) / PENALTY, rows)
     for block in range(blocks):
         span = pl.ds(block * size, size)
         initial = holdings_ref[:, span]
         primal = primal_ref[:, span] if last else initial
-        x_wire = primal.astype(jnp.bfloat16)
-        grad = jnp.dot(x_wire, diag_ref[block], preferred_element_type=jnp.float32) + terms[block]
+        grad = terms[block]
         expected = expected_ref[:, span]
         allowed = eligible_ref[:, span].astype(jnp.float32)
         if last:
@@ -392,10 +403,22 @@
                 )(plan, cov_pairs, *incoming)
                 partial_sums = [own, *partial_sums]
         returned = exchange(partial_sums)
+        offsets = order(owners)
+        rest = late + tuple(rank for rank in early if offsets[rank] == 1)
+        soon = tuple(rank for rank in early if rank not in rest)
+        terms = pl.pallas_call(
+            functools.partial(terms_kernel, [offsets[rank] for rank in soon]),
+            out_shape=jax.ShapeDtypeStruct((blocks, rows, size), jnp.float32),
+            in_specs=[SMEM] * 2 + [VMEM] * (2 + len(soon)),
+            out_specs=VMEM,
+            compiler_params=PARAMS,
+            cost_estimate=cost(blocks),
+            name="early_terms",
+        )(served, me, cov_diag, state[0] if last else holdings, *(returned[rank] for rank in soon))
         outs = pl.pallas_call(
-            functools.partial(update_kernel, last, owners),
+            functools.partial(update_kernel, last, [offsets[rank] for rank in rest]),
             out_shape=[whole] * 2 if last else [whole] * 3 + [sent] * owners,
-            in_specs=[SMEM] * 4 + [VMEM] * (5 + owners + len(state)),
+            in_specs=[SMEM] * 4 + [VMEM] * (5 + len(rest) + len(state)),
             out_specs=[VMEM] * (2 if last else 3 + owners),
             scratch_shapes=[pltpu.VMEM((blocks, rows, size), jnp.float32)] + ([] if last else [wire_scratch]),
             compiler_params=PARAMS,
@@ -409,8 +432,8 @@
             holdings,
             eligible,
             expected,
-            cov_diag,
-            *returned,
+            terms,
+            *(returned[rank] for rank in rest),
             *state,
         )
         if not last:

time: 76.2 us -> 76.8 us (level)
  starting transfers between devices: 43.7 us -> 45.4 us
    ppermute x28, starting transfers between devices: 43.7 us -> 45.4 us  [exchange(): lax.ppermute(value, 'blk', [(index, index ^ offset) for index in range(ow...]
    pallas_call x1, Pallas kernels: 5.33 us -> 3.76 us  [body(): pl.pallas_call(functools.partial(early_kernel, early), out_shape=jax.Shap...]
    pallas_call x2 -> x4, Pallas kernels: 3.17 us -> 4.39 us  [the longest x2 2.62 us: body(): pl.pallas_call(functools.partial(update_kernel, last, [offsets[rank] for...]
  transfers between devices with their start and end apart: 28 -> 28, of which waited for: 5 -> 7; matrix products, arithmetic and copies ran while one was open for 0% -> 0% of each run, Pallas kernels for 11% -> 11%
where the time goes in v8:
time: 76.8 us; the launch traced here: 77.5 us
  starting transfers between devices  45.4 us (59%)
  Pallas kernels  19.1 us (25%)
  waiting for transfers between devices  6.49 us (8%)
  local copies, waits for them, and re-layouts  5.54 us (7%)
  between operations  0.93 us (1%)
    ppermute x28, starting transfers between devices, exchange(): lax.ppermute(value, 'blk', [(index, index ^ offset) for index in range(ow...  45.4 us
    ppermute x28, waiting for transfers between devices, exchange(): lax.ppermute(value, 'blk', [(index, index ^ offset) for index in range(ow...  6.49 us
    unnamed x27, local copies, waits for them, and re-layouts  5.18 us
    pallas_call x1, Pallas kernels, body(): pl.pallas_call(functools.partial(pairs_kernel, owners), out_shape=[kept]...  5.05 us
    pallas_call x1, Pallas kernels, body(): pl.pallas_call(functools.partial(early_kernel, early), out_shape=jax.Shap...  3.76 us
    pallas_call x2, Pallas kernels, body(): pl.pallas_call(functools.partial(update_kernel, last, [offsets[rank] for...  2.62 us
    pallas_call x1, Pallas kernels, body(): pl.pallas_call(functools.partial(late_kernel, late), out_shape=([] if OWN...  2.46 us
    pallas_call x2, Pallas kernels, body(): pl.pallas_call(functools.partial(terms_kernel, [offsets[rank] for rank in...  1.77 us
  transfers between devices with their start and end apart: 28, of which 7 were waited for; matrix products, arithmetic and copies ran while one was open for 0% of the time, Pallas kernels for 11%

profile of v8, /device:TPU:0, one launch (start us, length us, event | category | flops | bytes accessed | tf_op | source)
XLA Modules:
  0.0 77.5 jit_solution(15533066678528810837)
XLA Ops:
  0.6 0.7 copy-done
  1.3 0.3 dynamic-slice_reduce_fusion
  1.7 1.0 %copy-done.2 = f32[64,1024]{1,0:T(8,128)S(1)} copy-done((f32[64,1024]{1,0:T(8,128)S(1)}, f32[64,1024]{1,0:T(8,128)}, u32[]{:S(2)}) %copy-start.2) | copy-done | bytes 262168
  2.7 0.6 pack_holdings.1
  3.3 5.1 %collective-permute-start = (bf16[2,64,256]{2,1,0:T(8,128)(2,1)S(1)}, bf16[2,64,256]{2,1,0:T(8,128)(2,1)S(1)}, u32[]{:S(2)}, u32[]{:S(2)}) collective-permute-start(bf16[2,64,256]{2,1,0:T(8,128)(2,1)S(1)} %get-tuple-element.41), channel_id=1, source_target_pairs={{0,12},{2,14},{4,8},{6,10},{8,4},{10,6},{12,0},{14,2},{1,13},{3,15... | collective-permute-start | bytes 196616 | tf_op jit(solution)/shard_map/ppermute | solution.py:317
  8.4 0.5 collective-permute-start.1
  8.9 1.3 %collective-permute-start.2 = (bf16[2,64,256]{2,1,0:T(8,128)(2,1)S(1)}, bf16[2,64,256]{2,1,0:T(8,128)(2,1)S(1)}, u32[]{:S(2)}, u32[]{:S(2)}) collective-permute-start(bf16[2,64,256]{2,1,0:T(8,128)(2,1)S(1)} %get-tuple-element.43), channel_id=1, source_target_pairs={{0,14},{2,12},{4,10},{6,8},{8,6},{10,4},{12,2},{14,0},{1,15},{3,13... | collective-permute-start | bytes 196616 | tf_op jit(solution)/shard_map/ppermute | solution.py:317
  10.2 1.2 %collective-permute-start.3 = (bf16[2,64,256]{2,1,0:T(8,128)(2,1)S(1)}, bf16[2,64,256]{2,1,0:T(8,128)(2,1)S(1)}, u32[]{:S(2)}, u32[]{:S(2)}) collective-permute-start(bf16[2,64,256]{2,1,0:T(8,128)(2,1)S(1)} %get-tuple-element.44), channel_id=1, source_target_pairs={{0,4},{2,6},{4,0},{6,2},{8,12},{10,14},{12,8},{14,10},{1,5},{3,7},... | collective-permute-start | bytes 196616 | tf_op jit(solution)/shard_map/ppermute | solution.py:317
  11.4 2.8 %collective-permute-start.4 = (bf16[2,64,256]{2,1,0:T(8,128)(2,1)S(1)}, bf16[2,64,256]{2,1,0:T(8,128)(2,1)S(1)}, u32[]{:S(2)}, u32[]{:S(2)}) collective-permute-start(bf16[2,64,256]{2,1,0:T(8,128)(2,1)S(1)} %get-tuple-element.45), channel_id=1, source_target_pairs={{0,10},{2,8},{4,14},{6,12},{8,2},{10,0},{12,6},{14,4},{1,11},{3,9}... | collective-permute-start | bytes 196616 | tf_op jit(solution)/shard_map/ppermute | solution.py:317
  14.2 0.3 collective-permute-start.5
  14.5 0.3 collective-permute-done.1.refs_2_
  14.8 1.6 %collective-permute-start.6 = (bf16[2,64,256]{2,1,0:T(8,128)(2,1)S(1)}, bf16[2,64,256]{2,1,0:T(8,128)(2,1)S(1)}, u32[]{:S(2)}, u32[]{:S(2)}) collective-permute-start(bf16[2,64,256]{2,1,0:T(8,128)(2,1)S(1)} %get-tuple-element.47), channel_id=1, source_target_pairs={{0,2},{2,0},{4,6},{6,4},{8,10},{10,8},{12,14},{14,12},{1,3},{3,1},... | collective-permute-start | bytes 196616 | tf_op jit(solution)/shard_map/ppermute | solution.py:317
  16.4 0.1 copy.14.pairs_ref
  16.5 3.4 %copy-done.1 = bf16[64,256,256]{2,1,0:T(8,128)(2,1)S(1)} copy-done((bf16[64,256,256]{2,1,0:T(8,128)(2,1)S(1)}, bf16[64,256,256]{2,1,0:T(8,128)(2,1)}, u32[]{:S(2)}) %copy-start.1) | copy-done | bytes 8388632
  19.9 0.7 stage_pairs.1
  20.7 0.5 collective-permute-done.4.refs_5_
  21.2 5.0 %pair_products.1 = (f32[2,64,256]{2,1,0:T(8,128)S(1)}, bf16[2,64,256]{2,1,0:T(8,128)(2,1)S(1)}, bf16[2,64,256]{2,1,0:T(8,128)(2,1)S(1)}, bf16[2,64,256]{2,1,0:T(...) custom-call(s32[8,128]{1,0:T(8,128)S(1)} %get-tuple-element.38.place, ...), custom_call_target="tpu_custom_call" | custom-call | tf_op jit(solution)/shard_map/pair_products/pallas_call | solution.py:350
  26.2 2.0 %collective-permute-start.7 = (bf16[2,64,256]{2,1,0:T(8,128)(2,1)S(1)}, bf16[2,64,256]{2,1,0:T(8,128)(2,1)S(1)}, u32[]{:S(2)}, u32[]{:S(2)}) collective-permute-start(bf16[2,64,256]{2,1,0:T(8,128)(2,1)S(1)} %get-tuple-element.49), channel_id=1, source_target_pairs={{0,12},{2,14},{4,8},{6,10},{8,4},{10,6},{12,0},{14,2},{1,13},{3,15... | collective-permute-start | bytes 196616 | tf_op jit(solution)/shard_map/ppermute | solution.py:317
  28.2 0.3 collective-permute-start.8
  28.6 2.2 %collective-permute-start.9 = (bf16[2,64,256]{2,1,0:T(8,128)(2,1)S(1)}, bf16[2,64,256]{2,1,0:T(8,128)(2,1)S(1)}, u32[]{:S(2)}, u32[]{:S(2)}) collective-permute-start(bf16[2,64,256]{2,1,0:T(8,128)(2,1)S(1)} %get-tuple-element.51), channel_id=1, source_target_pairs={{0,14},{2,12},{4,10},{6,8},{8,6},{10,4},{12,2},{14,0},{1,15},{3,13... | collective-permute-start | bytes 196616 | tf_op jit(solution)/shard_map/ppermute | solution.py:317
  30.8 1.3 %collective-permute-start.10 = (bf16[2,64,256]{2,1,0:T(8,128)(2,1)S(1)}, bf16[2,64,256]{2,1,0:T(8,128)(2,1)S(1)}, u32[]{:S(2)}, u32[]{:S(2)}) collective-permute-start(bf16[2,64,256]{2,1,0:T(8,128)(2,1)S(1)} %get-tuple-element.52), channel_id=1, source_target_pairs={{0,4},{2,6},{4,0},{6,2},{8,12},{10,14},{12,8},{14,10},{1,5},{3,7},... | collective-permute-start | bytes 196616 | tf_op jit(solution)/shard_map/ppermute | solution.py:317
  32.2 1.7 %collective-permute-start.11 = (bf16[2,64,256]{2,1,0:T(8,128)(2,1)S(1)}, bf16[2,64,256]{2,1,0:T(8,128)(2,1)S(1)}, u32[]{:S(2)}, u32[]{:S(2)}) collective-permute-start(bf16[2,64,256]{2,1,0:T(8,128)(2,1)S(1)} %get-tuple-element.53), channel_id=1, source_target_pairs={{0,10},{2,8},{4,14},{6,12},{8,2},{10,0},{12,6},{14,4},{1,11},{3,9}... | collective-permute-start | bytes 196616 | tf_op jit(solution)/shard_map/ppermute | solution.py:317
  33.9 1.9 %collective-permute-start.12 = (bf16[2,64,256]{2,1,0:T(8,128)(2,1)S(1)}, bf16[2,64,256]{2,1,0:T(8,128)(2,1)S(1)}, u32[]{:S(2)}, u32[]{:S(2)}) collective-permute-start(bf16[2,64,256]{2,1,0:T(8,128)(2,1)S(1)} %get-tuple-element.54), channel_id=1, source_target_pairs={{0,8},{2,10},{4,12},{6,14},{8,0},{10,2},{12,4},{14,6},{1,9},{3,11}... | collective-permute-start | bytes 196616 | tf_op jit(solution)/shard_map/ppermute | solution.py:317
  35.8 0.8 %collective-permute-start.13 = (bf16[2,64,256]{2,1,0:T(8,128)(2,1)S(1)}, bf16[2,64,256]{2,1,0:T(8,128)(2,1)S(1)}, u32[]{:S(2)}, u32[]{:S(2)}) collective-permute-start(bf16[2,64,256]{2,1,0:T(8,128)(2,1)S(1)} %get-tuple-element.55), channel_id=1, source_target_pairs={{0,2},{2,0},{4,6},{6,4},{8,10},{10,8},{12,14},{14,12},{1,3},{3,1},... | collective-permute-start | bytes 196616 | tf_op jit(solution)/shard_map/ppermute | solution.py:317
  36.6 0.9 %early_terms.2.terms_ref = f32[4,64,256]{2,1,0:T(8,128)S(1)} custom-call(s32[16]{0:T(128)S(1)} %reshape.14.served_ref, s32[1]{0:T(128)} %bitcast.me_ref, bf16[4,256,256]{2,1,0:T(8,128)(2,1)S(1)} %copy-done.4, f32[64,1024]{1,0:T(8,128)S(1)} %copy-done.3, f32[2,64,256]{2,1,0:T(8,128)S(1)} %get-tuple-element.48.refs_0_.after_ref, ...), custom_call_target="tpu_custom_call" | custom-call | flops 33554432 | bytes 524288 | tf_op jit(solution)/shard_map/early_terms/pallas_call | solution.py:409
  37.5 3.3 %collective-permute-done.11.refs_0_ = bf16[2,64,256]{2,1,0:T(8,128)(2,1)S(1)} collective-permute-done((bf16[2,64,256]{2,1,0:T(8,128)(2,1)S(1)}, bf16[2,64,256]{2,1,0:T(8,128)(2,1)S(1)}, u32[]{:S(2)}, u32[]{:S(2)}) %collective-permute-start.11) | collective-permute-done | bytes 65568 | tf_op jit(solution)/shard_map/ppermute | solution.py:317
  40.8 0.3 collective-permute-done.12.refs_1_
  41.1 0.9 %update.2 = (f32[64,1024]{1,0:T(8,128)S(1)}, f32[64,1024]{1,0:T(8,128)S(1)}, f32[64,1024]{1,0:T(8,128)S(1)}, bf16[2,64,256]{2,1,0:T(8,128)(2,1)S(1)}, bf16[2,64,...) custom-call(s32[16]{0:T(128)S(1)} %reshape.14.served_ref, ...), custom_call_target="tpu_custom_call" | custom-call | tf_op jit(solution)/shard_map/update/pallas_call | solution.py:418
  42.0 2.1 %collective-permute-start.14 = (bf16[2,64,256]{2,1,0:T(8,128)(2,1)S(1)}, bf16[2,64,256]{2,1,0:T(8,128)(2,1)S(1)}, u32[]{:S(2)}, u32[]{:S(2)}) collective-permute-start(bf16[2,64,256]{2,1,0:T(8,128)(2,1)S(1)} %get-tuple-element.58), channel_id=1, source_target_pairs={{0,12},{2,14},{4,8},{6,10},{8,4},{10,6},{12,0},{14,2},{1,13},{3,15... | collective-permute-start | bytes 196616 | tf_op jit(solution)/shard_map/ppermute | solution.py:317
  44.1 2.2 %collective-permute-start.16 = (bf16[2,64,256]{2,1,0:T(8,128)(2,1)S(1)}, bf16[2,64,256]{2,1,0:T(8,128)(2,1)S(1)}, u32[]{:S(2)}, u32[]{:S(2)}) collective-permute-start(bf16[2,64,256]{2,1,0:T(8,128)(2,1)S(1)} %get-tuple-element.60), channel_id=1, source_target_pairs={{0,14},{2,12},{4,10},{6,8},{8,6},{10,4},{12,2},{14,0},{1,15},{3,13... | collective-permute-start | bytes 196616 | tf_op jit(solution)/shard_map/ppermute | solution.py:317
  46.3 1.6 %collective-permute-start.17 = (bf16[2,64,256]{2,1,0:T(8,128)(2,1)S(1)}, bf16[2,64,256]{2,1,0:T(8,128)(2,1)S(1)}, u32[]{:S(2)}, u32[]{:S(2)}) collective-permute-start(bf16[2,64,256]{2,1,0:T(8,128)(2,1)S(1)} %get-tuple-element.61), channel_id=1, source_target_pairs={{0,4},{2,6},{4,0},{6,2},{8,12},{10,14},{12,8},{14,10},{1,5},{3,7},... | collective-permute-start | bytes 196616 | tf_op jit(solution)/shard_map/ppermute | solution.py:317
  47.9 1.0 %collective-permute-start.20 = (bf16[2,64,256]{2,1,0:T(8,128)(2,1)S(1)}, bf16[2,64,256]{2,1,0:T(8,128)(2,1)S(1)}, u32[]{:S(2)}, u32[]{:S(2)}) collective-permute-start(bf16[2,64,256]{2,1,0:T(8,128)(2,1)S(1)} %get-tuple-element.64), channel_id=1, source_target_pairs={{0,2},{2,0},{4,6},{6,4},{8,10},{10,8},{12,14},{14,12},{1,3},{3,1},... | collective-permute-start | bytes 196616 | tf_op jit(solution)/shard_map/ppermute | solution.py:317
  48.9 1.6 %collective-permute-start.18 = (bf16[2,64,256]{2,1,0:T(8,128)(2,1)S(1)}, bf16[2,64,256]{2,1,0:T(8,128)(2,1)S(1)}, u32[]{:S(2)}, u32[]{:S(2)}) collective-permute-start(bf16[2,64,256]{2,1,0:T(8,128)(2,1)S(1)} %get-tuple-element.62), channel_id=1, source_target_pairs={{0,10},{2,8},{4,14},{6,12},{8,2},{10,0},{12,6},{14,4},{1,11},{3,9}... | collective-permute-start | bytes 196616 | tf_op jit(solution)/shard_map/ppermute | solution.py:317
  50.6 1.8 %collective-permute-start.19 = (bf16[2,64,256]{2,1,0:T(8,128)(2,1)S(1)}, bf16[2,64,256]{2,1,0:T(8,128)(2,1)S(1)}, u32[]{:S(2)}, u32[]{:S(2)}) collective-permute-start(bf16[2,64,256]{2,1,0:T(8,128)(2,1)S(1)} %get-tuple-element.63), channel_id=1, source_target_pairs={{0,8},{2,10},{4,12},{6,14},{8,0},{10,2},{12,4},{14,6},{1,9},{3,11}... | collective-permute-start | bytes 196616 | tf_op jit(solution)/shard_map/ppermute | solution.py:317
  52.3 0.4 plan_products.1.plan_ref
  52.8 3.8 %early_products.1.early_ref = f32[17,64,256]{2,1,0:T(8,128)S(1)} custom-call(s32[8,128]{1,0:T(8,128)S(1)} %plan_products.1.plan_ref, bf16[64,256,256]{2,1,0:T(8,128)(2,1)S(1)} %bitcast.3, bf16[2,64,256]{2,1,0:T(8,128)(2,1)S(1)} %get-tuple-element.57.refs_0_, bf16[2,64,256]{2,1,0:T(8,128)(2,1)S(1)} %collective-permute-done.14.refs_1_, ...), custom_call_target="tpu_custom_call" | custom-call | flops 536870912 | bytes 8388608 | tf_op jit(solution)/shard_map/early_products/pallas_call | solution.py:373
  56.6 0.5 collective-permute-done.19.refs_6_.refs_1_
  57.1 2.5 %late_products.1 = (bf16[2,64,256]{2,1,0:T(8,128)(2,1)S(1)}, bf16[2,64,256]{2,1,0:T(8,128)(2,1)S(1)}, bf16[2,64,256]{2,1,0:T(8,128)(2,1)S(1)}, bf16[2,64,256]{2,...) custom-call(s32[8,128]{1,0:T(8,128)S(1)} %plan_products.1.plan_ref, ...), custom_call_target="tpu_custom_call" | custom-call | flops 536870912 | bytes 8388608 | tf_op jit(solution)/shard_map/late_products/pallas_call | solution.py:383
  59.5 1.5 %collective-permute-start.21 = (bf16[2,64,256]{2,1,0:T(8,128)(2,1)S(1)}, bf16[2,64,256]{2,1,0:T(8,128)(2,1)S(1)}, u32[]{:S(2)}, u32[]{:S(2)}) collective-permute-start(bf16[2,64,256]{2,1,0:T(8,128)(2,1)S(1)} %get-tuple-element.65), channel_id=1, source_target_pairs={{0,12},{2,14},{4,8},{6,10},{8,4},{10,6},{12,0},{14,2},{1,13},{3,15... | collective-permute-start | bytes 196616 | tf_op jit(solution)/shard_map/ppermute | solution.py:317
  61.0 0.7 collective-permute-start.22
  61.7 4.9 %collective-permute-start.23 = (bf16[2,64,256]{2,1,0:T(8,128)(2,1)S(1)}, bf16[2,64,256]{2,1,0:T(8,128)(2,1)S(1)}, u32[]{:S(2)}, u32[]{:S(2)}) collective-permute-start(bf16[2,64,256]{2,1,0:T(8,128)(2,1)S(1)} %get-tuple-element.67), channel_id=1, source_target_pairs={{0,14},{2,12},{4,10},{6,8},{8,6},{10,4},{12,2},{14,0},{1,15},{3,13... | collective-permute-start | bytes 196616 | tf_op jit(solution)/shard_map/ppermute | solution.py:317
  66.5 0.7 collective-permute-start.25
  67.3 4.2 %collective-permute-start.26 = (bf16[2,64,256]{2,1,0:T(8,128)(2,1)S(1)}, bf16[2,64,256]{2,1,0:T(8,128)(2,1)S(1)}, u32[]{:S(2)}, u32[]{:S(2)}) collective-permute-start(bf16[2,64,256]{2,1,0:T(8,128)(2,1)S(1)} %get-tuple-element.70), channel_id=1, source_target_pairs={{0,8},{2,10},{4,12},{6,14},{8,0},{10,2},{12,4},{14,6},{1,9},{3,11}... | collective-permute-start | bytes 196616 | tf_op jit(solution)/shard_map/ppermute | solution.py:317
  71.5 1.7 %own_products.1.refs_0_ = f32[2,64,256]{2,1,0:T(8,128)S(1)} custom-call(s32[8,128]{1,0:T(8,128)S(1)} %plan_products.1.plan_ref, bf16[64,256,256]{2,1,0:T(8,128)(2,1)S(1)} %bitcast.3, bf16[2,64,256]{2,1,0:T(8,128)(2,1)S(1)} %get-tuple-element.57.refs_0_, bf16[2,64,256]{2,1,0:T(8,128)(2,1)S(1)} %collective-permute-done.14.refs_1_, ...), custom_call_target="tpu_custom_call" | custom-call | flops 268435456 | bytes 4194304 | tf_op jit(solution)/shard_map/own_products/pallas_call | solution.py:394
  73.3 0.9 %early_terms.3.terms_ref = f32[4,64,256]{2,1,0:T(8,128)S(1)} custom-call(s32[16]{0:T(128)S(1)} %reshape.14.served_ref, s32[1]{0:T(128)} %bitcast.me_ref, bf16[4,256,256]{2,1,0:T(8,128)(2,1)S(1)} %copy-done.4, f32[64,1024]{1,0:T(8,128)S(1)} %get-tuple-element.56.primal_ref.refs_3_, f32[2,64,256]{2,1,0:T(8,128)S(1)} %own_products.1.refs_0_, ...), custom_call_target="tpu_custom_call" | custom-call | flops 33554432 | bytes 524288 | tf_op jit(solution)/shard_map/early_terms/pallas_call | solution.py:409
  74.2 1.1 %collective-permute-done.26.refs_1_ = bf16[2,64,256]{2,1,0:T(8,128)(2,1)S(1)} collective-permute-done((bf16[2,64,256]{2,1,0:T(8,128)(2,1)S(1)}, bf16[2,64,256]{2,1,0:T(8,128)(2,1)S(1)}, u32[]{:S(2)}, u32[]{:S(2)}) %collective-permute-start.26) | collective-permute-done | bytes 65568 | tf_op jit(solution)/shard_map/ppermute | solution.py:317
  75.3 0.5 collective-permute-done.27.refs_2_
  75.8 1.7 %update.3 = (f32[64,1024]{1,0:T(8,128)}, f32[64,1024]{1,0:T(8,128)}) custom-call(s32[16]{0:T(128)S(1)} %reshape.14.served_ref, s32[1]{0:T(128)} %bitcast.me_ref, s32[4]{0:T(128)S(1)} %copy-done.8, f32[8]{0:T(128)S(1)} %copy-done.9, f32[2,64]{1,0:T(2,128)S(1)} %copy-done.7, f32[64,1024]{1,0:T(8,128)S(1)} %copy-done.3, s32[64,1024]{1,0:T(8,128)S(1)} %copy-done.5, ...), custom_call_target="tpu_custom_call" | custom-call | tf_op jit(solution)/shard_map/update/pallas_call | solution.py:418
  (49 shorter events, 0.2 us)
Async XLA Ops:
  0.6 0.7 copy-start
  1.7 1.0 %copy-start.2 = (f32[64,1024]{1,0:T(8,128)S(1)}, f32[64,1024]{1,0:T(8,128)}, u32[]{:S(2)}) copy-start(f32[64,1024]{1,0:T(8,128)} %holdings_ref.5) | copy-start | bytes 786436
  2.7 13.7 %copy-start.10 = (s32[1,64,2]{1,2,0:T(2,128)S(1)}, s32[1,64,2]{1,2,0:T(2,128)}, u32[]{:S(2)}) copy-start(s32[1,64,2]{1,2,0:T(2,128)} %param.15) | copy-start | bytes 1540
  3.3 10.9 %collective-permute-start = (bf16[2,64,256]{2,1,0:T(8,128)(2,1)S(1)}, bf16[2,64,256]{2,1,0:T(8,128)(2,1)S(1)}, u32[]{:S(2)}, u32[]{:S(2)}) collective-permute-start(bf16[2,64,256]{2,1,0:T(8,128)(2,1)S(1)} %get-tuple-element.41), channel_id=1, source_target_pairs={{0,12},{2,14},{4,8},{6,10},{8,4},{10,6},{12,0},{14,2},{1,13},{3,15... | collective-permute-start | bytes 196616 | tf_op jit(solution)/shard_map/ppermute | solution.py:317
  8.4 6.4 %collective-permute-start.1 = (bf16[2,64,256]{2,1,0:T(8,128)(2,1)S(1)}, bf16[2,64,256]{2,1,0:T(8,128)(2,1)S(1)}, u32[]{:S(2)}, u32[]{:S(2)}) collective-permute-start(bf16[2,64,256]{2,1,0:T(8,128)(2,1)S(1)} %get-tuple-element.42), channel_id=1, source_target_pairs={{0,6},{2,4},{4,2},{6,0},{8,14},{10,12},{12,10},{14,8},{1,7},{3,5},... | collective-permute-start | bytes 196616 | tf_op jit(solution)/shard_map/ppermute | solution.py:317
  8.9 11.8 %collective-permute-start.2 = (bf16[2,64,256]{2,1,0:T(8,128)(2,1)S(1)}, bf16[2,64,256]{2,1,0:T(8,128)(2,1)S(1)}, u32[]{:S(2)}, u32[]{:S(2)}) collective-permute-start(bf16[2,64,256]{2,1,0:T(8,128)(2,1)S(1)} %get-tuple-element.43), channel_id=1, source_target_pairs={{0,14},{2,12},{4,10},{6,8},{8,6},{10,4},{12,2},{14,0},{1,15},{3,13... | collective-permute-start | bytes 196616 | tf_op jit(solution)/shard_map/ppermute | solution.py:317
  10.2 10.5 %collective-permute-start.3 = (bf16[2,64,256]{2,1,0:T(8,128)(2,1)S(1)}, bf16[2,64,256]{2,1,0:T(8,128)(2,1)S(1)}, u32[]{:S(2)}, u32[]{:S(2)}) collective-permute-start(bf16[2,64,256]{2,1,0:T(8,128)(2,1)S(1)} %get-tuple-element.44), channel_id=1, source_target_pairs={{0,4},{2,6},{4,0},{6,2},{8,12},{10,14},{12,8},{14,10},{1,5},{3,7},... | collective-permute-start | bytes 196616 | tf_op jit(solution)/shard_map/ppermute | solution.py:317
  11.4 9.8 %collective-permute-start.4 = (bf16[2,64,256]{2,1,0:T(8,128)(2,1)S(1)}, bf16[2,64,256]{2,1,0:T(8,128)(2,1)S(1)}, u32[]{:S(2)}, u32[]{:S(2)}) collective-permute-start(bf16[2,64,256]{2,1,0:T(8,128)(2,1)S(1)} %get-tuple-element.45), channel_id=1, source_target_pairs={{0,10},{2,8},{4,14},{6,12},{8,2},{10,0},{12,6},{14,4},{1,11},{3,9}... | collective-permute-start | bytes 196616 | tf_op jit(solution)/shard_map/ppermute | solution.py:317
  14.2 7.0 %collective-permute-start.5 = (bf16[2,64,256]{2,1,0:T(8,128)(2,1)S(1)}, bf16[2,64,256]{2,1,0:T(8,128)(2,1)S(1)}, u32[]{:S(2)}, u32[]{:S(2)}) collective-permute-start(bf16[2,64,256]{2,1,0:T(8,128)(2,1)S(1)} %get-tuple-element.46), channel_id=1, source_target_pairs={{0,8},{2,10},{4,12},{6,14},{8,0},{10,2},{12,4},{14,6},{1,9},{3,11}... | collective-permute-start | bytes 196616 | tf_op jit(solution)/shard_map/ppermute | solution.py:317
  14.8 6.4 %collective-permute-start.6 = (bf16[2,64,256]{2,1,0:T(8,128)(2,1)S(1)}, bf16[2,64,256]{2,1,0:T(8,128)(2,1)S(1)}, u32[]{:S(2)}, u32[]{:S(2)}) collective-permute-start(bf16[2,64,256]{2,1,0:T(8,128)(2,1)S(1)} %get-tuple-element.47), channel_id=1, source_target_pairs={{0,2},{2,0},{4,6},{6,4},{8,10},{10,8},{12,14},{14,12},{1,3},{3,1},... | collective-permute-start | bytes 196616 | tf_op jit(solution)/shard_map/ppermute | solution.py:317
  16.5 3.4 %copy-start.1 = (bf16[64,256,256]{2,1,0:T(8,128)(2,1)S(1)}, bf16[64,256,256]{2,1,0:T(8,128)(2,1)}, u32[]{:S(2)}) copy-start(bf16[64,256,256]{2,1,0:T(8,128)(2,1)} %cov_ref.7) | copy-start | bytes 25165828
  19.9 16.7 %copy-start.3 = (f32[64,1024]{1,0:T(8,128)S(1)}, f32[64,1024]{1,0:T(8,128)}, u32[]{:S(2)}) copy-start(f32[64,1024]{1,0:T(8,128)} %holdings_ref.5) | copy-start | bytes 786436
  19.9 16.7 %copy-start.4 = (bf16[4,256,256]{2,1,0:T(8,128)(2,1)S(1)}, bf16[4,256,256]{2,1,0:T(8,128)(2,1)}, u32[]{:S(2)}) copy-start(bf16[4,256,256]{2,1,0:T(8,128)(2,1)} %diag_ref.3) | copy-start | bytes 1572868
  19.9 21.2 %copy-start.5 = (s32[64,1024]{1,0:T(8,128)S(1)}, s32[64,1024]{1,0:T(8,128)}, u32[]{:S(2)}) copy-start(s32[64,1024]{1,0:T(8,128)} %eligible_ref.3) | copy-start | bytes 786436
  19.9 21.2 %copy-start.6 = (f32[1024]{0:T(1024)S(1)}, f32[1024]{0:T(1024)}, u32[]{:S(2)}) copy-start(f32[1024]{0:T(1024)} %param.12) | copy-start | bytes 12292
  19.9 21.2 %copy-start.7 = (f32[2,64]{1,0:T(2,128)S(1)}, f32[2,64]{1,0:T(2,128)}, u32[]{:S(2)}) copy-start(f32[2,64]{1,0:T(2,128)} %slopes_ref.3) | copy-start | bytes 1540
  19.9 21.2 %copy-start.8 = (s32[4]{0:T(128)S(1)}, s32[4]{0:T(128)}, u32[]{:S(2)}) copy-start(s32[4]{0:T(128)} %knee_index_ref.3) | copy-start | bytes 52
  19.9 21.2 %copy-start.9 = (f32[8]{0:T(128)S(1)}, f32[8]{0:T(128)}, u32[]{:S(2)}) copy-start(f32[8]{0:T(128)} %knee_levels_ref.3) | copy-start | bytes 100
  19.9 32.9 %slice-start = ((s8[8388608]{0:T(1024)(128)(4,1)}), s8[4194304]{0:T(1024)(128)(4,1)S(1)}, s32[]{:S(2)}) async-start(s8[8388608]{0:T(1024)(128)(4,1)} %bitcast.2), calls=%async_computation | async-start | bytes 8388608
  21.2 31.6 %slice-start.1 = ((s8[8388608]{0:T(1024)(128)(4,1)}), s8[4194304]{0:T(1024)(128)(4,1)S(1)}, s32[]{:S(2)}) async-start(s8[8388608]{0:T(1024)(128)(4,1)} %bitcast.2), calls=%async_computation.1 | async-start | bytes 8388608
  26.2 7.6 %collective-permute-start.7 = (bf16[2,64,256]{2,1,0:T(8,128)(2,1)S(1)}, bf16[2,64,256]{2,1,0:T(8,128)(2,1)S(1)}, u32[]{:S(2)}, u32[]{:S(2)}) collective-permute-start(bf16[2,64,256]{2,1,0:T(8,128)(2,1)S(1)} %get-tuple-element.49), channel_id=1, source_target_pairs={{0,12},{2,14},{4,8},{6,10},{8,4},{10,6},{12,0},{14,2},{1,13},{3,15... | collective-permute-start | bytes 196616 | tf_op jit(solution)/shard_map/ppermute | solution.py:317
  28.2 7.5 %collective-permute-start.8 = (bf16[2,64,256]{2,1,0:T(8,128)(2,1)S(1)}, bf16[2,64,256]{2,1,0:T(8,128)(2,1)S(1)}, u32[]{:S(2)}, u32[]{:S(2)}) collective-permute-start(bf16[2,64,256]{2,1,0:T(8,128)(2,1)S(1)} %get-tuple-element.50), channel_id=1, source_target_pairs={{0,6},{2,4},{4,2},{6,0},{8,14},{10,12},{12,10},{14,8},{1,7},{3,5},... | collective-permute-start | bytes 196616 | tf_op jit(solution)/shard_map/ppermute | solution.py:317
  28.6 8.0 %collective-permute-start.9 = (bf16[2,64,256]{2,1,0:T(8,128)(2,1)S(1)}, bf16[2,64,256]{2,1,0:T(8,128)(2,1)S(1)}, u32[]{:S(2)}, u32[]{:S(2)}) collective-permute-start(bf16[2,64,256]{2,1,0:T(8,128)(2,1)S(1)} %get-tuple-element.51), channel_id=1, source_target_pairs={{0,14},{2,12},{4,10},{6,8},{8,6},{10,4},{12,2},{14,0},{1,15},{3,13... | collective-permute-start | bytes 196616 | tf_op jit(solution)/shard_map/ppermute | solution.py:317
  30.8 5.7 %collective-permute-start.10 = (bf16[2,64,256]{2,1,0:T(8,128)(2,1)S(1)}, bf16[2,64,256]{2,1,0:T(8,128)(2,1)S(1)}, u32[]{:S(2)}, u32[]{:S(2)}) collective-permute-start(bf16[2,64,256]{2,1,0:T(8,128)(2,1)S(1)} %get-tuple-element.52), channel_id=1, source_target_pairs={{0,4},{2,6},{4,0},{6,2},{8,12},{10,14},{12,8},{14,10},{1,5},{3,7},... | collective-permute-start | bytes 196616 | tf_op jit(solution)/shard_map/ppermute | solution.py:317
  32.2 8.6 %collective-permute-start.11 = (bf16[2,64,256]{2,1,0:T(8,128)(2,1)S(1)}, bf16[2,64,256]{2,1,0:T(8,128)(2,1)S(1)}, u32[]{:S(2)}, u32[]{:S(2)}) collective-permute-start(bf16[2,64,256]{2,1,0:T(8,128)(2,1)S(1)} %get-tuple-element.53), channel_id=1, source_target_pairs={{0,10},{2,8},{4,14},{6,12},{8,2},{10,0},{12,6},{14,4},{1,11},{3,9}... | collective-permute-start | bytes 196616 | tf_op jit(solution)/shard_map/ppermute | solution.py:317
  33.9 7.1 %collective-permute-start.12 = (bf16[2,64,256]{2,1,0:T(8,128)(2,1)S(1)}, bf16[2,64,256]{2,1,0:T(8,128)(2,1)S(1)}, u32[]{:S(2)}, u32[]{:S(2)}) collective-permute-start(bf16[2,64,256]{2,1,0:T(8,128)(2,1)S(1)} %get-tuple-element.54), channel_id=1, source_target_pairs={{0,8},{2,10},{4,12},{6,14},{8,0},{10,2},{12,4},{14,6},{1,9},{3,11}... | collective-permute-start | bytes 196616 | tf_op jit(solution)/shard_map/ppermute | solution.py:317
  35.8 5.3 %collective-permute-start.13 = (bf16[2,64,256]{2,1,0:T(8,128)(2,1)S(1)}, bf16[2,64,256]{2,1,0:T(8,128)(2,1)S(1)}, u32[]{:S(2)}, u32[]{:S(2)}) collective-permute-start(bf16[2,64,256]{2,1,0:T(8,128)(2,1)S(1)} %get-tuple-element.55), channel_id=1, source_target_pairs={{0,2},{2,0},{4,6},{6,4},{8,10},{10,8},{12,14},{14,12},{1,3},{3,1},... | collective-permute-start | bytes 196616 | tf_op jit(solution)/shard_map/ppermute | solution.py:317
  42.0 6.9 %collective-permute-start.14 = (bf16[2,64,256]{2,1,0:T(8,128)(2,1)S(1)}, bf16[2,64,256]{2,1,0:T(8,128)(2,1)S(1)}, u32[]{:S(2)}, u32[]{:S(2)}) collective-permute-start(bf16[2,64,256]{2,1,0:T(8,128)(2,1)S(1)} %get-tuple-element.58), channel_id=1, source_target_pairs={{0,12},{2,14},{4,8},{6,10},{8,4},{10,6},{12,0},{14,2},{1,13},{3,15... | collective-permute-start | bytes 196616 | tf_op jit(solution)/shard_map/ppermute | solution.py:317
  44.1 6.5 %collective-permute-start.15 = (bf16[2,64,256]{2,1,0:T(8,128)(2,1)S(1)}, bf16[2,64,256]{2,1,0:T(8,128)(2,1)S(1)}, u32[]{:S(2)}, u32[]{:S(2)}) collective-permute-start(bf16[2,64,256]{2,1,0:T(8,128)(2,1)S(1)} %get-tuple-element.59), channel_id=1, source_target_pairs={{0,6},{2,4},{4,2},{6,0},{8,14},{10,12},{12,10},{14,8},{1,7},{3,5},... | collective-permute-start | bytes 196616 | tf_op jit(solution)/shard_map/ppermute | solution.py:317
  44.1 8.6 %collective-permute-start.16 = (bf16[2,64,256]{2,1,0:T(8,128)(2,1)S(1)}, bf16[2,64,256]{2,1,0:T(8,128)(2,1)S(1)}, u32[]{:S(2)}, u32[]{:S(2)}) collective-permute-start(bf16[2,64,256]{2,1,0:T(8,128)(2,1)S(1)} %get-tuple-element.60), channel_id=1, source_target_pairs={{0,14},{2,12},{4,10},{6,8},{8,6},{10,4},{12,2},{14,0},{1,15},{3,13... | collective-permute-start | bytes 196616 | tf_op jit(solution)/shard_map/ppermute | solution.py:317
  46.3 6.4 %collective-permute-start.17 = (bf16[2,64,256]{2,1,0:T(8,128)(2,1)S(1)}, bf16[2,64,256]{2,1,0:T(8,128)(2,1)S(1)}, u32[]{:S(2)}, u32[]{:S(2)}) collective-permute-start(bf16[2,64,256]{2,1,0:T(8,128)(2,1)S(1)} %get-tuple-element.61), channel_id=1, source_target_pairs={{0,4},{2,6},{4,0},{6,2},{8,12},{10,14},{12,8},{14,10},{1,5},{3,7},... | collective-permute-start | bytes 196616 | tf_op jit(solution)/shard_map/ppermute | solution.py:317
  47.9 4.8 %collective-permute-start.20 = (bf16[2,64,256]{2,1,0:T(8,128)(2,1)S(1)}, bf16[2,64,256]{2,1,0:T(8,128)(2,1)S(1)}, u32[]{:S(2)}, u32[]{:S(2)}) collective-permute-start(bf16[2,64,256]{2,1,0:T(8,128)(2,1)S(1)} %get-tuple-element.64), channel_id=1, source_target_pairs={{0,2},{2,0},{4,6},{6,4},{8,10},{10,8},{12,14},{14,12},{1,3},{3,1},... | collective-permute-start | bytes 196616 | tf_op jit(solution)/shard_map/ppermute | solution.py:317
  48.9 7.6 %collective-permute-start.18 = (bf16[2,64,256]{2,1,0:T(8,128)(2,1)S(1)}, bf16[2,64,256]{2,1,0:T(8,128)(2,1)S(1)}, u32[]{:S(2)}, u32[]{:S(2)}) collective-permute-start(bf16[2,64,256]{2,1,0:T(8,128)(2,1)S(1)} %get-tuple-element.62), channel_id=1, source_target_pairs={{0,10},{2,8},{4,14},{6,12},{8,2},{10,0},{12,6},{14,4},{1,11},{3,9}... | collective-permute-start | bytes 196616 | tf_op jit(solution)/shard_map/ppermute | solution.py:317
  50.6 6.5 %collective-permute-start.19 = (bf16[2,64,256]{2,1,0:T(8,128)(2,1)S(1)}, bf16[2,64,256]{2,1,0:T(8,128)(2,1)S(1)}, u32[]{:S(2)}, u32[]{:S(2)}) collective-permute-start(bf16[2,64,256]{2,1,0:T(8,128)(2,1)S(1)} %get-tuple-element.63), channel_id=1, source_target_pairs={{0,8},{2,10},{4,12},{6,14},{8,0},{10,2},{12,4},{14,6},{1,9},{3,11}... | collective-permute-start | bytes 196616 | tf_op jit(solution)/shard_map/ppermute | solution.py:317
  59.5 7.7 %collective-permute-start.21 = (bf16[2,64,256]{2,1,0:T(8,128)(2,1)S(1)}, bf16[2,64,256]{2,1,0:T(8,128)(2,1)S(1)}, u32[]{:S(2)}, u32[]{:S(2)}) collective-permute-start(bf16[2,64,256]{2,1,0:T(8,128)(2,1)S(1)} %get-tuple-element.65), channel_id=1, source_target_pairs={{0,12},{2,14},{4,8},{6,10},{8,4},{10,6},{12,0},{14,2},{1,13},{3,15... | collective-permute-start | bytes 196616 | tf_op jit(solution)/shard_map/ppermute | solution.py:317
  61.0 10.5 %collective-permute-start.22 = (bf16[2,64,256]{2,1,0:T(8,128)(2,1)S(1)}, bf16[2,64,256]{2,1,0:T(8,128)(2,1)S(1)}, u32[]{:S(2)}, u32[]{:S(2)}) collective-permute-start(bf16[2,64,256]{2,1,0:T(8,128)(2,1)S(1)} %get-tuple-element.66), channel_id=1, source_target_pairs={{0,6},{2,4},{4,2},{6,0},{8,14},{10,12},{12,10},{14,8},{1,7},{3,5},... | collective-permute-start | bytes 196616 | tf_op jit(solution)/shard_map/ppermute | solution.py:317
  61.7 11.6 %collective-permute-start.23 = (bf16[2,64,256]{2,1,0:T(8,128)(2,1)S(1)}, bf16[2,64,256]{2,1,0:T(8,128)(2,1)S(1)}, u32[]{:S(2)}, u32[]{:S(2)}) collective-permute-start(bf16[2,64,256]{2,1,0:T(8,128)(2,1)S(1)} %get-tuple-element.67), channel_id=1, source_target_pairs={{0,14},{2,12},{4,10},{6,8},{8,6},{10,4},{12,2},{14,0},{1,15},{3,13... | collective-permute-start | bytes 196616 | tf_op jit(solution)/shard_map/ppermute | solution.py:317
  66.5 6.7 %collective-permute-start.24 = (bf16[2,64,256]{2,1,0:T(8,128)(2,1)S(1)}, bf16[2,64,256]{2,1,0:T(8,128)(2,1)S(1)}, u32[]{:S(2)}, u32[]{:S(2)}) collective-permute-start(bf16[2,64,256]{2,1,0:T(8,128)(2,1)S(1)} %get-tuple-element.68), channel_id=1, source_target_pairs={{0,4},{2,6},{4,0},{6,2},{8,12},{10,14},{12,8},{14,10},{1,5},{3,7},... | collective-permute-start | bytes 196616 | tf_op jit(solution)/shard_map/ppermute | solution.py:317
  66.5 7.6 %collective-permute-start.25 = (bf16[2,64,256]{2,1,0:T(8,128)(2,1)S(1)}, bf16[2,64,256]{2,1,0:T(8,128)(2,1)S(1)}, u32[]{:S(2)}, u32[]{:S(2)}) collective-permute-start(bf16[2,64,256]{2,1,0:T(8,128)(2,1)S(1)} %get-tuple-element.69), channel_id=1, source_target_pairs={{0,10},{2,8},{4,14},{6,12},{8,2},{10,0},{12,6},{14,4},{1,11},{3,9}... | collective-permute-start | bytes 196616 | tf_op jit(solution)/shard_map/ppermute | solution.py:317
  67.3 8.0 %collective-permute-start.26 = (bf16[2,64,256]{2,1,0:T(8,128)(2,1)S(1)}, bf16[2,64,256]{2,1,0:T(8,128)(2,1)S(1)}, u32[]{:S(2)}, u32[]{:S(2)}) collective-permute-start(bf16[2,64,256]{2,1,0:T(8,128)(2,1)S(1)} %get-tuple-element.70), channel_id=1, source_target_pairs={{0,8},{2,10},{4,12},{6,14},{8,0},{10,2},{12,4},{14,6},{1,9},{3,11}... | collective-permute-start | bytes 196616 | tf_op jit(solution)/shard_map/ppermute | solution.py:317
  71.5 4.3 %collective-permute-start.27 = (bf16[2,64,256]{2,1,0:T(8,128)(2,1)S(1)}, bf16[2,64,256]{2,1,0:T(8,128)(2,1)S(1)}, u32[]{:S(2)}, u32[]{:S(2)}) collective-permute-start(bf16[2,64,256]{2,1,0:T(8,128)(2,1)S(1)} %get-tuple-element.71), channel_id=1, source_target_pairs={{0,2},{2,0},{4,6},{6,4},{8,10},{10,8},{12,14},{14,12},{1,3},{3,1},... | collective-permute-start | bytes 196616 | tf_op jit(solution)/shard_map/ppermute | solution.py:317

commit v9 on v8

--- a/solution.py
+++ b/solution.py
@@ -8,7 +8,7 @@
 from jax.sharding import PartitionSpec as P
 
 ITERS = 2
-LANES = 8
+LANES = 16
 LANES_LEFT = 4
 OWN = True
 STEP_SIZE = 0.5
@@ -96,7 +96,7 @@
         total[second] += to_second
         return carry
 
-    lax.fori_loop(0, cov_ref.shape[0], one, 0, unroll=32)
+    lax.fori_loop(0, cov_ref.shape[0], one, 0, unroll=64)
     for rank, out_ref in enumerate(partial):
         out_ref[...] = total[pl.ds(rank * capacity, capacity)].astype(out_ref.dtype)
 

time: 76.8 us -> 75.2 us (0.979)
  starting transfers between devices: 45.4 us -> 43.7 us
  waiting for transfers between devices: 6.49 us -> 5.56 us
    ppermute x28, starting transfers between devices: 45.4 us -> 43.7 us  [exchange(): lax.ppermute(value, 'blk', [(index, index ^ offset) for index in range(ow...]
    pallas_call x1, Pallas kernels: 1.73 us -> 3.06 us  [body(): pl.pallas_call(functools.partial(own_kernel, owners), out_shape=kept, in_...]
    ppermute x28, waiting for transfers between devices: 6.49 us -> 5.56 us  [exchange(): lax.ppermute(value, 'blk', [(index, index ^ offset) for index in range(ow...]
  transfers between devices with their start and end apart: 28 -> 28, of which waited for: 7 -> 6; matrix products, arithmetic and copies ran while one was open for 0% -> 0% of each run, Pallas kernels for 11% -> 12%
where the time goes in v9:
time: 75.2 us; the launch traced here: 75.1 us
  starting transfers between devices  43.7 us (58%)
  Pallas kernels  19.3 us (26%)
  waiting for transfers between devices  5.56 us (7%)
  local copies, waits for them, and re-layouts  5.54 us (7%)
  between operations  0.93 us (1%)
    ppermute x28, starting transfers between devices, exchange(): lax.ppermute(value, 'blk', [(index, index ^ offset) for index in range(ow...  43.7 us
    ppermute x28, waiting for transfers between devices, exchange(): lax.ppermute(value, 'blk', [(index, index ^ offset) for index in range(ow...  5.56 us
    unnamed x27, local copies, waits for them, and re-layouts  5.18 us
    pallas_call x1, Pallas kernels, body(): pl.pallas_call(functools.partial(pairs_kernel, owners), out_shape=[kept]...  4.71 us
    pallas_call x1, Pallas kernels, body(): pl.pallas_call(functools.partial(early_kernel, early), out_shape=jax.Shap...  3.11 us
    pallas_call x1, Pallas kernels, body(): pl.pallas_call(functools.partial(own_kernel, owners), out_shape=kept, in_...  3.06 us
    pallas_call x2, Pallas kernels, body(): pl.pallas_call(functools.partial(update_kernel, last, [offsets[rank] for...  2.59 us
    pallas_call x1, Pallas kernels, body(): pl.pallas_call(functools.partial(late_kernel, late), out_shape=([] if OWN...  2.35 us
  transfers between devices with their start and end apart: 28, of which 6 were waited for; matrix products, arithmetic and copies ran while one was open for 0% of the time, Pallas kernels for 12%

profile of v9, /device:TPU:0, one launch (start us, length us, event | category | flops | bytes accessed | tf_op | source)
XLA Modules:
  0.0 75.1 jit_solution(11203003713491842616)
XLA Ops:
  0.6 0.7 copy-done
  1.3 0.3 dynamic-slice_reduce_fusion
  1.7 1.0 %copy-done.2 = f32[64,1024]{1,0:T(8,128)S(1)} copy-done((f32[64,1024]{1,0:T(8,128)S(1)}, f32[64,1024]{1,0:T(8,128)}, u32[]{:S(2)}) %copy-start.2) | copy-done | bytes 262168
  2.7 0.6 pack_holdings.1
  3.3 5.1 %collective-permute-start = (bf16[2,64,256]{2,1,0:T(8,128)(2,1)S(1)}, bf16[2,64,256]{2,1,0:T(8,128)(2,1)S(1)}, u32[]{:S(2)}, u32[]{:S(2)}) collective-permute-start(bf16[2,64,256]{2,1,0:T(8,128)(2,1)S(1)} %get-tuple-element.41), channel_id=1, source_target_pairs={{0,12},{2,14},{4,8},{6,10},{8,4},{10,6},{12,0},{14,2},{1,13},{3,15... | collective-permute-start | bytes 196616 | tf_op jit(solution)/shard_map/ppermute | solution.py:317
  8.4 0.5 collective-permute-start.1
  8.9 1.3 %collective-permute-start.2 = (bf16[2,64,256]{2,1,0:T(8,128)(2,1)S(1)}, bf16[2,64,256]{2,1,0:T(8,128)(2,1)S(1)}, u32[]{:S(2)}, u32[]{:S(2)}) collective-permute-start(bf16[2,64,256]{2,1,0:T(8,128)(2,1)S(1)} %get-tuple-element.43), channel_id=1, source_target_pairs={{0,14},{2,12},{4,10},{6,8},{8,6},{10,4},{12,2},{14,0},{1,15},{3,13... | collective-permute-start | bytes 196616 | tf_op jit(solution)/shard_map/ppermute | solution.py:317
  10.2 1.2 %collective-permute-start.3 = (bf16[2,64,256]{2,1,0:T(8,128)(2,1)S(1)}, bf16[2,64,256]{2,1,0:T(8,128)(2,1)S(1)}, u32[]{:S(2)}, u32[]{:S(2)}) collective-permute-start(bf16[2,64,256]{2,1,0:T(8,128)(2,1)S(1)} %get-tuple-element.44), channel_id=1, source_target_pairs={{0,4},{2,6},{4,0},{6,2},{8,12},{10,14},{12,8},{14,10},{1,5},{3,7},... | collective-permute-start | bytes 196616 | tf_op jit(solution)/shard_map/ppermute | solution.py:317
  11.4 2.8 %collective-permute-start.4 = (bf16[2,64,256]{2,1,0:T(8,128)(2,1)S(1)}, bf16[2,64,256]{2,1,0:T(8,128)(2,1)S(1)}, u32[]{:S(2)}, u32[]{:S(2)}) collective-permute-start(bf16[2,64,256]{2,1,0:T(8,128)(2,1)S(1)} %get-tuple-element.45), channel_id=1, source_target_pairs={{0,10},{2,8},{4,14},{6,12},{8,2},{10,0},{12,6},{14,4},{1,11},{3,9}... | collective-permute-start | bytes 196616 | tf_op jit(solution)/shard_map/ppermute | solution.py:317
  14.2 0.3 collective-permute-start.5
  14.5 0.3 collective-permute-done.1.refs_2_
  14.8 1.6 %collective-permute-start.6 = (bf16[2,64,256]{2,1,0:T(8,128)(2,1)S(1)}, bf16[2,64,256]{2,1,0:T(8,128)(2,1)S(1)}, u32[]{:S(2)}, u32[]{:S(2)}) collective-permute-start(bf16[2,64,256]{2,1,0:T(8,128)(2,1)S(1)} %get-tuple-element.47), channel_id=1, source_target_pairs={{0,2},{2,0},{4,6},{6,4},{8,10},{10,8},{12,14},{14,12},{1,3},{3,1},... | collective-permute-start | bytes 196616 | tf_op jit(solution)/shard_map/ppermute | solution.py:317
  16.4 0.1 copy.14.pairs_ref
  16.5 3.4 %copy-done.1 = bf16[64,256,256]{2,1,0:T(8,128)(2,1)S(1)} copy-done((bf16[64,256,256]{2,1,0:T(8,128)(2,1)S(1)}, bf16[64,256,256]{2,1,0:T(8,128)(2,1)}, u32[]{:S(2)}) %copy-start.1) | copy-done | bytes 8388632
  19.9 0.7 stage_pairs.1
  20.7 0.5 collective-permute-done.4.refs_5_
  21.2 4.7 %pair_products.1 = (f32[2,64,256]{2,1,0:T(8,128)S(1)}, bf16[2,64,256]{2,1,0:T(8,128)(2,1)S(1)}, bf16[2,64,256]{2,1,0:T(8,128)(2,1)S(1)}, bf16[2,64,256]{2,1,0:T(...) custom-call(s32[8,128]{1,0:T(8,128)S(1)} %get-tuple-element.38.place, ...), custom_call_target="tpu_custom_call" | custom-call | tf_op jit(solution)/shard_map/pair_products/pallas_call | solution.py:350
  25.9 2.0 %collective-permute-start.7 = (bf16[2,64,256]{2,1,0:T(8,128)(2,1)S(1)}, bf16[2,64,256]{2,1,0:T(8,128)(2,1)S(1)}, u32[]{:S(2)}, u32[]{:S(2)}) collective-permute-start(bf16[2,64,256]{2,1,0:T(8,128)(2,1)S(1)} %get-tuple-element.49), channel_id=1, source_target_pairs={{0,12},{2,14},{4,8},{6,10},{8,4},{10,6},{12,0},{14,2},{1,13},{3,15... | collective-permute-start | bytes 196616 | tf_op jit(solution)/shard_map/ppermute | solution.py:317
  27.9 0.3 collective-permute-start.8
  28.3 2.2 %collective-permute-start.9 = (bf16[2,64,256]{2,1,0:T(8,128)(2,1)S(1)}, bf16[2,64,256]{2,1,0:T(8,128)(2,1)S(1)}, u32[]{:S(2)}, u32[]{:S(2)}) collective-permute-start(bf16[2,64,256]{2,1,0:T(8,128)(2,1)S(1)} %get-tuple-element.51), channel_id=1, source_target_pairs={{0,14},{2,12},{4,10},{6,8},{8,6},{10,4},{12,2},{14,0},{1,15},{3,13... | collective-permute-start | bytes 196616 | tf_op jit(solution)/shard_map/ppermute | solution.py:317
  30.5 1.3 %collective-permute-start.10 = (bf16[2,64,256]{2,1,0:T(8,128)(2,1)S(1)}, bf16[2,64,256]{2,1,0:T(8,128)(2,1)S(1)}, u32[]{:S(2)}, u32[]{:S(2)}) collective-permute-start(bf16[2,64,256]{2,1,0:T(8,128)(2,1)S(1)} %get-tuple-element.52), channel_id=1, source_target_pairs={{0,4},{2,6},{4,0},{6,2},{8,12},{10,14},{12,8},{14,10},{1,5},{3,7},... | collective-permute-start | bytes 196616 | tf_op jit(solution)/shard_map/ppermute | solution.py:317
  31.8 1.7 %collective-permute-start.11 = (bf16[2,64,256]{2,1,0:T(8,128)(2,1)S(1)}, bf16[2,64,256]{2,1,0:T(8,128)(2,1)S(1)}, u32[]{:S(2)}, u32[]{:S(2)}) collective-permute-start(bf16[2,64,256]{2,1,0:T(8,128)(2,1)S(1)} %get-tuple-element.53), channel_id=1, source_target_pairs={{0,10},{2,8},{4,14},{6,12},{8,2},{10,0},{12,6},{14,4},{1,11},{3,9}... | collective-permute-start | bytes 196616 | tf_op jit(solution)/shard_map/ppermute | solution.py:317
  33.6 1.9 %collective-permute-start.12 = (bf16[2,64,256]{2,1,0:T(8,128)(2,1)S(1)}, bf16[2,64,256]{2,1,0:T(8,128)(2,1)S(1)}, u32[]{:S(2)}, u32[]{:S(2)}) collective-permute-start(bf16[2,64,256]{2,1,0:T(8,128)(2,1)S(1)} %get-tuple-element.54), channel_id=1, source_target_pairs={{0,8},{2,10},{4,12},{6,14},{8,0},{10,2},{12,4},{14,6},{1,9},{3,11}... | collective-permute-start | bytes 196616 | tf_op jit(solution)/shard_map/ppermute | solution.py:317
  35.4 0.8 %collective-permute-start.13 = (bf16[2,64,256]{2,1,0:T(8,128)(2,1)S(1)}, bf16[2,64,256]{2,1,0:T(8,128)(2,1)S(1)}, u32[]{:S(2)}, u32[]{:S(2)}) collective-permute-start(bf16[2,64,256]{2,1,0:T(8,128)(2,1)S(1)} %get-tuple-element.55), channel_id=1, source_target_pairs={{0,2},{2,0},{4,6},{6,4},{8,10},{10,8},{12,14},{14,12},{1,3},{3,1},... | collective-permute-start | bytes 196616 | tf_op jit(solution)/shard_map/ppermute | solution.py:317
  36.2 0.9 %early_terms.2.terms_ref = f32[4,64,256]{2,1,0:T(8,128)S(1)} custom-call(s32[16]{0:T(128)S(1)} %reshape.14.served_ref, s32[1]{0:T(128)} %bitcast.me_ref, bf16[4,256,256]{2,1,0:T(8,128)(2,1)S(1)} %copy-done.4, f32[64,1024]{1,0:T(8,128)S(1)} %copy-done.3, f32[2,64,256]{2,1,0:T(8,128)S(1)} %get-tuple-element.48.refs_0_.after_ref, ...), custom_call_target="tpu_custom_call" | custom-call | flops 33554432 | bytes 524288 | tf_op jit(solution)/shard_map/early_terms/pallas_call | solution.py:409
  37.1 3.3 %collective-permute-done.11.refs_0_ = bf16[2,64,256]{2,1,0:T(8,128)(2,1)S(1)} collective-permute-done((bf16[2,64,256]{2,1,0:T(8,128)(2,1)S(1)}, bf16[2,64,256]{2,1,0:T(8,128)(2,1)S(1)}, u32[]{:S(2)}, u32[]{:S(2)}) %collective-permute-start.11) | collective-permute-done | bytes 65568 | tf_op jit(solution)/shard_map/ppermute | solution.py:317
  40.4 0.3 collective-permute-done.12.refs_1_
  40.7 0.9 %update.2 = (f32[64,1024]{1,0:T(8,128)S(1)}, f32[64,1024]{1,0:T(8,128)S(1)}, f32[64,1024]{1,0:T(8,128)S(1)}, bf16[2,64,256]{2,1,0:T(8,128)(2,1)S(1)}, bf16[2,64,...) custom-call(s32[16]{0:T(128)S(1)} %reshape.14.served_ref, ...), custom_call_target="tpu_custom_call" | custom-call | tf_op jit(solution)/shard_map/update/pallas_call | solution.py:418
  41.7 2.1 %collective-permute-start.14 = (bf16[2,64,256]{2,1,0:T(8,128)(2,1)S(1)}, bf16[2,64,256]{2,1,0:T(8,128)(2,1)S(1)}, u32[]{:S(2)}, u32[]{:S(2)}) collective-permute-start(bf16[2,64,256]{2,1,0:T(8,128)(2,1)S(1)} %get-tuple-element.58), channel_id=1, source_target_pairs={{0,12},{2,14},{4,8},{6,10},{8,4},{10,6},{12,0},{14,2},{1,13},{3,15... | collective-permute-start | bytes 196616 | tf_op jit(solution)/shard_map/ppermute | solution.py:317
  43.8 2.2 %collective-permute-start.16 = (bf16[2,64,256]{2,1,0:T(8,128)(2,1)S(1)}, bf16[2,64,256]{2,1,0:T(8,128)(2,1)S(1)}, u32[]{:S(2)}, u32[]{:S(2)}) collective-permute-start(bf16[2,64,256]{2,1,0:T(8,128)(2,1)S(1)} %get-tuple-element.60), channel_id=1, source_target_pairs={{0,14},{2,12},{4,10},{6,8},{8,6},{10,4},{12,2},{14,0},{1,15},{3,13... | collective-permute-start | bytes 196616 | tf_op jit(solution)/shard_map/ppermute | solution.py:317
  46.0 1.6 %collective-permute-start.17 = (bf16[2,64,256]{2,1,0:T(8,128)(2,1)S(1)}, bf16[2,64,256]{2,1,0:T(8,128)(2,1)S(1)}, u32[]{:S(2)}, u32[]{:S(2)}) collective-permute-start(bf16[2,64,256]{2,1,0:T(8,128)(2,1)S(1)} %get-tuple-element.61), channel_id=1, source_target_pairs={{0,4},{2,6},{4,0},{6,2},{8,12},{10,14},{12,8},{14,10},{1,5},{3,7},... | collective-permute-start | bytes 196616 | tf_op jit(solution)/shard_map/ppermute | solution.py:317
  47.6 1.0 %collective-permute-start.20 = (bf16[2,64,256]{2,1,0:T(8,128)(2,1)S(1)}, bf16[2,64,256]{2,1,0:T(8,128)(2,1)S(1)}, u32[]{:S(2)}, u32[]{:S(2)}) collective-permute-start(bf16[2,64,256]{2,1,0:T(8,128)(2,1)S(1)} %get-tuple-element.64), channel_id=1, source_target_pairs={{0,2},{2,0},{4,6},{6,4},{8,10},{10,8},{12,14},{14,12},{1,3},{3,1},... | collective-permute-start | bytes 196616 | tf_op jit(solution)/shard_map/ppermute | solution.py:317
  48.6 1.6 %collective-permute-start.18 = (bf16[2,64,256]{2,1,0:T(8,128)(2,1)S(1)}, bf16[2,64,256]{2,1,0:T(8,128)(2,1)S(1)}, u32[]{:S(2)}, u32[]{:S(2)}) collective-permute-start(bf16[2,64,256]{2,1,0:T(8,128)(2,1)S(1)} %get-tuple-element.62), channel_id=1, source_target_pairs={{0,10},{2,8},{4,14},{6,12},{8,2},{10,0},{12,6},{14,4},{1,11},{3,9}... | collective-permute-start | bytes 196616 | tf_op jit(solution)/shard_map/ppermute | solution.py:317
  50.2 1.7 %collective-permute-start.19 = (bf16[2,64,256]{2,1,0:T(8,128)(2,1)S(1)}, bf16[2,64,256]{2,1,0:T(8,128)(2,1)S(1)}, u32[]{:S(2)}, u32[]{:S(2)}) collective-permute-start(bf16[2,64,256]{2,1,0:T(8,128)(2,1)S(1)} %get-tuple-element.63), channel_id=1, source_target_pairs={{0,8},{2,10},{4,12},{6,14},{8,0},{10,2},{12,4},{14,6},{1,9},{3,11}... | collective-permute-start | bytes 196616 | tf_op jit(solution)/shard_map/ppermute | solution.py:317
  52.0 0.4 plan_products.1.plan_ref
  52.5 3.1 %early_products.1.early_ref = f32[17,64,256]{2,1,0:T(8,128)S(1)} custom-call(s32[8,128]{1,0:T(8,128)S(1)} %plan_products.1.plan_ref, bf16[64,256,256]{2,1,0:T(8,128)(2,1)S(1)} %bitcast.3, bf16[2,64,256]{2,1,0:T(8,128)(2,1)S(1)} %get-tuple-element.57.refs_0_, bf16[2,64,256]{2,1,0:T(8,128)(2,1)S(1)} %collective-permute-done.14.refs_1_, ...), custom_call_target="tpu_custom_call" | custom-call | flops 536870912 | bytes 8388608 | tf_op jit(solution)/shard_map/early_products/pallas_call | solution.py:373
  55.6 0.2 collective-permute-done.18.refs_5_.refs_0_
  55.8 1.0 %collective-permute-done.19.refs_6_.refs_1_ = bf16[2,64,256]{2,1,0:T(8,128)(2,1)S(1)} collective-permute-done((bf16[2,64,256]{2,1,0:T(8,128)(2,1)S(1)}, bf16[2,64,256]{2,1,0:T(8,128)(2,1)S(1)}, u32[]{:S(2)}, u32[]{:S(2)}) %collective-permute-start.19) | collective-permute-done | bytes 65568 | tf_op jit(solution)/shard_map/ppermute | solution.py:317
  56.7 2.4 %late_products.1 = (bf16[2,64,256]{2,1,0:T(8,128)(2,1)S(1)}, bf16[2,64,256]{2,1,0:T(8,128)(2,1)S(1)}, bf16[2,64,256]{2,1,0:T(8,128)(2,1)S(1)}, bf16[2,64,256]{2,...) custom-call(s32[8,128]{1,0:T(8,128)S(1)} %plan_products.1.plan_ref, ...), custom_call_target="tpu_custom_call" | custom-call | flops 536870912 | bytes 8388608 | tf_op jit(solution)/shard_map/late_products/pallas_call | solution.py:383
  59.1 3.1 %collective-permute-start.21 = (bf16[2,64,256]{2,1,0:T(8,128)(2,1)S(1)}, bf16[2,64,256]{2,1,0:T(8,128)(2,1)S(1)}, u32[]{:S(2)}, u32[]{:S(2)}) collective-permute-start(bf16[2,64,256]{2,1,0:T(8,128)(2,1)S(1)} %get-tuple-element.65), channel_id=1, source_target_pairs={{0,12},{2,14},{4,8},{6,10},{8,4},{10,6},{12,0},{14,2},{1,13},{3,15... | collective-permute-start | bytes 196616 | tf_op jit(solution)/shard_map/ppermute | solution.py:317
  62.1 1.3 %collective-permute-start.23 = (bf16[2,64,256]{2,1,0:T(8,128)(2,1)S(1)}, bf16[2,64,256]{2,1,0:T(8,128)(2,1)S(1)}, u32[]{:S(2)}, u32[]{:S(2)}) collective-permute-start(bf16[2,64,256]{2,1,0:T(8,128)(2,1)S(1)} %get-tuple-element.67), channel_id=1, source_target_pairs={{0,14},{2,12},{4,10},{6,8},{8,6},{10,4},{12,2},{14,0},{1,15},{3,13... | collective-permute-start | bytes 196616 | tf_op jit(solution)/shard_map/ppermute | solution.py:317
  63.4 1.6 %collective-permute-start.24 = (bf16[2,64,256]{2,1,0:T(8,128)(2,1)S(1)}, bf16[2,64,256]{2,1,0:T(8,128)(2,1)S(1)}, u32[]{:S(2)}, u32[]{:S(2)}) collective-permute-start(bf16[2,64,256]{2,1,0:T(8,128)(2,1)S(1)} %get-tuple-element.68), channel_id=1, source_target_pairs={{0,4},{2,6},{4,0},{6,2},{8,12},{10,14},{12,8},{14,10},{1,5},{3,7},... | collective-permute-start | bytes 196616 | tf_op jit(solution)/shard_map/ppermute | solution.py:317
  65.0 2.4 %collective-permute-start.25 = (bf16[2,64,256]{2,1,0:T(8,128)(2,1)S(1)}, bf16[2,64,256]{2,1,0:T(8,128)(2,1)S(1)}, u32[]{:S(2)}, u32[]{:S(2)}) collective-permute-start(bf16[2,64,256]{2,1,0:T(8,128)(2,1)S(1)} %get-tuple-element.69), channel_id=1, source_target_pairs={{0,10},{2,8},{4,14},{6,12},{8,2},{10,0},{12,6},{14,4},{1,11},{3,9}... | collective-permute-start | bytes 196616 | tf_op jit(solution)/shard_map/ppermute | solution.py:317
  67.4 0.9 %collective-permute-start.26 = (bf16[2,64,256]{2,1,0:T(8,128)(2,1)S(1)}, bf16[2,64,256]{2,1,0:T(8,128)(2,1)S(1)}, u32[]{:S(2)}, u32[]{:S(2)}) collective-permute-start(bf16[2,64,256]{2,1,0:T(8,128)(2,1)S(1)} %get-tuple-element.70), channel_id=1, source_target_pairs={{0,8},{2,10},{4,12},{6,14},{8,0},{10,2},{12,4},{14,6},{1,9},{3,11}... | collective-permute-start | bytes 196616 | tf_op jit(solution)/shard_map/ppermute | solution.py:317
  68.4 1.0 %collective-permute-start.27 = (bf16[2,64,256]{2,1,0:T(8,128)(2,1)S(1)}, bf16[2,64,256]{2,1,0:T(8,128)(2,1)S(1)}, u32[]{:S(2)}, u32[]{:S(2)}) collective-permute-start(bf16[2,64,256]{2,1,0:T(8,128)(2,1)S(1)} %get-tuple-element.71), channel_id=1, source_target_pairs={{0,2},{2,0},{4,6},{6,4},{8,10},{10,8},{12,14},{14,12},{1,3},{3,1},... | collective-permute-start | bytes 196616 | tf_op jit(solution)/shard_map/ppermute | solution.py:317
  69.4 3.1 %own_products.1.refs_0_ = f32[2,64,256]{2,1,0:T(8,128)S(1)} custom-call(s32[8,128]{1,0:T(8,128)S(1)} %plan_products.1.plan_ref, bf16[64,256,256]{2,1,0:T(8,128)(2,1)S(1)} %bitcast.3, bf16[2,64,256]{2,1,0:T(8,128)(2,1)S(1)} %get-tuple-element.57.refs_0_, bf16[2,64,256]{2,1,0:T(8,128)(2,1)S(1)} %collective-permute-done.14.refs_1_, ...), custom_call_target="tpu_custom_call" | custom-call | flops 268435456 | bytes 4194304 | tf_op jit(solution)/shard_map/own_products/pallas_call | solution.py:394
  72.5 0.9 %early_terms.3.terms_ref = f32[4,64,256]{2,1,0:T(8,128)S(1)} custom-call(s32[16]{0:T(128)S(1)} %reshape.14.served_ref, s32[1]{0:T(128)} %bitcast.me_ref, bf16[4,256,256]{2,1,0:T(8,128)(2,1)S(1)} %copy-done.4, f32[64,1024]{1,0:T(8,128)S(1)} %get-tuple-element.56.primal_ref.refs_3_, f32[2,64,256]{2,1,0:T(8,128)S(1)} %own_products.1.refs_0_, ...), custom_call_target="tpu_custom_call" | custom-call | flops 33554432 | bytes 524288 | tf_op jit(solution)/shard_map/early_terms/pallas_call | solution.py:409
  73.4 1.7 %update.3 = (f32[64,1024]{1,0:T(8,128)}, f32[64,1024]{1,0:T(8,128)}) custom-call(s32[16]{0:T(128)S(1)} %reshape.14.served_ref, s32[1]{0:T(128)} %bitcast.me_ref, s32[4]{0:T(128)S(1)} %copy-done.8, f32[8]{0:T(128)S(1)} %copy-done.9, f32[2,64]{1,0:T(2,128)S(1)} %copy-done.7, f32[64,1024]{1,0:T(8,128)S(1)} %copy-done.3, s32[64,1024]{1,0:T(8,128)S(1)} %copy-done.5, ...), custom_call_target="tpu_custom_call" | custom-call | tf_op jit(solution)/shard_map/update/pallas_call | solution.py:418
  (49 shorter events, 0.2 us)
Async XLA Ops:
  0.6 0.7 copy-start
  1.7 1.0 %copy-start.2 = (f32[64,1024]{1,0:T(8,128)S(1)}, f32[64,1024]{1,0:T(8,128)}, u32[]{:S(2)}) copy-start(f32[64,1024]{1,0:T(8,128)} %holdings_ref.5) | copy-start | bytes 786436
  2.7 13.7 %copy-start.10 = (s32[1,64,2]{1,2,0:T(2,128)S(1)}, s32[1,64,2]{1,2,0:T(2,128)}, u32[]{:S(2)}) copy-start(s32[1,64,2]{1,2,0:T(2,128)} %param.15) | copy-start | bytes 1540
  3.3 10.9 %collective-permute-start = (bf16[2,64,256]{2,1,0:T(8,128)(2,1)S(1)}, bf16[2,64,256]{2,1,0:T(8,128)(2,1)S(1)}, u32[]{:S(2)}, u32[]{:S(2)}) collective-permute-start(bf16[2,64,256]{2,1,0:T(8,128)(2,1)S(1)} %get-tuple-element.41), channel_id=1, source_target_pairs={{0,12},{2,14},{4,8},{6,10},{8,4},{10,6},{12,0},{14,2},{1,13},{3,15... | collective-permute-start | bytes 196616 | tf_op jit(solution)/shard_map/ppermute | solution.py:317
  8.4 6.4 %collective-permute-start.1 = (bf16[2,64,256]{2,1,0:T(8,128)(2,1)S(1)}, bf16[2,64,256]{2,1,0:T(8,128)(2,1)S(1)}, u32[]{:S(2)}, u32[]{:S(2)}) collective-permute-start(bf16[2,64,256]{2,1,0:T(8,128)(2,1)S(1)} %get-tuple-element.42), channel_id=1, source_target_pairs={{0,6},{2,4},{4,2},{6,0},{8,14},{10,12},{12,10},{14,8},{1,7},{3,5},... | collective-permute-start | bytes 196616 | tf_op jit(solution)/shard_map/ppermute | solution.py:317
  8.9 11.8 %collective-permute-start.2 = (bf16[2,64,256]{2,1,0:T(8,128)(2,1)S(1)}, bf16[2,64,256]{2,1,0:T(8,128)(2,1)S(1)}, u32[]{:S(2)}, u32[]{:S(2)}) collective-permute-start(bf16[2,64,256]{2,1,0:T(8,128)(2,1)S(1)} %get-tuple-element.43), channel_id=1, source_target_pairs={{0,14},{2,12},{4,10},{6,8},{8,6},{10,4},{12,2},{14,0},{1,15},{3,13... | collective-permute-start | bytes 196616 | tf_op jit(solution)/shard_map/ppermute | solution.py:317
  10.2 10.5 %collective-permute-start.3 = (bf16[2,64,256]{2,1,0:T(8,128)(2,1)S(1)}, bf16[2,64,256]{2,1,0:T(8,128)(2,1)S(1)}, u32[]{:S(2)}, u32[]{:S(2)}) collective-permute-start(bf16[2,64,256]{2,1,0:T(8,128)(2,1)S(1)} %get-tuple-element.44), channel_id=1, source_target_pairs={{0,4},{2,6},{4,0},{6,2},{8,12},{10,14},{12,8},{14,10},{1,5},{3,7},... | collective-permute-start | bytes 196616 | tf_op jit(solution)/shard_map/ppermute | solution.py:317
  11.4 9.8 %collective-permute-start.4 = (bf16[2,64,256]{2,1,0:T(8,128)(2,1)S(1)}, bf16[2,64,256]{2,1,0:T(8,128)(2,1)S(1)}, u32[]{:S(2)}, u32[]{:S(2)}) collective-permute-start(bf16[2,64,256]{2,1,0:T(8,128)(2,1)S(1)} %get-tuple-element.45), channel_id=1, source_target_pairs={{0,10},{2,8},{4,14},{6,12},{8,2},{10,0},{12,6},{14,4},{1,11},{3,9}... | collective-permute-start | bytes 196616 | tf_op jit(solution)/shard_map/ppermute | solution.py:317
  14.2 7.0 %collective-permute-start.5 = (bf16[2,64,256]{2,1,0:T(8,128)(2,1)S(1)}, bf16[2,64,256]{2,1,0:T(8,128)(2,1)S(1)}, u32[]{:S(2)}, u32[]{:S(2)}) collective-permute-start(bf16[2,64,256]{2,1,0:T(8,128)(2,1)S(1)} %get-tuple-element.46), channel_id=1, source_target_pairs={{0,8},{2,10},{4,12},{6,14},{8,0},{10,2},{12,4},{14,6},{1,9},{3,11}... | collective-permute-start | bytes 196616 | tf_op jit(solution)/shard_map/ppermute | solution.py:317
  14.8 6.4 %collective-permute-start.6 = (bf16[2,64,256]{2,1,0:T(8,128)(2,1)S(1)}, bf16[2,64,256]{2,1,0:T(8,128)(2,1)S(1)}, u32[]{:S(2)}, u32[]{:S(2)}) collective-permute-start(bf16[2,64,256]{2,1,0:T(8,128)(2,1)S(1)} %get-tuple-element.47), channel_id=1, source_target_pairs={{0,2},{2,0},{4,6},{6,4},{8,10},{10,8},{12,14},{14,12},{1,3},{3,1},... | collective-permute-start | bytes 196616 | tf_op jit(solution)/shard_map/ppermute | solution.py:317
  16.5 3.4 %copy-start.1 = (bf16[64,256,256]{2,1,0:T(8,128)(2,1)S(1)}, bf16[64,256,256]{2,1,0:T(8,128)(2,1)}, u32[]{:S(2)}) copy-start(bf16[64,256,256]{2,1,0:T(8,128)(2,1)} %cov_ref.7) | copy-start | bytes 25165828
  19.9 16.4 %copy-start.3 = (f32[64,1024]{1,0:T(8,128)S(1)}, f32[64,1024]{1,0:T(8,128)}, u32[]{:S(2)}) copy-start(f32[64,1024]{1,0:T(8,128)} %holdings_ref.5) | copy-start | bytes 786436
  19.9 16.4 %copy-start.4 = (bf16[4,256,256]{2,1,0:T(8,128)(2,1)S(1)}, bf16[4,256,256]{2,1,0:T(8,128)(2,1)}, u32[]{:S(2)}) copy-start(bf16[4,256,256]{2,1,0:T(8,128)(2,1)} %diag_ref.3) | copy-start | bytes 1572868
  19.9 20.8 %copy-start.5 = (s32[64,1024]{1,0:T(8,128)S(1)}, s32[64,1024]{1,0:T(8,128)}, u32[]{:S(2)}) copy-start(s32[64,1024]{1,0:T(8,128)} %eligible_ref.3) | copy-start | bytes 786436
  19.9 20.8 %copy-start.6 = (f32[1024]{0:T(1024)S(1)}, f32[1024]{0:T(1024)}, u32[]{:S(2)}) copy-start(f32[1024]{0:T(1024)} %param.12) | copy-start | bytes 12292
  19.9 20.8 %copy-start.7 = (f32[2,64]{1,0:T(2,128)S(1)}, f32[2,64]{1,0:T(2,128)}, u32[]{:S(2)}) copy-start(f32[2,64]{1,0:T(2,128)} %slopes_ref.3) | copy-start | bytes 1540
  19.9 20.8 %copy-start.8 = (s32[4]{0:T(128)S(1)}, s32[4]{0:T(128)}, u32[]{:S(2)}) copy-start(s32[4]{0:T(128)} %knee_index_ref.3) | copy-start | bytes 52
  19.9 20.8 %copy-start.9 = (f32[8]{0:T(128)S(1)}, f32[8]{0:T(128)}, u32[]{:S(2)}) copy-start(f32[8]{0:T(128)} %knee_levels_ref.3) | copy-start | bytes 100
  19.9 32.5 %slice-start = ((s8[8388608]{0:T(1024)(128)(4,1)}), s8[4194304]{0:T(1024)(128)(4,1)S(1)}, s32[]{:S(2)}) async-start(s8[8388608]{0:T(1024)(128)(4,1)} %bitcast.2), calls=%async_computation | async-start | bytes 8388608
  21.2 31.3 %slice-start.1 = ((s8[8388608]{0:T(1024)(128)(4,1)}), s8[4194304]{0:T(1024)(128)(4,1)S(1)}, s32[]{:S(2)}) async-start(s8[8388608]{0:T(1024)(128)(4,1)} %bitcast.2), calls=%async_computation.1 | async-start | bytes 8388608
  25.9 7.6 %collective-permute-start.7 = (bf16[2,64,256]{2,1,0:T(8,128)(2,1)S(1)}, bf16[2,64,256]{2,1,0:T(8,128)(2,1)S(1)}, u32[]{:S(2)}, u32[]{:S(2)}) collective-permute-start(bf16[2,64,256]{2,1,0:T(8,128)(2,1)S(1)} %get-tuple-element.49), channel_id=1, source_target_pairs={{0,12},{2,14},{4,8},{6,10},{8,4},{10,6},{12,0},{14,2},{1,13},{3,15... | collective-permute-start | bytes 196616 | tf_op jit(solution)/shard_map/ppermute | solution.py:317
  27.9 7.5 %collective-permute-start.8 = (bf16[2,64,256]{2,1,0:T(8,128)(2,1)S(1)}, bf16[2,64,256]{2,1,0:T(8,128)(2,1)S(1)}, u32[]{:S(2)}, u32[]{:S(2)}) collective-permute-start(bf16[2,64,256]{2,1,0:T(8,128)(2,1)S(1)} %get-tuple-element.50), channel_id=1, source_target_pairs={{0,6},{2,4},{4,2},{6,0},{8,14},{10,12},{12,10},{14,8},{1,7},{3,5},... | collective-permute-start | bytes 196616 | tf_op jit(solution)/shard_map/ppermute | solution.py:317
  28.3 8.0 %collective-permute-start.9 = (bf16[2,64,256]{2,1,0:T(8,128)(2,1)S(1)}, bf16[2,64,256]{2,1,0:T(8,128)(2,1)S(1)}, u32[]{:S(2)}, u32[]{:S(2)}) collective-permute-start(bf16[2,64,256]{2,1,0:T(8,128)(2,1)S(1)} %get-tuple-element.51), channel_id=1, source_target_pairs={{0,14},{2,12},{4,10},{6,8},{8,6},{10,4},{12,2},{14,0},{1,15},{3,13... | collective-permute-start | bytes 196616 | tf_op jit(solution)/shard_map/ppermute | solution.py:317
  30.5 5.7 %collective-permute-start.10 = (bf16[2,64,256]{2,1,0:T(8,128)(2,1)S(1)}, bf16[2,64,256]{2,1,0:T(8,128)(2,1)S(1)}, u32[]{:S(2)}, u32[]{:S(2)}) collective-permute-start(bf16[2,64,256]{2,1,0:T(8,128)(2,1)S(1)} %get-tuple-element.52), channel_id=1, source_target_pairs={{0,4},{2,6},{4,0},{6,2},{8,12},{10,14},{12,8},{14,10},{1,5},{3,7},... | collective-permute-start | bytes 196616 | tf_op jit(solution)/shard_map/ppermute | solution.py:317
  31.8 8.6 %collective-permute-start.11 = (bf16[2,64,256]{2,1,0:T(8,128)(2,1)S(1)}, bf16[2,64,256]{2,1,0:T(8,128)(2,1)S(1)}, u32[]{:S(2)}, u32[]{:S(2)}) collective-permute-start(bf16[2,64,256]{2,1,0:T(8,128)(2,1)S(1)} %get-tuple-element.53), channel_id=1, source_target_pairs={{0,10},{2,8},{4,14},{6,12},{8,2},{10,0},{12,6},{14,4},{1,11},{3,9}... | collective-permute-start | bytes 196616 | tf_op jit(solution)/shard_map/ppermute | solution.py:317
  33.6 7.1 %collective-permute-start.12 = (bf16[2,64,256]{2,1,0:T(8,128)(2,1)S(1)}, bf16[2,64,256]{2,1,0:T(8,128)(2,1)S(1)}, u32[]{:S(2)}, u32[]{:S(2)}) collective-permute-start(bf16[2,64,256]{2,1,0:T(8,128)(2,1)S(1)} %get-tuple-element.54), channel_id=1, source_target_pairs={{0,8},{2,10},{4,12},{6,14},{8,0},{10,2},{12,4},{14,6},{1,9},{3,11}... | collective-permute-start | bytes 196616 | tf_op jit(solution)/shard_map/ppermute | solution.py:317
  35.4 5.3 %collective-permute-start.13 = (bf16[2,64,256]{2,1,0:T(8,128)(2,1)S(1)}, bf16[2,64,256]{2,1,0:T(8,128)(2,1)S(1)}, u32[]{:S(2)}, u32[]{:S(2)}) collective-permute-start(bf16[2,64,256]{2,1,0:T(8,128)(2,1)S(1)} %get-tuple-element.55), channel_id=1, source_target_pairs={{0,2},{2,0},{4,6},{6,4},{8,10},{10,8},{12,14},{14,12},{1,3},{3,1},... | collective-permute-start | bytes 196616 | tf_op jit(solution)/shard_map/ppermute | solution.py:317
  41.7 6.9 %collective-permute-start.14 = (bf16[2,64,256]{2,1,0:T(8,128)(2,1)S(1)}, bf16[2,64,256]{2,1,0:T(8,128)(2,1)S(1)}, u32[]{:S(2)}, u32[]{:S(2)}) collective-permute-start(bf16[2,64,256]{2,1,0:T(8,128)(2,1)S(1)} %get-tuple-element.58), channel_id=1, source_target_pairs={{0,12},{2,14},{4,8},{6,10},{8,4},{10,6},{12,0},{14,2},{1,13},{3,15... | collective-permute-start | bytes 196616 | tf_op jit(solution)/shard_map/ppermute | solution.py:317
  43.8 6.5 %collective-permute-start.15 = (bf16[2,64,256]{2,1,0:T(8,128)(2,1)S(1)}, bf16[2,64,256]{2,1,0:T(8,128)(2,1)S(1)}, u32[]{:S(2)}, u32[]{:S(2)}) collective-permute-start(bf16[2,64,256]{2,1,0:T(8,128)(2,1)S(1)} %get-tuple-element.59), channel_id=1, source_target_pairs={{0,6},{2,4},{4,2},{6,0},{8,14},{10,12},{12,10},{14,8},{1,7},{3,5},... | collective-permute-start | bytes 196616 | tf_op jit(solution)/shard_map/ppermute | solution.py:317
  43.8 8.6 %collective-permute-start.16 = (bf16[2,64,256]{2,1,0:T(8,128)(2,1)S(1)}, bf16[2,64,256]{2,1,0:T(8,128)(2,1)S(1)}, u32[]{:S(2)}, u32[]{:S(2)}) collective-permute-start(bf16[2,64,256]{2,1,0:T(8,128)(2,1)S(1)} %get-tuple-element.60), channel_id=1, source_target_pairs={{0,14},{2,12},{4,10},{6,8},{8,6},{10,4},{12,2},{14,0},{1,15},{3,13... | collective-permute-start | bytes 196616 | tf_op jit(solution)/shard_map/ppermute | solution.py:317
  46.0 6.4 %collective-permute-start.17 = (bf16[2,64,256]{2,1,0:T(8,128)(2,1)S(1)}, bf16[2,64,256]{2,1,0:T(8,128)(2,1)S(1)}, u32[]{:S(2)}, u32[]{:S(2)}) collective-permute-start(bf16[2,64,256]{2,1,0:T(8,128)(2,1)S(1)} %get-tuple-element.61), channel_id=1, source_target_pairs={{0,4},{2,6},{4,0},{6,2},{8,12},{10,14},{12,8},{14,10},{1,5},{3,7},... | collective-permute-start | bytes 196616 | tf_op jit(solution)/shard_map/ppermute | solution.py:317
  47.6 4.8 %collective-permute-start.20 = (bf16[2,64,256]{2,1,0:T(8,128)(2,1)S(1)}, bf16[2,64,256]{2,1,0:T(8,128)(2,1)S(1)}, u32[]{:S(2)}, u32[]{:S(2)}) collective-permute-start(bf16[2,64,256]{2,1,0:T(8,128)(2,1)S(1)} %get-tuple-element.64), channel_id=1, source_target_pairs={{0,2},{2,0},{4,6},{6,4},{8,10},{10,8},{12,14},{14,12},{1,3},{3,1},... | collective-permute-start | bytes 196616 | tf_op jit(solution)/shard_map/ppermute | solution.py:317
  48.6 7.2 %collective-permute-start.18 = (bf16[2,64,256]{2,1,0:T(8,128)(2,1)S(1)}, bf16[2,64,256]{2,1,0:T(8,128)(2,1)S(1)}, u32[]{:S(2)}, u32[]{:S(2)}) collective-permute-start(bf16[2,64,256]{2,1,0:T(8,128)(2,1)S(1)} %get-tuple-element.62), channel_id=1, source_target_pairs={{0,10},{2,8},{4,14},{6,12},{8,2},{10,0},{12,6},{14,4},{1,11},{3,9}... | collective-permute-start | bytes 196616 | tf_op jit(solution)/shard_map/ppermute | solution.py:317
  50.2 6.5 %collective-permute-start.19 = (bf16[2,64,256]{2,1,0:T(8,128)(2,1)S(1)}, bf16[2,64,256]{2,1,0:T(8,128)(2,1)S(1)}, u32[]{:S(2)}, u32[]{:S(2)}) collective-permute-start(bf16[2,64,256]{2,1,0:T(8,128)(2,1)S(1)} %get-tuple-element.63), channel_id=1, source_target_pairs={{0,8},{2,10},{4,12},{6,14},{8,0},{10,2},{12,4},{14,6},{1,9},{3,11}... | collective-permute-start | bytes 196616 | tf_op jit(solution)/shard_map/ppermute | solution.py:317
  59.1 8.4 %collective-permute-start.21 = (bf16[2,64,256]{2,1,0:T(8,128)(2,1)S(1)}, bf16[2,64,256]{2,1,0:T(8,128)(2,1)S(1)}, u32[]{:S(2)}, u32[]{:S(2)}) collective-permute-start(bf16[2,64,256]{2,1,0:T(8,128)(2,1)S(1)} %get-tuple-element.65), channel_id=1, source_target_pairs={{0,12},{2,14},{4,8},{6,10},{8,4},{10,6},{12,0},{14,2},{1,13},{3,15... | collective-permute-start | bytes 196616 | tf_op jit(solution)/shard_map/ppermute | solution.py:317
  62.1 6.2 %collective-permute-start.22 = (bf16[2,64,256]{2,1,0:T(8,128)(2,1)S(1)}, bf16[2,64,256]{2,1,0:T(8,128)(2,1)S(1)}, u32[]{:S(2)}, u32[]{:S(2)}) collective-permute-start(bf16[2,64,256]{2,1,0:T(8,128)(2,1)S(1)} %get-tuple-element.66), channel_id=1, source_target_pairs={{0,6},{2,4},{4,2},{6,0},{8,14},{10,12},{12,10},{14,8},{1,7},{3,5},... | collective-permute-start | bytes 196616 | tf_op jit(solution)/shard_map/ppermute | solution.py:317
  62.1 10.3 %collective-permute-start.23 = (bf16[2,64,256]{2,1,0:T(8,128)(2,1)S(1)}, bf16[2,64,256]{2,1,0:T(8,128)(2,1)S(1)}, u32[]{:S(2)}, u32[]{:S(2)}) collective-permute-start(bf16[2,64,256]{2,1,0:T(8,128)(2,1)S(1)} %get-tuple-element.67), channel_id=1, source_target_pairs={{0,14},{2,12},{4,10},{6,8},{8,6},{10,4},{12,2},{14,0},{1,15},{3,13... | collective-permute-start | bytes 196616 | tf_op jit(solution)/shard_map/ppermute | solution.py:317
  63.4 9.1 %collective-permute-start.24 = (bf16[2,64,256]{2,1,0:T(8,128)(2,1)S(1)}, bf16[2,64,256]{2,1,0:T(8,128)(2,1)S(1)}, u32[]{:S(2)}, u32[]{:S(2)}) collective-permute-start(bf16[2,64,256]{2,1,0:T(8,128)(2,1)S(1)} %get-tuple-element.68), channel_id=1, source_target_pairs={{0,4},{2,6},{4,0},{6,2},{8,12},{10,14},{12,8},{14,10},{1,5},{3,7},... | collective-permute-start | bytes 196616 | tf_op jit(solution)/shard_map/ppermute | solution.py:317
  65.0 8.4 %collective-permute-start.25 = (bf16[2,64,256]{2,1,0:T(8,128)(2,1)S(1)}, bf16[2,64,256]{2,1,0:T(8,128)(2,1)S(1)}, u32[]{:S(2)}, u32[]{:S(2)}) collective-permute-start(bf16[2,64,256]{2,1,0:T(8,128)(2,1)S(1)} %get-tuple-element.69), channel_id=1, source_target_pairs={{0,10},{2,8},{4,14},{6,12},{8,2},{10,0},{12,6},{14,4},{1,11},{3,9}... | collective-permute-start | bytes 196616 | tf_op jit(solution)/shard_map/ppermute | solution.py:317
  67.4 6.0 %collective-permute-start.26 = (bf16[2,64,256]{2,1,0:T(8,128)(2,1)S(1)}, bf16[2,64,256]{2,1,0:T(8,128)(2,1)S(1)}, u32[]{:S(2)}, u32[]{:S(2)}) collective-permute-start(bf16[2,64,256]{2,1,0:T(8,128)(2,1)S(1)} %get-tuple-element.70), channel_id=1, source_target_pairs={{0,8},{2,10},{4,12},{6,14},{8,0},{10,2},{12,4},{14,6},{1,9},{3,11}... | collective-permute-start | bytes 196616 | tf_op jit(solution)/shard_map/ppermute | solution.py:317
  68.4 5.0 %collective-permute-start.27 = (bf16[2,64,256]{2,1,0:T(8,128)(2,1)S(1)}, bf16[2,64,256]{2,1,0:T(8,128)(2,1)S(1)}, u32[]{:S(2)}, u32[]{:S(2)}) collective-permute-start(bf16[2,64,256]{2,1,0:T(8,128)(2,1)S(1)} %get-tuple-element.71), channel_id=1, source_target_pairs={{0,2},{2,0},{4,6},{6,4},{8,10},{10,8},{12,14},{14,12},{1,3},{3,1},... | collective-permute-start | bytes 196616 | tf_op jit(solution)/shard_map/ppermute | solution.py:317
